TPU v7x, 32 devices: a whole 2x2x4 slice. The times are simulated.
32 devices in a mesh: grp: 2 (over x), dap: 16 (over z, y, core).
Axes of the slice: x: 2, y: 2, z: 4, core: 2. Of those that a mesh axis runs over, the one named last changes fastest.
Arguments:
- alignment_input: bfloat16 [256, 64, 256], P(('grp', 'dap')), parts along dimension 0, may hold values from -17 to 17
- pair_state_input: bfloat16 [128, 64, 128], P(('grp', 'dap')), parts along dimension 0, may hold values from -17 to 17
- residue_number_index: int32 [128], P('grp'), parts along dimension 0, may hold values from 0 to 63
- chain_label: int32 [128], P('grp'), parts along dimension 0, may hold values from 0 to 3, never falling along the last dimension, each value on 1 to 32 neighbouring positions
- alignment_row_mask: int32 [256], P('grp'), parts along dimension 0, may hold values from 0 to 1
- relative_position_table: bfloat16 [66, 128], replicated, may hold values from -3 to 3
- column_query_weight: bfloat16 [256, 256], replicated, may hold values from -12.625 to 12.625
- column_key_weight: bfloat16 [256, 256], replicated, may hold values from -0.25 to 0.25
- column_value_gate_weight: bfloat16 [256, 512], replicated, may hold values from -0.375 to 0.375
- column_output_weight: bfloat16 [256, 256], replicated, may hold values from -0.375 to 0.375
- alignment_transition_up: bfloat16 [256, 1024], replicated, may hold values from -0.375 to 0.375
- alignment_transition_down: bfloat16 [1024, 256], replicated, may hold values from -0.1875 to 0.1875
- outer_input_weight: bfloat16 [256, 64], replicated, may hold values from -0.375 to 0.375
- outer_output_weight: bfloat16 [1024, 128], replicated, may hold values from -2.5 to 2.5
- outgoing_projection_weight: bfloat16 [128, 512], replicated, may hold values from -0.5 to 0.5
- outgoing_output_gate: bfloat16 [128, 128], replicated, may hold values from -0.5 to 0.5
- outgoing_output_weight: bfloat16 [128, 128], replicated, may hold values from -0.5 to 0.5
- incoming_projection_weight: bfloat16 [128, 512], replicated, may hold values from -0.5 to 0.5
- incoming_output_gate: bfloat16 [128, 128], replicated, may hold values from -0.5 to 0.5
- incoming_output_weight: bfloat16 [128, 128], replicated, may hold values from -0.5 to 0.5
- pair_transition_up: bfloat16 [128, 512], replicated, may hold values from -0.5 to 0.5
- pair_transition_down: bfloat16 [512, 128], replicated, may hold values from -0.25 to 0.25
Outputs:
- alignment_output: bfloat16 [256, 64, 256], P('grp', 'dap'), parts along dimension 0
- pair_state_output: bfloat16 [128, 64, 128], P(('grp', 'dap')), parts along dimension 0
There are 2 independent parts, one for each index of `grp`. A program takes and returns all parts, laid end to end along the dimension named above; an argument that names none is the same for every part. Nothing has to cross between parts.
Inputs may be any that keep to these rules, and one draw needn't show every extreme that they name: `chain_label`: chain ids never fall along the residues.
All inputs are finite; a program needn't handle non-finite values.
Results may differ from a plain program's by a relative error of at most 0.012.
Values may be sent and summed in bfloat16 or wider, within the bound.
No kernel may reach another device: no remote copies, remote signals or barrier semaphores. Data moves between devices by JAX's collectives and lax.ppermute only.
A program may use at most 128 MiB of HBM per device.

v0:
```python
import jax
import jax.numpy as jnp
from jax import lax
from jax.sharding import PartitionSpec as P

HM = 8
HEAD_SIZE = 32
CO = 32
MAXREL = 32
NBINS = 66


EPSILON = 1e-05


def layer_normalize(values):
    center = jnp.mean(values, axis=-1, keepdims=True)
    shifted = values - center
    spread = jnp.mean(shifted * shifted, axis=-1, keepdims=True)
    return shifted * lax.rsqrt(spread + EPSILON)


def triangle_inputs(pair_now, weight, gate_weight):
    normed = layer_normalize(pair_now).astype(jnp.bfloat16)
    combined = jnp.einsum("ijc,cf->fij", normed, weight, preferred_element_type=jnp.float32)
    hidden_width = weight.shape[1] // 4
    left_side = (
        jax.nn.sigmoid(combined[hidden_width : 2 * hidden_width]) * combined[:hidden_width]
    ).astype(jnp.bfloat16)
    right_side = (
        jax.nn.sigmoid(combined[3 * hidden_width :]) * combined[2 * hidden_width : 3 * hidden_width]
    ).astype(jnp.bfloat16)
    gating = jax.nn.sigmoid(
        jnp.einsum("ijc,cd->ijd", normed, gate_weight, preferred_element_type=jnp.float32)
    )
    return (left_side, right_side, gating)


def triangle_finish(pair_now, product, gating, final_weight):
    product = lax.optimization_barrier(product)
    normed = layer_normalize(product.transpose(1, 2, 0).astype(jnp.float32)).astype(jnp.bfloat16)
    return pair_now + gating * jnp.einsum(
        "ijc,cd->ijd", normed, final_weight, preferred_element_type=jnp.float32
    )


def incoming_channels(left_side, right_side):
    left_all, right_all = (
        lax.all_to_all(left_side, "dap", split_axis=0, concat_axis=1, tiled=True),
        lax.all_to_all(right_side, "dap", split_axis=0, concat_axis=1, tiled=True),
    )
    partial_out = jnp.einsum(
        "cki,ckj->cij", left_all, right_all, preferred_element_type=jnp.float32
    ).astype(jnp.bfloat16)
    return lax.all_to_all(partial_out, "dap", split_axis=1, concat_axis=0, tiled=True)


def outgoing_gathered(left_side, right_side):
    return jnp.einsum(
        "cik,cjk->cij",
        left_side,
        lax.all_gather(right_side, "dap", axis=1, tiled=True),
        preferred_element_type=jnp.float32,
    ).astype(jnp.bfloat16)


def local(
    alignment_input,
    pair_state_input,
    residue_number_index,
    chain_label,
    alignment_row_mask,
    relative_position_table,
    column_query_weight,
    column_key_weight,
    column_value_gate_weight,
    column_output_weight,
    alignment_transition_up,
    alignment_transition_down,
    outer_input_weight,
    outer_output_weight,
    outgoing_projection_weight,
    outgoing_output_gate,
    outgoing_output_weight,
    incoming_projection_weight,
    incoming_output_gate,
    incoming_output_weight,
    pair_transition_up,
    pair_transition_down,
):
    shard_pieces = lax.axis_size("dap")
    own_rows = pair_state_input.shape[0]
    residue_count = pair_state_input.shape[1]
    channel_count = alignment_input.shape[2]
    head_width = HM * HEAD_SIZE
    first_row = lax.axis_index("dap") * own_rows
    own_index = lax.dynamic_slice_in_dim(residue_number_index, first_row, own_rows)
    own_chain = lax.dynamic_slice_in_dim(chain_label, first_row, own_rows)
    offset = own_index[:, None] - residue_number_index[None, :]
    bin_index = jnp.where(
        own_chain[:, None] == chain_label[None, :],
        jnp.clip(offset + MAXREL, 0, 2 * MAXREL),
        2 * MAXREL + 1,
    )
    one_hot = (bin_index[:, :, None] == jnp.arange(NBINS, dtype=jnp.int32)[None, None, :]).astype(
        jnp.bfloat16
    )
    pair_start = pair_state_input.astype(jnp.float32) + jnp.einsum(
        "ijb,bc->ijc", one_hot, relative_position_table, preferred_element_type=jnp.float32
    )
    live_rows = alignment_row_mask > 0
    live_row_float = live_rows.astype(jnp.float32)

    def attend_one(operands):
        query_col, key_col, value_col = operands
        scores = jnp.einsum("shd,thd->hst", query_col, key_col, preferred_element_type=jnp.float32)
        scores = jnp.where(live_rows[None, None, :], scores, -1000000000.0)
        row_top = jnp.max(scores, axis=-1, keepdims=True)
        raised = jnp.exp(scores - row_top)
        attention = (raised / jnp.sum(raised, axis=-1, keepdims=True)).astype(jnp.bfloat16)
        return jnp.einsum("hst,thd->shd", attention, value_col, preferred_element_type=jnp.float32)

    blocked_view = alignment_input.reshape(
        alignment_input.shape[0], shard_pieces, residue_count // shard_pieces, channel_count
    )
    block_in = lax.all_to_all(blocked_view, "dap", split_axis=1, concat_axis=0, tiled=True)
    depth_rows = block_in.shape[0]
    count_cols = block_in.shape[2]
    current = block_in.reshape(depth_rows, count_cols, channel_count).astype(jnp.float32)
    normed = layer_normalize(current).astype(jnp.bfloat16)
    query_rows = (
        jnp.einsum("sic,ce->sie", normed, column_query_weight, preferred_element_type=jnp.float32)
        * HEAD_SIZE ** (-0.5)
    ).astype(jnp.bfloat16)
    key_row_block = jnp.einsum(
        "sic,ce->sie", normed, column_key_weight, preferred_element_type=jnp.float32
    ).astype(jnp.bfloat16)
    value_gate_pair = jnp.einsum(
        "sic,ce->sie", normed, column_value_gate_weight, preferred_element_type=jnp.float32
    )
    value_rows = value_gate_pair[..., :head_width].astype(jnp.bfloat16)

    def by_column(values):
        return values.transpose(1, 0, 2).reshape(count_cols, depth_rows, HM, HEAD_SIZE)

    attended = lax.map(
        attend_one, (by_column(query_rows), by_column(key_row_block), by_column(value_rows))
    )
    attended = attended.reshape(count_cols, depth_rows, head_width).transpose(1, 0, 2)
    gated_out = (jax.nn.sigmoid(value_gate_pair[..., head_width:]) * attended).astype(jnp.bfloat16)
    current = current + jnp.einsum(
        "sie,ec->sic", gated_out, column_output_weight, preferred_element_type=jnp.float32
    )
    hidden = jax.nn.relu(
        jnp.einsum(
            "sic,cf->sif",
            layer_normalize(current).astype(jnp.bfloat16),
            alignment_transition_up,
            preferred_element_type=jnp.float32,
        )
    ).astype(jnp.bfloat16)
    current = current + jnp.einsum(
        "sif,fc->sic", hidden, alignment_transition_down, preferred_element_type=jnp.float32
    )
    result = current.astype(jnp.bfloat16)
    outer_product_input = jnp.einsum(
        "sic,cf->sif",
        layer_normalize(result.astype(jnp.float32)).astype(jnp.bfloat16),
        outer_input_weight,
        preferred_element_type=jnp.float32,
    )
    outer_product_input = outer_product_input * live_row_float[:, None, None]
    left_part = outer_product_input[..., :CO].astype(jnp.bfloat16)
    right_part = outer_product_input[..., CO:].astype(jnp.bfloat16)
    all_rows = result.shape[0]
    left_cols = left_part.transpose(1, 0, 2)
    right_cols = right_part.transpose(1, 0, 2).reshape(own_rows, all_rows * CO)
    live_count = jnp.sum(live_row_float)
    right_piece = lax.all_gather(right_cols, "dap", axis=0, tiled=True)
    span_rows = right_piece.shape[0]
    products = jnp.einsum(
        "isc,jsd->ijcd",
        left_cols,
        right_piece.reshape(span_rows, all_rows, CO),
        preferred_element_type=jnp.float32,
    )
    products = products.astype(jnp.bfloat16).reshape(own_rows, span_rows, CO * CO)
    outer_mean = (
        jnp.einsum("ijf,fc->ijc", products, outer_output_weight, preferred_element_type=jnp.float32)
        / live_count
    )
    pair_mid = pair_start + outer_mean
    out_left, out_right, out_gating = triangle_inputs(
        pair_mid, outgoing_projection_weight, outgoing_output_gate
    )
    out_product = outgoing_gathered(out_left, out_right)
    pair_after_out = triangle_finish(pair_mid, out_product, out_gating, outgoing_output_weight)
    in_left, in_right, in_gating = triangle_inputs(
        pair_after_out, incoming_projection_weight, incoming_output_gate
    )
    in_product = incoming_channels(in_left, in_right)
    pair_after_in = triangle_finish(pair_after_out, in_product, in_gating, incoming_output_weight)
    pair_expanded = jax.nn.relu(
        jnp.einsum(
            "ijc,cf->ijf",
            layer_normalize(pair_after_in).astype(jnp.bfloat16),
            pair_transition_up,
            preferred_element_type=jnp.float32,
        )
    ).astype(jnp.bfloat16)
    pair_state_output = (
        pair_after_in
        + jnp.einsum(
            "ijf,fc->ijc", pair_expanded, pair_transition_down, preferred_element_type=jnp.float32
        )
    ).astype(jnp.bfloat16)
    return (result, pair_state_output)


def solution(mesh):
    in_specs = (
        P(("grp", "dap"), None, None),
        P(("grp", "dap"), None, None),
        P("grp"),
        P("grp"),
        P("grp"),
        P(),
        P(),
        P(),
        P(),
        P(),
        P(),
        P(),
        P(),
        P(),
        P(),
        P(),
        P(),
        P(),
        P(),
        P(),
        P(),
        P(),
    )
    out_specs = (P("grp", "dap", None), P(("grp", "dap"), None, None))
    return jax.shard_map(local, mesh=mesh, in_specs=in_specs, out_specs=out_specs, check_vma=False)
```

profile of v0, /device:TPU:0, one launch (start us, length us, event | category | flops | bytes accessed | tf_op | source)
XLA Modules:
  0.0 152.0 jit_solution(3229508729659951826)
XLA Ops:
  7.2 1.9 %copy.112 = bf16[8,64,256]{2,0,1:T(8,128)(2,1)} copy(bf16[8,64,256]{2,1,0:T(8,128)(2,1)} %param.24) | data formatting | bytes 524288 | tf_op args[0]
  9.1 7.5 %all-to-all-start = ((bf16[8,16,4,256]{3,0,2,1:T(8,128)(2,1)}), bf16[8,16,4,256]{3,0,2,1:T(8,128)(2,1)S(1)}, u32[]{:S(2)}, u32[]{:S(2)}) async-start(bf16[8,16,4,256]{3,0,2,1:T(8,128)(2,1)} %bitcast.5), calls=%async_computation | async-start | bytes 524288 | tf_op jit(solution)/shard_map/all_to_all | solution.py:126
  16.6 1.3 convert_reduce_fusion.1
  17.9 0.7 dynamic_slice.16
  18.6 0.7 dynamic_slice.17
  19.4 0.7 fusion.143
  20.0 0.7 clamp_select_fusion
  20.8 5.9 %all-to-all-done = bf16[8,16,4,256]{3,0,2,1:T(8,128)(2,1)S(1)} async-done(((bf16[8,16,4,256]{3,0,2,1:T(8,128)(2,1)}), bf16[8,16,4,256]{3,0,2,1:T(8,128)(2,1)S(1)}, u32[]{:S(2)}, u32[]{:S(2)}) %all-to-all-start) | async-done | bytes 262176 | tf_op jit(solution)/shard_map/all_to_all | solution.py:126
  29.4 3.3 %while.10 = (s32[]{:T(128)}, f32[4,128,8,32]{1,3,2,0:T(8,128)S(1)}, bf16[4,128,8,32]{1,3,2,0:T(8,128)(2,1)S(1)}, pred[128]{0:T(512)(128)(4,1)S(1)}, bf16[4,128,8...) while((s32[]{:T(128)}, f32[4,128,8,32]{1,3,2,0:T(8,128)S(1)}, ...), condition=%wide.region_5.6_spmd, body=%wide.region_2.5_spmd.sunk | while | flops 26084608 | bytes 471117 | solution.py:146
  29.7 0.5 fusion.178
  30.6 0.5 fusion.178
  33.6 2.0 %convert_reduce_fusion = (f32[128,4]{0,1:T(4,128)S(1)}, bf16[128,4,256]{2,0,1:T(8,128)(2,1)S(1)}) fusion(f32[128,4,256]{2,0,1:T(8,128)S(1)} %get-tuple-element.70, bf16[1024,256]{1,0:T(8,128)(2,1)S(1)} %copy-done, bf16[256,1024]{1,0:T(8,128)(2,1)} %param.34, f32[128,4]{0,1:T(4,128)S(1)} %add_rsqrt_fusion.7, f32[128,4]{0,1:T(4,128)S(1)} %broadcast_multiply_fusion.7), kind=kOutput, calls=%fused_computation.62 | convolution fusion | flops 538836480 | bytes 1841152 | tf_op jit(solution)/shard_map/sif,fc->sic/dot_general | solution.py:162
  36.5 20.4 %all-gather = bf16[16,4,4096]{2,1,0:T(4,128)(2,1)S(1)} all-gather(bf16[1,4,4096]{2,1,0:T(4,128)(2,1)S(1)} %reshape.221), channel_id=1, replica_groups=mesh['grp'=2,'dap'=16] {'dap'}, dimensions={0}, use_global_device_ids=true | all-gather | bytes 557056 | tf_op jit(solution)/shard_map/all_gather | solution.py:179
  56.9 1.2 reshape.216
  58.1 2.6 %convert_bitcast_fusion = bf16[4,64,32,32]{2,3,0,1:T(8,128)(2,1)} fusion(bf16[64,128,32]{2,1,0:T(8,128)(2,1)S(1)} %reshape.216, bf16[128,4,64]{0,2,1:T(8,128)(2,1)S(1)} %fusion.60), kind=kOutput, calls=%fused_computation.23 | convolution fusion | flops 67371008 | bytes 2654208 | tf_op jit(solution)/shard_map/isc,jsd->ijcd/dot_general | solution.py:181
  60.7 4.5 %copy.125 = bf16[4,64,32,32]{1,3,2,0:T(8,128)(2,1)S(1)} copy(bf16[4,64,32,32]{2,3,0,1:T(8,128)(2,1)} %convert_bitcast_fusion) | data formatting | bytes 1048576 | tf_op jit(solution)/shard_map/convert_element_type | solution.py:187
  65.2 1.1 convolution_divide_fusion
  67.1 0.7 fusion.109
  68.3 35.0 %all-gather.3.cloned.1.call-done = bf16[128,64,64]{0,2,1:T(8,128)(2,1)} async-done(((bf16[128,4,64]{0,2,1:T(8,128)(2,1)}), bf16[128,64,64]{0,2,1:T(8,128)(2,1)}) %all-gather.3.cloned.1.call-update) | async-done | bytes 1048592 | tf_op jit(solution)/shard_map/all_gather | solution.py:62
  103.2 3.9 %copy.128 = bf16[128,64,64]{2,1,0:T(8,128)(2,1)S(1)} copy(bf16[128,64,64]{0,2,1:T(8,128)(2,1)} %all-gather.3.cloned.1.call-done) | data formatting | bytes 2097152 | tf_op jit(solution)/shard_map/all_gather | solution.py:62
  107.1 1.2 convolution_convert_fusion.2
  109.8 0.8 reshape.246
  110.6 3.6 %all-to-all-start.1 = ((bf16[16,2,1024]{2,1,0:T(2,128)(2,1)}), bf16[16,2,1024]{2,1,0:T(2,128)(2,1)S(1)}, u32[]{:S(2)}, u32[]{:S(2)}) async-start(bf16[16,2,1024]{2,1,0:T(2,128)(2,1)} %reshape.246), calls=%async_computation.1 | async-start | bytes 131072 | tf_op jit(solution)/shard_map/all_to_all | solution.py:49
  114.3 0.8 reshape.244
  115.1 6.0 %all-to-all-done.1 = bf16[16,2,1024]{2,1,0:T(2,128)(2,1)S(1)} async-done(((bf16[16,2,1024]{2,1,0:T(2,128)(2,1)}), bf16[16,2,1024]{2,1,0:T(2,128)(2,1)S(1)}, u32[]{:S(2)}, u32[]{:S(2)}) %all-to-all-start.1) | async-done | bytes 65568 | tf_op jit(solution)/shard_map/all_to_all | solution.py:49
  121.1 3.5 %all-to-all-start.2 = ((bf16[16,2,1024]{2,1,0:T(2,128)(2,1)}), bf16[16,2,1024]{2,1,0:T(2,128)(2,1)S(1)}, u32[]{:S(2)}, u32[]{:S(2)}) async-start(bf16[16,2,1024]{2,1,0:T(2,128)(2,1)} %reshape.244), calls=%async_computation.2 | async-start | bytes 131072 | tf_op jit(solution)/shard_map/all_to_all | solution.py:50
  124.6 0.9 copy.140
  125.8 5.7 %all-to-all-done.2 = bf16[16,2,1024]{2,1,0:T(2,128)(2,1)S(1)} async-done(((bf16[16,2,1024]{2,1,0:T(2,128)(2,1)}), bf16[16,2,1024]{2,1,0:T(2,128)(2,1)S(1)}, u32[]{:S(2)}, u32[]{:S(2)}) %all-to-all-start.2) | async-done | bytes 65568 | tf_op jit(solution)/shard_map/all_to_all | solution.py:50
  132.1 0.8 reshape.248
  132.8 3.5 %all-to-all-start.3 = ((bf16[16,2,1024]{2,1,0:T(2,128)(2,1)}), bf16[16,2,1024]{2,1,0:T(2,128)(2,1)S(1)}, u32[]{:S(2)}, u32[]{:S(2)}) async-start(bf16[16,2,1024]{2,1,0:T(2,128)(2,1)} %reshape.248), calls=%async_computation.3 | async-start | bytes 131072 | tf_op jit(solution)/shard_map/all_to_all | solution.py:55
  136.6 6.6 %all-to-all-done.3 = bf16[16,2,1024]{2,1,0:T(2,128)(2,1)S(1)} async-done(((bf16[16,2,1024]{2,1,0:T(2,128)(2,1)}), bf16[16,2,1024]{2,1,0:T(2,128)(2,1)S(1)}, u32[]{:S(2)}, u32[]{:S(2)}) %all-to-all-start.3) | async-done | bytes 65568 | tf_op jit(solution)/shard_map/all_to_all | solution.py:55
  144.1 1.0 fusion.61
  (112 shorter events, 11.4 us)
Async XLA Ops:
  7.2 26.4 %copy-start = (bf16[1024,256]{1,0:T(8,128)(2,1)S(1)}, bf16[1024,256]{1,0:T(8,128)(2,1)}, u32[]{:S(2)}) copy-start(bf16[1024,256]{1,0:T(8,128)(2,1)} %param.35) | copy-start | bytes 1572868
  7.2 20.5 %copy-start.1 = (bf16[256,512]{1,0:T(8,128)(2,1)S(1)}, bf16[256,512]{1,0:T(8,128)(2,1)}, u32[]{:S(2)}) copy-start(bf16[256,512]{1,0:T(8,128)(2,1)} %param.32) | copy-start | bytes 786436
  9.1 19.3 %copy-start.9 = (bf16[256,256]{1,0:T(8,128)(2,1)S(1)}, bf16[256,256]{1,0:T(8,128)(2,1)}, u32[]{:S(2)}) copy-start(bf16[256,256]{1,0:T(8,128)(2,1)} %param.30) | copy-start | bytes 393220
  9.1 17.6 %all-to-all-start = ((bf16[8,16,4,256]{3,0,2,1:T(8,128)(2,1)}), bf16[8,16,4,256]{3,0,2,1:T(8,128)(2,1)S(1)}, u32[]{:S(2)}, u32[]{:S(2)}) async-start(bf16[8,16,4,256]{3,0,2,1:T(8,128)(2,1)} %bitcast.5), calls=%async_computation | async-start | bytes 524288 | tf_op jit(solution)/shard_map/all_to_all | solution.py:126
  16.6 86.7 %all-gather.3.cloned.1.call-start = ((), (), s32[]{:S(2)}) async-start(), calls=%async_computation.4 | async-start | bytes 1114112 | tf_op jit(solution)/shard_map/all_gather | solution.py:62
  27.5 1.3 copy-start.10
  29.4 3.6 %copy-start.11 = (bf16[256,256]{1,0:T(8,128)(2,1)S(1)}, bf16[256,256]{1,0:T(8,128)(2,1)}, u32[]{:S(2)}) copy-start(bf16[256,256]{1,0:T(8,128)(2,1)} %param.33) | copy-start | bytes 393220
  33.3 2.5 %copy-start.14 = (bf16[256,64]{0,1:T(8,128)(2,1)S(1)}, bf16[256,64]{0,1:T(8,128)(2,1)}, u32[]{:S(2)}) copy-start(bf16[256,64]{0,1:T(8,128)(2,1)} %param.36) | copy-start | bytes 98308
  60.7 4.5 %copy-start.8 = (bf16[1024,128]{1,0:T(8,128)(2,1)S(1)}, bf16[1024,128]{1,0:T(8,128)(2,1)}, u32[]{:S(2)}) copy-start(bf16[1024,128]{1,0:T(8,128)(2,1)} %param.37) | copy-start | bytes 786436
  60.7 5.6 %copy-start.4 = (bf16[4,64,128]{2,1,0:T(8,128)(2,1)S(1)}, bf16[4,64,128]{2,1,0:T(8,128)(2,1)}, u32[]{:S(2)}) copy-start(bf16[4,64,128]{2,1,0:T(8,128)(2,1)} %param.25) | copy-start | bytes 196612
  60.7 5.6 %copy-start.7 = (bf16[66,128]{1,0:T(8,128)(2,1)S(1)}, bf16[66,128]{1,0:T(8,128)(2,1)}, u32[]{:S(2)}) copy-start(bf16[66,128]{1,0:T(8,128)(2,1)} %param.29) | copy-start | bytes 50692
  60.7 6.1 %copy-start.2 = (bf16[128,512]{1,0:T(8,128)(2,1)S(1)}, bf16[128,512]{1,0:T(8,128)(2,1)}, u32[]{:S(2)}) copy-start(bf16[128,512]{1,0:T(8,128)(2,1)} %param.38) | copy-start | bytes 393220
  65.2 2.8 %copy-start.15 = (bf16[128,128]{1,0:T(8,128)(2,1)S(1)}, bf16[128,128]{1,0:T(8,128)(2,1)}, u32[]{:S(2)}) copy-start(bf16[128,128]{1,0:T(8,128)(2,1)} %param.39) | copy-start | bytes 98308
  107.1 1.6 %copy-start.5 = (bf16[128,128]{1,0:T(8,128)(2,1)S(1)}, bf16[128,128]{1,0:T(8,128)(2,1)}, u32[]{:S(2)}) copy-start(bf16[128,128]{1,0:T(8,128)(2,1)} %param.40) | copy-start | bytes 98308
  107.1 2.1 %copy-start.3 = (bf16[128,512]{1,0:T(8,128)(2,1)S(1)}, bf16[128,512]{1,0:T(8,128)(2,1)}, u32[]{:S(2)}) copy-start(bf16[128,512]{1,0:T(8,128)(2,1)} %param.41) | copy-start | bytes 393220
  109.6 26.7 %copy-start.16 = (bf16[128,128]{1,0:T(8,128)(2,1)S(1)}, bf16[128,128]{1,0:T(8,128)(2,1)}, u32[]{:S(2)}) copy-start(bf16[128,128]{1,0:T(8,128)(2,1)} %param.42) | copy-start | bytes 98308
  110.6 10.5 %all-to-all-start.1 = ((bf16[16,2,1024]{2,1,0:T(2,128)(2,1)}), bf16[16,2,1024]{2,1,0:T(2,128)(2,1)S(1)}, u32[]{:S(2)}, u32[]{:S(2)}) async-start(bf16[16,2,1024]{2,1,0:T(2,128)(2,1)} %reshape.246), calls=%async_computation.1 | async-start | bytes 131072 | tf_op jit(solution)/shard_map/all_to_all | solution.py:49
  121.1 10.4 %all-to-all-start.2 = ((bf16[16,2,1024]{2,1,0:T(2,128)(2,1)}), bf16[16,2,1024]{2,1,0:T(2,128)(2,1)S(1)}, u32[]{:S(2)}, u32[]{:S(2)}) async-start(bf16[16,2,1024]{2,1,0:T(2,128)(2,1)} %reshape.244), calls=%async_computation.2 | async-start | bytes 131072 | tf_op jit(solution)/shard_map/all_to_all | solution.py:50
  124.6 18.9 %copy-start.6 = (bf16[128,128]{1,0:T(8,128)(2,1)S(1)}, bf16[128,128]{1,0:T(8,128)(2,1)}, u32[]{:S(2)}) copy-start(bf16[128,128]{1,0:T(8,128)(2,1)} %param.43) | copy-start | bytes 98308
  125.7 18.4 %copy-start.12 = (bf16[512,128]{1,0:T(8,128)(2,1)S(1)}, bf16[512,128]{1,0:T(8,128)(2,1)}, u32[]{:S(2)}) copy-start(bf16[512,128]{1,0:T(8,128)(2,1)} %param.45) | copy-start | bytes 393220
  125.7 18.4 %copy-start.13 = (bf16[128,512]{1,0:T(8,128)(2,1)S(1)}, bf16[128,512]{1,0:T(8,128)(2,1)}, u32[]{:S(2)}) copy-start(bf16[128,512]{1,0:T(8,128)(2,1)} %param.44) | copy-start | bytes 393220
  132.8 10.4 %all-to-all-start.3 = ((bf16[16,2,1024]{2,1,0:T(2,128)(2,1)}), bf16[16,2,1024]{2,1,0:T(2,128)(2,1)S(1)}, u32[]{:S(2)}, u32[]{:S(2)}) async-start(bf16[16,2,1024]{2,1,0:T(2,128)(2,1)} %reshape.248), calls=%async_computation.3 | async-start | bytes 131072 | tf_op jit(solution)/shard_map/all_to_all | solution.py:55
Sparse Core Ops, SparseCore 0:
  68.0 35.2 all-gather.2
where the time goes:
time: 153 us; the launch traced here: 152 us
  waiting for transfers between devices  59.1 us (39%)
  blocking collectives  20.4 us (13%)
  local copies, waits for them, and re-layouts  18.9 us (12%)
  starting transfers between devices  18.2 us (12%)
  matrix products  15.1 us (10%)
  between operations  14.6 us (10%)
  other arithmetic  5.58 us (4%)
    all_gather x1, waiting for transfers between devices, outgoing_gathered(): lax.all_gather(right_side, 'dap', axis=1, tiled=True)  35 us
    all_gather x1, blocking collectives, local(): right_piece = lax.all_gather(right_cols, 'dap', axis=0, tiled=True)  20.4 us
    all_to_all x1, starting transfers between devices, local(): lax.all_to_all(blocked_view, 'dap', split_axis=1, concat_axis=0, tiled=True)  7.52 us
    all_to_all x1, waiting for transfers between devices, incoming_channels(): lax.all_to_all(partial_out, 'dap', split_axis=1, concat_axis=0, tiled=True)  6.58 us
    all_to_all x1, waiting for transfers between devices, incoming_channels(): lax.all_to_all(left_side, 'dap', split_axis=0, concat_axis=1, tiled=True)  5.98 us
    all_to_all x1, waiting for transfers between devices, local(): lax.all_to_all(blocked_view, 'dap', split_axis=1, concat_axis=0, tiled=True)  5.87 us
    unnamed x43, local copies, waits for them, and re-layouts  5.77 us
    all_to_all x1, waiting for transfers between devices, incoming_channels(): lax.all_to_all(right_side, 'dap', split_axis=0, concat_axis=1, tiled=True)  5.71 us
  transfers between devices with their start and end apart: 5, of which 5 were waited for; matrix products, arithmetic and copies ran while one was open for 4% of the time, Pallas kernels for 0%

commit v1 on v0

--- a/solution.py
+++ b/solution.py
@@ -44,24 +44,30 @@
     )
 
 
-def incoming_channels(left_side, right_side):
-    left_all, right_all = (
-        lax.all_to_all(left_side, "dap", split_axis=0, concat_axis=1, tiled=True),
-        lax.all_to_all(right_side, "dap", split_axis=0, concat_axis=1, tiled=True),
-    )
-    partial_out = jnp.einsum(
-        "cki,ckj->cij", left_all, right_all, preferred_element_type=jnp.float32
-    ).astype(jnp.bfloat16)
-    return lax.all_to_all(partial_out, "dap", split_axis=1, concat_axis=0, tiled=True)
-
-
-def outgoing_gathered(left_side, right_side):
-    return jnp.einsum(
-        "cik,cjk->cij",
-        left_side,
-        lax.all_gather(right_side, "dap", axis=1, tiled=True),
-        preferred_element_type=jnp.float32,
-    ).astype(jnp.bfloat16)
+def by_channels(left_side, right_side, form):
+    both = jnp.stack([left_side, right_side])
+    both = lax.all_to_all(both, "dap", split_axis=1, concat_axis=2, tiled=True)
+    partial_out = jnp.einsum(form, both[0], both[1], preferred_element_type=jnp.float32)
+    return lax.all_to_all(
+        partial_out.astype(jnp.bfloat16), "dap", split_axis=1, concat_axis=0, tiled=True
+    )
+
+
+def gather_doubling(block):
+    shard_pieces = lax.axis_size("dap")
+    place = lax.axis_index("dap")
+    held = block
+    depth = 0
+    bit = shard_pieces // 2
+    while bit:
+        other = lax.ppermute(held, "dap", [(q, q ^ bit) for q in range(shard_pieces)])
+        upper = (place & bit) != 0
+        first = jnp.where(upper, other, held)
+        second = jnp.where(upper, held, other)
+        held = jnp.stack([first, second], axis=depth)
+        depth += 1
+        bit //= 2
+    return held.reshape((shard_pieces,) + block.shape)
 
 
 def local(
@@ -176,7 +182,7 @@
     left_cols = left_part.transpose(1, 0, 2)
     right_cols = right_part.transpose(1, 0, 2).reshape(own_rows, all_rows * CO)
     live_count = jnp.sum(live_row_float)
-    right_piece = lax.all_gather(right_cols, "dap", axis=0, tiled=True)
+    right_piece = gather_doubling(right_cols).reshape(-1, all_rows * CO)
     span_rows = right_piece.shape[0]
     products = jnp.einsum(
         "isc,jsd->ijcd",
@@ -193,12 +199,12 @@
     out_left, out_right, out_gating = triangle_inputs(
         pair_mid, outgoing_projection_weight, outgoing_output_gate
     )
-    out_product = outgoing_gathered(out_left, out_right)
+    out_product = by_channels(out_left, out_right, "cik,cjk->cij")
     pair_after_out = triangle_finish(pair_mid, out_product, out_gating, outgoing_output_weight)
     in_left, in_right, in_gating = triangle_inputs(
         pair_after_out, incoming_projection_weight, incoming_output_gate
     )
-    in_product = incoming_channels(in_left, in_right)
+    in_product = by_channels(in_left, in_right, "cki,ckj->cij")
     pair_after_in = triangle_finish(pair_after_out, in_product, in_gating, incoming_output_weight)
     pair_expanded = jax.nn.relu(
         jnp.einsum(

time: 153 us -> 109 us (0.71)
  waiting for transfers between devices: 59.1 us -> 43 us
  between operations: 14.6 us -> 1.41 us
  blocking collectives: 20.4 us -> 10.7 us
  local copies, waits for them, and re-layouts: 18.9 us -> 15 us
    all_gather x1 -> x0, waiting for transfers between devices: 35 us -> none  [outgoing_gathered(): lax.all_gather(right_side, 'dap', axis=1, tiled=True)]
    all_gather x1 -> x0, blocking collectives: 20.4 us -> none  [local(): right_piece = lax.all_gather(right_cols, 'dap', axis=0, tiled=True)]
    ppermute x0 -> x4, waiting for transfers between devices: none -> 13.5 us  [gather_doubling(): lax.ppermute(held, 'dap', [(q, q ^ bit) for q in range(shard_pieces)])]
    all_to_all x0 -> x1, blocking collectives: none -> 10.7 us  [by_channels(): both = lax.all_to_all(both, 'dap', split_axis=1, concat_axis=2, tiled=True)]
    all_gather x1 -> x0, local copies, waits for them, and re-layouts: 3.87 us -> none  [outgoing_gathered(): lax.all_gather(right_side, 'dap', axis=1, tiled=True)]
    all_to_all x1, waiting for transfers between devices: 5.87 us -> 9.37 us  [local(): lax.all_to_all(blocked_view, 'dap', split_axis=1, concat_axis=0, tiled=True)]
    all_to_all x3, waiting for transfers between devices: 18.3 us -> 20.1 us  [the longest x2 13.2 us: by_channels(): lax.all_to_all(partial_out.astype(jnp.bfloat16), 'dap', split_axis=1, con...]
    another operation x0 -> x4, local copies, waits for them, and re-layouts: none -> 1.77 us  [the longest x1 1.19 us: local(): right_piece.reshape(span_rows, all_rows, CO)]
  transfers between devices with their start and end apart: 5 -> 8, of which waited for: 5 -> 8; matrix products, arithmetic and copies ran while one was open for 4% -> 3% of each run, Pallas kernels for 0% -> 0%
where the time goes in v1:
time: 109 us; the launch traced here: 108 us
  waiting for transfers between devices  43 us (39%)
  starting transfers between devices  19.5 us (18%)
  local copies, waits for them, and re-layouts  15 us (14%)
  matrix products  14.1 us (13%)
  blocking collectives  10.7 us (10%)
  other arithmetic  4.6 us (4%)
  between operations  1.41 us (1%)
    ppermute x4, waiting for transfers between devices, gather_doubling(): lax.ppermute(held, 'dap', [(q, q ^ bit) for q in range(shard_pieces)])  13.5 us
    all_to_all x2, waiting for transfers between devices, by_channels(): lax.all_to_all(partial_out.astype(jnp.bfloat16), 'dap', split_axis=1, con...  13.2 us
    all_to_all x1, blocking collectives, by_channels(): both = lax.all_to_all(both, 'dap', split_axis=1, concat_axis=2, tiled=True)  10.7 us
    all_to_all x1, waiting for transfers between devices, local(): lax.all_to_all(blocked_view, 'dap', split_axis=1, concat_axis=0, tiled=True)  9.37 us
    all_to_all x1, starting transfers between devices, local(): lax.all_to_all(blocked_view, 'dap', split_axis=1, concat_axis=0, tiled=True)  7.52 us
    all_to_all x2, starting transfers between devices, by_channels(): lax.all_to_all(partial_out.astype(jnp.bfloat16), 'dap', split_axis=1, con...  7.01 us
    all_to_all x1, waiting for transfers between devices, by_channels(): both = lax.all_to_all(both, 'dap', split_axis=1, concat_axis=2, tiled=True)  6.99 us
    unnamed x50, local copies, waits for them, and re-layouts  6.23 us
  transfers between devices with their start and end apart: 8, of which 8 were waited for; matrix products, arithmetic and copies ran while one was open for 3% of the time, Pallas kernels for 0%

profile of v1, /device:TPU:0, one launch (start us, length us, event | category | flops | bytes accessed | tf_op | source)
XLA Modules:
  0.0 108.4 jit_solution(4500750442958835969)
XLA Ops:
  0.7 1.9 %copy.122 = bf16[8,64,256]{2,0,1:T(8,128)(2,1)} copy(bf16[8,64,256]{2,1,0:T(8,128)(2,1)} %param.24) | data formatting | bytes 524288 | tf_op args[0]
  2.5 7.5 %all-to-all-start = ((bf16[8,16,4,256]{3,0,2,1:T(8,128)(2,1)}), bf16[8,16,4,256]{3,0,2,1:T(8,128)(2,1)S(1)}, u32[]{:S(2)}, u32[]{:S(2)}) async-start(bf16[8,16,4,256]{3,0,2,1:T(8,128)(2,1)} %bitcast.5), calls=%async_computation | async-start | bytes 524288 | tf_op jit(solution)/shard_map/all_to_all | solution.py:132
  10.1 0.7 fusion.149
  10.7 9.4 %all-to-all-done = bf16[8,16,4,256]{3,0,2,1:T(8,128)(2,1)S(1)} async-done(((bf16[8,16,4,256]{3,0,2,1:T(8,128)(2,1)}), bf16[8,16,4,256]{3,0,2,1:T(8,128)(2,1)S(1)}, u32[]{:S(2)}, u32[]{:S(2)}) %all-to-all-start) | async-done | bytes 262176 | tf_op jit(solution)/shard_map/all_to_all | solution.py:132
  22.8 3.3 %while.10 = (s32[]{:T(128)}, f32[4,128,8,32]{1,3,2,0:T(8,128)S(1)}, bf16[4,128,8,32]{1,3,2,0:T(8,128)(2,1)S(1)}, pred[128]{0:T(512)(128)(4,1)S(1)}, bf16[4,128,8...) while((s32[]{:T(128)}, f32[4,128,8,32]{1,3,2,0:T(8,128)S(1)}, ...), condition=%wide.region_5.6_spmd, body=%wide.region_2.5_spmd.sunk | while | flops 26084608 | bytes 471117 | solution.py:152
  23.2 0.5 fusion.186
  24.0 0.5 fusion.186
  24.8 0.5 fusion.186
  25.7 0.5 fusion.186
  27.0 2.0 %convert_reduce_fusion = (f32[128,4]{0,1:T(4,128)S(1)}, bf16[128,4,256]{2,0,1:T(8,128)(2,1)S(1)}) fusion(f32[128,4,256]{2,0,1:T(8,128)S(1)} %get-tuple-element.82, bf16[1024,256]{1,0:T(8,128)(2,1)S(1)} %copy-done, bf16[256,1024]{1,0:T(8,128)(2,1)} %param.34, f32[128,4]{0,1:T(4,128)S(1)} %add_rsqrt_fusion.7, f32[128,4]{0,1:T(4,128)S(1)} %broadcast_multiply_fusion.7), kind=kOutput, calls=%fused_computation.62 | convolution fusion | flops 538836480 | bytes 1841152 | tf_op jit(solution)/shard_map/sif,fc->sic/dot_general | solution.py:168
  30.0 1.1 %collective-permute-start = (bf16[4,4096]{1,0:T(4,128)(2,1)S(1)}, bf16[4,4096]{1,0:T(4,128)(2,1)S(1)}, u32[]{:S(2)}, u32[]{:S(2)}) collective-permute-start(bf16[4,4096]{1,0:T(4,128)(2,1)S(1)} %reshape.220), channel_id=1, source_target_pairs={{0,8},{1,9},{2,10},{3,11},{4,12},{5,13},{6,14},{7,15},{8,0},{9,1},... | collective-permute-start | bytes 98312 | tf_op jit(solution)/shard_map/ppermute | solution.py:63
  31.1 3.8 %collective-permute-done = bf16[4,4096]{1,0:T(4,128)(2,1)S(1)} collective-permute-done((bf16[4,4096]{1,0:T(4,128)(2,1)S(1)}, bf16[4,4096]{1,0:T(4,128)(2,1)S(1)}, u32[]{:S(2)}, u32[]{:S(2)}) %collective-permute-start) | collective-permute-done | bytes 32800 | tf_op jit(solution)/shard_map/ppermute | solution.py:63
  35.2 4.1 %collective-permute-done.1 = bf16[2,4,4096]{2,1,0:T(4,128)(2,1)S(1)} collective-permute-done((bf16[2,4,4096]{2,1,0:T(4,128)(2,1)S(1)}, bf16[2,4,4096]{2,1,0:T(4,128)(2,1)S(1)}, u32[]{:S(2)}, u32[]{:S(2)}) %collective-permute-start.1) | collective-permute-done | bytes 65568 | tf_op jit(solution)/shard_map/ppermute | solution.py:63
  39.5 4.9 %collective-permute-done.2 = bf16[2,2,4,4096]{3,2,0,1:T(4,128)(2,1)S(1)} collective-permute-done((bf16[2,2,4,4096]{3,2,0,1:T(4,128)(2,1)S(1)}, bf16[2,2,4,4096]{3,2,0,1:T(4,128)(2,1)S(1)}, u32[]{:S(2)}, u32[]{:S(2)}) %collective-permute-start.2) | collective-permute-done | bytes 131104 | tf_op jit(solution)/shard_map/ppermute | solution.py:63
  44.9 0.6 convert_reduce_fusion.1
  45.7 0.7 collective-permute-done.3
  47.3 1.2 %reshape_reshape_reshape.3 = bf16[64,128,32]{2,1,0:T(8,128)(2,1)S(1)} reshape(bf16[2,2,2,2,4,4096]{5,4,3,2,1,0:T(4,128)(2,1)S(1)} %copy.134) | data formatting | bytes 1048576 | tf_op jit(solution)/shard_map/reshape;reshape;reshape | solution.py:190
  48.5 2.6 %convert_bitcast_fusion = bf16[4,64,32,32]{2,3,0,1:T(8,128)(2,1)} fusion(bf16[64,128,32]{2,1,0:T(8,128)(2,1)S(1)} %reshape_reshape_reshape.3, bf16[128,4,64]{0,2,1:T(8,128)(2,1)S(1)} %fusion.60), kind=kOutput, calls=%fused_computation.23 | convolution fusion | flops 67371008 | bytes 2654208 | tf_op jit(solution)/shard_map/isc,jsd->ijcd/dot_general | solution.py:187
  51.1 4.5 %copy.136 = bf16[4,64,32,32]{1,3,2,0:T(8,128)(2,1)S(1)} copy(bf16[4,64,32,32]{2,3,0,1:T(8,128)(2,1)} %convert_bitcast_fusion) | data formatting | bytes 1048576 | tf_op jit(solution)/shard_map/convert_element_type | solution.py:193
  55.6 1.1 %convolution_divide_fusion = f32[4,64,128]{2,1,0:T(8,128)S(1)} fusion(bf16[4,64,1024]{1,2,0:T(8,128)(2,1)S(1)} %bitcast.307, bf16[1024,128]{1,0:T(8,128)(2,1)S(1)} %copy-done.10, f32[]{:T(128)} %convert_reduce_fusion.1), kind=kOutput, calls=%fused_computation.52 | convolution fusion | flops 67141632 | bytes 917508 | tf_op jit(solution)/shard_map/ijf,fc->ijc/dot_general | solution.py:195
  58.1 10.7 %all_to_all.75 = bf16[16,2,2048]{2,1,0:T(2,128)(2,1)S(1)} all-to-all(bf16[16,2,2048]{2,1,0:T(2,128)(2,1)S(1)} %reshape.244), channel_id=1, replica_groups=mesh['grp'=2,'dap'=16] {'dap'}, dimensions={0} | all-to-all | bytes 262144 | tf_op jit(solution)/shard_map/all_to_all | solution.py:49
  69.7 0.8 reshape.246
  70.4 3.5 %all-to-all-start.2 = ((bf16[16,2,1024]{2,1,0:T(2,128)(2,1)}), bf16[16,2,1024]{2,1,0:T(2,128)(2,1)S(1)}, u32[]{:S(2)}, u32[]{:S(2)}) async-start(bf16[16,2,1024]{2,1,0:T(2,128)(2,1)} %reshape.246), calls=%async_computation.2 | async-start | bytes 131072 | tf_op jit(solution)/shard_map/all_to_all | solution.py:51
  74.2 6.6 %all-to-all-done.2 = bf16[16,2,1024]{2,1,0:T(2,128)(2,1)S(1)} async-done(((bf16[16,2,1024]{2,1,0:T(2,128)(2,1)}), bf16[16,2,1024]{2,1,0:T(2,128)(2,1)S(1)}, u32[]{:S(2)}, u32[]{:S(2)}) %all-to-all-start.2) | async-done | bytes 65568 | tf_op jit(solution)/shard_map/all_to_all | solution.py:51
  82.2 0.9 reshape.248
  83.1 3.5 %all-to-all-start.3 = ((bf16[16,2,2048]{2,1,0:T(2,128)(2,1)}), bf16[16,2,2048]{2,1,0:T(2,128)(2,1)S(1)}, u32[]{:S(2)}, u32[]{:S(2)}) async-start(bf16[16,2,2048]{2,1,0:T(2,128)(2,1)} %reshape.248), calls=%async_computation.3 | async-start | bytes 262144 | tf_op jit(solution)/shard_map/all_to_all | solution.py:49
  86.6 0.9 copy.153
  87.6 7.0 %all-to-all-done.3 = bf16[16,2,2048]{2,1,0:T(2,128)(2,1)S(1)} async-done(((bf16[16,2,2048]{2,1,0:T(2,128)(2,1)}), bf16[16,2,2048]{2,1,0:T(2,128)(2,1)S(1)}, u32[]{:S(2)}, u32[]{:S(2)}) %all-to-all-start.3) | async-done | bytes 131104 | tf_op jit(solution)/shard_map/all_to_all | solution.py:49
  95.3 0.8 reshape.250
  96.1 3.5 %all-to-all-start.4 = ((bf16[16,2,1024]{2,1,0:T(2,128)(2,1)}), bf16[16,2,1024]{2,1,0:T(2,128)(2,1)S(1)}, u32[]{:S(2)}, u32[]{:S(2)}) async-start(bf16[16,2,1024]{2,1,0:T(2,128)(2,1)} %reshape.250), calls=%async_computation.4 | async-start | bytes 131072 | tf_op jit(solution)/shard_map/all_to_all | solution.py:51
  99.9 6.6 %all-to-all-done.4 = bf16[16,2,1024]{2,1,0:T(2,128)(2,1)S(1)} async-done(((bf16[16,2,1024]{2,1,0:T(2,128)(2,1)}), bf16[16,2,1024]{2,1,0:T(2,128)(2,1)S(1)}, u32[]{:S(2)}, u32[]{:S(2)}) %all-to-all-start.4) | async-done | bytes 65568 | tf_op jit(solution)/shard_map/all_to_all | solution.py:51
  107.3 1.0 fusion.61
  (139 shorter events, 13.3 us)
Async XLA Ops:
  0.6 26.4 %copy-start = (bf16[1024,256]{1,0:T(8,128)(2,1)S(1)}, bf16[1024,256]{1,0:T(8,128)(2,1)}, u32[]{:S(2)}) copy-start(bf16[1024,256]{1,0:T(8,128)(2,1)} %param.35) | copy-start | bytes 1572868
  0.6 20.5 %copy-start.1 = (bf16[256,512]{1,0:T(8,128)(2,1)S(1)}, bf16[256,512]{1,0:T(8,128)(2,1)}, u32[]{:S(2)}) copy-start(bf16[256,512]{1,0:T(8,128)(2,1)} %param.32) | copy-start | bytes 786436
  2.5 19.2 %copy-start.11 = (bf16[256,256]{1,0:T(8,128)(2,1)S(1)}, bf16[256,256]{1,0:T(8,128)(2,1)}, u32[]{:S(2)}) copy-start(bf16[256,256]{1,0:T(8,128)(2,1)} %param.30) | copy-start | bytes 393220
  2.5 17.6 %all-to-all-start = ((bf16[8,16,4,256]{3,0,2,1:T(8,128)(2,1)}), bf16[8,16,4,256]{3,0,2,1:T(8,128)(2,1)S(1)}, u32[]{:S(2)}, u32[]{:S(2)}) async-start(bf16[8,16,4,256]{3,0,2,1:T(8,128)(2,1)} %bitcast.5), calls=%async_computation | async-start | bytes 524288 | tf_op jit(solution)/shard_map/all_to_all | solution.py:132
  21.0 1.3 %copy-start.12 = (bf16[256,256]{1,0:T(8,128)(2,1)S(1)}, bf16[256,256]{1,0:T(8,128)(2,1)}, u32[]{:S(2)}) copy-start(bf16[256,256]{1,0:T(8,128)(2,1)} %param.31) | copy-start | bytes 393220
  22.8 3.5 %copy-start.13 = (bf16[256,256]{1,0:T(8,128)(2,1)S(1)}, bf16[256,256]{1,0:T(8,128)(2,1)}, u32[]{:S(2)}) copy-start(bf16[256,256]{1,0:T(8,128)(2,1)} %param.33) | copy-start | bytes 393220
  26.7 2.6 %copy-start.16 = (bf16[256,64]{0,1:T(8,128)(2,1)S(1)}, bf16[256,64]{0,1:T(8,128)(2,1)}, u32[]{:S(2)}) copy-start(bf16[256,64]{0,1:T(8,128)(2,1)} %param.36) | copy-start | bytes 98308
  29.0 15.9 %copy-start.19 = (s32[128]{0:T(128)S(1)}, s32[128]{0:T(128)}, u32[]{:S(2)}) copy-start(s32[128]{0:T(128)} %param.28) | copy-start | bytes 1540
  29.0 16.5 %copy-start.9 = (s32[64]{0:T(128)S(1)}, s32[64]{0:T(128)}, u32[]{:S(2)}) copy-start(s32[64]{0:T(128)} %param.27) | copy-start | bytes 772
  29.0 16.6 %copy-start.8 = (s32[64]{0:T(128)S(1)}, s32[64]{0:T(128)}, u32[]{:S(2)}) copy-start(s32[64]{0:T(128)} %param.26) | copy-start | bytes 772
  30.0 4.9 %collective-permute-start = (bf16[4,4096]{1,0:T(4,128)(2,1)S(1)}, bf16[4,4096]{1,0:T(4,128)(2,1)S(1)}, u32[]{:S(2)}, u32[]{:S(2)}) collective-permute-start(bf16[4,4096]{1,0:T(4,128)(2,1)S(1)} %reshape.220), channel_id=1, source_target_pairs={{0,8},{1,9},{2,10},{3,11},{4,12},{5,13},{6,14},{7,15},{8,0},{9,1},... | collective-permute-start | bytes 98312 | tf_op jit(solution)/shard_map/ppermute | solution.py:63
  34.9 4.3 %collective-permute-start.1 = (bf16[2,4,4096]{2,1,0:T(4,128)(2,1)S(1)}, bf16[2,4,4096]{2,1,0:T(4,128)(2,1)S(1)}, u32[]{:S(2)}, u32[]{:S(2)}) collective-permute-start(bf16[2,4,4096]{2,1,0:T(4,128)(2,1)S(1)} %pad_maximum_fusion.5), channel_id=1, source_target_pairs={{0,4},{1,5},{2,6},{3,7},{4,0},{5,1},{6,2},{7,3},{8,12},{9,13},{10,... | collective-permute-start | bytes 196616 | tf_op jit(solution)/shard_map/ppermute | solution.py:63
  39.4 5.0 %collective-permute-start.2 = (bf16[2,2,4,4096]{3,2,0,1:T(4,128)(2,1)S(1)}, bf16[2,2,4,4096]{3,2,0,1:T(4,128)(2,1)S(1)}, u32[]{:S(2)}, u32[]{:S(2)}) collective-permute-start(bf16[2,2,4,4096]{3,2,0,1:T(4,128)(2,1)S(1)} %pad_maximum_fusion.2), channel_id=1, source_target_pairs={{0,2},{1,3},{2,0},{3,1},{4,6},{5,7},{6,4},{7,5},{8,10},{9,11},{10,... | collective-permute-start | bytes 393224 | tf_op jit(solution)/shard_map/ppermute | solution.py:63
  44.8 1.6 %collective-permute-start.3 = (bf16[2,2,2,4,4096]{4,3,0,1,2:T(4,128)(2,1)S(1)}, bf16[2,2,2,4,4096]{4,3,0,1,2:T(4,128)(2,1)S(1)}, u32[]{:S(2)}, u32[]{:S(2)}) collective-permute-start(bf16[2,2,2,4,4096]{4,3,0,1,2:T(4,128)(2,1)S(1)} %pad_maximum_fusion.1), channel_id=1, source_target_pairs={{0,1},{1,0},{2,3},{3,2},{4,5},{5,4},{6,7},{7,6},{8,9},{9,8},{10,11... | collective-permute-start | bytes 786440 | tf_op jit(solution)/shard_map/ppermute | solution.py:63
  51.1 4.5 %copy-start.10 = (bf16[1024,128]{1,0:T(8,128)(2,1)S(1)}, bf16[1024,128]{1,0:T(8,128)(2,1)}, u32[]{:S(2)}) copy-start(bf16[1024,128]{1,0:T(8,128)(2,1)} %param.37) | copy-start | bytes 786436
  51.1 5.6 %copy-start.4 = (bf16[4,64,128]{2,1,0:T(8,128)(2,1)S(1)}, bf16[4,64,128]{2,1,0:T(8,128)(2,1)}, u32[]{:S(2)}) copy-start(bf16[4,64,128]{2,1,0:T(8,128)(2,1)} %param.25) | copy-start | bytes 196612
  51.1 5.6 %copy-start.7 = (bf16[66,128]{1,0:T(8,128)(2,1)S(1)}, bf16[66,128]{1,0:T(8,128)(2,1)}, u32[]{:S(2)}) copy-start(bf16[66,128]{1,0:T(8,128)(2,1)} %param.29) | copy-start | bytes 50692
  51.1 6.2 %copy-start.2 = (bf16[128,512]{1,0:T(8,128)(2,1)S(1)}, bf16[128,512]{1,0:T(8,128)(2,1)}, u32[]{:S(2)}) copy-start(bf16[128,512]{1,0:T(8,128)(2,1)} %param.38) | copy-start | bytes 393220
  57.7 16.3 %copy-start.17 = (bf16[128,128]{1,0:T(8,128)(2,1)S(1)}, bf16[128,128]{1,0:T(8,128)(2,1)}, u32[]{:S(2)}) copy-start(bf16[128,128]{1,0:T(8,128)(2,1)} %param.39) | copy-start | bytes 98308
  68.8 12.3 %copy-start.5 = (bf16[128,128]{1,0:T(8,128)(2,1)S(1)}, bf16[128,128]{1,0:T(8,128)(2,1)}, u32[]{:S(2)}) copy-start(bf16[128,128]{1,0:T(8,128)(2,1)} %param.40) | copy-start | bytes 98308
  69.1 12.5 %copy-start.3 = (bf16[128,512]{1,0:T(8,128)(2,1)S(1)}, bf16[128,512]{1,0:T(8,128)(2,1)}, u32[]{:S(2)}) copy-start(bf16[128,512]{1,0:T(8,128)(2,1)} %param.41) | copy-start | bytes 393220
  70.4 10.4 %all-to-all-start.2 = ((bf16[16,2,1024]{2,1,0:T(2,128)(2,1)}), bf16[16,2,1024]{2,1,0:T(2,128)(2,1)S(1)}, u32[]{:S(2)}, u32[]{:S(2)}) async-start(bf16[16,2,1024]{2,1,0:T(2,128)(2,1)} %reshape.246), calls=%async_computation.2 | async-start | bytes 131072 | tf_op jit(solution)/shard_map/all_to_all | solution.py:51
  82.2 17.4 %copy-start.18 = (bf16[128,128]{1,0:T(8,128)(2,1)S(1)}, bf16[128,128]{1,0:T(8,128)(2,1)}, u32[]{:S(2)}) copy-start(bf16[128,128]{1,0:T(8,128)(2,1)} %param.42) | copy-start | bytes 98308
  83.1 11.4 %all-to-all-start.3 = ((bf16[16,2,2048]{2,1,0:T(2,128)(2,1)}), bf16[16,2,2048]{2,1,0:T(2,128)(2,1)S(1)}, u32[]{:S(2)}, u32[]{:S(2)}) async-start(bf16[16,2,2048]{2,1,0:T(2,128)(2,1)} %reshape.248), calls=%async_computation.3 | async-start | bytes 262144 | tf_op jit(solution)/shard_map/all_to_all | solution.py:49
  87.6 19.2 %copy-start.6 = (bf16[128,128]{1,0:T(8,128)(2,1)S(1)}, bf16[128,128]{1,0:T(8,128)(2,1)}, u32[]{:S(2)}) copy-start(bf16[128,128]{1,0:T(8,128)(2,1)} %param.43) | copy-start | bytes 98308
  94.8 12.5 %copy-start.14 = (bf16[512,128]{1,0:T(8,128)(2,1)S(1)}, bf16[512,128]{1,0:T(8,128)(2,1)}, u32[]{:S(2)}) copy-start(bf16[512,128]{1,0:T(8,128)(2,1)} %param.45) | copy-start | bytes 393220
  94.8 12.5 %copy-start.15 = (bf16[128,512]{1,0:T(8,128)(2,1)S(1)}, bf16[128,512]{1,0:T(8,128)(2,1)}, u32[]{:S(2)}) copy-start(bf16[128,512]{1,0:T(8,128)(2,1)} %param.44) | copy-start | bytes 393220
  96.1 10.4 %all-to-all-start.4 = ((bf16[16,2,1024]{2,1,0:T(2,128)(2,1)}), bf16[16,2,1024]{2,1,0:T(2,128)(2,1)S(1)}, u32[]{:S(2)}, u32[]{:S(2)}) async-start(bf16[16,2,1024]{2,1,0:T(2,128)(2,1)} %reshape.250), calls=%async_computation.4 | async-start | bytes 131072 | tf_op jit(solution)/shard_map/all_to_all | solution.py:51

commit v2 on v1

--- a/solution.py
+++ b/solution.py
@@ -1,6 +1,8 @@
 import jax
 import jax.numpy as jnp
 from jax import lax
+from jax.experimental import pallas as pl
+from jax.experimental.pallas import tpu as pltpu
 from jax.sharding import PartitionSpec as P
 
 HM = 8
@@ -68,6 +70,295 @@
         depth += 1
         bit //= 2
     return held.reshape((shard_pieces,) + block.shape)
+
+
+LANES = 128
+
+
+def gate_curve(values):
+    return 0.5 + 0.5 * jnp.tanh(0.5 * values)
+
+
+def normalize_channels(values):
+    center = jnp.mean(values, axis=0, keepdims=True)
+    shifted = values - center
+    spread = jnp.mean(shifted * shifted, axis=0, keepdims=True)
+    return (shifted * lax.rsqrt(spread + EPSILON)).astype(jnp.bfloat16)
+
+
+def mix(weight, values):
+    return jnp.dot(weight, values, preferred_element_type=jnp.float32)
+
+
+def fold_halves(first_even, second_even, first_odd, second_odd, low_half):
+    straight = jnp.where(low_half, first_even, second_odd)
+    crossed = jnp.where(low_half, second_even, first_odd)
+    return straight + pltpu.roll(crossed, LANES // 2, 1)
+
+
+def pair_kernel(
+    place_ref,
+    live_ref,
+    parts_ref,
+    pair_ref,
+    bins_ref,
+    table_ref,
+    mean_weight_ref,
+    out_mix_ref,
+    out_gate_ref,
+    out_final_ref,
+    in_mix_ref,
+    in_gate_ref,
+    in_final_ref,
+    up_ref,
+    down_ref,
+    result_ref,
+    wide_ref,
+    right_cols_ref,
+    stack_ref,
+    pair_now_ref,
+    left_ref,
+    right_ref,
+    product_ref,
+    gating_ref,
+    chosen_ref,
+    own_left_ref,
+    own_product_ref,
+):
+    place = place_ref[0]
+    inverse_live = 1.0 / live_ref[0]
+    half = LANES // 2
+    low_half = lax.broadcasted_iota(jnp.int32, (LANES, LANES), 1) < half
+    low_short = lax.broadcasted_iota(jnp.int32, (32, LANES), 1) < half
+    channel = lax.broadcasted_iota(jnp.int32, (LANES, LANES), 0)
+
+    for p in range(16):
+        wide_ref[p * 128 : (p + 1) * 128, :] = parts_ref[p, 128:256, :].astype(jnp.float32)
+    for d in range(0, CO, 2):
+        rows = [
+            wide_ref[pl.ds(par * CO + d + e, 32, stride=2 * CO), :]
+            for e in range(2)
+            for par in range(2)
+        ]
+        right_cols_ref[:, d * half : d * half + LANES] = (
+            jnp.concatenate(rows, axis=0).T.astype(jnp.bfloat16)
+        )
+
+    def first_chunk(g, carry):
+        left_rows = parts_ref[pl.ds(2 * g, 2), 0:128, :].reshape(256, LANES)
+        outer = mix(left_rows, right_cols_ref[...]).astype(jnp.bfloat16)
+        for i in range(8):
+            for d in range(16):
+                stack_ref[d * 32 : (d + 1) * 32, i * LANES : (i + 1) * LANES] = outer[
+                    i * 32 : (i + 1) * 32, d * LANES : (d + 1) * LANES
+                ]
+        mixed = mix(mean_weight_ref[...], stack_ref[...])
+        slabs = []
+        for q in range(4):
+            h = 4 * g + q
+            even = slice(2 * q * LANES, (2 * q + 1) * LANES)
+            odd = slice((2 * q + 1) * LANES, (2 * q + 2) * LANES)
+            outer_mean = fold_halves(
+                mixed[0:128, even], mixed[0:128, odd], mixed[128:256, even], mixed[128:256, odd], low_half
+            )
+            one_hot = (channel == bins_ref[pl.ds(h, 1), :]).astype(jnp.float32).astype(jnp.bfloat16)
+            start = pair_ref[h].astype(jnp.float32) + mix(table_ref[...], one_hot)
+            slab = start + outer_mean * inverse_live
+            pair_now_ref[h] = slab
+            slabs.append(normalize_channels(slab))
+        normed = jnp.concatenate(slabs, axis=1)
+        combined = mix(out_mix_ref[...], normed)
+        left = gate_curve(combined[128:256]) * combined[0:128]
+        right = gate_curve(combined[384:512]) * combined[256:384]
+        gating = gate_curve(mix(out_gate_ref[...], normed))
+        for q in range(4):
+            h = 4 * g + q
+            lanes = slice(q * LANES, (q + 1) * LANES)
+            left_ref[pl.ds(h * 128, 128), :] = left[:, lanes]
+            right_ref[pl.ds(h * 128, 128), :] = right[:, lanes]
+            gating_ref[h] = gating[:, lanes]
+        return carry
+
+    lax.fori_loop(0, 8, first_chunk, 0)
+
+    def outgoing_channels(block, carry):
+        for e in range(8):
+            c = block * 8 + e
+            left = left_ref[pl.ds(c, 32, stride=128), :].astype(jnp.bfloat16)
+            right = right_ref[pl.ds(c, 32, stride=128), :]
+            turned = pltpu.roll(right, half, 1)
+            spread = jnp.concatenate(
+                [
+                    jnp.where(low_short, right, 0.0),
+                    jnp.where(low_short, turned, 0.0),
+                    jnp.where(low_short, 0.0, turned),
+                    jnp.where(low_short, 0.0, right),
+                ],
+                axis=0,
+            ).astype(jnp.bfloat16)
+            product_ref[pl.ds(c, 32, stride=128), :] = lax.dot_general(
+                left, spread, (((1,), (1,)), ((), ())), preferred_element_type=jnp.float32
+            )
+        return carry
+
+    lax.fori_loop(0, 16, outgoing_channels, 0)
+
+    column = lax.broadcasted_iota(jnp.int32, (1, 256), 1)
+    which = column // 32
+    own = which % 4
+    wanted = half * (which // 4) + 32 * (own % 2) + 2 * place + own // 2
+    slab_of = column % 32
+    source = lax.broadcasted_iota(jnp.int32, (LANES, 256), 0)
+    chosen_ref[...] = jnp.zeros_like(chosen_ref)
+
+    def second_chunk(g, carry):
+        products = [
+            normalize_channels(product_ref[pl.ds((4 * g + q) * 128, 128), :]) for q in range(4)
+        ]
+        finished = mix(out_final_ref[...], jnp.concatenate(products, axis=1))
+        slabs = []
+        picks = []
+        for q in range(4):
+            h = 4 * g + q
+            lanes = slice(q * LANES, (q + 1) * LANES)
+            slab = pair_now_ref[h] + gating_ref[h] * finished[:, lanes]
+            pair_now_ref[h] = slab
+            slabs.append(normalize_channels(slab))
+            here = jnp.where(slab_of == h, wanted, -1)
+            picks.append((source == here).astype(jnp.float32).astype(jnp.bfloat16))
+        normed = jnp.concatenate(slabs, axis=1)
+        chosen_ref[...] += mix(normed, jnp.concatenate(picks, axis=0))
+        combined = mix(in_mix_ref[256:512, :], normed)
+        right = gate_curve(combined[128:256]) * combined[0:128]
+        for q in range(4):
+            right_ref[pl.ds((4 * g + q) * 128, 128), :] = right[:, q * LANES : (q + 1) * LANES]
+        return carry
+
+    lax.fori_loop(0, 8, second_chunk, 0)
+
+    combined = mix(in_mix_ref[0:256, :], chosen_ref[...].astype(jnp.bfloat16))
+    own_left = gate_curve(combined[128:256]) * combined[0:128]
+    for m in range(8):
+        part = own_left[:, (m // 4) * LANES : (m // 4 + 1) * LANES]
+        if m % 4:
+            part = pltpu.roll(part, LANES - 32 * (m % 4), 1)
+        own_left_ref[m * 128 : (m + 1) * 128, :] = part
+
+    def incoming_channels(block, carry):
+        for e in range(8):
+            c = block * 8 + e
+            left = own_left_ref[pl.ds(c, 8, stride=128), :][:, 0:32].astype(jnp.bfloat16)
+            right = right_ref[pl.ds(c, 32, stride=128), :].astype(jnp.bfloat16)
+            own_product_ref[pl.ds(c, 8, stride=128), :] = mix(left, right)
+        return carry
+
+    lax.fori_loop(0, 16, incoming_channels, 0)
+
+    def own_block(m):
+        return own_product_ref[m * 128 : (m + 1) * 128, :]
+
+    products = [
+        normalize_channels(
+            fold_halves(
+                own_block(2 * t), own_block(2 * t + 1), own_block(4 + 2 * t), own_block(5 + 2 * t), low_half
+            )
+        )
+        for t in range(2)
+    ]
+    finished = mix(in_final_ref[...], jnp.concatenate(products, axis=1))
+    own_pair = jnp.concatenate([pair_now_ref[2 * place + t] for t in range(2)], axis=1)
+    gating = gate_curve(mix(in_gate_ref[...], normalize_channels(own_pair)))
+    own_pair = own_pair + gating * finished
+    hidden = jnp.maximum(mix(up_ref[...], normalize_channels(own_pair)), 0.0).astype(jnp.bfloat16)
+    own_pair = (own_pair + mix(down_ref[...], hidden)).astype(jnp.bfloat16)
+    lane = lax.broadcasted_iota(jnp.int32, (LANES, LANES), 1)
+    back = half * (channel // half) + 32 * (channel % 2) + (channel % half) // 2
+    order = (lane == back).astype(jnp.float32).astype(jnp.bfloat16)
+    for t in range(2):
+        result_ref[t * 128 : (t + 1) * 128, :] = lax.dot_general(
+            order,
+            own_pair[:, t * LANES : (t + 1) * LANES],
+            (((1,), (1,)), ((), ())),
+            preferred_element_type=jnp.float32,
+        ).astype(jnp.bfloat16)
+
+
+def lanes_order(values):
+    lead = values.shape[:-1]
+    halves = values.reshape(lead + (values.shape[-1] // 2, 2))
+    return jnp.swapaxes(halves, -1, -2).reshape(values.shape)
+
+
+def pair_whole(
+    left_part,
+    right_part,
+    pair_state_input,
+    bin_all,
+    live_count,
+    relative_position_table,
+    outer_output_weight,
+    outgoing_projection_weight,
+    outgoing_output_gate,
+    outgoing_output_weight,
+    incoming_projection_weight,
+    incoming_output_gate,
+    incoming_output_weight,
+    pair_transition_up,
+    pair_transition_down,
+):
+    width = pair_state_input.shape[2]
+    own_pair = lanes_order(pair_state_input.transpose(0, 2, 1))
+    own_pair = own_pair.reshape(2, 2, width, 64).transpose(0, 2, 1, 3).reshape(2, width, LANES)
+    pair_all = gather_doubling(own_pair).reshape(32, width, LANES)
+    parts = jnp.concatenate([left_part.reshape(128, LANES), right_part.reshape(128, LANES)], axis=0)
+    parts_all = gather_doubling(parts)
+    bins = lanes_order(bin_all).reshape(32, LANES)
+    table = jnp.pad(relative_position_table, ((0, LANES - NBINS), (0, 0))).T
+    mean_weight = (
+        outer_output_weight.reshape(CO, 16, 2, width).transpose(2, 3, 1, 0).reshape(2 * width, 16 * CO)
+    )
+    place = lax.axis_index("dap").astype(jnp.int32).reshape(1)
+    vmem = pl.BlockSpec(memory_space=pltpu.VMEM)
+    smem = pl.BlockSpec(memory_space=pltpu.SMEM)
+    tall = (32 * 128, LANES)
+    result = pl.pallas_call(
+        pair_kernel,
+        out_shape=jax.ShapeDtypeStruct((256, LANES), jnp.bfloat16),
+        in_specs=[smem, smem] + [vmem] * 13,
+        out_specs=vmem,
+        scratch_shapes=[
+            pltpu.VMEM((2048, LANES), jnp.float32),
+            pltpu.VMEM((128, 2048), jnp.bfloat16),
+            pltpu.VMEM((512, 1024), jnp.bfloat16),
+            pltpu.VMEM((32, 128, LANES), jnp.float32),
+            pltpu.VMEM(tall, jnp.float32),
+            pltpu.VMEM(tall, jnp.float32),
+            pltpu.VMEM(tall, jnp.float32),
+            pltpu.VMEM((32, 128, LANES), jnp.float32),
+            pltpu.VMEM((128, 256), jnp.float32),
+            pltpu.VMEM((1024, LANES), jnp.float32),
+            pltpu.VMEM((1024, LANES), jnp.float32),
+        ],
+        compiler_params=pltpu.CompilerParams(vmem_limit_bytes=40 * 1024 * 1024),
+        name="pair_whole",
+    )(
+        place,
+        live_count.reshape(1),
+        parts_all,
+        pair_all,
+        bins,
+        table,
+        mean_weight,
+        outgoing_projection_weight.T,
+        outgoing_output_gate.T,
+        outgoing_output_weight.T,
+        incoming_projection_weight.T,
+        incoming_output_gate.T,
+        incoming_output_weight.T,
+        pair_transition_up.T,
+        pair_transition_down.T,
+    )
+    return result.reshape(pair_state_input.shape)
 
 
 def local(
@@ -102,12 +393,16 @@
     first_row = lax.axis_index("dap") * own_rows
     own_index = lax.dynamic_slice_in_dim(residue_number_index, first_row, own_rows)
     own_chain = lax.dynamic_slice_in_dim(chain_label, first_row, own_rows)
-    offset = own_index[:, None] - residue_number_index[None, :]
-    bin_index = jnp.where(
-        own_chain[:, None] == chain_label[None, :],
-        jnp.clip(offset + MAXREL, 0, 2 * MAXREL),
-        2 * MAXREL + 1,
-    )
+
+    def bins_of(index, chain):
+        offset = index[:, None] - residue_number_index[None, :]
+        return jnp.where(
+            chain[:, None] == chain_label[None, :],
+            jnp.clip(offset + MAXREL, 0, 2 * MAXREL),
+            2 * MAXREL + 1,
+        )
+
+    bin_index = bins_of(own_index, own_chain)
     one_hot = (bin_index[:, :, None] == jnp.arange(NBINS, dtype=jnp.int32)[None, None, :]).astype(
         jnp.bfloat16
     )
@@ -179,6 +474,27 @@
     left_part = outer_product_input[..., :CO].astype(jnp.bfloat16)
     right_part = outer_product_input[..., CO:].astype(jnp.bfloat16)
     all_rows = result.shape[0]
+    if all_rows == LANES and 2 * residue_count == LANES and own_rows == 4:
+        return (
+            result,
+            pair_whole(
+                left_part.transpose(1, 2, 0),
+                right_part.transpose(1, 2, 0),
+                pair_state_input,
+                bins_of(residue_number_index, chain_label),
+                jnp.sum(live_row_float),
+                relative_position_table,
+                outer_output_weight,
+                outgoing_projection_weight,
+                outgoing_output_gate,
+                outgoing_output_weight,
+                incoming_projection_weight,
+                incoming_output_gate,
+                incoming_output_weight,
+                pair_transition_up,
+                pair_transition_down,
+            ),
+        )
     left_cols = left_part.transpose(1, 0, 2)
     right_cols = right_part.transpose(1, 0, 2).reshape(own_rows, all_rows * CO)
     live_count = jnp.sum(live_row_float)

time: 109 us -> 93.2 us (0.86)
  Pallas kernels: 0 us -> 26.7 us
  waiting for transfers between devices: 43 us -> 23.2 us
  blocking collectives: 10.7 us -> 0 us
  local copies, waits for them, and re-layouts: 15 us -> 9.82 us
  starting transfers between devices: 19.5 us -> 14.9 us
  matrix products: 14.1 us -> 9.65 us
  other arithmetic: 4.6 us -> 7.23 us
    pallas_call x0 -> x1, Pallas kernels: none -> 26.7 us  [pair_whole(): pl.pallas_call(pair_kernel, out_shape=jax.ShapeDtypeStruct((256, LANES),...]
    all_to_all x3 -> x0, waiting for transfers between devices: 20.1 us -> none  [the longest x2 13.2 us: by_channels(): lax.all_to_all(partial_out.astype(jnp.bfloat16), 'dap', split_axis=1, con...]
    all_to_all x1 -> x0, blocking collectives: 10.7 us -> none  [by_channels(): both = lax.all_to_all(both, 'dap', split_axis=1, concat_axis=2, tiled=True)]
    all_to_all x3 -> x0, starting transfers between devices: 10.5 us -> none  [the longest x2 7.01 us: by_channels(): lax.all_to_all(partial_out.astype(jnp.bfloat16), 'dap', split_axis=1, con...]
    ppermute x4 -> x8, waiting for transfers between devices: 13.5 us -> 23.2 us  [gather_doubling(): lax.ppermute(held, 'dap', [(q, q ^ bit) for q in range(shard_pieces)])]
    all_to_all x1, waiting for transfers between devices: 9.37 us -> 0.01 us  [local(): lax.all_to_all(blocked_view, 'dap', split_axis=1, concat_axis=0, tiled=True)]
    dot_general x12 -> x0, matrix products: 7.14 us -> none  [the longest x1 2.61 us: local(): jnp.einsum('isc,jsd->ijcd', left_cols, right_piece.reshape(span_rows, all...]
    ppermute x4 -> x8, starting transfers between devices: 1.49 us -> 7.37 us  [gather_doubling(): lax.ppermute(held, 'dap', [(q, q ^ bit) for q in range(shard_pieces)])]
  transfers between devices with their start and end apart: 8 -> 9, of which waited for: 8 -> 6; matrix products, arithmetic and copies ran while one was open for 3% -> 10% of each run, Pallas kernels for 0% -> 0%
where the time goes in v2:
time: 93.2 us; the launch traced here: 92.6 us
  Pallas kernels  26.7 us (29%)
  waiting for transfers between devices  23.2 us (25%)
  starting transfers between devices  14.9 us (16%)
  local copies, waits for them, and re-layouts  9.82 us (11%)
  matrix products  9.65 us (10%)
  other arithmetic  7.23 us (8%)
  between operations  1.18 us (1%)
    pallas_call x1, Pallas kernels, pair_whole(): pl.pallas_call(pair_kernel, out_shape=jax.ShapeDtypeStruct((256, LANES),...  26.7 us
    ppermute x8, waiting for transfers between devices, gather_doubling(): lax.ppermute(held, 'dap', [(q, q ^ bit) for q in range(shard_pieces)])  23.2 us
    all_to_all x1, starting transfers between devices, local(): lax.all_to_all(blocked_view, 'dap', split_axis=1, concat_axis=0, tiled=True)  7.52 us
    ppermute x8, starting transfers between devices, gather_doubling(): lax.ppermute(held, 'dap', [(q, q ^ bit) for q in range(shard_pieces)])  7.37 us
    another operation x16, other arithmetic, gather_doubling(): held = jnp.stack([first, second], axis=depth)  5.36 us
    unnamed x50, local copies, waits for them, and re-layouts  4.24 us
    dot_general x1, matrix products, local(): jnp.einsum('sif,fc->sic', hidden, alignment_transition_down, preferred_el...  1.98 us
    dot_general x1, matrix products, local(): jnp.einsum('sic,ce->sie', normed, column_key_weight, preferred_element_ty...  1.94 us
  transfers between devices with their start and end apart: 9, of which 6 were waited for; matrix products, arithmetic and copies ran while one was open for 10% of the time, Pallas kernels for 0%

profile of v2, /device:TPU:0, one launch (start us, length us, event | category | flops | bytes accessed | tf_op | source)
XLA Modules:
  0.0 92.6 jit_solution(9677517440351969386)
XLA Ops:
  0.7 1.9 %copy.154 = bf16[8,64,256]{2,0,1:T(8,128)(2,1)} copy(bf16[8,64,256]{2,1,0:T(8,128)(2,1)} %param.24) | data formatting | bytes 524288 | tf_op args[0]
  2.5 7.5 %all-to-all-start = ((bf16[8,16,4,256]{3,0,2,1:T(8,128)(2,1)}), bf16[8,16,4,256]{3,0,2,1:T(8,128)(2,1)S(1)}, u32[]{:S(2)}, u32[]{:S(2)}) async-start(bf16[8,16,4,256]{3,0,2,1:T(8,128)(2,1)} %bitcast.5), calls=%async_computation | async-start | bytes 524288 | tf_op jit(solution)/shard_map/all_to_all | solution.py:427
  10.1 2.9 %collective-permute-start.4 = (bf16[2,128,128]{1,2,0:T(8,128)(2,1)S(1)}, bf16[2,128,128]{1,2,0:T(8,128)(2,1)S(1)}, u32[]{:S(2)}, u32[]{:S(2)}) collective-permute-start(bf16[2,128,128]{1,2,0:T(8,128)(2,1)S(1)} %bitcast.250), channel_id=1, source_target_pairs={{0,8},{1,9},{2,10},{3,11},{4,12},{5,13},{6,14},{7,15},{8,0},{9,1},... | collective-permute-start | bytes 196616 | tf_op jit(solution)/shard_map/ppermute | solution.py:65
  13.6 8.9 %collective-permute-done.4 = bf16[2,128,128]{1,2,0:T(8,128)(2,1)S(1)} collective-permute-done((bf16[2,128,128]{1,2,0:T(8,128)(2,1)S(1)}, bf16[2,128,128]{1,2,0:T(8,128)(2,1)S(1)}, u32[]{:S(2)}, u32[]{:S(2)}) %collective-permute-start.4) | collective-permute-done | bytes 65568 | tf_op jit(solution)/shard_map/ppermute | solution.py:65
  23.7 0.4 fusion.64
  25.1 1.9 %fusion.43 = bf16[4,128,256]{2,1,0:T(8,128)(2,1)} fusion(bf16[256,256]{1,0:T(8,128)(2,1)} %param.31, f32[128,4]{0,1:T(4,128)S(1)} %rsqrt.28, f32[128,4]{0,1:T(4,128)S(1)} %div.32, bf16[8,16,4,256]{3,0,2,1:T(8,128)(2,1)S(1)} %all-to-all-done), kind=kOutput, calls=%fused_computation.30 | convolution fusion | flops 67764224 | bytes 659456 | tf_op jit(solution)/shard_map/sic,ce->sie/dot_general | solution.py:436
  27.0 1.1 %copy.163 = bf16[4,128,256]{1,2,0:T(8,128)(2,1)S(1)} copy(bf16[4,128,256]{2,1,0:T(8,128)(2,1)} %fusion.43) | data formatting | bytes 524288 | tf_op jit(solution)/shard_map/convert_element_type | solution.py:438
  28.1 3.3 %while.10 = (s32[]{:T(128)}, f32[4,128,8,32]{1,3,2,0:T(8,128)S(1)}, bf16[4,128,8,32]{1,3,2,0:T(8,128)(2,1)S(1)}, pred[128]{0:T(512)(128)(4,1)S(1)}, bf16[4,128,8...) while((s32[]{:T(128)}, f32[4,128,8,32]{1,3,2,0:T(8,128)S(1)}, ...), condition=%wide.region_5.6_spmd, body=%wide.region_2.5_spmd.sunk | while | flops 26084608 | bytes 471125 | solution.py:447
  28.5 0.5 fusion.108
  29.3 0.5 fusion.108
  30.1 0.5 fusion.108
  31.0 0.5 fusion.108
  31.4 1.0 %copy.164 = f32[4,128,256]{2,1,0:T(8,128)} copy(f32[4,128,256]{1,2,0:T(8,128)S(1)} %bitcast.241) | data formatting | bytes 1048576 | tf_op jit(solution)/shard_map/reshape | solution.py:450
  32.5 1.4 %fusion.86 = (f32[128,4]{0,1:T(4,128)S(1)}, f32[128,4,256]{2,0,1:T(8,128)S(1)}) fusion(bf16[256,256]{1,0:T(8,128)(2,1)S(1)} %copy-done.16, f32[4,128,256]{2,1,0:T(8,128)} %copy.164, f32[128,4,512]{2,0,1:T(8,128)S(1)} %fusion.64, bf16[8,16,4,256]{3,0,2,1:T(8,128)(2,1)S(1)} %all-to-all-done), kind=kOutput, calls=%fused_computation.110 | convolution fusion | flops 68156928 | bytes 1968128 | tf_op jit(solution)/shard_map/sie,ec->sic/dot_general | solution.py:452
  34.2 2.0 %convert_reduce_fusion = (f32[128,4]{0,1:T(4,128)S(1)}, bf16[128,4,256]{2,0,1:T(8,128)(2,1)S(1)}) fusion(f32[128,4,256]{2,0,1:T(8,128)S(1)} %get-tuple-element.86, bf16[1024,256]{1,0:T(8,128)(2,1)S(1)} %copy-done, bf16[256,1024]{1,0:T(8,128)(2,1)} %param.34, f32[128,4]{0,1:T(4,128)S(1)} %add_rsqrt_fusion.2, f32[128,4]{0,1:T(4,128)S(1)} %broadcast_multiply_fusion.2), kind=kOutput, calls=%fused_computation.37 | convolution fusion | flops 538836480 | bytes 1841152 | tf_op jit(solution)/shard_map/sif,fc->sic/dot_general | solution.py:463
  37.2 1.8 %collective-permute-start.5 = (bf16[2,2,128,128]{2,3,1,0:T(8,128)(2,1)S(1)}, bf16[2,2,128,128]{2,3,1,0:T(8,128)(2,1)S(1)}, u32[]{:S(2)}, u32[]{:S(2)}) collective-permute-start(bf16[2,2,128,128]{2,3,1,0:T(8,128)(2,1)S(1)} %pad_maximum_fusion.7), channel_id=1, source_target_pairs={{0,4},{1,5},{2,6},{3,7},{4,0},{5,1},{6,2},{7,3},{8,12},{9,13},{10,... | collective-permute-start | bytes 393224 | tf_op jit(solution)/shard_map/ppermute | solution.py:65
  39.0 3.7 %collective-permute-done = bf16[256,128]{1,0:T(8,128)(2,1)S(1)} collective-permute-done((bf16[256,128]{1,0:T(8,128)(2,1)S(1)}, bf16[256,128]{1,0:T(8,128)(2,1)S(1)}, u32[]{:S(2)}, u32[]{:S(2)}) %collective-permute-start) | collective-permute-done | bytes 65568 | tf_op jit(solution)/shard_map/ppermute | solution.py:65
  42.8 0.7 collective-permute-done.5
  43.6 1.6 %collective-permute-start.6 = (bf16[2,2,2,128,128]{3,4,2,0,1:T(8,128)(2,1)S(1)}, bf16[2,2,2,128,128]{3,4,2,0,1:T(8,128)(2,1)S(1)}, u32[]{:S(2)}, u32[]{:S(2)}) collective-permute-start(bf16[2,2,2,128,128]{3,4,2,0,1:T(8,128)(2,1)S(1)} %pad_maximum_fusion.5), channel_id=1, source_target_pairs={{0,2},{1,3},{2,0},{3,1},{4,6},{5,7},{6,4},{7,5},{8,10},{9,11},{10,... | collective-permute-start | bytes 786440 | tf_op jit(solution)/shard_map/ppermute | solution.py:65
  45.2 2.9 %collective-permute-done.1 = bf16[2,256,128]{2,1,0:T(8,128)(2,1)S(1)} collective-permute-done((bf16[2,256,128]{2,1,0:T(8,128)(2,1)S(1)}, bf16[2,256,128]{2,1,0:T(8,128)(2,1)S(1)}, u32[]{:S(2)}, u32[]{:S(2)}) %collective-permute-start.1) | collective-permute-done | bytes 131104 | tf_op jit(solution)/shard_map/ppermute | solution.py:65
  48.1 0.7 collective-permute-start.2
  48.8 3.4 %collective-permute-done.6 = bf16[2,2,2,128,128]{3,4,2,0,1:T(8,128)(2,1)S(1)} collective-permute-done((bf16[2,2,2,128,128]{3,4,2,0,1:T(8,128)(2,1)S(1)}, bf16[2,2,2,128,128]{3,4,2,0,1:T(8,128)(2,1)S(1)}, u32[]{:S(2)}, u32[]{:S(2)}) %collective-permute-start.6) | collective-permute-done | bytes 262176 | tf_op jit(solution)/shard_map/ppermute | solution.py:65
  52.2 0.9 pad_maximum_fusion.3
  53.1 3.6 %collective-permute-done.2 = bf16[2,2,256,128]{3,2,1,0:T(8,128)(2,1)S(1)} collective-permute-done((bf16[2,2,256,128]{3,2,1,0:T(8,128)(2,1)S(1)}, bf16[2,2,256,128]{3,2,1,0:T(8,128)(2,1)S(1)}, u32[]{:S(2)}, u32[]{:S(2)}) %collective-permute-start.2) | collective-permute-done | bytes 262176 | tf_op jit(solution)/shard_map/ppermute | solution.py:65
  56.7 0.9 pad_maximum_fusion.2
  57.6 0.6 convert_reduce_fusion.1
  60.0 0.9 copy.183
  60.9 1.1 %select_bitcast_fusion.1 = (bf16[2,2,2,1,2,128,128]{5,6,4,0,1,2,3:T(8,128)(2,1)S(1)}, bf16[2,2,2,1,2,128,128]{5,6,4,0,1,2,3:T(8,128)(2,1)S(1)}) fusion(bf16[2,2,2,2,128,128]{4,5,3,0,1,2:T(8,128)(2,1)} %collective-permute-done.7, pred[]{:T(512)S(6)} %ne.16, bf16[2,2,1,2,128,128]{4,5,3,0,1,2:T(8,128)(2,1)S(1)} %get-tuple-element.70, ...), kind=kLoop, calls=%fused_computation.57 | loop fusion | flops 786432 | bytes 2097153 | tf_op jit(solution)/shard_map/stack | solution.py:69
  62.0 1.1 %pad_maximum_fusion.1 = bf16[2,2,2,2,2,128,128]{5,6,4,0,1,2,3:T(8,128)(2,1)} fusion(bf16[2,2,2,1,2,128,128]{5,6,4,0,1,2,3:T(8,128)(2,1)S(1)} %get-tuple-element.66, bf16[2,2,2,1,2,128,128]{5,6,4,0,1,2,3:T(8,128)(2,1)S(1)} %get-tuple-element.65), kind=kLoop, calls=%fused_computation.34 | loop fusion | flops 524288 | bytes 2097152 | tf_op jit(solution)/shard_map/stack | solution.py:69
  63.1 1.6 %copy.169 = bf16[2,2,2,2,2,128,128]{6,5,4,3,2,1,0:T(8,128)(2,1)S(1)} copy(bf16[2,2,2,2,2,128,128]{5,6,4,0,1,2,3:T(8,128)(2,1)} %pad_maximum_fusion.1) | data formatting | bytes 2097152 | tf_op jit(solution)/shard_map/stack | solution.py:69
  64.7 1.1 %select_bitcast_fusion.3 = (bf16[2,2,2,1,256,128]{5,4,3,2,1,0:T(8,128)(2,1)S(1)}, bf16[2,2,2,1,256,128]{5,4,3,2,1,0:T(8,128)(2,1)S(1)}) fusion(bf16[2,2,2,256,128]{4,3,2,1,0:T(8,128)(2,1)} %collective-permute-done.3, pred[]{:T(512)S(6)} %ne.16, bf16[2,2,1,256,128]{4,3,2,1,0:T(8,128)(2,1)S(1)} %get-tuple-element.72, ...), kind=kLoop, calls=%fused_computation.59 | loop fusion | flops 786432 | bytes 2097153 | tf_op jit(solution)/shard_map/stack | solution.py:69
  66.0 26.7 %pair_whole.1 = bf16[256,128]{1,0:T(8,128)(2,1)} custom-call(s32[1]{0:T(128)} %bitcast.24.place_ref, f32[1]{0:T(128)} %bitcast.25.live_ref, bf16[16,256,128]{2,1,0:T(8,128)(2,1)S(1)} %bitcast.230, bf16[32,128,128]{2,1,0:T(8,128)(2,1)S(1)} %bitcast.229, s32[32,128]{1,0:T(8,128)S(1)} %select_n.135.bins_ref, bf16[128,128]{1,0:T(8,128)(2,1)S(1)} %pad_bitcast_fusion.table_ref, ...), custom_call_target="tpu_custom_call" | custom-call | tf_op jit(solution)/shard_map/pair_whole/pallas_call | solution.py:324
  (106 shorter events, 7.4 us)
Async XLA Ops:
  0.6 33.5 %copy-start = (bf16[1024,256]{1,0:T(8,128)(2,1)S(1)}, bf16[1024,256]{1,0:T(8,128)(2,1)}, u32[]{:S(2)}) copy-start(bf16[1024,256]{1,0:T(8,128)(2,1)} %param.35) | copy-start | bytes 1572868
  0.6 9.4 %copy-start.7 = (bf16[4,64,128]{2,1,0:T(8,128)(2,1)S(1)}, bf16[4,64,128]{2,1,0:T(8,128)(2,1)}, u32[]{:S(2)}) copy-start(bf16[4,64,128]{2,1,0:T(8,128)(2,1)} %param.25) | copy-start | bytes 196612
  0.7 12.3 %copy-start.13 = (s32[64]{0:T(128)S(1)}, s32[64]{0:T(128)}, u32[]{:S(2)}) copy-start(s32[64]{0:T(128)} %param.26) | copy-start | bytes 772
  0.7 12.5 %copy-start.14 = (s32[64]{0:T(128)S(1)}, s32[64]{0:T(128)}, u32[]{:S(2)}) copy-start(s32[64]{0:T(128)} %param.27) | copy-start | bytes 772
  0.7 12.9 %copy-start.18 = (s32[128]{0:T(128)S(1)}, s32[128]{0:T(128)}, u32[]{:S(2)}) copy-start(s32[128]{0:T(128)} %param.28) | copy-start | bytes 1540
  2.5 21.1 %copy-start.2 = (bf16[256,512]{1,0:T(8,128)(2,1)S(1)}, bf16[256,512]{1,0:T(8,128)(2,1)}, u32[]{:S(2)}) copy-start(bf16[256,512]{1,0:T(8,128)(2,1)} %param.32) | copy-start | bytes 786436
  2.5 20.0 %all-to-all-start = ((bf16[8,16,4,256]{3,0,2,1:T(8,128)(2,1)}), bf16[8,16,4,256]{3,0,2,1:T(8,128)(2,1)S(1)}, u32[]{:S(2)}, u32[]{:S(2)}) async-start(bf16[8,16,4,256]{3,0,2,1:T(8,128)(2,1)} %bitcast.5), calls=%async_computation | async-start | bytes 524288 | tf_op jit(solution)/shard_map/all_to_all | solution.py:427
  10.1 12.4 %collective-permute-start.4 = (bf16[2,128,128]{1,2,0:T(8,128)(2,1)S(1)}, bf16[2,128,128]{1,2,0:T(8,128)(2,1)S(1)}, u32[]{:S(2)}, u32[]{:S(2)}) collective-permute-start(bf16[2,128,128]{1,2,0:T(8,128)(2,1)S(1)} %bitcast.250), channel_id=1, source_target_pairs={{0,8},{1,9},{2,10},{3,11},{4,12},{5,13},{6,14},{7,15},{8,0},{9,1},... | collective-permute-start | bytes 196616 | tf_op jit(solution)/shard_map/ppermute | solution.py:65
  23.6 0.9 copy-start.15
  31.4 1.0 %copy-start.16 = (bf16[256,256]{1,0:T(8,128)(2,1)S(1)}, bf16[256,256]{1,0:T(8,128)(2,1)}, u32[]{:S(2)}) copy-start(bf16[256,256]{1,0:T(8,128)(2,1)} %param.33) | copy-start | bytes 393220
  34.1 2.3 %copy-start.17 = (bf16[256,64]{0,1:T(8,128)(2,1)S(1)}, bf16[256,64]{0,1:T(8,128)(2,1)}, u32[]{:S(2)}) copy-start(bf16[256,64]{0,1:T(8,128)(2,1)} %param.36) | copy-start | bytes 98308
  36.8 5.9 %collective-permute-start = (bf16[256,128]{1,0:T(8,128)(2,1)S(1)}, bf16[256,128]{1,0:T(8,128)(2,1)S(1)}, u32[]{:S(2)}, u32[]{:S(2)}) collective-permute-start(bf16[256,128]{1,0:T(8,128)(2,1)S(1)} %pad_maximum_fusion.8), channel_id=1, source_target_pairs={{0,8},{1,9},{2,10},{3,11},{4,12},{5,13},{6,14},{7,15},{8,0},{9,1},... | collective-permute-start | bytes 196616 | tf_op jit(solution)/shard_map/ppermute | solution.py:65
  37.2 6.4 %collective-permute-start.5 = (bf16[2,2,128,128]{2,3,1,0:T(8,128)(2,1)S(1)}, bf16[2,2,128,128]{2,3,1,0:T(8,128)(2,1)S(1)}, u32[]{:S(2)}, u32[]{:S(2)}) collective-permute-start(bf16[2,2,128,128]{2,3,1,0:T(8,128)(2,1)S(1)} %pad_maximum_fusion.7), channel_id=1, source_target_pairs={{0,4},{1,5},{2,6},{3,7},{4,0},{5,1},{6,2},{7,3},{8,12},{9,13},{10,... | collective-permute-start | bytes 393224 | tf_op jit(solution)/shard_map/ppermute | solution.py:65
  42.7 5.4 %collective-permute-start.1 = (bf16[2,256,128]{2,1,0:T(8,128)(2,1)S(1)}, bf16[2,256,128]{2,1,0:T(8,128)(2,1)S(1)}, u32[]{:S(2)}, u32[]{:S(2)}) collective-permute-start(bf16[2,256,128]{2,1,0:T(8,128)(2,1)S(1)} %pad_maximum_fusion.6), channel_id=1, source_target_pairs={{0,4},{1,5},{2,6},{3,7},{4,0},{5,1},{6,2},{7,3},{8,12},{9,13},{10,... | collective-permute-start | bytes 393224 | tf_op jit(solution)/shard_map/ppermute | solution.py:65
  43.6 8.6 %collective-permute-start.6 = (bf16[2,2,2,128,128]{3,4,2,0,1:T(8,128)(2,1)S(1)}, bf16[2,2,2,128,128]{3,4,2,0,1:T(8,128)(2,1)S(1)}, u32[]{:S(2)}, u32[]{:S(2)}) collective-permute-start(bf16[2,2,2,128,128]{3,4,2,0,1:T(8,128)(2,1)S(1)} %pad_maximum_fusion.5), channel_id=1, source_target_pairs={{0,2},{1,3},{2,0},{3,1},{4,6},{5,7},{6,4},{7,5},{8,10},{9,11},{10,... | collective-permute-start | bytes 786440 | tf_op jit(solution)/shard_map/ppermute | solution.py:65
  48.1 8.5 %collective-permute-start.2 = (bf16[2,2,256,128]{3,2,1,0:T(8,128)(2,1)S(1)}, bf16[2,2,256,128]{3,2,1,0:T(8,128)(2,1)S(1)}, u32[]{:S(2)}, u32[]{:S(2)}) collective-permute-start(bf16[2,2,256,128]{3,2,1,0:T(8,128)(2,1)S(1)} %pad_maximum_fusion.4), channel_id=1, source_target_pairs={{0,2},{1,3},{2,0},{3,1},{4,6},{5,7},{6,4},{7,5},{8,10},{9,11},{10,... | collective-permute-start | bytes 786440 | tf_op jit(solution)/shard_map/ppermute | solution.py:65
  53.1 5.2 %copy-start.12 = (bf16[66,128]{1,0:T(8,128)(2,1)S(1)}, bf16[66,128]{1,0:T(8,128)(2,1)}, u32[]{:S(2)}) copy-start(bf16[66,128]{1,0:T(8,128)(2,1)} %param.29) | copy-start | bytes 50692
  53.1 5.4 %copy-start.1 = (bf16[1024,128]{1,0:T(8,128)(2,1)S(1)}, bf16[1024,128]{1,0:T(8,128)(2,1)}, u32[]{:S(2)}) copy-start(bf16[1024,128]{1,0:T(8,128)(2,1)} %param.37) | copy-start | bytes 786436
  53.1 7.8 %collective-permute-start.7 = (bf16[2,2,2,2,128,128]{4,5,3,0,1,2:T(8,128)(2,1)}, bf16[2,2,2,2,128,128]{4,5,3,0,1,2:T(8,128)(2,1)}, u32[]{:S(2)}, u32[]{:S(2)}) collective-permute-start(bf16[2,2,2,2,128,128]{4,5,3,0,1,2:T(8,128)(2,1)} %pad_maximum_fusion.3), channel_id=1, source_target_pairs={{0,1},{1,0},{2,3},{3,2},{4,5},{5,4},{6,7},{7,6},{8,9},{9,8},{10,11... | collective-permute-start | bytes 1572872 | tf_op jit(solution)/shard_map/ppermute | solution.py:65
  57.6 1.4 %copy-start.3 = (bf16[128,512]{1,0:T(8,128)(2,1)S(1)}, bf16[128,512]{1,0:T(8,128)(2,1)}, u32[]{:S(2)}) copy-start(bf16[128,512]{1,0:T(8,128)(2,1)} %param.38) | copy-start | bytes 393220
  57.6 1.5 %copy-start.8 = (bf16[128,128]{1,0:T(8,128)(2,1)S(1)}, bf16[128,128]{1,0:T(8,128)(2,1)}, u32[]{:S(2)}) copy-start(bf16[128,128]{1,0:T(8,128)(2,1)} %param.39) | copy-start | bytes 98308
  57.6 1.6 %copy-start.9 = (bf16[128,128]{1,0:T(8,128)(2,1)S(1)}, bf16[128,128]{1,0:T(8,128)(2,1)}, u32[]{:S(2)}) copy-start(bf16[128,128]{1,0:T(8,128)(2,1)} %param.40) | copy-start | bytes 98308
  57.6 7.2 %collective-permute-start.3 = (bf16[2,2,2,256,128]{4,3,2,1,0:T(8,128)(2,1)}, bf16[2,2,2,256,128]{4,3,2,1,0:T(8,128)(2,1)}, u32[]{:S(2)}, u32[]{:S(2)}) collective-permute-start(bf16[2,2,2,256,128]{4,3,2,1,0:T(8,128)(2,1)} %pad_maximum_fusion.2), channel_id=1, source_target_pairs={{0,1},{1,0},{2,3},{3,2},{4,5},{5,4},{6,7},{7,6},{8,9},{9,8},{10,11... | collective-permute-start | bytes 1572872 | tf_op jit(solution)/shard_map/ppermute | solution.py:65
  58.2 1.1 %copy-start.4 = (bf16[128,512]{1,0:T(8,128)(2,1)S(1)}, bf16[128,512]{1,0:T(8,128)(2,1)}, u32[]{:S(2)}) copy-start(bf16[128,512]{1,0:T(8,128)(2,1)} %param.41) | copy-start | bytes 393220
  58.5 1.0 %copy-start.10 = (bf16[128,128]{1,0:T(8,128)(2,1)S(1)}, bf16[128,128]{1,0:T(8,128)(2,1)}, u32[]{:S(2)}) copy-start(bf16[128,128]{1,0:T(8,128)(2,1)} %param.42) | copy-start | bytes 98308
  58.5 1.1 %copy-start.11 = (bf16[128,128]{1,0:T(8,128)(2,1)S(1)}, bf16[128,128]{1,0:T(8,128)(2,1)}, u32[]{:S(2)}) copy-start(bf16[128,128]{1,0:T(8,128)(2,1)} %param.43) | copy-start | bytes 98308
  58.7 1.0 %copy-start.5 = (bf16[128,512]{1,0:T(8,128)(2,1)S(1)}, bf16[128,512]{1,0:T(8,128)(2,1)}, u32[]{:S(2)}) copy-start(bf16[128,512]{1,0:T(8,128)(2,1)} %param.44) | copy-start | bytes 393220
  58.7 1.1 %copy-start.6 = (bf16[512,128]{1,0:T(8,128)(2,1)S(1)}, bf16[512,128]{1,0:T(8,128)(2,1)}, u32[]{:S(2)}) copy-start(bf16[512,128]{1,0:T(8,128)(2,1)} %param.45) | copy-start | bytes 393220

commit v3 on v2

--- a/solution.py
+++ b/solution.py
@@ -132,8 +132,14 @@
     low_short = lax.broadcasted_iota(jnp.int32, (32, LANES), 1) < half
     channel = lax.broadcasted_iota(jnp.int32, (LANES, LANES), 0)
 
-    for p in range(16):
-        wide_ref[p * 128 : (p + 1) * 128, :] = parts_ref[p, 128:256, :].astype(jnp.float32)
+    def owner_of(m):
+        turned = (m & 1) * 8 + (m & 2) * 2 + (m & 4) // 2 + (m & 8) // 8
+        return place ^ turned
+
+    for m in range(16):
+        wide_ref[pl.ds(pl.multiple_of(owner_of(m) * 128, 128), 128), :] = parts_ref[
+            m, 128:256, :
+        ].astype(jnp.float32)
     for d in range(0, CO, 2):
         rows = [
             wide_ref[pl.ds(par * CO + d + e, 32, stride=2 * CO), :]
@@ -155,14 +161,14 @@
         mixed = mix(mean_weight_ref[...], stack_ref[...])
         slabs = []
         for q in range(4):
-            h = 4 * g + q
+            h = 2 * owner_of(2 * g + q // 2) + q % 2
             even = slice(2 * q * LANES, (2 * q + 1) * LANES)
             odd = slice((2 * q + 1) * LANES, (2 * q + 2) * LANES)
             outer_mean = fold_halves(
                 mixed[0:128, even], mixed[0:128, odd], mixed[128:256, even], mixed[128:256, odd], low_half
             )
             one_hot = (channel == bins_ref[pl.ds(h, 1), :]).astype(jnp.float32).astype(jnp.bfloat16)
-            start = pair_ref[h].astype(jnp.float32) + mix(table_ref[...], one_hot)
+            start = pair_ref[4 * g + q].astype(jnp.float32) + mix(table_ref[...], one_hot)
             slab = start + outer_mean * inverse_live
             pair_now_ref[h] = slab
             slabs.append(normalize_channels(slab))
@@ -172,7 +178,7 @@
         right = gate_curve(combined[384:512]) * combined[256:384]
         gating = gate_curve(mix(out_gate_ref[...], normed))
         for q in range(4):
-            h = 4 * g + q
+            h = 2 * owner_of(2 * g + q // 2) + q % 2
             lanes = slice(q * LANES, (q + 1) * LANES)
             left_ref[pl.ds(h * 128, 128), :] = left[:, lanes]
             right_ref[pl.ds(h * 128, 128), :] = right[:, lanes]
@@ -283,6 +289,143 @@
         ).astype(jnp.bfloat16)
 
 
+def rows_kernel(rows_ref, blocks_ref, wide_ref):
+    residues = rows_ref.shape[1]
+    count = 8 * residues
+    rows = rows_ref[...].astype(jnp.float32).reshape(count, 2 * LANES)
+    for e in range(2):
+        wide_ref[e * count : (e + 1) * count, :] = rows[:, e * LANES : (e + 1) * LANES]
+    for p in range(16):
+        for e in range(2):
+            block = [
+                wide_ref[pl.ds(e * count + 4 * p + i, 8, stride=residues), :] for i in range(4)
+            ]
+            blocks_ref[p, :, e * LANES : (e + 1) * LANES] = jnp.concatenate(block, axis=0).astype(
+                jnp.bfloat16
+            )
+
+
+def normalize_rows(values):
+    center = jnp.mean(values, axis=1, keepdims=True)
+    shifted = values - center
+    spread = jnp.mean(shifted * shifted, axis=1, keepdims=True)
+    return (shifted * lax.rsqrt(spread + EPSILON)).astype(jnp.bfloat16)
+
+
+def contract_last(first, second):
+    return lax.dot_general(
+        first, second, (((1,), (1,)), ((), ())), preferred_element_type=jnp.float32
+    )
+
+
+def msa_kernel(
+    blocks_ref,
+    live_ref,
+    query_ref,
+    key_ref,
+    value_gate_ref,
+    output_ref,
+    up_ref,
+    down_ref,
+    outer_ref,
+    result_ref,
+    parts_ref,
+    wide_ref,
+    final_ref,
+):
+    for p in range(16):
+        block = blocks_ref[p].astype(jnp.float32)
+        for i in range(4):
+            wide_ref[i * 128 + p * 8 : i * 128 + p * 8 + 8, :] = block[i * 8 : i * 8 + 8, :]
+    live = live_ref[...]
+    alive = live > 0.0
+    width = HM * HEAD_SIZE
+    head_of = lax.broadcasted_iota(jnp.int32, (128, width), 1) // HEAD_SIZE
+    zero = jnp.zeros((128, width), jnp.bfloat16)
+    for i in range(4):
+        rows = slice(i * 128, (i + 1) * 128)
+        current = wide_ref[rows, :]
+        normed = normalize_rows(current)
+        query = (mix(normed, query_ref[...]) * HEAD_SIZE ** (-0.5)).astype(jnp.bfloat16)
+        key = mix(normed, key_ref[...]).astype(jnp.bfloat16)
+        value_gate = mix(normed, value_gate_ref[...])
+        value = value_gate[:, :width].astype(jnp.bfloat16)
+        keys = jnp.concatenate([jnp.where(head_of == h, key, zero) for h in range(HM)], axis=0)
+        values = jnp.concatenate([jnp.where(head_of == h, value, zero) for h in range(HM)], axis=0)
+        scores = contract_last(query, keys)
+        heads = []
+        for h in range(HM):
+            score = jnp.where(alive, scores[:, h * 128 : (h + 1) * 128], -1000000000.0)
+            raised = jnp.exp(score - jnp.max(score, axis=1, keepdims=True))
+            heads.append((raised / jnp.sum(raised, axis=1, keepdims=True)).astype(jnp.bfloat16))
+        attended = mix(jnp.concatenate(heads, axis=1), values)
+        gated = (gate_curve(value_gate[:, width:]) * attended).astype(jnp.bfloat16)
+        current = current + mix(gated, output_ref[...])
+        hidden = jnp.maximum(mix(normalize_rows(current), up_ref[...]), 0.0).astype(jnp.bfloat16)
+        final = (current + mix(hidden, down_ref[...])).astype(jnp.bfloat16).astype(jnp.float32)
+        final_ref[pl.ds(i, 128, stride=4), :] = final[:, :128]
+        final_ref[pl.ds(512 + i, 128, stride=4), :] = final[:, 128:]
+        outer = (contract_last(outer_ref[...], normalize_rows(final)) * live).astype(jnp.bfloat16)
+        parts_ref[i * CO : (i + 1) * CO, :] = outer[:CO, :]
+        parts_ref[128 + i * CO : 128 + (i + 1) * CO, :] = outer[CO:, :]
+    result_ref[:, :128] = final_ref[:512, :].astype(jnp.bfloat16)
+    result_ref[:, 128:] = final_ref[512:, :].astype(jnp.bfloat16)
+
+
+def msa_whole(
+    alignment_input,
+    live_row_float,
+    column_query_weight,
+    column_key_weight,
+    column_value_gate_weight,
+    column_output_weight,
+    alignment_transition_up,
+    alignment_transition_down,
+    outer_input_weight,
+):
+    channels = alignment_input.shape[2]
+    vmem = pl.BlockSpec(memory_space=pltpu.VMEM)
+    blocks = pl.pallas_call(
+        rows_kernel,
+        out_shape=jax.ShapeDtypeStruct((16, 32, channels), jnp.bfloat16),
+        in_specs=[vmem],
+        out_specs=vmem,
+        scratch_shapes=[pltpu.VMEM((1024, LANES), jnp.float32)],
+        compiler_params=pltpu.CompilerParams(vmem_limit_bytes=16 * 1024 * 1024),
+        name="rows_by_device",
+    )(alignment_input)
+    blocks = lax.all_to_all(blocks, "dap", split_axis=0, concat_axis=0, tiled=True)
+    result, parts = pl.pallas_call(
+        msa_kernel,
+        out_shape=(
+            jax.ShapeDtypeStruct((512, channels), jnp.bfloat16),
+            jax.ShapeDtypeStruct((256, LANES), jnp.bfloat16),
+        ),
+        in_specs=[vmem] * 9,
+        out_specs=(vmem, vmem),
+        scratch_shapes=[
+            pltpu.VMEM((512, channels), jnp.float32),
+            pltpu.VMEM((1024, LANES), jnp.float32),
+        ],
+        compiler_params=pltpu.CompilerParams(vmem_limit_bytes=32 * 1024 * 1024),
+        cost_estimate=pl.CostEstimate(
+            flops=1_000_000_000, bytes_accessed=2_500_000, transcendentals=1_000_000
+        ),
+        name="msa_whole",
+    )(
+        blocks,
+        live_row_float.reshape(1, LANES),
+        column_query_weight,
+        column_key_weight,
+        column_value_gate_weight,
+        column_output_weight,
+        alignment_transition_up,
+        alignment_transition_down,
+        outer_input_weight.T,
+    )
+    return result.reshape(128, 4, channels), parts
+
+
 def lanes_order(values):
     lead = values.shape[:-1]
     halves = values.reshape(lead + (values.shape[-1] // 2, 2))
@@ -290,8 +433,7 @@
 
 
 def pair_whole(
-    left_part,
-    right_part,
+    parts,
     pair_state_input,
     bin_all,
     live_count,
@@ -309,9 +451,8 @@
     width = pair_state_input.shape[2]
     own_pair = lanes_order(pair_state_input.transpose(0, 2, 1))
     own_pair = own_pair.reshape(2, 2, width, 64).transpose(0, 2, 1, 3).reshape(2, width, LANES)
-    pair_all = gather_doubling(own_pair).reshape(32, width, LANES)
-    parts = jnp.concatenate([left_part.reshape(128, LANES), right_part.reshape(128, LANES)], axis=0)
-    parts_all = gather_doubling(parts)
+    pair_all = gather_exchange(own_pair).reshape(32, width, LANES)
+    parts_all = gather_exchange(parts)
     bins = lanes_order(bin_all).reshape(32, LANES)
     table = jnp.pad(relative_position_table, ((0, LANES - NBINS), (0, 0))).T
     mean_weight = (
@@ -361,6 +502,17 @@
     return result.reshape(pair_state_input.shape)
 
 
+def gather_exchange(block):
+    shard_pieces = lax.axis_size("dap")
+    held = block[None]
+    bit = shard_pieces // 2
+    while bit:
+        other = lax.ppermute(held, "dap", [(q, q ^ bit) for q in range(shard_pieces)])
+        held = jnp.concatenate([held, other], axis=0)
+        bit //= 2
+    return held
+
+
 def local(
     alignment_input,
     pair_state_input,
@@ -412,6 +564,36 @@
     live_rows = alignment_row_mask > 0
     live_row_float = live_rows.astype(jnp.float32)
 
+    if alignment_row_mask.shape[0] == LANES and 2 * residue_count == LANES and own_rows == 4:
+        result, parts = msa_whole(
+            alignment_input,
+            live_row_float,
+            column_query_weight,
+            column_key_weight,
+            column_value_gate_weight,
+            column_output_weight,
+            alignment_transition_up,
+            alignment_transition_down,
+            outer_input_weight,
+        )
+        pair_state_output = pair_whole(
+            parts,
+            pair_state_input,
+            bins_of(residue_number_index, chain_label),
+            jnp.sum(live_row_float),
+            relative_position_table,
+            outer_output_weight,
+            outgoing_projection_weight,
+            outgoing_output_gate,
+            outgoing_output_weight,
+            incoming_projection_weight,
+            incoming_output_gate,
+            incoming_output_weight,
+            pair_transition_up,
+            pair_transition_down,
+        )
+        return (result, pair_state_output)
+
     def attend_one(operands):
         query_col, key_col, value_col = operands
         scores = jnp.einsum("shd,thd->hst", query_col, key_col, preferred_element_type=jnp.float32)
@@ -474,27 +656,6 @@
     left_part = outer_product_input[..., :CO].astype(jnp.bfloat16)
     right_part = outer_product_input[..., CO:].astype(jnp.bfloat16)
     all_rows = result.shape[0]
-    if all_rows == LANES and 2 * residue_count == LANES and own_rows == 4:
-        return (
-            result,
-            pair_whole(
-                left_part.transpose(1, 2, 0),
-                right_part.transpose(1, 2, 0),
-                pair_state_input,
-                bins_of(residue_number_index, chain_label),
-                jnp.sum(live_row_float),
-                relative_position_table,
-                outer_output_weight,
-                outgoing_projection_weight,
-                outgoing_output_gate,
-                outgoing_output_weight,
-                incoming_projection_weight,
-                incoming_output_gate,
-                incoming_output_weight,
-                pair_transition_up,
-                pair_transition_down,
-            ),
-        )
     left_cols = left_part.transpose(1, 0, 2)
     right_cols = right_part.transpose(1, 0, 2).reshape(own_rows, all_rows * CO)
     live_count = jnp.sum(live_row_float)

time: 93.2 us -> 87 us (0.933)
  matrix products: 9.65 us -> 0 us
  Pallas kernels: 26.7 us -> 34.9 us
  waiting for transfers between devices: 23.2 us -> 15.3 us
  local copies, waits for them, and re-layouts: 9.82 us -> 16.7 us
  other arithmetic: 7.23 us -> 2.62 us
    pallas_call x0 -> x2, Pallas kernels: none -> 8.26 us  [the longest x1 7.22 us: msa_whole(): pl.pallas_call(msa_kernel, out_shape=(jax.ShapeDtypeStruct((512, channels...]
    dot_general x10 -> x0, matrix products: 8.22 us -> none  [the longest x1 1.98 us: local(): jnp.einsum('sif,fc->sic', hidden, alignment_transition_down, preferred_el...]
    ppermute x8, waiting for transfers between devices: 23.2 us -> 15.3 us  [gather_exchange(): lax.ppermute(held, 'dap', [(q, q ^ bit) for q in range(shard_pieces)])]
    unnamed x50 -> x62, local copies, waits for them, and re-layouts: 4.24 us -> 10.4 us
    another operation x16 -> x0, other arithmetic: 5.36 us -> none  [gather_doubling(): held = jnp.stack([first, second], axis=depth)]
    concatenate x0 -> x3, local copies, waits for them, and re-layouts: none -> 4.62 us  [gather_exchange(): held = jnp.concatenate([held, other], axis=0)]
    concatenate x1 -> x6, other arithmetic: 0.01 us -> 1.8 us  [gather_exchange(): held = jnp.concatenate([held, other], axis=0)]
    another operation x1 -> x0, local copies, waits for them, and re-layouts: 1.62 us -> none  [gather_doubling(): held = jnp.stack([first, second], axis=depth)]
  transfers between devices with their start and end apart: 9 -> 9, of which waited for: 6 -> 4; matrix products, arithmetic and copies ran while one was open for 10% -> 13% of each run, Pallas kernels for 0% -> 8%
where the time goes in v3:
time: 87 us; the launch traced here: 86.2 us
  Pallas kernels  34.9 us (40%)
  local copies, waits for them, and re-layouts  16.7 us (19%)
  starting transfers between devices  15.7 us (18%)
  waiting for transfers between devices  15.3 us (18%)
  other arithmetic  2.62 us (3%)
  between operations  1 us (1%)
    pallas_call x1, Pallas kernels, pair_whole(): pl.pallas_call(pair_kernel, out_shape=jax.ShapeDtypeStruct((256, LANES),...  26.6 us
    ppermute x8, waiting for transfers between devices, gather_exchange(): lax.ppermute(held, 'dap', [(q, q ^ bit) for q in range(shard_pieces)])  15.3 us
    unnamed x62, local copies, waits for them, and re-layouts  10.4 us
    ppermute x8, starting transfers between devices, gather_exchange(): lax.ppermute(held, 'dap', [(q, q ^ bit) for q in range(shard_pieces)])  8.17 us
    all_to_all x1, starting transfers between devices, msa_whole(): lax.all_to_all(blocks, 'dap', split_axis=0, concat_axis=0, tiled=True)  7.53 us
    pallas_call x1, Pallas kernels, msa_whole(): pl.pallas_call(msa_kernel, out_shape=(jax.ShapeDtypeStruct((512, channels...  7.22 us
    concatenate x3, local copies, waits for them, and re-layouts, gather_exchange(): held = jnp.concatenate([held, other], axis=0)  4.62 us
    concatenate x6, other arithmetic, gather_exchange(): held = jnp.concatenate([held, other], axis=0)  1.8 us
  transfers between devices with their start and end apart: 9, of which 4 were waited for; matrix products, arithmetic and copies ran while one was open for 13% of the time, Pallas kernels for 8%

profile of v3, /device:TPU:0, one launch (start us, length us, event | category | flops | bytes accessed | tf_op | source)
XLA Modules:
  0.0 86.2 jit_solution(2518835705218544014)
XLA Ops:
  0.6 0.9 %copy-done = bf16[8,64,256]{2,1,0:T(8,128)(2,1)S(1)} copy-done((bf16[8,64,256]{2,1,0:T(8,128)(2,1)S(1)}, bf16[8,64,256]{2,1,0:T(8,128)(2,1)}, u32[]{:S(2)}) %copy-start) | copy-done | bytes 262168
  1.6 1.0 %rows_by_device.1 = bf16[16,32,256]{2,1,0:T(8,128)(2,1)} custom-call(bf16[8,64,256]{2,1,0:T(8,128)(2,1)S(1)} %copy-done), custom_call_target="tpu_custom_call" | custom-call | tf_op jit(solution)/shard_map/rows_by_device/pallas_call | solution.py:388
  2.7 7.5 %all-to-all-start = ((bf16[16,32,256]{2,1,0:T(8,128)(2,1)}), bf16[16,32,256]{2,1,0:T(8,128)(2,1)S(1)}, u32[]{:S(2)}, u32[]{:S(2)}) async-start(bf16[16,32,256]{2,1,0:T(8,128)(2,1)} %rows_by_device.1), calls=%async_computation | async-start | bytes 524288 | tf_op jit(solution)/shard_map/all_to_all | solution.py:397
  10.2 2.9 %collective-permute-start.4 = (bf16[1,2,128,128]{2,3,1,0:T(8,128)(2,1)S(1)}, bf16[1,2,128,128]{2,3,1,0:T(8,128)(2,1)S(1)}, u32[]{:S(2)}, u32[]{:S(2)}) collective-permute-start(bf16[1,2,128,128]{2,3,1,0:T(8,128)(2,1)S(1)} %bitcast.54), channel_id=1, source_target_pairs={{0,8},{1,9},{2,10},{3,11},{4,12},{5,13},{6,14},{7,15},{8,0},{9,1},... | collective-permute-start | bytes 196616 | tf_op jit(solution)/shard_map/ppermute | solution.py:510
  13.1 0.6 constant_dynamic-update-slice_fusion.9
  14.5 8.1 %collective-permute-done.4 = bf16[1,2,128,128]{2,3,1,0:T(8,128)(2,1)S(1)} collective-permute-done((bf16[1,2,128,128]{2,3,1,0:T(8,128)(2,1)S(1)}, bf16[1,2,128,128]{2,3,1,0:T(8,128)(2,1)S(1)}, u32[]{:S(2)}, u32[]{:S(2)}) %collective-permute-start.4) | collective-permute-done | bytes 65568 | tf_op jit(solution)/shard_map/ppermute | solution.py:510
  22.8 7.2 %msa_whole.1 = (bf16[512,256]{1,0:T(8,128)(2,1)S(1)}, bf16[256,128]{1,0:T(8,128)(2,1)S(1)}) custom-call(bf16[16,32,256]{2,1,0:T(8,128)(2,1)S(1)} %all-to-all-done.blocks_ref, f32[1,128]{1,0:T(1,128)S(1)} %fusion.1.live_ref, bf16[256,256]{1,0:T(8,128)(2,1)S(1)} %copy-done.4, bf16[256,256]{1,0:T(8,128)(2,1)S(1)} %copy-done.5, bf16[256,512]{1,0:T(8,128)(2,1)S(1)} %copy-done.3, ...), custom_call_target="tpu_custom_call" | custom-call | flops 1000000000 | bytes 2500000 | tf_op jit(solution)/shard_map/msa_whole/pallas_call | solution.py:398
  30.1 2.1 %collective-permute-start = (bf16[1,256,128]{2,1,0:T(8,128)(2,1)S(1)}, bf16[1,256,128]{2,1,0:T(8,128)(2,1)S(1)}, u32[]{:S(2)}, u32[]{:S(2)}) collective-permute-start(bf16[1,256,128]{2,1,0:T(8,128)(2,1)S(1)} %bitcast.41), channel_id=1, source_target_pairs={{0,8},{1,9},{2,10},{3,11},{4,12},{5,13},{6,14},{7,15},{8,0},{9,1},... | collective-permute-start | bytes 196616 | tf_op jit(solution)/shard_map/ppermute | solution.py:510
  32.1 0.6 fusion
  33.2 0.7 copy-done.9
  34.1 0.8 copy-done.10
  35.0 0.8 copy-done.11
  35.9 0.8 copy-done.12
  36.9 0.6 copy-done.14
  37.6 0.6 copy-done.15
  38.4 0.6 copy-done.16
  39.2 0.6 copy-done.17
  40.1 1.5 %collective-permute-start.6 = (bf16[4,2,128,128]{2,3,1,0:T(8,128)(2,1)S(1)}, bf16[4,2,128,128]{2,3,1,0:T(8,128)(2,1)S(1)}, u32[]{:S(2)}, u32[]{:S(2)}) collective-permute-start(bf16[4,2,128,128]{2,3,1,0:T(8,128)(2,1)S(1)} %pad_maximum_fusion.3), channel_id=1, source_target_pairs={{0,2},{1,3},{2,0},{3,1},{4,6},{5,7},{6,4},{7,5},{8,10},{9,11},{10,... | collective-permute-start | bytes 786440 | tf_op jit(solution)/shard_map/ppermute | solution.py:510
  41.6 0.6 constant_dynamic-update-slice_fusion.8
  42.2 2.7 %collective-permute-done.1 = bf16[2,256,128]{2,1,0:T(8,128)(2,1)S(1)} collective-permute-done((bf16[2,256,128]{2,1,0:T(8,128)(2,1)S(1)}, bf16[2,256,128]{2,1,0:T(8,128)(2,1)S(1)}, u32[]{:S(2)}, u32[]{:S(2)}) %collective-permute-start.1) | collective-permute-done | bytes 131104 | tf_op jit(solution)/shard_map/ppermute | solution.py:510
  45.0 1.5 %collective-permute-start.2 = (bf16[4,256,128]{2,1,0:T(8,128)(2,1)S(1)}, bf16[4,256,128]{2,1,0:T(8,128)(2,1)S(1)}, u32[]{:S(2)}, u32[]{:S(2)}) collective-permute-start(bf16[4,256,128]{2,1,0:T(8,128)(2,1)S(1)} %pad_maximum_fusion.2), channel_id=1, source_target_pairs={{0,2},{1,3},{2,0},{3,1},{4,6},{5,7},{6,4},{7,5},{8,10},{9,11},{10,... | collective-permute-start | bytes 786440 | tf_op jit(solution)/shard_map/ppermute | solution.py:510
  46.5 0.7 constant_dynamic-update-slice_fusion.7
  47.2 2.1 %collective-permute-done.6 = bf16[4,2,128,128]{2,3,1,0:T(8,128)(2,1)S(1)} collective-permute-done((bf16[4,2,128,128]{2,3,1,0:T(8,128)(2,1)S(1)}, bf16[4,2,128,128]{2,3,1,0:T(8,128)(2,1)S(1)}, u32[]{:S(2)}, u32[]{:S(2)}) %collective-permute-start.6) | collective-permute-done | bytes 262176 | tf_op jit(solution)/shard_map/ppermute | solution.py:510
  49.3 0.8 pad_maximum_fusion.1
  50.2 0.7 constant_dynamic-update-slice_fusion.6
  50.9 2.3 %collective-permute-done.2 = bf16[4,256,128]{2,1,0:T(8,128)(2,1)S(1)} collective-permute-done((bf16[4,256,128]{2,1,0:T(8,128)(2,1)S(1)}, bf16[4,256,128]{2,1,0:T(8,128)(2,1)S(1)}, u32[]{:S(2)}, u32[]{:S(2)}) %collective-permute-start.2) | collective-permute-done | bytes 262176 | tf_op jit(solution)/shard_map/ppermute | solution.py:510
  53.2 0.9 %pad_maximum_fusion = bf16[8,256,128]{2,1,0:T(8,128)(2,1)} fusion(bf16[4,256,128]{2,1,0:T(8,128)(2,1)S(1)} %collective-permute-done.2, bf16[2,256,128]{2,1,0:T(8,128)(2,1)S(1)} %collective-permute-done.1, bf16[1,256,128]{2,1,0:T(8,128)(2,1)S(1)} %collective-permute-done, bf16[1,256,128]{2,1,0:T(8,128)(2,1)S(1)} %bitcast.44), kind=kLoop, calls=%fused_computation | loop fusion | flops 786432 | bytes 1048576 | tf_op jit(solution)/shard_map/concatenate | solution.py:511
  54.1 0.8 reshape.70
  54.9 1.9 %constant_dynamic-update-slice_fusion.5 = bf16[16,2,128,128]{2,3,1,0:T(8,128)(2,1)} fusion(bf16[16,2,128,128]{2,3,1,0:T(8,128)(2,1)} %constant_dynamic-update-slice_fusion.6, bf16[8,2,128,128]{2,3,1,0:T(8,128)(2,1)} %collective-permute-done.7), kind=kLoop, calls=%fused_computation.14 | loop fusion | bytes 1048576 | tf_op jit(solution)/shard_map/concatenate | solution.py:511
  56.8 1.6 %copy.51 = bf16[16,2,128,128]{3,2,1,0:T(8,128)(2,1)S(1)} copy(bf16[16,2,128,128]{2,3,1,0:T(8,128)(2,1)} %constant_dynamic-update-slice_fusion.5) | data formatting | bytes 2097152 | tf_op jit(solution)/shard_map/concatenate | solution.py:511
  58.4 1.1 %constant_dynamic-update-slice_fusion.parts_ref = bf16[16,256,128]{2,1,0:T(8,128)(2,1)S(1)} fusion(bf16[16,256,128]{2,1,0:T(8,128)(2,1)S(1)} %constant_dynamic-update-slice_fusion.1, bf16[8,256,128]{2,1,0:T(8,128)(2,1)} %collective-permute-done.3), kind=kLoop, calls=%fused_computation.9 | loop fusion | bytes 1048576 | tf_op jit(solution)/shard_map/concatenate | solution.py:511
  59.6 26.6 %pair_whole.1 = bf16[256,128]{1,0:T(8,128)(2,1)} custom-call(s32[1]{0:T(128)} %bitcast.2.place_ref, f32[1]{0:T(128)} %bitcast.3.live_ref, bf16[16,256,128]{2,1,0:T(8,128)(2,1)S(1)} %constant_dynamic-update-slice_fusion.parts_ref, bf16[32,128,128]{2,1,0:T(8,128)(2,1)S(1)} %bitcast.40, s32[32,128]{1,0:T(8,128)S(1)} %select_n.11.bins_ref, ...), custom_call_target="tpu_custom_call" | custom-call | tf_op jit(solution)/shard_map/pair_whole/pallas_call | solution.py:465
  (73 shorter events, 2.6 us)
Async XLA Ops:
  0.6 1.0 %copy-start = (bf16[8,64,256]{2,1,0:T(8,128)(2,1)S(1)}, bf16[8,64,256]{2,1,0:T(8,128)(2,1)}, u32[]{:S(2)}) copy-start(bf16[8,64,256]{2,1,0:T(8,128)(2,1)} %rows_ref.1) | copy-start | bytes 786436
  1.6 8.6 %copy-start.13 = (bf16[4,64,128]{2,1,0:T(8,128)(2,1)S(1)}, bf16[4,64,128]{2,1,0:T(8,128)(2,1)}, u32[]{:S(2)}) copy-start(bf16[4,64,128]{2,1,0:T(8,128)(2,1)} %param.23) | copy-start | bytes 196612
  1.6 12.6 %copy-start.18 = (bf16[66,128]{1,0:T(8,128)(2,1)S(1)}, bf16[66,128]{1,0:T(8,128)(2,1)}, u32[]{:S(2)}) copy-start(bf16[66,128]{1,0:T(8,128)(2,1)} %param.27) | copy-start | bytes 50692
  1.6 21.2 %copy-start.4 = (bf16[256,256]{1,0:T(8,128)(2,1)S(1)}, bf16[256,256]{1,0:T(8,128)(2,1)}, u32[]{:S(2)}) copy-start(bf16[256,256]{1,0:T(8,128)(2,1)} %query_ref.1) | copy-start | bytes 393220
  1.6 21.2 %copy-start.5 = (bf16[256,256]{1,0:T(8,128)(2,1)S(1)}, bf16[256,256]{1,0:T(8,128)(2,1)}, u32[]{:S(2)}) copy-start(bf16[256,256]{1,0:T(8,128)(2,1)} %key_ref.1) | copy-start | bytes 393220
  1.6 21.2 %copy-start.6 = (bf16[256,256]{1,0:T(8,128)(2,1)S(1)}, bf16[256,256]{1,0:T(8,128)(2,1)}, u32[]{:S(2)}) copy-start(bf16[256,256]{1,0:T(8,128)(2,1)} %output_ref.1) | copy-start | bytes 393220
  1.6 21.2 %copy-start.7 = (bf16[256,64]{0,1:T(8,128)(2,1)S(1)}, bf16[256,64]{0,1:T(8,128)(2,1)}, u32[]{:S(2)}) copy-start(bf16[256,64]{0,1:T(8,128)(2,1)} %param.34) | copy-start | bytes 98308
  2.7 10.5 %copy-start.21 = (s32[128]{0:T(128)S(1)}, s32[128]{0:T(128)}, u32[]{:S(2)}) copy-start(s32[128]{0:T(128)} %param.26) | copy-start | bytes 1540
  2.7 11.1 %copy-start.20 = (s32[64]{0:T(128)S(1)}, s32[64]{0:T(128)}, u32[]{:S(2)}) copy-start(s32[64]{0:T(128)} %param.25) | copy-start | bytes 772
  2.7 11.3 %copy-start.19 = (s32[64]{0:T(128)S(1)}, s32[64]{0:T(128)}, u32[]{:S(2)}) copy-start(s32[64]{0:T(128)} %param.24) | copy-start | bytes 772
  2.7 20.1 %copy-start.2 = (bf16[1024,256]{1,0:T(8,128)(2,1)S(1)}, bf16[1024,256]{1,0:T(8,128)(2,1)}, u32[]{:S(2)}) copy-start(bf16[1024,256]{1,0:T(8,128)(2,1)} %down_ref.1) | copy-start | bytes 1572868
  2.7 20.1 %all-to-all-start = ((bf16[16,32,256]{2,1,0:T(8,128)(2,1)}), bf16[16,32,256]{2,1,0:T(8,128)(2,1)S(1)}, u32[]{:S(2)}, u32[]{:S(2)}) async-start(bf16[16,32,256]{2,1,0:T(8,128)(2,1)} %rows_by_device.1), calls=%async_computation | async-start | bytes 524288 | tf_op jit(solution)/shard_map/all_to_all | solution.py:397
  10.2 12.6 %copy-start.1 = (bf16[256,1024]{1,0:T(8,128)(2,1)S(1)}, bf16[256,1024]{1,0:T(8,128)(2,1)}, u32[]{:S(2)}) copy-start(bf16[256,1024]{1,0:T(8,128)(2,1)} %up_ref.1) | copy-start | bytes 1572868
  10.2 12.4 %collective-permute-start.4 = (bf16[1,2,128,128]{2,3,1,0:T(8,128)(2,1)S(1)}, bf16[1,2,128,128]{2,3,1,0:T(8,128)(2,1)S(1)}, u32[]{:S(2)}, u32[]{:S(2)}) collective-permute-start(bf16[1,2,128,128]{2,3,1,0:T(8,128)(2,1)S(1)} %bitcast.54), channel_id=1, source_target_pairs={{0,8},{1,9},{2,10},{3,11},{4,12},{5,13},{6,14},{7,15},{8,0},{9,1},... | collective-permute-start | bytes 196616 | tf_op jit(solution)/shard_map/ppermute | solution.py:510
  13.8 9.1 %copy-start.3 = (bf16[256,512]{1,0:T(8,128)(2,1)S(1)}, bf16[256,512]{1,0:T(8,128)(2,1)}, u32[]{:S(2)}) copy-start(bf16[256,512]{1,0:T(8,128)(2,1)} %value_gate_ref.1) | copy-start | bytes 786436
  22.7 17.4 %collective-permute-start.5 = (bf16[2,2,128,128]{2,3,1,0:T(8,128)(2,1)S(1)}, bf16[2,2,128,128]{2,3,1,0:T(8,128)(2,1)S(1)}, u32[]{:S(2)}, u32[]{:S(2)}) collective-permute-start(bf16[2,2,128,128]{2,3,1,0:T(8,128)(2,1)S(1)} %pad_maximum_fusion.5), channel_id=1, source_target_pairs={{0,4},{1,5},{2,6},{3,7},{4,0},{5,1},{6,2},{7,3},{8,12},{9,13},{10,... | collective-permute-start | bytes 393224 | tf_op jit(solution)/shard_map/ppermute | solution.py:510
  22.8 9.9 %copy-start.8 = (bf16[1024,128]{1,0:T(8,128)(2,1)S(1)}, bf16[1024,128]{1,0:T(8,128)(2,1)}, u32[]{:S(2)}) copy-start(bf16[1024,128]{1,0:T(8,128)(2,1)} %param.35) | copy-start | bytes 786436
  30.1 9.8 %collective-permute-start = (bf16[1,256,128]{2,1,0:T(8,128)(2,1)S(1)}, bf16[1,256,128]{2,1,0:T(8,128)(2,1)S(1)}, u32[]{:S(2)}, u32[]{:S(2)}) collective-permute-start(bf16[1,256,128]{2,1,0:T(8,128)(2,1)S(1)} %bitcast.41), channel_id=1, source_target_pairs={{0,8},{1,9},{2,10},{3,11},{4,12},{5,13},{6,14},{7,15},{8,0},{9,1},... | collective-permute-start | bytes 196616 | tf_op jit(solution)/shard_map/ppermute | solution.py:510
  33.0 0.9 %copy-start.9 = (bf16[128,512]{1,0:T(8,128)(2,1)S(1)}, bf16[128,512]{1,0:T(8,128)(2,1)}, u32[]{:S(2)}) copy-start(bf16[128,512]{1,0:T(8,128)(2,1)} %param.36) | copy-start | bytes 393220
  33.9 0.9 %copy-start.10 = (bf16[128,512]{1,0:T(8,128)(2,1)S(1)}, bf16[128,512]{1,0:T(8,128)(2,1)}, u32[]{:S(2)}) copy-start(bf16[128,512]{1,0:T(8,128)(2,1)} %param.39) | copy-start | bytes 393220
  34.8 0.9 %copy-start.11 = (bf16[128,512]{1,0:T(8,128)(2,1)S(1)}, bf16[128,512]{1,0:T(8,128)(2,1)}, u32[]{:S(2)}) copy-start(bf16[128,512]{1,0:T(8,128)(2,1)} %param.42) | copy-start | bytes 393220
  35.7 0.9 %copy-start.12 = (bf16[512,128]{1,0:T(8,128)(2,1)S(1)}, bf16[512,128]{1,0:T(8,128)(2,1)}, u32[]{:S(2)}) copy-start(bf16[512,128]{1,0:T(8,128)(2,1)} %param.43) | copy-start | bytes 393220
  36.8 0.8 copy-start.14
  37.5 0.8 copy-start.15
  38.3 0.8 copy-start.16
  39.0 0.8 copy-start.17
  40.0 5.0 %collective-permute-start.1 = (bf16[2,256,128]{2,1,0:T(8,128)(2,1)S(1)}, bf16[2,256,128]{2,1,0:T(8,128)(2,1)S(1)}, u32[]{:S(2)}, u32[]{:S(2)}) collective-permute-start(bf16[2,256,128]{2,1,0:T(8,128)(2,1)S(1)} %pad_maximum_fusion.4), channel_id=1, source_target_pairs={{0,4},{1,5},{2,6},{3,7},{4,0},{5,1},{6,2},{7,3},{8,12},{9,13},{10,... | collective-permute-start | bytes 393224 | tf_op jit(solution)/shard_map/ppermute | solution.py:510
  40.1 9.2 %collective-permute-start.6 = (bf16[4,2,128,128]{2,3,1,0:T(8,128)(2,1)S(1)}, bf16[4,2,128,128]{2,3,1,0:T(8,128)(2,1)S(1)}, u32[]{:S(2)}, u32[]{:S(2)}) collective-permute-start(bf16[4,2,128,128]{2,3,1,0:T(8,128)(2,1)S(1)} %pad_maximum_fusion.3), channel_id=1, source_target_pairs={{0,2},{1,3},{2,0},{3,1},{4,6},{5,7},{6,4},{7,5},{8,10},{9,11},{10,... | collective-permute-start | bytes 786440 | tf_op jit(solution)/shard_map/ppermute | solution.py:510
  45.0 8.2 %collective-permute-start.2 = (bf16[4,256,128]{2,1,0:T(8,128)(2,1)S(1)}, bf16[4,256,128]{2,1,0:T(8,128)(2,1)S(1)}, u32[]{:S(2)}, u32[]{:S(2)}) collective-permute-start(bf16[4,256,128]{2,1,0:T(8,128)(2,1)S(1)} %pad_maximum_fusion.2), channel_id=1, source_target_pairs={{0,2},{1,3},{2,0},{3,1},{4,6},{5,7},{6,4},{7,5},{8,10},{9,11},{10,... | collective-permute-start | bytes 786440 | tf_op jit(solution)/shard_map/ppermute | solution.py:510
  50.2 4.8 %collective-permute-start.7 = (bf16[8,2,128,128]{2,3,1,0:T(8,128)(2,1)}, bf16[8,2,128,128]{2,3,1,0:T(8,128)(2,1)}, u32[]{:S(2)}, u32[]{:S(2)}) collective-permute-start(bf16[8,2,128,128]{2,3,1,0:T(8,128)(2,1)} %pad_maximum_fusion.1), channel_id=1, source_target_pairs={{0,1},{1,0},{2,3},{3,2},{4,5},{5,4},{6,7},{7,6},{8,9},{9,8},{10,11... | collective-permute-start | bytes 1572872 | tf_op jit(solution)/shard_map/ppermute | solution.py:510
  54.0 4.4 %collective-permute-start.3 = (bf16[8,256,128]{2,1,0:T(8,128)(2,1)}, bf16[8,256,128]{2,1,0:T(8,128)(2,1)}, u32[]{:S(2)}, u32[]{:S(2)}) collective-permute-start(bf16[8,256,128]{2,1,0:T(8,128)(2,1)} %pad_maximum_fusion), channel_id=1, source_target_pairs={{0,1},{1,0},{2,3},{3,2},{4,5},{5,4},{6,7},{7,6},{8,9},{9,8},{10,11... | collective-permute-start | bytes 1572872 | tf_op jit(solution)/shard_map/ppermute | solution.py:510

commit v4 on v3

--- a/solution.py
+++ b/solution.py
@@ -1,3 +1,5 @@
+import functools
+
 import jax
 import jax.numpy as jnp
 from jax import lax
@@ -99,10 +101,17 @@
 def pair_kernel(
     place_ref,
     live_ref,
-    parts_ref,
-    pair_ref,
-    bins_ref,
-    table_ref,
+    *rest,
+):
+    pair_body(place_ref, live_ref, rest[:4], rest[4:8], *rest[8:])
+
+
+def pair_body(
+    place_ref,
+    live_ref,
+    part_refs,
+    pair_refs,
+    embedding_ref,
     mean_weight_ref,
     out_mix_ref,
     out_gate_ref,
@@ -130,16 +139,16 @@
     half = LANES // 2
     low_half = lax.broadcasted_iota(jnp.int32, (LANES, LANES), 1) < half
     low_short = lax.broadcasted_iota(jnp.int32, (32, LANES), 1) < half
-    channel = lax.broadcasted_iota(jnp.int32, (LANES, LANES), 0)
-
-    def owner_of(m):
-        turned = (m & 1) * 8 + (m & 2) * 2 + (m & 4) // 2 + (m & 8) // 8
-        return place ^ turned
-
-    for m in range(16):
-        wide_ref[pl.ds(pl.multiple_of(owner_of(m) * 128, 128), 128), :] = parts_ref[
-            m, 128:256, :
-        ].astype(jnp.float32)
+
+    offsets = (0, 2, 1, 3)
+
+    def owner_of(piece, m):
+        return place ^ (offsets[piece] + (m & 1) * 8 + (m & 2) * 2)
+
+    for piece in range(4):
+        for m in range(4):
+            first = pl.multiple_of(owner_of(piece, m) * 128, 128)
+            wide_ref[pl.ds(first, 128), :] = part_refs[piece][m, 128:256, :].astype(jnp.float32)
     for d in range(0, CO, 2):
         rows = [
             wide_ref[pl.ds(par * CO + d + e, 32, stride=2 * CO), :]
@@ -150,8 +159,8 @@
             jnp.concatenate(rows, axis=0).T.astype(jnp.bfloat16)
         )
 
-    def first_chunk(g, carry):
-        left_rows = parts_ref[pl.ds(2 * g, 2), 0:128, :].reshape(256, LANES)
+    def first_chunk(piece, g, carry):
+        left_rows = part_refs[piece][pl.ds(2 * g, 2), 0:128, :].reshape(256, LANES)
         outer = mix(left_rows, right_cols_ref[...]).astype(jnp.bfloat16)
         for i in range(8):
             for d in range(16):
@@ -161,14 +170,14 @@
         mixed = mix(mean_weight_ref[...], stack_ref[...])
         slabs = []
         for q in range(4):
-            h = 2 * owner_of(2 * g + q // 2) + q % 2
+            h = 2 * owner_of(piece, 2 * g + q // 2) + q % 2
             even = slice(2 * q * LANES, (2 * q + 1) * LANES)
             odd = slice((2 * q + 1) * LANES, (2 * q + 2) * LANES)
             outer_mean = fold_halves(
                 mixed[0:128, even], mixed[0:128, odd], mixed[128:256, even], mixed[128:256, odd], low_half
             )
-            one_hot = (channel == bins_ref[pl.ds(h, 1), :]).astype(jnp.float32).astype(jnp.bfloat16)
-            start = pair_ref[4 * g + q].astype(jnp.float32) + mix(table_ref[...], one_hot)
+            start = pair_refs[piece][2 * g + q // 2, q % 2].astype(jnp.float32)
+            start = start + embedding_ref[h].astype(jnp.float32)
             slab = start + outer_mean * inverse_live
             pair_now_ref[h] = slab
             slabs.append(normalize_channels(slab))
@@ -178,14 +187,15 @@
         right = gate_curve(combined[384:512]) * combined[256:384]
         gating = gate_curve(mix(out_gate_ref[...], normed))
         for q in range(4):
-            h = 2 * owner_of(2 * g + q // 2) + q % 2
+            h = 2 * owner_of(piece, 2 * g + q // 2) + q % 2
             lanes = slice(q * LANES, (q + 1) * LANES)
             left_ref[pl.ds(h * 128, 128), :] = left[:, lanes]
             right_ref[pl.ds(h * 128, 128), :] = right[:, lanes]
             gating_ref[h] = gating[:, lanes]
         return carry
 
-    lax.fori_loop(0, 8, first_chunk, 0)
+    for piece in range(4):
+        lax.fori_loop(0, 2, functools.partial(first_chunk, piece), 0)
 
     def outgoing_channels(block, carry):
         for e in range(8):
@@ -277,9 +287,7 @@
     own_pair = own_pair + gating * finished
     hidden = jnp.maximum(mix(up_ref[...], normalize_channels(own_pair)), 0.0).astype(jnp.bfloat16)
     own_pair = (own_pair + mix(down_ref[...], hidden)).astype(jnp.bfloat16)
-    lane = lax.broadcasted_iota(jnp.int32, (LANES, LANES), 1)
-    back = half * (channel // half) + 32 * (channel % 2) + (channel % half) // 2
-    order = (lane == back).astype(jnp.float32).astype(jnp.bfloat16)
+    order = lane_order_matrix()
     for t in range(2):
         result_ref[t * 128 : (t + 1) * 128, :] = lax.dot_general(
             order,
@@ -289,20 +297,107 @@
         ).astype(jnp.bfloat16)
 
 
-def rows_kernel(rows_ref, blocks_ref, wide_ref):
+def lane_order_matrix():
+    half = LANES // 2
+    member = lax.broadcasted_iota(jnp.int32, (LANES, LANES), 0)
+    lane = lax.broadcasted_iota(jnp.int32, (LANES, LANES), 1)
+    back = half * (member // half) + 32 * (member % 2) + (member % half) // 2
+    return (lane == back).astype(jnp.float32).astype(jnp.bfloat16)
+
+
+def contract_first(first, second):
+    return lax.dot_general(
+        first, second, (((0,), (0,)), ((), ())), preferred_element_type=jnp.float32
+    )
+
+
+def rows_kernel(place_ref, rows_ref, pair_ref, own_pair_ref, *rest):
+    block_refs, wide_ref = rest[:-1], rest[-1]
     residues = rows_ref.shape[1]
     count = 8 * residues
     rows = rows_ref[...].astype(jnp.float32).reshape(count, 2 * LANES)
     for e in range(2):
         wide_ref[e * count : (e + 1) * count, :] = rows[:, e * LANES : (e + 1) * LANES]
-    for p in range(16):
+    for m in range(16):
+        first = 4 * (place_ref[0] ^ m)
         for e in range(2):
             block = [
-                wide_ref[pl.ds(e * count + 4 * p + i, 8, stride=residues), :] for i in range(4)
+                wide_ref[pl.ds(e * count + first + i, 8, stride=residues), :] for i in range(4)
             ]
-            blocks_ref[p, :, e * LANES : (e + 1) * LANES] = jnp.concatenate(block, axis=0).astype(
+            block_refs[m][:, e * LANES : (e + 1) * LANES] = jnp.concatenate(block, axis=0).astype(
                 jnp.bfloat16
             )
+    order = lane_order_matrix()
+    for t in range(2):
+        own_pair_ref[t] = contract_first(
+            pair_ref[2 * t : 2 * t + 2].reshape(LANES, LANES), order
+        ).astype(jnp.bfloat16)
+
+
+def weights_kernel(
+    bins_ref,
+    table_ref,
+    mean_weight_ref,
+    out_mix_ref,
+    out_gate_ref,
+    out_final_ref,
+    in_mix_ref,
+    in_gate_ref,
+    in_final_ref,
+    up_ref,
+    down_ref,
+    embedding_out,
+    mean_weight_out,
+    out_mix_out,
+    out_gate_out,
+    out_final_out,
+    in_mix_out,
+    in_gate_out,
+    in_final_out,
+    up_out,
+    down_out,
+    table_wide_ref,
+    mean_wide_ref,
+):
+    table_wide_ref[...] = jnp.zeros_like(table_wide_ref)
+    table_wide_ref[0:NBINS, :] = table_ref[...].astype(jnp.float32)
+    table = table_wide_ref[...].T.astype(jnp.bfloat16)
+    channel = lax.broadcasted_iota(jnp.int32, (LANES, LANES), 0)
+
+    def embed(g, carry):
+        for q in range(4):
+            h = 4 * g + q
+            one_hot = (channel == bins_ref[pl.ds(h, 1), :]).astype(jnp.float32).astype(jnp.bfloat16)
+            embedding_out[h] = mix(table, one_hot).astype(jnp.bfloat16)
+        return carry
+
+    lax.fori_loop(0, 8, embed, 0)
+    mean_wide_ref[...] = mean_weight_ref[...].astype(jnp.float32)
+    for e in range(2):
+        for block in range(4):
+            rows = [
+                mean_wide_ref[pl.ds(2 * (4 * block + k) + e, CO, stride=CO), :] for k in range(4)
+            ]
+            mean_weight_out[e * LANES : (e + 1) * LANES, block * LANES : (block + 1) * LANES] = (
+                jnp.concatenate(rows, axis=0).T.astype(jnp.bfloat16)
+            )
+    for source, target in (
+        (out_mix_ref, out_mix_out),
+        (out_gate_ref, out_gate_out),
+        (out_final_ref, out_final_out),
+        (in_mix_ref, in_mix_out),
+        (in_gate_ref, in_gate_out),
+        (in_final_ref, in_final_out),
+        (up_ref, up_out),
+        (down_ref, down_out),
+    ):
+        rows, columns = source.shape
+        for a in range(rows // LANES):
+            for b in range(columns // LANES):
+                part = source[a * LANES : (a + 1) * LANES, b * LANES : (b + 1) * LANES]
+                target[b * LANES : (b + 1) * LANES, a * LANES : (a + 1) * LANES] = (
+                    part.astype(jnp.float32).T.astype(jnp.bfloat16)
+                )
 
 
 def normalize_rows(values):
@@ -318,9 +413,15 @@
     )
 
 
-def msa_kernel(
-    blocks_ref,
+def msa_kernel(place_ref, live_ref, *rest):
+    block_refs = rest[:16]
+    msa_body(place_ref, live_ref, block_refs, *rest[16:])
+
+
+def msa_body(
+    place_ref,
     live_ref,
+    block_refs,
     query_ref,
     key_ref,
     value_gate_ref,
@@ -333,10 +434,11 @@
     wide_ref,
     final_ref,
 ):
-    for p in range(16):
-        block = blocks_ref[p].astype(jnp.float32)
+    for m in range(16):
+        block = block_refs[m][...].astype(jnp.float32)
+        first = (place_ref[0] ^ m) * 8
         for i in range(4):
-            wide_ref[i * 128 + p * 8 : i * 128 + p * 8 + 8, :] = block[i * 8 : i * 8 + 8, :]
+            wide_ref[pl.ds(pl.multiple_of(i * 128 + first, 8), 8), :] = block[i * 8 : i * 8 + 8, :]
     live = live_ref[...]
     alive = live > 0.0
     width = HM * HEAD_SIZE
@@ -372,9 +474,17 @@
     result_ref[:, 128:] = final_ref[512:, :].astype(jnp.bfloat16)
 
 
-def msa_whole(
+def exchange(values, offset):
+    pieces = lax.axis_size("dap")
+    return lax.ppermute(values, "dap", [(q, q ^ offset) for q in range(pieces)])
+
+
+def whole_block(
     alignment_input,
+    pair_state_input,
+    bin_all,
     live_row_float,
+    relative_position_table,
     column_query_weight,
     column_key_weight,
     column_value_gate_weight,
@@ -382,39 +492,78 @@
     alignment_transition_up,
     alignment_transition_down,
     outer_input_weight,
+    outer_output_weight,
+    *pair_weights,
 ):
     channels = alignment_input.shape[2]
+    width = pair_state_input.shape[2]
+    place = lax.axis_index("dap").astype(jnp.int32).reshape(1)
     vmem = pl.BlockSpec(memory_space=pltpu.VMEM)
-    blocks = pl.pallas_call(
+    smem = pl.BlockSpec(memory_space=pltpu.SMEM)
+
+    def array(*shape):
+        return jax.ShapeDtypeStruct(shape, jnp.bfloat16)
+
+    def limit(mebibytes):
+        return pltpu.CompilerParams(vmem_limit_bytes=mebibytes * 1024 * 1024)
+
+    own_pair, *blocks = pl.pallas_call(
         rows_kernel,
-        out_shape=jax.ShapeDtypeStruct((16, 32, channels), jnp.bfloat16),
-        in_specs=[vmem],
-        out_specs=vmem,
+        out_shape=[array(2, width, LANES)] + [array(32, channels)] * 16,
+        in_specs=[smem, vmem, vmem],
+        out_specs=[vmem] * 17,
         scratch_shapes=[pltpu.VMEM((1024, LANES), jnp.float32)],
-        compiler_params=pltpu.CompilerParams(vmem_limit_bytes=16 * 1024 * 1024),
+        compiler_params=limit(16),
         name="rows_by_device",
-    )(alignment_input)
-    blocks = lax.all_to_all(blocks, "dap", split_axis=0, concat_axis=0, tiled=True)
+    )(place, alignment_input, pair_state_input)
+    blocks = [blocks[0]] + [exchange(blocks[m], m) for m in range(1, 16)]
+
+    pair_far = exchange(own_pair, 8)
+    pair_near = [exchange(own_pair, 4), exchange(pair_far, 4)]
+    pair_line = jnp.stack([own_pair, pair_far] + pair_near)
+
+    embedding, *turned = pl.pallas_call(
+        weights_kernel,
+        out_shape=[array(32, width, LANES), array(2 * width, 16 * CO)]
+        + [array(*w.shape[::-1]) for w in pair_weights],
+        in_specs=[vmem] * 11,
+        out_specs=[vmem] * 10,
+        scratch_shapes=[
+            pltpu.VMEM((LANES, LANES), jnp.float32),
+            pltpu.VMEM((1024, LANES), jnp.float32),
+        ],
+        compiler_params=limit(24),
+        cost_estimate=pl.CostEstimate(
+            flops=200_000_000, bytes_accessed=4_000_000, transcendentals=0
+        ),
+        name="turn_weights",
+    )(
+        lanes_order(bin_all).reshape(32, LANES),
+        relative_position_table,
+        outer_output_weight,
+        *pair_weights,
+    )
+    blocks, pair_line, turned = lax.optimization_barrier((blocks, pair_line, turned))
+    pair_pieces = [pair_line, exchange(pair_line, 2), exchange(pair_line, 1)]
+
     result, parts = pl.pallas_call(
         msa_kernel,
-        out_shape=(
-            jax.ShapeDtypeStruct((512, channels), jnp.bfloat16),
-            jax.ShapeDtypeStruct((256, LANES), jnp.bfloat16),
-        ),
-        in_specs=[vmem] * 9,
+        out_shape=(array(512, channels), array(256, LANES)),
+        in_specs=[smem] + [vmem] * 24,
         out_specs=(vmem, vmem),
         scratch_shapes=[
             pltpu.VMEM((512, channels), jnp.float32),
             pltpu.VMEM((1024, LANES), jnp.float32),
         ],
-        compiler_params=pltpu.CompilerParams(vmem_limit_bytes=32 * 1024 * 1024),
+        compiler_params=limit(32),
         cost_estimate=pl.CostEstimate(
-            flops=1_000_000_000, bytes_accessed=2_500_000, transcendentals=1_000_000
+            flops=2_000_000_000, bytes_accessed=10_000_000, transcendentals=1_000_000
         ),
         name="msa_whole",
     )(
-        blocks,
+        place,
         live_row_float.reshape(1, LANES),
+        *blocks,
         column_query_weight,
         column_key_weight,
         column_value_gate_weight,
@@ -423,49 +572,19 @@
         alignment_transition_down,
         outer_input_weight.T,
     )
-    return result.reshape(128, 4, channels), parts
-
-
-def lanes_order(values):
-    lead = values.shape[:-1]
-    halves = values.reshape(lead + (values.shape[-1] // 2, 2))
-    return jnp.swapaxes(halves, -1, -2).reshape(values.shape)
-
-
-def pair_whole(
-    parts,
-    pair_state_input,
-    bin_all,
-    live_count,
-    relative_position_table,
-    outer_output_weight,
-    outgoing_projection_weight,
-    outgoing_output_gate,
-    outgoing_output_weight,
-    incoming_projection_weight,
-    incoming_output_gate,
-    incoming_output_weight,
-    pair_transition_up,
-    pair_transition_down,
-):
-    width = pair_state_input.shape[2]
-    own_pair = lanes_order(pair_state_input.transpose(0, 2, 1))
-    own_pair = own_pair.reshape(2, 2, width, 64).transpose(0, 2, 1, 3).reshape(2, width, LANES)
-    pair_all = gather_exchange(own_pair).reshape(32, width, LANES)
-    parts_all = gather_exchange(parts)
-    bins = lanes_order(bin_all).reshape(32, LANES)
-    table = jnp.pad(relative_position_table, ((0, LANES - NBINS), (0, 0))).T
-    mean_weight = (
-        outer_output_weight.reshape(CO, 16, 2, width).transpose(2, 3, 1, 0).reshape(2 * width, 16 * CO)
-    )
-    place = lax.axis_index("dap").astype(jnp.int32).reshape(1)
-    vmem = pl.BlockSpec(memory_space=pltpu.VMEM)
-    smem = pl.BlockSpec(memory_space=pltpu.SMEM)
+    parts, pair_pieces = lax.optimization_barrier((parts, pair_pieces))
+    far = exchange(parts, 8)
+    near = [exchange(parts, 4), exchange(far, 4)]
+    pair_pieces.append(exchange(pair_pieces[1], 1))
+    line = jnp.stack([parts, far] + near)
+    across = exchange(line, 2)
+    pieces = [line, across, exchange(line, 1), exchange(across, 1)]
+
     tall = (32 * 128, LANES)
-    result = pl.pallas_call(
+    pair_output = pl.pallas_call(
         pair_kernel,
-        out_shape=jax.ShapeDtypeStruct((256, LANES), jnp.bfloat16),
-        in_specs=[smem, smem] + [vmem] * 13,
+        out_shape=array(256, LANES),
+        in_specs=[smem, smem] + [vmem] * 18,
         out_specs=vmem,
         scratch_shapes=[
             pltpu.VMEM((2048, LANES), jnp.float32),
@@ -480,37 +599,16 @@
             pltpu.VMEM((1024, LANES), jnp.float32),
             pltpu.VMEM((1024, LANES), jnp.float32),
         ],
-        compiler_params=pltpu.CompilerParams(vmem_limit_bytes=40 * 1024 * 1024),
+        compiler_params=limit(40),
         name="pair_whole",
-    )(
-        place,
-        live_count.reshape(1),
-        parts_all,
-        pair_all,
-        bins,
-        table,
-        mean_weight,
-        outgoing_projection_weight.T,
-        outgoing_output_gate.T,
-        outgoing_output_weight.T,
-        incoming_projection_weight.T,
-        incoming_output_gate.T,
-        incoming_output_weight.T,
-        pair_transition_up.T,
-        pair_transition_down.T,
-    )
-    return result.reshape(pair_state_input.shape)
-
-
-def gather_exchange(block):
-    shard_pieces = lax.axis_size("dap")
-    held = block[None]
-    bit = shard_pieces // 2
-    while bit:
-        other = lax.ppermute(held, "dap", [(q, q ^ bit) for q in range(shard_pieces)])
-        held = jnp.concatenate([held, other], axis=0)
-        bit //= 2
-    return held
+    )(place, jnp.sum(live_row_float).reshape(1), *pieces, *pair_pieces, embedding, *turned)
+    return result.reshape(128, 4, channels), pair_output.reshape(pair_state_input.shape)
+
+
+def lanes_order(values):
+    lead = values.shape[:-1]
+    halves = values.reshape(lead + (values.shape[-1] // 2, 2))
+    return jnp.swapaxes(halves, -1, -2).reshape(values.shape)
 
 
 def local(
@@ -565,9 +663,12 @@
     live_row_float = live_rows.astype(jnp.float32)
 
     if alignment_row_mask.shape[0] == LANES and 2 * residue_count == LANES and own_rows == 4:
-        result, parts = msa_whole(
+        return whole_block(
             alignment_input,
+            pair_state_input,
+            bins_of(residue_number_index, chain_label),
             live_row_float,
+            relative_position_table,
             column_query_weight,
             column_key_weight,
             column_value_gate_weight,
@@ -575,13 +676,6 @@
             alignment_transition_up,
             alignment_transition_down,
             outer_input_weight,
-        )
-        pair_state_output = pair_whole(
-            parts,
-            pair_state_input,
-            bins_of(residue_number_index, chain_label),
-            jnp.sum(live_row_float),
-            relative_position_table,
             outer_output_weight,
             outgoing_projection_weight,
             outgoing_output_gate,
@@ -592,7 +686,6 @@
             pair_transition_up,
             pair_transition_down,
         )
-        return (result, pair_state_output)
 
     def attend_one(operands):
         query_col, key_col, value_col = operands

time: 87 us -> 104 us (1.20)
  starting transfers between devices: 15.7 us -> 32.2 us
  other arithmetic: 2.62 us -> 0.88 us
  Pallas kernels: 34.9 us -> 36.4 us
  waiting for transfers between devices: 15.3 us -> 16.6 us
    ppermute x8 -> x27, starting transfers between devices: 8.17 us -> 32.2 us  [exchange(): return lax.ppermute(values, 'dap', [(q, q ^ offset) for q in range(pieces)])]
    all_to_all x1 -> x0, starting transfers between devices: 7.53 us -> none  [msa_whole(): lax.all_to_all(blocks, 'dap', split_axis=0, concat_axis=0, tiled=True)]
    concatenate x3 -> x0, local copies, waits for them, and re-layouts: 4.62 us -> none  [gather_exchange(): held = jnp.concatenate([held, other], axis=0)]
    unnamed x62 -> x74, local copies, waits for them, and re-layouts: 10.4 us -> 14.2 us
    concatenate x6 -> x0, other arithmetic: 1.8 us -> none  [gather_exchange(): held = jnp.concatenate([held, other], axis=0)]
    pallas_call x3 -> x4, Pallas kernels: 34.9 us -> 36.4 us  [the longest x1 26.6 us: whole_block(): pl.pallas_call(pair_kernel, out_shape=array(256, LANES), in_specs=[smem,...]
    ppermute x8 -> x27, waiting for transfers between devices: 15.3 us -> 16.6 us  [exchange(): return lax.ppermute(values, 'dap', [(q, q ^ offset) for q in range(pieces)])]
  transfers between devices with their start and end apart: 9 -> 27, of which waited for: 4 -> 7; matrix products, arithmetic and copies ran while one was open for 13% -> 3% of each run, Pallas kernels for 8% -> 9%
where the time goes in v4:
time: 104 us
  Pallas kernels  36.4 us (35%)
  starting transfers between devices  32.2 us (31%)
  waiting for transfers between devices  16.6 us (16%)
  local copies, waits for them, and re-layouts  16.4 us (16%)
    ppermute x27, starting transfers between devices, exchange(): return lax.ppermute(values, 'dap', [(q, q ^ offset) for q in range(pieces)])  32.2 us
    pallas_call x1, Pallas kernels, whole_block(): pl.pallas_call(pair_kernel, out_shape=array(256, LANES), in_specs=[smem,...  26.6 us
    ppermute x27, waiting for transfers between devices, exchange(): return lax.ppermute(values, 'dap', [(q, q ^ offset) for q in range(pieces)])  16.6 us
    unnamed x74, local copies, waits for them, and re-layouts  14.2 us
    pallas_call x1, Pallas kernels, whole_block(): pl.pallas_call(msa_kernel, out_shape=(array(512, channels), array(256, LA...  7.28 us
  transfers between devices with their start and end apart: 27, of which 7 were waited for; matrix products, arithmetic and copies ran while one was open for 3% of the time, Pallas kernels for 9%

profile of v4, /device:TPU:0, one launch (start us, length us, event | category | flops | bytes accessed | tf_op | source)
XLA Modules:
  0.0 103.5 jit_solution(17235690182464017323)
XLA Ops:
  0.7 1.0 copy-done
  3.0 4.1 %collective-permute-start.15 = (bf16[2,128,128]{2,1,0:T(8,128)(2,1)S(1)}, bf16[2,128,128]{2,1,0:T(8,128)(2,1)S(1)}, u32[]{:S(2)}, u32[]{:S(2)}) collective-permute-start(bf16[2,128,128]{2,1,0:T(8,128)(2,1)S(1)} %get-tuple-element.77), channel_id=1, source_target_pairs={{0,8},{1,9},{2,10},{3,11},{4,12},{5,13},{6,14},{7,15},{8,0},{9,1},... | collective-permute-start | bytes 196616 | tf_op jit(solution)/shard_map/ppermute | solution.py:479
  7.1 1.5 %collective-permute-start.1 = (bf16[32,256]{1,0:T(8,128)(2,1)S(1)}, bf16[32,256]{1,0:T(8,128)(2,1)S(1)}, u32[]{:S(2)}, u32[]{:S(2)}) collective-permute-start(bf16[32,256]{1,0:T(8,128)(2,1)S(1)} %get-tuple-element.63), channel_id=1, source_target_pairs={{0,2},{1,3},{2,0},{3,1},{4,6},{5,7},{6,4},{7,5},{8,10},{9,11},{10,... | collective-permute-start | bytes 49160 | tf_op jit(solution)/shard_map/ppermute | solution.py:479
  8.9 1.6 %collective-permute-start.3 = (bf16[32,256]{1,0:T(8,128)(2,1)S(1)}, bf16[32,256]{1,0:T(8,128)(2,1)S(1)}, u32[]{:S(2)}, u32[]{:S(2)}) collective-permute-start(bf16[32,256]{1,0:T(8,128)(2,1)S(1)} %get-tuple-element.65), channel_id=1, source_target_pairs={{0,4},{1,5},{2,6},{3,7},{4,0},{5,1},{6,2},{7,3},{8,12},{9,13},{10,... | collective-permute-start | bytes 49160 | tf_op jit(solution)/shard_map/ppermute | solution.py:479
  11.4 0.9 collective-permute-start.4
  12.3 1.7 %collective-permute-start.5 = (bf16[32,256]{1,0:T(8,128)(2,1)S(1)}, bf16[32,256]{1,0:T(8,128)(2,1)S(1)}, u32[]{:S(2)}, u32[]{:S(2)}) collective-permute-start(bf16[32,256]{1,0:T(8,128)(2,1)S(1)} %get-tuple-element.67), channel_id=1, source_target_pairs={{0,6},{1,7},{2,4},{3,5},{4,2},{5,3},{6,0},{7,1},{8,14},{9,15},{10,... | collective-permute-start | bytes 49160 | tf_op jit(solution)/shard_map/ppermute | solution.py:479
  14.0 1.3 %collective-permute-start.6 = (bf16[32,256]{1,0:T(8,128)(2,1)S(1)}, bf16[32,256]{1,0:T(8,128)(2,1)S(1)}, u32[]{:S(2)}, u32[]{:S(2)}) collective-permute-start(bf16[32,256]{1,0:T(8,128)(2,1)S(1)} %get-tuple-element.68), channel_id=1, source_target_pairs={{0,7},{1,6},{2,5},{3,4},{4,3},{5,2},{6,1},{7,0},{8,15},{9,14},{10,... | collective-permute-start | bytes 49160 | tf_op jit(solution)/shard_map/ppermute | solution.py:479
  16.9 1.8 %collective-permute-start.8 = (bf16[32,256]{1,0:T(8,128)(2,1)S(1)}, bf16[32,256]{1,0:T(8,128)(2,1)S(1)}, u32[]{:S(2)}, u32[]{:S(2)}) collective-permute-start(bf16[32,256]{1,0:T(8,128)(2,1)S(1)} %get-tuple-element.70), channel_id=1, source_target_pairs={{0,9},{1,8},{2,11},{3,10},{4,13},{5,12},{6,15},{7,14},{8,1},{9,0},... | collective-permute-start | bytes 49160 | tf_op jit(solution)/shard_map/ppermute | solution.py:479
  18.8 1.4 %collective-permute-start.9 = (bf16[32,256]{1,0:T(8,128)(2,1)S(1)}, bf16[32,256]{1,0:T(8,128)(2,1)S(1)}, u32[]{:S(2)}, u32[]{:S(2)}) collective-permute-start(bf16[32,256]{1,0:T(8,128)(2,1)S(1)} %get-tuple-element.71), channel_id=1, source_target_pairs={{0,10},{1,11},{2,8},{3,9},{4,14},{5,15},{6,12},{7,13},{8,2},{9,3},... | collective-permute-start | bytes 49160 | tf_op jit(solution)/shard_map/ppermute | solution.py:479
  20.2 0.9 copy-done.11
  21.1 0.9 copy-done.12
  25.0 2.1 %turn_weights.1 = (bf16[32,128,128]{2,1,0:T(8,128)(2,1)S(1)}, bf16[256,512]{1,0:T(8,128)(2,1)S(1)}, bf16[512,128]{1,0:T(8,128)(2,1)S(1)}, bf16[128,128]{1,0:T(8,...) custom-call(s32[32,128]{1,0:T(8,128)S(1)} %select_n.11.bins_ref, ...), custom_call_target="tpu_custom_call" | custom-call | flops 200000000 | bytes 4000000 | tf_op jit(solution)/shard_map/turn_weights/pallas_call | solution.py:525
  27.1 2.4 %collective-permute-start.10 = (bf16[32,256]{1,0:T(8,128)(2,1)S(1)}, bf16[32,256]{1,0:T(8,128)(2,1)S(1)}, u32[]{:S(2)}, u32[]{:S(2)}) collective-permute-start(bf16[32,256]{1,0:T(8,128)(2,1)S(1)} %get-tuple-element.72), channel_id=1, source_target_pairs={{0,11},{1,10},{2,9},{3,8},{4,15},{5,14},{6,13},{7,12},{8,3},{9,2},... | collective-permute-start | bytes 49160 | tf_op jit(solution)/shard_map/ppermute | solution.py:479
  29.5 1.3 %collective-permute-start.11 = (bf16[32,256]{1,0:T(8,128)(2,1)S(1)}, bf16[32,256]{1,0:T(8,128)(2,1)S(1)}, u32[]{:S(2)}, u32[]{:S(2)}) collective-permute-start(bf16[32,256]{1,0:T(8,128)(2,1)S(1)} %get-tuple-element.73), channel_id=1, source_target_pairs={{0,12},{1,13},{2,14},{3,15},{4,8},{5,9},{6,10},{7,11},{8,4},{9,5},... | collective-permute-start | bytes 49160 | tf_op jit(solution)/shard_map/ppermute | solution.py:479
  30.8 2.1 %collective-permute-start.12 = (bf16[32,256]{1,0:T(8,128)(2,1)S(1)}, bf16[32,256]{1,0:T(8,128)(2,1)S(1)}, u32[]{:S(2)}, u32[]{:S(2)}) collective-permute-start(bf16[32,256]{1,0:T(8,128)(2,1)S(1)} %get-tuple-element.74), channel_id=1, source_target_pairs={{0,13},{1,12},{2,15},{3,14},{4,9},{5,8},{6,11},{7,10},{8,5},{9,4},... | collective-permute-start | bytes 49160 | tf_op jit(solution)/shard_map/ppermute | solution.py:479
  32.9 2.4 %collective-permute-start.13 = (bf16[32,256]{1,0:T(8,128)(2,1)S(1)}, bf16[32,256]{1,0:T(8,128)(2,1)S(1)}, u32[]{:S(2)}, u32[]{:S(2)}) collective-permute-start(bf16[32,256]{1,0:T(8,128)(2,1)S(1)} %get-tuple-element.75), channel_id=1, source_target_pairs={{0,14},{1,15},{2,12},{3,13},{4,10},{5,11},{6,8},{7,9},{8,6},{9,7},... | collective-permute-start | bytes 49160 | tf_op jit(solution)/shard_map/ppermute | solution.py:479
  35.3 2.2 %collective-permute-start.14 = (bf16[32,256]{1,0:T(8,128)(2,1)S(1)}, bf16[32,256]{1,0:T(8,128)(2,1)S(1)}, u32[]{:S(2)}, u32[]{:S(2)}) collective-permute-start(bf16[32,256]{1,0:T(8,128)(2,1)S(1)} %get-tuple-element.76), channel_id=1, source_target_pairs={{0,15},{1,14},{2,13},{3,12},{4,11},{5,10},{6,9},{7,8},{8,7},{9,6},... | collective-permute-start | bytes 49160 | tf_op jit(solution)/shard_map/ppermute | solution.py:479
  37.6 1.7 %collective-permute-done.13.rest_14_ = bf16[32,256]{1,0:T(8,128)(2,1)S(1)} collective-permute-done((bf16[32,256]{1,0:T(8,128)(2,1)S(1)}, bf16[32,256]{1,0:T(8,128)(2,1)S(1)}, u32[]{:S(2)}, u32[]{:S(2)}) %collective-permute-start.13) | collective-permute-done | bytes 16416 | tf_op jit(solution)/shard_map/ppermute | solution.py:479
  39.3 1.8 %collective-permute-done.14.rest_15_ = bf16[32,256]{1,0:T(8,128)(2,1)S(1)} collective-permute-done((bf16[32,256]{1,0:T(8,128)(2,1)S(1)}, bf16[32,256]{1,0:T(8,128)(2,1)S(1)}, u32[]{:S(2)}, u32[]{:S(2)}) %collective-permute-start.14) | collective-permute-done | bytes 16416 | tf_op jit(solution)/shard_map/ppermute | solution.py:479
  41.9 0.9 copy-done.31
  42.8 0.9 copy-done.32
  43.7 7.3 %msa_whole.1 = (bf16[512,256]{1,0:T(8,128)(2,1)S(1)}, bf16[256,128]{1,0:T(8,128)(2,1)S(1)}) custom-call(s32[1]{0:T(128)} %bitcast.place_ref, f32[1,128]{1,0:T(1,128)S(1)} %fusion.1.live_ref, bf16[32,256]{1,0:T(8,128)(2,1)S(1)} %get-tuple-element.87.rest_0_, bf16[32,256]{1,0:T(8,128)(2,1)S(1)} %collective-permute-done.rest_1_, ...), custom_call_target="tpu_custom_call" | custom-call | flops 2000000000 | bytes 10000000 | tf_op jit(solution)/shard_map/msa_whole/pallas_call | solution.py:549
  51.1 3.0 %collective-permute-start.21 = (bf16[256,128]{1,0:T(8,128)(2,1)S(1)}, bf16[256,128]{1,0:T(8,128)(2,1)S(1)}, u32[]{:S(2)}, u32[]{:S(2)}) collective-permute-start(bf16[256,128]{1,0:T(8,128)(2,1)S(1)} %get-tuple-element.106), channel_id=1, source_target_pairs={{0,4},{1,5},{2,6},{3,7},{4,0},{5,1},{6,2},{7,3},{8,12},{9,13},{10,... | collective-permute-start | bytes 196616 | tf_op jit(solution)/shard_map/ppermute | solution.py:479
  54.1 3.3 %collective-permute-done.20 = bf16[256,128]{1,0:T(8,128)(2,1)S(1)} collective-permute-done((bf16[256,128]{1,0:T(8,128)(2,1)S(1)}, bf16[256,128]{1,0:T(8,128)(2,1)S(1)}, u32[]{:S(2)}, u32[]{:S(2)}) %collective-permute-start.20) | collective-permute-done | bytes 65568 | tf_op jit(solution)/shard_map/ppermute | solution.py:479
  57.7 4.0 %collective-permute-done.22 = bf16[256,128]{1,0:T(8,128)(2,1)S(1)} collective-permute-done((bf16[256,128]{1,0:T(8,128)(2,1)S(1)}, bf16[256,128]{1,0:T(8,128)(2,1)S(1)}, u32[]{:S(2)}, u32[]{:S(2)}) %collective-permute-start.22) | collective-permute-done | bytes 65568 | tf_op jit(solution)/shard_map/ppermute | solution.py:479
  61.7 1.2 %collective-permute-start.23 = (bf16[4,256,128]{2,1,0:T(8,128)(2,1)S(1)}, bf16[4,256,128]{2,1,0:T(8,128)(2,1)S(1)}, u32[]{:S(2)}, u32[]{:S(2)}) collective-permute-start(bf16[4,256,128]{2,1,0:T(8,128)(2,1)S(1)} %pad_maximum_fusion.1.rest_0_), channel_id=1, source_target_pairs={{0,2},{1,3},{2,0},{3,1},{4,6},{5,7},{6,4},{7,5},{8,10},{9,11},{10,... | collective-permute-start | bytes 786440 | tf_op jit(solution)/shard_map/ppermute | solution.py:479
  63.4 5.4 %collective-permute-done.23.rest_1_ = bf16[4,256,128]{2,1,0:T(8,128)(2,1)S(1)} collective-permute-done((bf16[4,256,128]{2,1,0:T(8,128)(2,1)S(1)}, bf16[4,256,128]{2,1,0:T(8,128)(2,1)S(1)}, u32[]{:S(2)}, u32[]{:S(2)}) %collective-permute-start.23) | collective-permute-done | bytes 262176 | tf_op jit(solution)/shard_map/ppermute | solution.py:479
  69.4 1.7 %reshape.59 = bf16[128,4,256]{2,1,0:T(4,128)(2,1)} reshape(bf16[512,256]{1,0:T(8,128)(2,1)} %copy-done.1) | data formatting | bytes 524288 | tf_op jit(solution)/shard_map/reshape | solution.py:605
  71.2 0.9 copy-done.4
  72.1 0.9 copy-done.6
  73.0 0.9 copy-done.8
  76.9 26.6 %pair_whole.1 = bf16[256,128]{1,0:T(8,128)(2,1)} custom-call(s32[1]{0:T(128)} %bitcast.place_ref, f32[1]{0:T(128)} %bitcast.9.live_ref, bf16[4,256,128]{2,1,0:T(8,128)(2,1)S(1)} %pad_maximum_fusion.1.rest_0_, bf16[4,256,128]{2,1,0:T(8,128)(2,1)S(1)} %collective-permute-done.23.rest_1_, bf16[4,256,128]{2,1,0:T(8,128)(2,1)S(1)} %collective-permute-done.24.rest_2_, ...), custom_call_target="tpu_custom_call" | custom-call | tf_op jit(solution)/shard_map/pair_whole/pallas_call | solution.py:584
  (111 shorter events, 12.4 us)
Async XLA Ops:
  2.5 17.7 %copy-start.2 = (bf16[1024,128]{1,0:T(8,128)(2,1)S(1)}, bf16[1024,128]{1,0:T(8,128)(2,1)}, u32[]{:S(2)}) copy-start(bf16[1024,128]{1,0:T(8,128)(2,1)} %mean_weight_ref.1) | copy-start | bytes 786436
  2.5 17.7 %copy-start.10 = (bf16[128,512]{1,0:T(8,128)(2,1)S(1)}, bf16[128,512]{1,0:T(8,128)(2,1)}, u32[]{:S(2)}) copy-start(bf16[128,512]{1,0:T(8,128)(2,1)} %in_mix_ref.1) | copy-start | bytes 393220
  3.0 17.2 %copy-start.9 = (bf16[128,512]{1,0:T(8,128)(2,1)S(1)}, bf16[128,512]{1,0:T(8,128)(2,1)}, u32[]{:S(2)}) copy-start(bf16[128,512]{1,0:T(8,128)(2,1)} %out_mix_ref.1) | copy-start | bytes 393220
  3.0 12.3 %collective-permute-start.15 = (bf16[2,128,128]{2,1,0:T(8,128)(2,1)S(1)}, bf16[2,128,128]{2,1,0:T(8,128)(2,1)S(1)}, u32[]{:S(2)}, u32[]{:S(2)}) collective-permute-start(bf16[2,128,128]{2,1,0:T(8,128)(2,1)S(1)} %get-tuple-element.77), channel_id=1, source_target_pairs={{0,8},{1,9},{2,10},{3,11},{4,12},{5,13},{6,14},{7,15},{8,0},{9,1},... | collective-permute-start | bytes 196616 | tf_op jit(solution)/shard_map/ppermute | solution.py:479
  7.1 3.8 %collective-permute-start = (bf16[32,256]{1,0:T(8,128)(2,1)S(1)}, bf16[32,256]{1,0:T(8,128)(2,1)S(1)}, u32[]{:S(2)}, u32[]{:S(2)}) collective-permute-start(bf16[32,256]{1,0:T(8,128)(2,1)S(1)} %get-tuple-element.62), channel_id=1, source_target_pairs={{0,1},{1,0},{2,3},{3,2},{4,5},{5,4},{6,7},{7,6},{8,9},{9,8},{10,11... | collective-permute-start | bytes 49160 | tf_op jit(solution)/shard_map/ppermute | solution.py:479
  7.1 4.3 %collective-permute-start.1 = (bf16[32,256]{1,0:T(8,128)(2,1)S(1)}, bf16[32,256]{1,0:T(8,128)(2,1)S(1)}, u32[]{:S(2)}, u32[]{:S(2)}) collective-permute-start(bf16[32,256]{1,0:T(8,128)(2,1)S(1)} %get-tuple-element.63), channel_id=1, source_target_pairs={{0,2},{1,3},{2,0},{3,1},{4,6},{5,7},{6,4},{7,5},{8,10},{9,11},{10,... | collective-permute-start | bytes 49160 | tf_op jit(solution)/shard_map/ppermute | solution.py:479
  8.6 3.7 %collective-permute-start.2 = (bf16[32,256]{1,0:T(8,128)(2,1)S(1)}, bf16[32,256]{1,0:T(8,128)(2,1)S(1)}, u32[]{:S(2)}, u32[]{:S(2)}) collective-permute-start(bf16[32,256]{1,0:T(8,128)(2,1)S(1)} %get-tuple-element.64), channel_id=1, source_target_pairs={{0,3},{1,2},{2,1},{3,0},{4,7},{5,6},{6,5},{7,4},{8,11},{9,10},{10,... | collective-permute-start | bytes 49160 | tf_op jit(solution)/shard_map/ppermute | solution.py:479
  8.9 5.0 %collective-permute-start.3 = (bf16[32,256]{1,0:T(8,128)(2,1)S(1)}, bf16[32,256]{1,0:T(8,128)(2,1)S(1)}, u32[]{:S(2)}, u32[]{:S(2)}) collective-permute-start(bf16[32,256]{1,0:T(8,128)(2,1)S(1)} %get-tuple-element.65), channel_id=1, source_target_pairs={{0,4},{1,5},{2,6},{3,7},{4,0},{5,1},{6,2},{7,3},{8,12},{9,13},{10,... | collective-permute-start | bytes 49160 | tf_op jit(solution)/shard_map/ppermute | solution.py:479
  10.9 22.0 %collective-permute-start.16 = (bf16[2,128,128]{2,1,0:T(8,128)(2,1)S(1)}, bf16[2,128,128]{2,1,0:T(8,128)(2,1)S(1)}, u32[]{:S(2)}, u32[]{:S(2)}) collective-permute-start(bf16[2,128,128]{2,1,0:T(8,128)(2,1)S(1)} %get-tuple-element.77), channel_id=1, source_target_pairs={{0,4},{1,5},{2,6},{3,7},{4,0},{5,1},{6,2},{7,3},{8,12},{9,13},{10,... | collective-permute-start | bytes 196616 | tf_op jit(solution)/shard_map/ppermute | solution.py:479
  11.4 4.8 %collective-permute-start.4 = (bf16[32,256]{1,0:T(8,128)(2,1)S(1)}, bf16[32,256]{1,0:T(8,128)(2,1)S(1)}, u32[]{:S(2)}, u32[]{:S(2)}) collective-permute-start(bf16[32,256]{1,0:T(8,128)(2,1)S(1)} %get-tuple-element.66), channel_id=1, source_target_pairs={{0,5},{1,4},{2,7},{3,6},{4,1},{5,0},{6,3},{7,2},{8,13},{9,12},{10,... | collective-permute-start | bytes 49160 | tf_op jit(solution)/shard_map/ppermute | solution.py:479
  12.3 4.6 %collective-permute-start.5 = (bf16[32,256]{1,0:T(8,128)(2,1)S(1)}, bf16[32,256]{1,0:T(8,128)(2,1)S(1)}, u32[]{:S(2)}, u32[]{:S(2)}) collective-permute-start(bf16[32,256]{1,0:T(8,128)(2,1)S(1)} %get-tuple-element.67), channel_id=1, source_target_pairs={{0,6},{1,7},{2,4},{3,5},{4,2},{5,3},{6,0},{7,1},{8,14},{9,15},{10,... | collective-permute-start | bytes 49160 | tf_op jit(solution)/shard_map/ppermute | solution.py:479
  14.0 4.8 %collective-permute-start.6 = (bf16[32,256]{1,0:T(8,128)(2,1)S(1)}, bf16[32,256]{1,0:T(8,128)(2,1)S(1)}, u32[]{:S(2)}, u32[]{:S(2)}) collective-permute-start(bf16[32,256]{1,0:T(8,128)(2,1)S(1)} %get-tuple-element.68), channel_id=1, source_target_pairs={{0,7},{1,6},{2,5},{3,4},{4,3},{5,2},{6,1},{7,0},{8,15},{9,14},{10,... | collective-permute-start | bytes 49160 | tf_op jit(solution)/shard_map/ppermute | solution.py:479
  15.3 20.0 %collective-permute-start.17 = (bf16[2,128,128]{2,1,0:T(8,128)(2,1)S(1)}, bf16[2,128,128]{2,1,0:T(8,128)(2,1)S(1)}, u32[]{:S(2)}, u32[]{:S(2)}) collective-permute-start(bf16[2,128,128]{2,1,0:T(8,128)(2,1)S(1)} %collective-permute-done.15), channel_id=1, source_target_pairs={{0,4},{1,5},{2,6},{3,7},{4,0},{5,1},{6,2},{7,3},{8,12},{9,13},{10,... | collective-permute-start | bytes 196616 | tf_op jit(solution)/shard_map/ppermute | solution.py:479
  16.2 11.0 %collective-permute-start.7 = (bf16[32,256]{1,0:T(8,128)(2,1)S(1)}, bf16[32,256]{1,0:T(8,128)(2,1)S(1)}, u32[]{:S(2)}, u32[]{:S(2)}) collective-permute-start(bf16[32,256]{1,0:T(8,128)(2,1)S(1)} %get-tuple-element.69), channel_id=1, source_target_pairs={{0,8},{1,9},{2,10},{3,11},{4,12},{5,13},{6,14},{7,15},{8,0},{9,1},... | collective-permute-start | bytes 49160 | tf_op jit(solution)/shard_map/ppermute | solution.py:479
  16.9 12.6 %collective-permute-start.8 = (bf16[32,256]{1,0:T(8,128)(2,1)S(1)}, bf16[32,256]{1,0:T(8,128)(2,1)S(1)}, u32[]{:S(2)}, u32[]{:S(2)}) collective-permute-start(bf16[32,256]{1,0:T(8,128)(2,1)S(1)} %get-tuple-element.70), channel_id=1, source_target_pairs={{0,9},{1,8},{2,11},{3,10},{4,13},{5,12},{6,15},{7,14},{8,1},{9,0},... | collective-permute-start | bytes 49160 | tf_op jit(solution)/shard_map/ppermute | solution.py:479
  18.8 12.0 %collective-permute-start.9 = (bf16[32,256]{1,0:T(8,128)(2,1)S(1)}, bf16[32,256]{1,0:T(8,128)(2,1)S(1)}, u32[]{:S(2)}, u32[]{:S(2)}) collective-permute-start(bf16[32,256]{1,0:T(8,128)(2,1)S(1)} %get-tuple-element.71), channel_id=1, source_target_pairs={{0,10},{1,11},{2,8},{3,9},{4,14},{5,15},{6,12},{7,13},{8,2},{9,3},... | collective-permute-start | bytes 49160 | tf_op jit(solution)/shard_map/ppermute | solution.py:479
  25.0 16.9 %copy-start.27 = (bf16[256,1024]{1,0:T(8,128)(2,1)S(1)}, bf16[256,1024]{1,0:T(8,128)(2,1)}, u32[]{:S(2)}) copy-start(bf16[256,1024]{1,0:T(8,128)(2,1)} %rest_20_.1) | copy-start | bytes 1572868
  25.0 16.9 %copy-start.28 = (bf16[1024,256]{1,0:T(8,128)(2,1)S(1)}, bf16[1024,256]{1,0:T(8,128)(2,1)}, u32[]{:S(2)}) copy-start(bf16[1024,256]{1,0:T(8,128)(2,1)} %rest_21_.1) | copy-start | bytes 1572868
  27.1 10.5 %collective-permute-start.10 = (bf16[32,256]{1,0:T(8,128)(2,1)S(1)}, bf16[32,256]{1,0:T(8,128)(2,1)S(1)}, u32[]{:S(2)}, u32[]{:S(2)}) collective-permute-start(bf16[32,256]{1,0:T(8,128)(2,1)S(1)} %get-tuple-element.72), channel_id=1, source_target_pairs={{0,11},{1,10},{2,9},{3,8},{4,15},{5,14},{6,13},{7,12},{8,3},{9,2},... | collective-permute-start | bytes 49160 | tf_op jit(solution)/shard_map/ppermute | solution.py:479
  29.5 8.1 %collective-permute-start.11 = (bf16[32,256]{1,0:T(8,128)(2,1)S(1)}, bf16[32,256]{1,0:T(8,128)(2,1)S(1)}, u32[]{:S(2)}, u32[]{:S(2)}) collective-permute-start(bf16[32,256]{1,0:T(8,128)(2,1)S(1)} %get-tuple-element.73), channel_id=1, source_target_pairs={{0,12},{1,13},{2,14},{3,15},{4,8},{5,9},{6,10},{7,11},{8,4},{9,5},... | collective-permute-start | bytes 49160 | tf_op jit(solution)/shard_map/ppermute | solution.py:479
  30.8 6.8 %collective-permute-start.12 = (bf16[32,256]{1,0:T(8,128)(2,1)S(1)}, bf16[32,256]{1,0:T(8,128)(2,1)S(1)}, u32[]{:S(2)}, u32[]{:S(2)}) collective-permute-start(bf16[32,256]{1,0:T(8,128)(2,1)S(1)} %get-tuple-element.74), channel_id=1, source_target_pairs={{0,13},{1,12},{2,15},{3,14},{4,9},{5,8},{6,11},{7,10},{8,5},{9,4},... | collective-permute-start | bytes 49160 | tf_op jit(solution)/shard_map/ppermute | solution.py:479
  32.9 6.4 %collective-permute-start.13 = (bf16[32,256]{1,0:T(8,128)(2,1)S(1)}, bf16[32,256]{1,0:T(8,128)(2,1)S(1)}, u32[]{:S(2)}, u32[]{:S(2)}) collective-permute-start(bf16[32,256]{1,0:T(8,128)(2,1)S(1)} %get-tuple-element.75), channel_id=1, source_target_pairs={{0,14},{1,15},{2,12},{3,13},{4,10},{5,11},{6,8},{7,9},{8,6},{9,7},... | collective-permute-start | bytes 49160 | tf_op jit(solution)/shard_map/ppermute | solution.py:479
  35.3 5.9 %collective-permute-start.14 = (bf16[32,256]{1,0:T(8,128)(2,1)S(1)}, bf16[32,256]{1,0:T(8,128)(2,1)S(1)}, u32[]{:S(2)}, u32[]{:S(2)}) collective-permute-start(bf16[32,256]{1,0:T(8,128)(2,1)S(1)} %get-tuple-element.76), channel_id=1, source_target_pairs={{0,15},{1,14},{2,13},{3,12},{4,11},{5,10},{6,9},{7,8},{8,7},{9,6},... | collective-permute-start | bytes 49160 | tf_op jit(solution)/shard_map/ppermute | solution.py:479
  41.2 9.8 %collective-permute-start.19 = (bf16[4,2,128,128]{3,2,1,0:T(8,128)(2,1)S(1)}, bf16[4,2,128,128]{3,2,1,0:T(8,128)(2,1)S(1)}, u32[]{:S(2)}, u32[]{:S(2)}) collective-permute-start(bf16[4,2,128,128]{3,2,1,0:T(8,128)(2,1)S(1)} %pad_maximum_fusion.rest_4_), channel_id=1, source_target_pairs={{0,1},{1,0},{2,3},{3,2},{4,5},{5,4},{6,7},{7,6},{8,9},{9,8},{10,11... | collective-permute-start | bytes 786440 | tf_op jit(solution)/shard_map/ppermute | solution.py:479
  41.3 9.7 %collective-permute-start.18 = (bf16[4,2,128,128]{3,2,1,0:T(8,128)(2,1)S(1)}, bf16[4,2,128,128]{3,2,1,0:T(8,128)(2,1)S(1)}, u32[]{:S(2)}, u32[]{:S(2)}) collective-permute-start(bf16[4,2,128,128]{3,2,1,0:T(8,128)(2,1)S(1)} %pad_maximum_fusion.rest_4_), channel_id=1, source_target_pairs={{0,2},{1,3},{2,0},{3,1},{4,6},{5,7},{6,4},{7,5},{8,10},{9,11},{10,... | collective-permute-start | bytes 786440 | tf_op jit(solution)/shard_map/ppermute | solution.py:479
  51.0 6.4 %collective-permute-start.20 = (bf16[256,128]{1,0:T(8,128)(2,1)S(1)}, bf16[256,128]{1,0:T(8,128)(2,1)S(1)}, u32[]{:S(2)}, u32[]{:S(2)}) collective-permute-start(bf16[256,128]{1,0:T(8,128)(2,1)S(1)} %get-tuple-element.106), channel_id=1, source_target_pairs={{0,8},{1,9},{2,10},{3,11},{4,12},{5,13},{6,14},{7,15},{8,0},{9,1},... | collective-permute-start | bytes 196616 | tf_op jit(solution)/shard_map/ppermute | solution.py:479
  51.1 6.6 %collective-permute-start.21 = (bf16[256,128]{1,0:T(8,128)(2,1)S(1)}, bf16[256,128]{1,0:T(8,128)(2,1)S(1)}, u32[]{:S(2)}, u32[]{:S(2)}) collective-permute-start(bf16[256,128]{1,0:T(8,128)(2,1)S(1)} %get-tuple-element.106), channel_id=1, source_target_pairs={{0,4},{1,5},{2,6},{3,7},{4,0},{5,1},{6,2},{7,3},{8,12},{9,13},{10,... | collective-permute-start | bytes 196616 | tf_op jit(solution)/shard_map/ppermute | solution.py:479
  57.4 4.3 %collective-permute-start.22 = (bf16[256,128]{1,0:T(8,128)(2,1)S(1)}, bf16[256,128]{1,0:T(8,128)(2,1)S(1)}, u32[]{:S(2)}, u32[]{:S(2)}) collective-permute-start(bf16[256,128]{1,0:T(8,128)(2,1)S(1)} %collective-permute-done.20), channel_id=1, source_target_pairs={{0,4},{1,5},{2,6},{3,7},{4,0},{5,1},{6,2},{7,3},{8,12},{9,13},{10,... | collective-permute-start | bytes 196616 | tf_op jit(solution)/shard_map/ppermute | solution.py:479
  61.7 7.1 %collective-permute-start.23 = (bf16[4,256,128]{2,1,0:T(8,128)(2,1)S(1)}, bf16[4,256,128]{2,1,0:T(8,128)(2,1)S(1)}, u32[]{:S(2)}, u32[]{:S(2)}) collective-permute-start(bf16[4,256,128]{2,1,0:T(8,128)(2,1)S(1)} %pad_maximum_fusion.1.rest_0_), channel_id=1, source_target_pairs={{0,2},{1,3},{2,0},{3,1},{4,6},{5,7},{6,4},{7,5},{8,10},{9,11},{10,... | collective-permute-start | bytes 786440 | tf_op jit(solution)/shard_map/ppermute | solution.py:479
  62.9 8.3 %collective-permute-start.26 = (bf16[4,2,128,128]{3,2,1,0:T(8,128)(2,1)S(1)}, bf16[4,2,128,128]{3,2,1,0:T(8,128)(2,1)S(1)}, u32[]{:S(2)}, u32[]{:S(2)}) collective-permute-start(bf16[4,2,128,128]{3,2,1,0:T(8,128)(2,1)S(1)} %collective-permute-done.18.rest_5_), channel_id=1, source_target_pairs={{0,1},{1,0},{2,3},{3,2},{4,5},{5,4},{6,7},{7,6},{8,9},{9,8},{10,11... | collective-permute-start | bytes 786440 | tf_op jit(solution)/shard_map/ppermute | solution.py:479
  62.9 8.3 %collective-permute-start.24 = (bf16[4,256,128]{2,1,0:T(8,128)(2,1)S(1)}, bf16[4,256,128]{2,1,0:T(8,128)(2,1)S(1)}, u32[]{:S(2)}, u32[]{:S(2)}) collective-permute-start(bf16[4,256,128]{2,1,0:T(8,128)(2,1)S(1)} %pad_maximum_fusion.1.rest_0_), channel_id=1, source_target_pairs={{0,1},{1,0},{2,3},{3,2},{4,5},{5,4},{6,7},{7,6},{8,9},{9,8},{10,11... | collective-permute-start | bytes 786440 | tf_op jit(solution)/shard_map/ppermute | solution.py:479
  68.8 2.3 %collective-permute-start.25 = (bf16[4,256,128]{2,1,0:T(8,128)(2,1)S(1)}, bf16[4,256,128]{2,1,0:T(8,128)(2,1)S(1)}, u32[]{:S(2)}, u32[]{:S(2)}) collective-permute-start(bf16[4,256,128]{2,1,0:T(8,128)(2,1)S(1)} %collective-permute-done.23.rest_1_), channel_id=1, source_target_pairs={{0,1},{1,0},{2,3},{3,2},{4,5},{5,4},{6,7},{7,6},{8,9},{9,8},{10,11... | collective-permute-start | bytes 786440 | tf_op jit(solution)/shard_map/ppermute | solution.py:479
  (32 other events, 136.3 us)

commit v5 on v4

--- a/solution.py
+++ b/solution.py
@@ -1,5 +1,3 @@
-import functools
-
 import jax
 import jax.numpy as jnp
 from jax import lax
@@ -98,57 +96,47 @@
     return straight + pltpu.roll(crossed, LANES // 2, 1)
 
 
-def pair_kernel(
+def turned(ref, name):
+    first, last = TURNED[name]
+    return ref[first:last, :]
+
+
+OFFSETS = (0, 8, 4, 12)
+
+
+def start_kernel(
     place_ref,
     live_ref,
-    *rest,
-):
-    pair_body(place_ref, live_ref, rest[:4], rest[4:8], *rest[8:])
-
-
-def pair_body(
-    place_ref,
-    live_ref,
-    part_refs,
-    pair_refs,
+    line_ref,
+    across_ref,
+    core_line_ref,
+    core_across_ref,
+    pair_line_ref,
+    pair_across_ref,
     embedding_ref,
-    mean_weight_ref,
-    out_mix_ref,
-    out_gate_ref,
-    out_final_ref,
-    in_mix_ref,
-    in_gate_ref,
-    in_final_ref,
-    up_ref,
-    down_ref,
-    result_ref,
+    turned_ref,
+    wide_weight_ref,
+    pair_mid_ref,
+    left_ref,
+    gating_ref,
+    right_ref,
     wide_ref,
     right_cols_ref,
-    stack_ref,
-    pair_now_ref,
-    left_ref,
-    right_ref,
-    product_ref,
-    gating_ref,
-    chosen_ref,
-    own_left_ref,
-    own_product_ref,
+    *stack_refs,
 ):
     place = place_ref[0]
     inverse_live = 1.0 / live_ref[0]
     half = LANES // 2
     low_half = lax.broadcasted_iota(jnp.int32, (LANES, LANES), 1) < half
-    low_short = lax.broadcasted_iota(jnp.int32, (32, LANES), 1) < half
-
-    offsets = (0, 2, 1, 3)
-
-    def owner_of(piece, m):
-        return place ^ (offsets[piece] + (m & 1) * 8 + (m & 2) * 2)
-
-    for piece in range(4):
-        for m in range(4):
-            first = pl.multiple_of(owner_of(piece, m) * 128, 128)
-            wide_ref[pl.ds(first, 128), :] = part_refs[piece][m, 128:256, :].astype(jnp.float32)
+
+    for m in range(4):
+        for part, device in (
+            (line_ref[m, 128:256, :], place ^ OFFSETS[m]),
+            (across_ref[m, 128:256, :], place ^ OFFSETS[m] ^ 2),
+            (core_line_ref[m], place ^ OFFSETS[m] ^ 1),
+            (core_across_ref[m], place ^ OFFSETS[m] ^ 3),
+        ):
+            wide_ref[pl.ds(pl.multiple_of(device * 128, 128), 128), :] = part.astype(jnp.float32)
     for d in range(0, CO, 2):
         rows = [
             wide_ref[pl.ds(par * CO + d + e, 32, stride=2 * CO), :]
@@ -159,141 +147,181 @@
             jnp.concatenate(rows, axis=0).T.astype(jnp.bfloat16)
         )
 
-    def first_chunk(piece, g, carry):
-        left_rows = part_refs[piece][pl.ds(2 * g, 2), 0:128, :].reshape(256, LANES)
+    for g in range(4):
+        parts_ref = (line_ref, across_ref)[g // 2]
+        pair_ref = (pair_line_ref, pair_across_ref)[g // 2]
+        stack_ref = stack_refs[g % 2]
+        first = 2 * (g % 2)
+        left_rows = parts_ref[first : first + 2, 0:128, :].reshape(256, LANES)
         outer = mix(left_rows, right_cols_ref[...]).astype(jnp.bfloat16)
         for i in range(8):
             for d in range(16):
                 stack_ref[d * 32 : (d + 1) * 32, i * LANES : (i + 1) * LANES] = outer[
                     i * 32 : (i + 1) * 32, d * LANES : (d + 1) * LANES
                 ]
-        mixed = mix(mean_weight_ref[...], stack_ref[...])
+        mixed = mix(wide_weight_ref[0:256, :], stack_ref[...])
         slabs = []
+        places = []
         for q in range(4):
-            h = 2 * owner_of(piece, 2 * g + q // 2) + q % 2
+            m = first + q // 2
+            device = place ^ OFFSETS[m] ^ (2 * (g // 2))
+            here = 2 * (device // 2) + q % 2
             even = slice(2 * q * LANES, (2 * q + 1) * LANES)
             odd = slice((2 * q + 1) * LANES, (2 * q + 2) * LANES)
             outer_mean = fold_halves(
                 mixed[0:128, even], mixed[0:128, odd], mixed[128:256, even], mixed[128:256, odd], low_half
             )
-            start = pair_refs[piece][2 * g + q // 2, q % 2].astype(jnp.float32)
-            start = start + embedding_ref[h].astype(jnp.float32)
+            start = pair_ref[m, q % 2].astype(jnp.float32)
+            start = start + embedding_ref[2 * device + q % 2].astype(jnp.float32)
             slab = start + outer_mean * inverse_live
-            pair_now_ref[h] = slab
+            pair_mid_ref[here] = slab
             slabs.append(normalize_channels(slab))
+            places.append(here)
         normed = jnp.concatenate(slabs, axis=1)
-        combined = mix(out_mix_ref[...], normed)
+        combined = mix(turned(turned_ref, "out_mix"), normed)
         left = gate_curve(combined[128:256]) * combined[0:128]
         right = gate_curve(combined[384:512]) * combined[256:384]
-        gating = gate_curve(mix(out_gate_ref[...], normed))
+        gating = gate_curve(mix(turned(turned_ref, "out_gate"), normed))
         for q in range(4):
-            h = 2 * owner_of(piece, 2 * g + q // 2) + q % 2
             lanes = slice(q * LANES, (q + 1) * LANES)
-            left_ref[pl.ds(h * 128, 128), :] = left[:, lanes]
-            right_ref[pl.ds(h * 128, 128), :] = right[:, lanes]
-            gating_ref[h] = gating[:, lanes]
-        return carry
-
-    for piece in range(4):
-        lax.fori_loop(0, 2, functools.partial(first_chunk, piece), 0)
+            rows = pl.ds(pl.multiple_of(places[q] * 128, 128), 128)
+            left_ref[rows, :] = left[:, lanes]
+            right_ref[rows, :] = right[:, lanes].astype(jnp.bfloat16)
+            gating_ref[places[q]] = gating[:, lanes]
+
+
+def triangle_kernel(
+    place_ref,
+    pair_mid_ref,
+    left_ref,
+    gating_ref,
+    right_own_ref,
+    right_other_ref,
+    turned_ref,
+    own_pair_ref,
+    own_part_ref,
+    other_part_ref,
+    right_ref,
+    product_ref,
+    pair_now_ref,
+    chosen_ref,
+    own_left_ref,
+    own_product_ref,
+):
+    place = place_ref[0]
+    core = place % 2
+    half = LANES // 2
+    low_half = lax.broadcasted_iota(jnp.int32, (LANES, LANES), 1) < half
+    low_short = lax.broadcasted_iota(jnp.int32, (32, LANES), 1) < half
+    for chip in range(8):
+        for source, side in ((right_own_ref, core), (right_other_ref, 1 - core)):
+            rows = pl.ds(pl.multiple_of((4 * chip + 2 * side) * 128, 256), 256)
+            right_ref[rows, :] = source[chip * 256 : (chip + 1) * 256, :].astype(jnp.float32)
 
     def outgoing_channels(block, carry):
         for e in range(8):
             c = block * 8 + e
-            left = left_ref[pl.ds(c, 32, stride=128), :].astype(jnp.bfloat16)
+            left = left_ref[pl.ds(c, 16, stride=128), :].astype(jnp.bfloat16)
             right = right_ref[pl.ds(c, 32, stride=128), :]
-            turned = pltpu.roll(right, half, 1)
+            moved = pltpu.roll(right, half, 1)
             spread = jnp.concatenate(
                 [
                     jnp.where(low_short, right, 0.0),
-                    jnp.where(low_short, turned, 0.0),
-                    jnp.where(low_short, 0.0, turned),
+                    jnp.where(low_short, moved, 0.0),
+                    jnp.where(low_short, 0.0, moved),
                     jnp.where(low_short, 0.0, right),
                 ],
                 axis=0,
             ).astype(jnp.bfloat16)
-            product_ref[pl.ds(c, 32, stride=128), :] = lax.dot_general(
-                left, spread, (((1,), (1,)), ((), ())), preferred_element_type=jnp.float32
-            )
+            product_ref[pl.ds(c, 16, stride=128), :] = contract_last(left, spread)
         return carry
 
     lax.fori_loop(0, 16, outgoing_channels, 0)
 
     column = lax.broadcasted_iota(jnp.int32, (1, 256), 1)
-    which = column // 32
-    own = which % 4
-    wanted = half * (which // 4) + 32 * (own % 2) + 2 * place + own // 2
-    slab_of = column % 32
-    source = lax.broadcasted_iota(jnp.int32, (LANES, 256), 0)
-    chosen_ref[...] = jnp.zeros_like(chosen_ref)
-
-    def second_chunk(g, carry):
+    which = column // 16
+    residue = which % 4
+    device = place ^ ((which // 4) % 2)
+    wanted = half * (which // 8) + 32 * (residue % 2) + 2 * device + residue // 2
+    slab_of = column % 16
+    source_lane = lax.broadcasted_iota(jnp.int32, (LANES, 256), 0)
+    for g in range(4):
         products = [
-            normalize_channels(product_ref[pl.ds((4 * g + q) * 128, 128), :]) for q in range(4)
+            normalize_channels(product_ref[(4 * g + q) * 128 : (4 * g + q + 1) * 128, :])
+            for q in range(4)
         ]
-        finished = mix(out_final_ref[...], jnp.concatenate(products, axis=1))
+        finished = mix(turned(turned_ref, "out_final"), jnp.concatenate(products, axis=1))
         slabs = []
         picks = []
         for q in range(4):
             h = 4 * g + q
             lanes = slice(q * LANES, (q + 1) * LANES)
-            slab = pair_now_ref[h] + gating_ref[h] * finished[:, lanes]
+            slab = pair_mid_ref[h] + gating_ref[h] * finished[:, lanes]
             pair_now_ref[h] = slab
             slabs.append(normalize_channels(slab))
             here = jnp.where(slab_of == h, wanted, -1)
-            picks.append((source == here).astype(jnp.float32).astype(jnp.bfloat16))
+            picks.append((source_lane == here).astype(jnp.float32).astype(jnp.bfloat16))
         normed = jnp.concatenate(slabs, axis=1)
-        chosen_ref[...] += mix(normed, jnp.concatenate(picks, axis=0))
-        combined = mix(in_mix_ref[256:512, :], normed)
+        chosen = mix(normed, jnp.concatenate(picks, axis=0))
+        if g:
+            chosen_ref[...] += chosen
+        else:
+            chosen_ref[...] = chosen
+        combined = mix(turned(turned_ref, "in_mix")[256:512, :], normed)
         right = gate_curve(combined[128:256]) * combined[0:128]
         for q in range(4):
-            right_ref[pl.ds((4 * g + q) * 128, 128), :] = right[:, q * LANES : (q + 1) * LANES]
-        return carry
-
-    lax.fori_loop(0, 8, second_chunk, 0)
-
-    combined = mix(in_mix_ref[0:256, :], chosen_ref[...].astype(jnp.bfloat16))
+            right_ref[(4 * g + q) * 128 : (4 * g + q + 1) * 128, :] = right[
+                :, q * LANES : (q + 1) * LANES
+            ]
+    for t in range(2):
+        own_pair_ref[t] = pair_now_ref[2 * (place // 2) + t]
+
+    combined = mix(turned(turned_ref, "in_mix")[0:256, :], chosen_ref[...].astype(jnp.bfloat16))
     own_left = gate_curve(combined[128:256]) * combined[0:128]
-    for m in range(8):
-        part = own_left[:, (m // 4) * LANES : (m // 4 + 1) * LANES]
-        if m % 4:
-            part = pltpu.roll(part, LANES - 32 * (m % 4), 1)
+    for m in range(16):
+        part = own_left[:, (m // 8) * LANES : (m // 8 + 1) * LANES]
+        if m % 8:
+            part = pltpu.roll(part, LANES - 16 * (m % 8), 1)
         own_left_ref[m * 128 : (m + 1) * 128, :] = part
 
     def incoming_channels(block, carry):
         for e in range(8):
             c = block * 8 + e
-            left = own_left_ref[pl.ds(c, 8, stride=128), :][:, 0:32].astype(jnp.bfloat16)
-            right = right_ref[pl.ds(c, 32, stride=128), :].astype(jnp.bfloat16)
-            own_product_ref[pl.ds(c, 8, stride=128), :] = mix(left, right)
+            left = own_left_ref[pl.ds(c, 16, stride=128), :][:, 0:16].astype(jnp.bfloat16)
+            right = right_ref[pl.ds(c, 16, stride=128), :].astype(jnp.bfloat16)
+            own_product_ref[pl.ds(c, 16, stride=128), :] = mix(left, right)
         return carry
 
     lax.fori_loop(0, 16, incoming_channels, 0)
 
-    def own_block(m):
+    def block_of(b, e, residue):
+        m = 8 * b + 4 * e + residue
         return own_product_ref[m * 128 : (m + 1) * 128, :]
 
-    products = [
-        normalize_channels(
-            fold_halves(
-                own_block(2 * t), own_block(2 * t + 1), own_block(4 + 2 * t), own_block(5 + 2 * t), low_half
+    for e, target in ((0, own_part_ref), (1, other_part_ref)):
+        for t in range(2):
+            target[t] = fold_halves(
+                block_of(0, e, 2 * t),
+                block_of(0, e, 2 * t + 1),
+                block_of(1, e, 2 * t),
+                block_of(1, e, 2 * t + 1),
+                low_half,
             )
-        )
-        for t in range(2)
-    ]
-    finished = mix(in_final_ref[...], jnp.concatenate(products, axis=1))
-    own_pair = jnp.concatenate([pair_now_ref[2 * place + t] for t in range(2)], axis=1)
-    gating = gate_curve(mix(in_gate_ref[...], normalize_channels(own_pair)))
+
+
+def finish_kernel(own_pair_ref, own_part_ref, other_part_ref, turned_ref, wide_weight_ref, result_ref):
+    products = [normalize_channels(own_part_ref[t] + other_part_ref[t]) for t in range(2)]
+    finished = mix(turned(turned_ref, "in_final"), jnp.concatenate(products, axis=1))
+    own_pair = jnp.concatenate([own_pair_ref[t] for t in range(2)], axis=1)
+    gating = gate_curve(mix(turned(turned_ref, "in_gate"), normalize_channels(own_pair)))
     own_pair = own_pair + gating * finished
-    hidden = jnp.maximum(mix(up_ref[...], normalize_channels(own_pair)), 0.0).astype(jnp.bfloat16)
-    own_pair = (own_pair + mix(down_ref[...], hidden)).astype(jnp.bfloat16)
+    hidden = jnp.maximum(mix(turned(turned_ref, "up"), normalize_channels(own_pair)), 0.0)
+    own_pair = own_pair + mix(wide_weight_ref[256:384, :], hidden.astype(jnp.bfloat16))
+    own_pair = own_pair.astype(jnp.bfloat16)
     order = lane_order_matrix()
     for t in range(2):
-        result_ref[t * 128 : (t + 1) * 128, :] = lax.dot_general(
-            order,
-            own_pair[:, t * LANES : (t + 1) * LANES],
-            (((1,), (1,)), ((), ())),
-            preferred_element_type=jnp.float32,
+        result_ref[t * 128 : (t + 1) * 128, :] = contract_last(
+            order, own_pair[:, t * LANES : (t + 1) * LANES]
         ).astype(jnp.bfloat16)
 
 
@@ -311,20 +339,18 @@
     )
 
 
-def rows_kernel(place_ref, rows_ref, pair_ref, own_pair_ref, *rest):
-    block_refs, wide_ref = rest[:-1], rest[-1]
+def rows_kernel(rows_ref, pair_ref, blocks_ref, own_pair_ref, wide_ref):
     residues = rows_ref.shape[1]
     count = 8 * residues
     rows = rows_ref[...].astype(jnp.float32).reshape(count, 2 * LANES)
     for e in range(2):
         wide_ref[e * count : (e + 1) * count, :] = rows[:, e * LANES : (e + 1) * LANES]
-    for m in range(16):
-        first = 4 * (place_ref[0] ^ m)
+    for p in range(16):
         for e in range(2):
             block = [
-                wide_ref[pl.ds(e * count + first + i, 8, stride=residues), :] for i in range(4)
+                wide_ref[pl.ds(e * count + 4 * p + i, 8, stride=residues), :] for i in range(4)
             ]
-            block_refs[m][:, e * LANES : (e + 1) * LANES] = jnp.concatenate(block, axis=0).astype(
+            blocks_ref[p, :, e * LANES : (e + 1) * LANES] = jnp.concatenate(block, axis=0).astype(
                 jnp.bfloat16
             )
     order = lane_order_matrix()
@@ -334,31 +360,29 @@
         ).astype(jnp.bfloat16)
 
 
+TURNED = {
+    "out_mix": (0, 512),
+    "out_gate": (512, 640),
+    "out_final": (640, 768),
+    "in_mix": (768, 1280),
+    "in_gate": (1280, 1408),
+    "in_final": (1408, 1536),
+    "up": (1536, 2048),
+}
+
+
 def weights_kernel(
     bins_ref,
     table_ref,
-    mean_weight_ref,
-    out_mix_ref,
-    out_gate_ref,
-    out_final_ref,
-    in_mix_ref,
-    in_gate_ref,
-    in_final_ref,
-    up_ref,
-    down_ref,
-    embedding_out,
-    mean_weight_out,
-    out_mix_out,
-    out_gate_out,
-    out_final_out,
-    in_mix_out,
-    in_gate_out,
-    in_final_out,
-    up_out,
-    down_out,
-    table_wide_ref,
-    mean_wide_ref,
+    *rest,
 ):
+    sources, (embedding_out, turned_out, wide_out) = rest[:9], rest[9:12]
+    landed, (table_wide_ref, mean_wide_ref, arrived) = rest[12:21], rest[21:]
+    copies = [
+        pltpu.make_async_copy(sources[k], landed[k], arrived.at[k]) for k in range(len(sources))
+    ]
+    for copy in copies:
+        copy.start()
     table_wide_ref[...] = jnp.zeros_like(table_wide_ref)
     table_wide_ref[0:NBINS, :] = table_ref[...].astype(jnp.float32)
     table = table_wide_ref[...].T.astype(jnp.bfloat16)
@@ -372,32 +396,26 @@
         return carry
 
     lax.fori_loop(0, 8, embed, 0)
-    mean_wide_ref[...] = mean_weight_ref[...].astype(jnp.float32)
+    for copy in copies:
+        copy.wait()
+    mean_wide_ref[...] = landed[0][...].astype(jnp.float32)
     for e in range(2):
         for block in range(4):
             rows = [
                 mean_wide_ref[pl.ds(2 * (4 * block + k) + e, CO, stride=CO), :] for k in range(4)
             ]
-            mean_weight_out[e * LANES : (e + 1) * LANES, block * LANES : (block + 1) * LANES] = (
+            wide_out[e * LANES : (e + 1) * LANES, block * LANES : (block + 1) * LANES] = (
                 jnp.concatenate(rows, axis=0).T.astype(jnp.bfloat16)
             )
-    for source, target in (
-        (out_mix_ref, out_mix_out),
-        (out_gate_ref, out_gate_out),
-        (out_final_ref, out_final_out),
-        (in_mix_ref, in_mix_out),
-        (in_gate_ref, in_gate_out),
-        (in_final_ref, in_final_out),
-        (up_ref, up_out),
-        (down_ref, down_out),
-    ):
-        rows, columns = source.shape
-        for a in range(rows // LANES):
-            for b in range(columns // LANES):
-                part = source[a * LANES : (a + 1) * LANES, b * LANES : (b + 1) * LANES]
-                target[b * LANES : (b + 1) * LANES, a * LANES : (a + 1) * LANES] = (
-                    part.astype(jnp.float32).T.astype(jnp.bfloat16)
-                )
+    first = 0
+    for source in landed[1:8]:
+        for b in range(source.shape[1] // LANES):
+            part = source[:, b * LANES : (b + 1) * LANES].astype(jnp.float32)
+            turned_out[first : first + LANES, :] = part.T.astype(jnp.bfloat16)
+            first += LANES
+    for a in range(4):
+        part = landed[8][a * LANES : (a + 1) * LANES, :].astype(jnp.float32)
+        wide_out[256:384, a * LANES : (a + 1) * LANES] = part.T.astype(jnp.bfloat16)
 
 
 def normalize_rows(values):
@@ -413,15 +431,9 @@
     )
 
 
-def msa_kernel(place_ref, live_ref, *rest):
-    block_refs = rest[:16]
-    msa_body(place_ref, live_ref, block_refs, *rest[16:])
-
-
-def msa_body(
-    place_ref,
+def msa_kernel(
     live_ref,
-    block_refs,
+    blocks_ref,
     query_ref,
     key_ref,
     value_gate_ref,
@@ -434,11 +446,10 @@
     wide_ref,
     final_ref,
 ):
-    for m in range(16):
-        block = block_refs[m][...].astype(jnp.float32)
-        first = (place_ref[0] ^ m) * 8
+    for p in range(16):
+        block = blocks_ref[p].astype(jnp.float32)
         for i in range(4):
-            wide_ref[pl.ds(pl.multiple_of(i * 128 + first, 8), 8), :] = block[i * 8 : i * 8 + 8, :]
+            wide_ref[i * 128 + p * 8 : i * 128 + p * 8 + 8, :] = block[i * 8 : i * 8 + 8, :]
     live = live_ref[...]
     alive = live > 0.0
     width = HM * HEAD_SIZE
@@ -492,7 +503,6 @@
     alignment_transition_up,
     alignment_transition_down,
     outer_input_weight,
-    outer_output_weight,
     *pair_weights,
 ):
     channels = alignment_input.shape[2]
@@ -500,56 +510,60 @@
     place = lax.axis_index("dap").astype(jnp.int32).reshape(1)
     vmem = pl.BlockSpec(memory_space=pltpu.VMEM)
     smem = pl.BlockSpec(memory_space=pltpu.SMEM)
-
-    def array(*shape):
-        return jax.ShapeDtypeStruct(shape, jnp.bfloat16)
+    hbm = pl.BlockSpec(memory_space=pltpu.HBM)
+
+    def array(*shape, dtype=jnp.bfloat16):
+        return jax.ShapeDtypeStruct(shape, dtype)
+
+    def wide(*shape):
+        return jax.ShapeDtypeStruct(shape, jnp.float32)
 
     def limit(mebibytes):
         return pltpu.CompilerParams(vmem_limit_bytes=mebibytes * 1024 * 1024)
 
-    own_pair, *blocks = pl.pallas_call(
+    blocks, own_pair = pl.pallas_call(
         rows_kernel,
-        out_shape=[array(2, width, LANES)] + [array(32, channels)] * 16,
-        in_specs=[smem, vmem, vmem],
-        out_specs=[vmem] * 17,
+        out_shape=[array(16, 32, channels), array(2, width, LANES)],
+        in_specs=[vmem, vmem],
+        out_specs=[vmem, vmem],
         scratch_shapes=[pltpu.VMEM((1024, LANES), jnp.float32)],
         compiler_params=limit(16),
         name="rows_by_device",
-    )(place, alignment_input, pair_state_input)
-    blocks = [blocks[0]] + [exchange(blocks[m], m) for m in range(1, 16)]
+    )(alignment_input, pair_state_input)
+    blocks = lax.all_to_all(blocks, "dap", split_axis=0, concat_axis=0, tiled=True)
 
     pair_far = exchange(own_pair, 8)
-    pair_near = [exchange(own_pair, 4), exchange(pair_far, 4)]
-    pair_line = jnp.stack([own_pair, pair_far] + pair_near)
-
-    embedding, *turned = pl.pallas_call(
+    pair_near = exchange(jnp.stack([own_pair, pair_far]), 4)
+    pair_line = jnp.concatenate([jnp.stack([own_pair, pair_far]), pair_near])
+
+    embedding, turned_weights, wide_weights = pl.pallas_call(
         weights_kernel,
-        out_shape=[array(32, width, LANES), array(2 * width, 16 * CO)]
-        + [array(*w.shape[::-1]) for w in pair_weights],
-        in_specs=[vmem] * 11,
-        out_specs=[vmem] * 10,
-        scratch_shapes=[
+        out_shape=[array(32, width, LANES), array(2048, LANES), array(384, 512)],
+        in_specs=[vmem] * 2 + [hbm] * 9,
+        out_specs=[vmem] * 3,
+        scratch_shapes=[pltpu.VMEM(w.shape, jnp.bfloat16) for w in pair_weights]
+        + [
             pltpu.VMEM((LANES, LANES), jnp.float32),
             pltpu.VMEM((1024, LANES), jnp.float32),
+            pltpu.SemaphoreType.DMA((9,)),
         ],
         compiler_params=limit(24),
         cost_estimate=pl.CostEstimate(
-            flops=200_000_000, bytes_accessed=4_000_000, transcendentals=0
+            flops=200_000_000, bytes_accessed=8_000_000, transcendentals=0
         ),
         name="turn_weights",
     )(
         lanes_order(bin_all).reshape(32, LANES),
         relative_position_table,
-        outer_output_weight,
         *pair_weights,
     )
-    blocks, pair_line, turned = lax.optimization_barrier((blocks, pair_line, turned))
-    pair_pieces = [pair_line, exchange(pair_line, 2), exchange(pair_line, 1)]
+    blocks, pair_line = lax.optimization_barrier((blocks, pair_line))
+    pair_across = exchange(pair_line, 2)
 
     result, parts = pl.pallas_call(
         msa_kernel,
         out_shape=(array(512, channels), array(256, LANES)),
-        in_specs=[smem] + [vmem] * 24,
+        in_specs=[vmem] * 9,
         out_specs=(vmem, vmem),
         scratch_shapes=[
             pltpu.VMEM((512, channels), jnp.float32),
@@ -561,9 +575,8 @@
         ),
         name="msa_whole",
     )(
-        place,
         live_row_float.reshape(1, LANES),
-        *blocks,
+        blocks,
         column_query_weight,
         column_key_weight,
         column_value_gate_weight,
@@ -572,36 +585,66 @@
         alignment_transition_down,
         outer_input_weight.T,
     )
-    parts, pair_pieces = lax.optimization_barrier((parts, pair_pieces))
+    parts, pair_across = lax.optimization_barrier((parts, pair_across))
     far = exchange(parts, 8)
     near = [exchange(parts, 4), exchange(far, 4)]
-    pair_pieces.append(exchange(pair_pieces[1], 1))
     line = jnp.stack([parts, far] + near)
     across = exchange(line, 2)
-    pieces = [line, across, exchange(line, 1), exchange(across, 1)]
-
-    tall = (32 * 128, LANES)
-    pair_output = pl.pallas_call(
-        pair_kernel,
-        out_shape=array(256, LANES),
-        in_specs=[smem, smem] + [vmem] * 18,
-        out_specs=vmem,
+    core_line = exchange(jnp.stack([part[128:256] for part in (parts, far, *near)]), 1)
+    core_across = exchange(across[:, 128:256, :], 1)
+
+    slabs = (16, 128, LANES)
+    tall = (16 * 128, LANES)
+    pair_mid, left, gating, right = pl.pallas_call(
+        start_kernel,
+        out_shape=[wide(*slabs), wide(*tall), wide(*slabs), array(*tall)],
+        in_specs=[smem, smem] + [vmem] * 9,
+        out_specs=[vmem] * 4,
         scratch_shapes=[
             pltpu.VMEM((2048, LANES), jnp.float32),
             pltpu.VMEM((128, 2048), jnp.bfloat16),
             pltpu.VMEM((512, 1024), jnp.bfloat16),
-            pltpu.VMEM((32, 128, LANES), jnp.float32),
+            pltpu.VMEM((512, 1024), jnp.bfloat16),
+        ],
+        compiler_params=limit(32),
+        name="pair_start",
+    )(
+        place,
+        jnp.sum(live_row_float).reshape(1),
+        line,
+        across,
+        core_line,
+        core_across,
+        pair_line,
+        pair_across,
+        embedding,
+        turned_weights,
+        wide_weights,
+    )
+    own_pair, own_part, other_part = pl.pallas_call(
+        triangle_kernel,
+        out_shape=[wide(2, 128, LANES)] * 3,
+        in_specs=[smem] + [vmem] * 6,
+        out_specs=[vmem] * 3,
+        scratch_shapes=[
+            pltpu.VMEM((32 * 128, LANES), jnp.float32),
+            pltpu.VMEM(tall, jnp.float32),
+            pltpu.VMEM(slabs, jnp.float32),
+            pltpu.VMEM((128, 256), jnp.float32),
             pltpu.VMEM(tall, jnp.float32),
             pltpu.VMEM(tall, jnp.float32),
-            pltpu.VMEM(tall, jnp.float32),
-            pltpu.VMEM((32, 128, LANES), jnp.float32),
-            pltpu.VMEM((128, 256), jnp.float32),
-            pltpu.VMEM((1024, LANES), jnp.float32),
-            pltpu.VMEM((1024, LANES), jnp.float32),
         ],
-        compiler_params=limit(40),
-        name="pair_whole",
-    )(place, jnp.sum(live_row_float).reshape(1), *pieces, *pair_pieces, embedding, *turned)
+        compiler_params=limit(32),
+        name="pair_triangles",
+    )(place, pair_mid, left, gating, right, exchange(right, 1), turned_weights)
+    pair_output = pl.pallas_call(
+        finish_kernel,
+        out_shape=array(256, LANES),
+        in_specs=[vmem] * 5,
+        out_specs=vmem,
+        compiler_params=limit(16),
+        name="pair_finish",
+    )(own_pair, own_part, exchange(other_part, 1), turned_weights, wide_weights)
     return result.reshape(128, 4, channels), pair_output.reshape(pair_state_input.shape)
 
 

time: 104 us -> 73.9 us (0.71)
  starting transfers between devices: 32.2 us -> 16.2 us
  local copies, waits for them, and re-layouts: 16.4 us -> 3.72 us
  Pallas kernels: 36.4 us -> 29.4 us
  waiting for transfers between devices: 16.6 us -> 22.3 us
    ppermute x27 -> x11, starting transfers between devices: 32.2 us -> 12.2 us  [exchange(): return lax.ppermute(values, 'dap', [(q, q ^ offset) for q in range(pieces)])]
    unnamed x74 -> x44, local copies, waits for them, and re-layouts: 14.2 us -> 2.47 us
    pallas_call x2 -> x4, Pallas kernels: 27.1 us -> 19.2 us  [the longest x1 10.9 us: whole_block(): pl.pallas_call(triangle_kernel, out_shape=[wide(2, 128, LANES)] * 3, in_s...]
    ppermute x27 -> x11, waiting for transfers between devices: 16.6 us -> 21.9 us  [exchange(): return lax.ppermute(values, 'dap', [(q, q ^ offset) for q in range(pieces)])]
    all_to_all x0 -> x1, starting transfers between devices: none -> 4.04 us  [whole_block(): lax.all_to_all(blocks, 'dap', split_axis=0, concat_axis=0, tiled=True)]
  transfers between devices with their start and end apart: 27 -> 12, of which waited for: 7 -> 8; matrix products, arithmetic and copies ran while one was open for 3% -> 3% of each run, Pallas kernels for 9% -> 14%
where the time goes in v5:
time: 73.9 us; the launch traced here: 73.5 us
  Pallas kernels  29.4 us (40%)
  waiting for transfers between devices  22.3 us (30%)
  starting transfers between devices  16.2 us (22%)
  local copies, waits for them, and re-layouts  3.72 us (5%)
  between operations  0.97 us (1%)
  other arithmetic  0.91 us (1%)
    ppermute x11, waiting for transfers between devices, exchange(): return lax.ppermute(values, 'dap', [(q, q ^ offset) for q in range(pieces)])  21.9 us
    ppermute x11, starting transfers between devices, exchange(): return lax.ppermute(values, 'dap', [(q, q ^ offset) for q in range(pieces)])  12.2 us
    pallas_call x1, Pallas kernels, whole_block(): pl.pallas_call(triangle_kernel, out_shape=[wide(2, 128, LANES)] * 3, in_s...  10.9 us
    pallas_call x1, Pallas kernels, whole_block(): pl.pallas_call(msa_kernel, out_shape=(array(512, channels), array(256, LA...  7.22 us
    pallas_call x1, Pallas kernels, whole_block(): pl.pallas_call(start_kernel, out_shape=[wide(*slabs), wide(*tall), wide(*...  5.61 us
    all_to_all x1, starting transfers between devices, whole_block(): lax.all_to_all(blocks, 'dap', split_axis=0, concat_axis=0, tiled=True)  4.04 us
    pallas_call x1, Pallas kernels, whole_block(): pl.pallas_call(weights_kernel, out_shape=[array(32, width, LANES), array(...  3.03 us
    unnamed x44, local copies, waits for them, and re-layouts  2.47 us
  transfers between devices with their start and end apart: 12, of which 8 were waited for; matrix products, arithmetic and copies ran while one was open for 3% of the time, Pallas kernels for 14%

profile of v5, /device:TPU:0, one launch (start us, length us, event | category | flops | bytes accessed | tf_op | source)
XLA Modules:
  0.0 73.5 jit_solution(12794225601932123548)
XLA Ops:
  0.6 0.9 %copy-done = bf16[8,64,256]{2,1,0:T(8,128)(2,1)S(1)} copy-done((bf16[8,64,256]{2,1,0:T(8,128)(2,1)S(1)}, bf16[8,64,256]{2,1,0:T(8,128)(2,1)}, u32[]{:S(2)}) %copy-start) | copy-done | bytes 262168
  1.6 0.8 %copy-done.6 = bf16[4,64,128]{2,1,0:T(8,128)(2,1)S(1)} copy-done((bf16[4,64,128]{2,1,0:T(8,128)(2,1)S(1)}, bf16[4,64,128]{2,1,0:T(8,128)(2,1)}, u32[]{:S(2)}) %copy-start.6) | copy-done | bytes 65560
  2.4 1.1 %rows_by_device.1 = (bf16[16,32,256]{2,1,0:T(8,128)(2,1)}, bf16[2,128,128]{2,1,0:T(8,128)(2,1)S(1)}) custom-call(bf16[8,64,256]{2,1,0:T(8,128)(2,1)S(1)} %copy-done, bf16[4,64,128]{2,1,0:T(8,128)(2,1)S(1)} %copy-done.6), custom_call_target="tpu_custom_call" | custom-call | tf_op jit(solution)/shard_map/rows_by_device/pallas_call | solution.py:524
  3.6 4.0 %collective-permute-start = (bf16[2,128,128]{2,1,0:T(8,128)(2,1)S(1)}, bf16[2,128,128]{2,1,0:T(8,128)(2,1)S(1)}, u32[]{:S(2)}, u32[]{:S(2)}) collective-permute-start(bf16[2,128,128]{2,1,0:T(8,128)(2,1)S(1)} %get-tuple-element.21), channel_id=1, source_target_pairs={{0,8},{1,9},{2,10},{3,11},{4,12},{5,13},{6,14},{7,15},{8,0},{9,1},... | collective-permute-start | bytes 196616 | tf_op jit(solution)/shard_map/ppermute | solution.py:490
  7.6 4.0 %all-to-all-start = ((bf16[16,32,256]{2,1,0:T(8,128)(2,1)}), bf16[16,32,256]{2,1,0:T(8,128)(2,1)S(1)}, u32[]{:S(2)}, u32[]{:S(2)}) async-start(bf16[16,32,256]{2,1,0:T(8,128)(2,1)} %get-tuple-element.20), calls=%async_computation | async-start | bytes 524288 | tf_op jit(solution)/shard_map/all_to_all | solution.py:533
  11.9 0.1 eq.22
  12.1 2.0 %collective-permute-start.1 = (bf16[2,2,128,128]{3,2,1,0:T(8,128)(2,1)S(1)}, bf16[2,2,128,128]{3,2,1,0:T(8,128)(2,1)S(1)}, u32[]{:S(2)}, u32[]{:S(2)}) collective-permute-start(bf16[2,2,128,128]{3,2,1,0:T(8,128)(2,1)S(1)} %pad_maximum_fusion.2), channel_id=1, source_target_pairs={{0,4},{1,5},{2,6},{3,7},{4,0},{5,1},{6,2},{7,3},{8,12},{9,13},{10,... | collective-permute-start | bytes 393224 | tf_op jit(solution)/shard_map/ppermute | solution.py:490
  14.1 0.2 compare_select_fusion
  14.3 7.5 %collective-permute-done.1 = bf16[2,2,128,128]{3,2,1,0:T(8,128)(2,1)S(1)} collective-permute-done((bf16[2,2,128,128]{3,2,1,0:T(8,128)(2,1)S(1)}, bf16[2,2,128,128]{3,2,1,0:T(8,128)(2,1)S(1)}, u32[]{:S(2)}, u32[]{:S(2)}) %collective-permute-start.1) | collective-permute-done | bytes 131104 | tf_op jit(solution)/shard_map/ppermute | solution.py:490
  21.8 0.3 all-to-all-done.blocks_ref
  22.2 1.2 %collective-permute-start.2 = (bf16[4,2,128,128]{3,2,1,0:T(8,128)(2,1)S(1)}, bf16[4,2,128,128]{3,2,1,0:T(8,128)(2,1)S(1)}, u32[]{:S(2)}, u32[]{:S(2)}) collective-permute-start(bf16[4,2,128,128]{3,2,1,0:T(8,128)(2,1)S(1)} %pad_maximum_fusion.pair_line_ref), channel_id=1, source_target_pairs={{0,2},{1,3},{2,0},{3,1},{4,6},{5,7},{6,4},{7,5},{8,10},{9,11},{10,... | collective-permute-start | bytes 786440 | tf_op jit(solution)/shard_map/ppermute | solution.py:490
  23.4 0.1 select_n.11.bins_ref
  23.5 0.6 copy-done.18
  24.1 7.2 %msa_whole.1 = (bf16[512,256]{1,0:T(8,128)(2,1)S(1)}, bf16[256,128]{1,0:T(8,128)(2,1)S(1)}) custom-call(f32[1,128]{1,0:T(1,128)S(1)} %fusion.1.live_ref, bf16[16,32,256]{2,1,0:T(8,128)(2,1)S(1)} %all-to-all-done.blocks_ref, bf16[256,256]{1,0:T(8,128)(2,1)S(1)} %copy-done.15, bf16[256,256]{1,0:T(8,128)(2,1)S(1)} %copy-done.16, ...), custom_call_target="tpu_custom_call" | custom-call | flops 2000000000 | bytes 10000000 | tf_op jit(solution)/shard_map/msa_whole/pallas_call | solution.py:563
  31.4 2.4 %collective-permute-start.3 = (bf16[256,128]{1,0:T(8,128)(2,1)S(1)}, bf16[256,128]{1,0:T(8,128)(2,1)S(1)}, u32[]{:S(2)}, u32[]{:S(2)}) collective-permute-start(bf16[256,128]{1,0:T(8,128)(2,1)S(1)} %get-tuple-element.26), channel_id=1, source_target_pairs={{0,8},{1,9},{2,10},{3,11},{4,12},{5,13},{6,14},{7,15},{8,0},{9,1},... | collective-permute-start | bytes 196616 | tf_op jit(solution)/shard_map/ppermute | solution.py:490
  33.8 0.6 collective-permute-start.4
  34.4 2.9 %collective-permute-done.3 = bf16[256,128]{1,0:T(8,128)(2,1)S(1)} collective-permute-done((bf16[256,128]{1,0:T(8,128)(2,1)S(1)}, bf16[256,128]{1,0:T(8,128)(2,1)S(1)}, u32[]{:S(2)}, u32[]{:S(2)}) %collective-permute-start.3) | collective-permute-done | bytes 65568 | tf_op jit(solution)/shard_map/ppermute | solution.py:490
  37.3 0.1 collective-permute-start.5
  37.5 0.6 collective-permute-done.4
  38.1 3.5 %collective-permute-done.5 = bf16[256,128]{1,0:T(8,128)(2,1)S(1)} collective-permute-done((bf16[256,128]{1,0:T(8,128)(2,1)S(1)}, bf16[256,128]{1,0:T(8,128)(2,1)S(1)}, u32[]{:S(2)}, u32[]{:S(2)}) %collective-permute-start.5) | collective-permute-done | bytes 65568 | tf_op jit(solution)/shard_map/ppermute | solution.py:490
  41.6 0.7 collective-permute-start.6
  42.5 5.6 %collective-permute-done.6.across_ref = bf16[4,256,128]{2,1,0:T(8,128)(2,1)S(1)} collective-permute-done((bf16[4,256,128]{2,1,0:T(8,128)(2,1)S(1)}, bf16[4,256,128]{2,1,0:T(8,128)(2,1)S(1)}, u32[]{:S(2)}, u32[]{:S(2)}) %collective-permute-start.6) | collective-permute-done | bytes 262176 | tf_op jit(solution)/shard_map/ppermute | solution.py:490
  48.3 3.0 %turn_weights.1 = (bf16[32,128,128]{2,1,0:T(8,128)(2,1)S(1)}, bf16[2048,128]{1,0:T(8,128)(2,1)S(1)}, bf16[384,512]{1,0:T(8,128)(2,1)S(1)}) custom-call(s32[32,128]{1,0:T(8,128)S(1)} %select_n.11.bins_ref, bf16[66,128]{1,0:T(8,128)(2,1)S(1)} %copy-done.11, bf16[1024,128]{1,0:T(8,128)(2,1)S(1)} %copy-done.1, bf16[128,512]{1,0:T(8,128)(2,1)S(1)} %copy-done.2, ...), custom_call_target="tpu_custom_call" | custom-call | flops 200000000 | bytes 8000000 | tf_op jit(solution)/shard_map/turn_weights/pallas_call | solution.py:539
  51.3 0.6 fusion
  51.9 5.6 %pair_start.1 = (f32[16,128,128]{2,1,0:T(8,128)S(1)}, f32[2048,128]{1,0:T(8,128)S(1)}, f32[16,128,128]{2,1,0:T(8,128)S(1)}, bf16[2048,128]{1,0:T(8,128)(2,1)S(1)}) custom-call(s32[1]{0:T(128)} %bitcast.4.place_ref, f32[1]{0:T(128)} %bitcast.5.live_ref, bf16[4,256,128]{2,1,0:T(8,128)(2,1)S(1)} %pad_maximum_fusion.1.line_ref, ...), custom_call_target="tpu_custom_call" | custom-call | tf_op jit(solution)/shard_map/pair_start/pallas_call | solution.py:598
  57.5 0.5 collective-permute-start.9
  58.1 1.5 %collective-permute-done.9.right_other_ref = bf16[2048,128]{1,0:T(8,128)(2,1)S(1)} collective-permute-done((bf16[2048,128]{1,0:T(8,128)(2,1)S(1)}, bf16[2048,128]{1,0:T(8,128)(2,1)S(1)}, u32[]{:S(2)}, u32[]{:S(2)}) %collective-permute-start.9) | collective-permute-done | bytes 524320 | tf_op jit(solution)/shard_map/ppermute | solution.py:490
  59.6 10.9 %pair_triangles.1 = (f32[2,128,128]{2,1,0:T(8,128)S(1)}, f32[2,128,128]{2,1,0:T(8,128)S(1)}, f32[2,128,128]{2,1,0:T(8,128)S(1)}) custom-call(s32[1]{0:T(128)} %bitcast.4.place_ref, f32[16,128,128]{2,1,0:T(8,128)S(1)} %get-tuple-element.31.pair_mid_ref, f32[2048,128]{1,0:T(8,128)S(1)} %get-tuple-element.32.left_ref, ...), custom_call_target="tpu_custom_call" | custom-call | tf_op jit(solution)/shard_map/pair_triangles/pallas_call | solution.py:624
  70.6 0.4 collective-permute-start.10
  71.0 0.8 %reshape.58 = bf16[128,4,256]{2,1,0:T(4,128)(2,1)} reshape(bf16[512,256]{1,0:T(8,128)(2,1)S(1)} %get-tuple-element.23) | data formatting | bytes 524288 | tf_op jit(solution)/shard_map/reshape | solution.py:648
  71.8 0.2 collective-permute-done.10.other_part_ref
  72.0 1.5 %pair_finish.1 = bf16[256,128]{1,0:T(8,128)(2,1)} custom-call(f32[2,128,128]{2,1,0:T(8,128)S(1)} %get-tuple-element.35.own_pair_ref, f32[2,128,128]{2,1,0:T(8,128)S(1)} %get-tuple-element.36.own_part_ref, f32[2,128,128]{2,1,0:T(8,128)S(1)} %collective-permute-done.10.other_part_ref, bf16[2048,128]{1,0:T(8,128)(2,1)S(1)} %get-tuple-element.29.turned_ref, ...), custom_call_target="tpu_custom_call" | custom-call | tf_op jit(solution)/shard_map/pair_finish/pallas_call | solution.py:640
  (60 shorter events, 0.6 us)
Async XLA Ops:
  0.6 1.0 %copy-start = (bf16[8,64,256]{2,1,0:T(8,128)(2,1)S(1)}, bf16[8,64,256]{2,1,0:T(8,128)(2,1)}, u32[]{:S(2)}) copy-start(bf16[8,64,256]{2,1,0:T(8,128)(2,1)} %rows_ref.1) | copy-start | bytes 786436
  2.4 9.2 %copy-start.19 = (s32[64]{0:T(128)S(1)}, s32[64]{0:T(128)}, u32[]{:S(2)}) copy-start(s32[64]{0:T(128)} %param.24) | copy-start | bytes 772
  2.4 21.1 %copy-start.16 = (bf16[256,256]{1,0:T(8,128)(2,1)S(1)}, bf16[256,256]{1,0:T(8,128)(2,1)}, u32[]{:S(2)}) copy-start(bf16[256,256]{1,0:T(8,128)(2,1)} %key_ref.1) | copy-start | bytes 393220
  2.4 21.1 %copy-start.17 = (bf16[256,256]{1,0:T(8,128)(2,1)S(1)}, bf16[256,256]{1,0:T(8,128)(2,1)}, u32[]{:S(2)}) copy-start(bf16[256,256]{1,0:T(8,128)(2,1)} %output_ref.1) | copy-start | bytes 393220
  3.6 8.5 %collective-permute-start = (bf16[2,128,128]{2,1,0:T(8,128)(2,1)S(1)}, bf16[2,128,128]{2,1,0:T(8,128)(2,1)S(1)}, u32[]{:S(2)}, u32[]{:S(2)}) collective-permute-start(bf16[2,128,128]{2,1,0:T(8,128)(2,1)S(1)} %get-tuple-element.21), channel_id=1, source_target_pairs={{0,8},{1,9},{2,10},{3,11},{4,12},{5,13},{6,14},{7,15},{8,0},{9,1},... | collective-permute-start | bytes 196616 | tf_op jit(solution)/shard_map/ppermute | solution.py:490
  7.6 4.3 %copy-start.20 = (s32[64]{0:T(128)S(1)}, s32[64]{0:T(128)}, u32[]{:S(2)}) copy-start(s32[64]{0:T(128)} %param.25) | copy-start | bytes 772
  7.6 15.9 %copy-start.13 = (bf16[1024,256]{1,0:T(8,128)(2,1)S(1)}, bf16[1024,256]{1,0:T(8,128)(2,1)}, u32[]{:S(2)}) copy-start(bf16[1024,256]{1,0:T(8,128)(2,1)} %down_ref.1) | copy-start | bytes 1572868
  7.6 14.6 %all-to-all-start = ((bf16[16,32,256]{2,1,0:T(8,128)(2,1)}), bf16[16,32,256]{2,1,0:T(8,128)(2,1)S(1)}, u32[]{:S(2)}, u32[]{:S(2)}) async-start(bf16[16,32,256]{2,1,0:T(8,128)(2,1)} %get-tuple-element.20), calls=%async_computation | async-start | bytes 524288 | tf_op jit(solution)/shard_map/all_to_all | solution.py:533
  11.7 11.9 %copy-start.12 = (bf16[256,1024]{1,0:T(8,128)(2,1)S(1)}, bf16[256,1024]{1,0:T(8,128)(2,1)}, u32[]{:S(2)}) copy-start(bf16[256,1024]{1,0:T(8,128)(2,1)} %up_ref.1) | copy-start | bytes 1572868
  12.1 9.7 %collective-permute-start.1 = (bf16[2,2,128,128]{3,2,1,0:T(8,128)(2,1)S(1)}, bf16[2,2,128,128]{3,2,1,0:T(8,128)(2,1)S(1)}, u32[]{:S(2)}, u32[]{:S(2)}) collective-permute-start(bf16[2,2,128,128]{3,2,1,0:T(8,128)(2,1)S(1)} %pad_maximum_fusion.2), channel_id=1, source_target_pairs={{0,4},{1,5},{2,6},{3,7},{4,0},{5,1},{6,2},{7,3},{8,12},{9,13},{10,... | collective-permute-start | bytes 393224 | tf_op jit(solution)/shard_map/ppermute | solution.py:490
  14.3 9.1 %copy-start.21 = (s32[128]{0:T(128)S(1)}, s32[128]{0:T(128)}, u32[]{:S(2)}) copy-start(s32[128]{0:T(128)} %param.26) | copy-start | bytes 1540
  14.3 9.2 %copy-start.14 = (bf16[256,512]{1,0:T(8,128)(2,1)S(1)}, bf16[256,512]{1,0:T(8,128)(2,1)}, u32[]{:S(2)}) copy-start(bf16[256,512]{1,0:T(8,128)(2,1)} %value_gate_ref.1) | copy-start | bytes 786436
  14.3 9.2 %copy-start.15 = (bf16[256,256]{1,0:T(8,128)(2,1)S(1)}, bf16[256,256]{1,0:T(8,128)(2,1)}, u32[]{:S(2)}) copy-start(bf16[256,256]{1,0:T(8,128)(2,1)} %query_ref.1) | copy-start | bytes 393220
  22.2 9.2 %collective-permute-start.2 = (bf16[4,2,128,128]{3,2,1,0:T(8,128)(2,1)S(1)}, bf16[4,2,128,128]{3,2,1,0:T(8,128)(2,1)S(1)}, u32[]{:S(2)}, u32[]{:S(2)}) collective-permute-start(bf16[4,2,128,128]{3,2,1,0:T(8,128)(2,1)S(1)} %pad_maximum_fusion.pair_line_ref), channel_id=1, source_target_pairs={{0,2},{1,3},{2,0},{3,1},{4,6},{5,7},{6,4},{7,5},{8,10},{9,11},{10,... | collective-permute-start | bytes 786440 | tf_op jit(solution)/shard_map/ppermute | solution.py:490
  31.4 5.9 %collective-permute-start.3 = (bf16[256,128]{1,0:T(8,128)(2,1)S(1)}, bf16[256,128]{1,0:T(8,128)(2,1)S(1)}, u32[]{:S(2)}, u32[]{:S(2)}) collective-permute-start(bf16[256,128]{1,0:T(8,128)(2,1)S(1)} %get-tuple-element.26), channel_id=1, source_target_pairs={{0,8},{1,9},{2,10},{3,11},{4,12},{5,13},{6,14},{7,15},{8,0},{9,1},... | collective-permute-start | bytes 196616 | tf_op jit(solution)/shard_map/ppermute | solution.py:490
  33.8 4.3 %collective-permute-start.4 = (bf16[256,128]{1,0:T(8,128)(2,1)S(1)}, bf16[256,128]{1,0:T(8,128)(2,1)S(1)}, u32[]{:S(2)}, u32[]{:S(2)}) collective-permute-start(bf16[256,128]{1,0:T(8,128)(2,1)S(1)} %get-tuple-element.26), channel_id=1, source_target_pairs={{0,4},{1,5},{2,6},{3,7},{4,0},{5,1},{6,2},{7,3},{8,12},{9,13},{10,... | collective-permute-start | bytes 196616 | tf_op jit(solution)/shard_map/ppermute | solution.py:490
  37.3 4.3 %collective-permute-start.5 = (bf16[256,128]{1,0:T(8,128)(2,1)S(1)}, bf16[256,128]{1,0:T(8,128)(2,1)S(1)}, u32[]{:S(2)}, u32[]{:S(2)}) collective-permute-start(bf16[256,128]{1,0:T(8,128)(2,1)S(1)} %collective-permute-done.3), channel_id=1, source_target_pairs={{0,4},{1,5},{2,6},{3,7},{4,0},{5,1},{6,2},{7,3},{8,12},{9,13},{10,... | collective-permute-start | bytes 196616 | tf_op jit(solution)/shard_map/ppermute | solution.py:490
  41.6 6.6 %copy-start.4 = (bf16[128,512]{1,0:T(8,128)(2,1)S(1)}, bf16[128,512]{1,0:T(8,128)(2,1)}, u32[]{:S(2)}) copy-start(bf16[128,512]{1,0:T(8,128)(2,1)} %rest_7_.1) | copy-start | bytes 393220
  41.6 6.6 %copy-start.5 = (bf16[512,128]{1,0:T(8,128)(2,1)S(1)}, bf16[512,128]{1,0:T(8,128)(2,1)}, u32[]{:S(2)}) copy-start(bf16[512,128]{1,0:T(8,128)(2,1)} %rest_8_.1) | copy-start | bytes 393220
  41.6 6.6 %copy-start.9 = (bf16[128,128]{1,0:T(8,128)(2,1)S(1)}, bf16[128,128]{1,0:T(8,128)(2,1)}, u32[]{:S(2)}) copy-start(bf16[128,128]{1,0:T(8,128)(2,1)} %rest_5_.1) | copy-start | bytes 98308
  41.6 6.6 %copy-start.10 = (bf16[128,128]{1,0:T(8,128)(2,1)S(1)}, bf16[128,128]{1,0:T(8,128)(2,1)}, u32[]{:S(2)}) copy-start(bf16[128,128]{1,0:T(8,128)(2,1)} %rest_6_.1) | copy-start | bytes 98308
  41.6 6.6 %copy-start.11 = (bf16[66,128]{1,0:T(8,128)(2,1)S(1)}, bf16[66,128]{1,0:T(8,128)(2,1)}, u32[]{:S(2)}) copy-start(bf16[66,128]{1,0:T(8,128)(2,1)} %table_ref.1) | copy-start | bytes 50692
  41.6 6.4 %collective-permute-start.6 = (bf16[4,256,128]{2,1,0:T(8,128)(2,1)S(1)}, bf16[4,256,128]{2,1,0:T(8,128)(2,1)S(1)}, u32[]{:S(2)}, u32[]{:S(2)}) collective-permute-start(bf16[4,256,128]{2,1,0:T(8,128)(2,1)S(1)} %pad_maximum_fusion.1.line_ref), channel_id=1, source_target_pairs={{0,2},{1,3},{2,0},{3,1},{4,6},{5,7},{6,4},{7,5},{8,10},{9,11},{10,... | collective-permute-start | bytes 786440 | tf_op jit(solution)/shard_map/ppermute | solution.py:490
  42.3 5.9 %copy-start.7 = (bf16[128,128]{1,0:T(8,128)(2,1)S(1)}, bf16[128,128]{1,0:T(8,128)(2,1)}, u32[]{:S(2)}) copy-start(bf16[128,128]{1,0:T(8,128)(2,1)} %rest_2_.1) | copy-start | bytes 98308
  42.3 5.9 %copy-start.8 = (bf16[128,128]{1,0:T(8,128)(2,1)S(1)}, bf16[128,128]{1,0:T(8,128)(2,1)}, u32[]{:S(2)}) copy-start(bf16[128,128]{1,0:T(8,128)(2,1)} %rest_3_.1) | copy-start | bytes 98308
  42.3 5.9 %copy-start.1 = (bf16[1024,128]{1,0:T(8,128)(2,1)S(1)}, bf16[1024,128]{1,0:T(8,128)(2,1)}, u32[]{:S(2)}) copy-start(bf16[1024,128]{1,0:T(8,128)(2,1)} %rest_0_.1) | copy-start | bytes 786436
  42.4 5.9 %copy-start.2 = (bf16[128,512]{1,0:T(8,128)(2,1)S(1)}, bf16[128,512]{1,0:T(8,128)(2,1)}, u32[]{:S(2)}) copy-start(bf16[128,512]{1,0:T(8,128)(2,1)} %rest_1_.1) | copy-start | bytes 393220
  42.4 5.9 %copy-start.3 = (bf16[128,512]{1,0:T(8,128)(2,1)S(1)}, bf16[128,512]{1,0:T(8,128)(2,1)}, u32[]{:S(2)}) copy-start(bf16[128,512]{1,0:T(8,128)(2,1)} %rest_4_.1) | copy-start | bytes 393220
  42.4 9.5 %collective-permute-start.7 = (bf16[4,128,128]{2,1,0:T(8,128)(2,1)S(1)}, bf16[4,128,128]{2,1,0:T(8,128)(2,1)S(1)}, u32[]{:S(2)}, u32[]{:S(2)}) collective-permute-start(bf16[4,128,128]{2,1,0:T(8,128)(2,1)S(1)} %pad_maximum_fusion.3), channel_id=1, source_target_pairs={{0,1},{1,0},{2,3},{3,2},{4,5},{5,4},{6,7},{7,6},{8,9},{9,8},{10,11... | collective-permute-start | bytes 393224 | tf_op jit(solution)/shard_map/ppermute | solution.py:490
  48.1 3.8 %collective-permute-start.8 = (bf16[4,128,128]{2,1,0:T(8,128)(2,1)S(1)}, bf16[4,128,128]{2,1,0:T(8,128)(2,1)S(1)}, u32[]{:S(2)}, u32[]{:S(2)}) collective-permute-start(bf16[4,128,128]{2,1,0:T(8,128)(2,1)S(1)} %slice.23), channel_id=1, source_target_pairs={{0,1},{1,0},{2,3},{3,2},{4,5},{5,4},{6,7},{7,6},{8,9},{9,8},{10,11... | collective-permute-start | bytes 393224 | tf_op jit(solution)/shard_map/ppermute | solution.py:490
  57.5 2.1 %collective-permute-start.9 = (bf16[2048,128]{1,0:T(8,128)(2,1)S(1)}, bf16[2048,128]{1,0:T(8,128)(2,1)S(1)}, u32[]{:S(2)}, u32[]{:S(2)}) collective-permute-start(bf16[2048,128]{1,0:T(8,128)(2,1)S(1)} %get-tuple-element.34.right_own_ref), channel_id=1, source_target_pairs={{0,1},{1,0},{2,3},{3,2},{4,5},{5,4},{6,7},{7,6},{8,9},{9,8},{10,11... | collective-permute-start | bytes 1572872 | tf_op jit(solution)/shard_map/ppermute | solution.py:490
  70.6 1.4 %collective-permute-start.10 = (f32[2,128,128]{2,1,0:T(8,128)S(1)}, f32[2,128,128]{2,1,0:T(8,128)S(1)}, u32[]{:S(2)}, u32[]{:S(2)}) collective-permute-start(f32[2,128,128]{2,1,0:T(8,128)S(1)} %get-tuple-element.37), channel_id=1, source_target_pairs={{0,1},{1,0},{2,3},{3,2},{4,5},{5,4},{6,7},{7,6},{8,9},{9,8},{10,11... | collective-permute-start | bytes 393224 | tf_op jit(solution)/shard_map/ppermute | solution.py:490
  (2 other events, 1.6 us)

commit v6 on v5

--- a/solution.py
+++ b/solution.py
@@ -125,7 +125,7 @@
     *stack_refs,
 ):
     place = place_ref[0]
-    inverse_live = 1.0 / live_ref[0]
+    inverse_live = 1.0 / jnp.sum(live_ref[...], axis=1, keepdims=True)
     half = LANES // 2
     low_half = lax.broadcasted_iota(jnp.int32, (LANES, LANES), 1) < half
 
@@ -218,25 +218,28 @@
             rows = pl.ds(pl.multiple_of((4 * chip + 2 * side) * 128, 256), 256)
             right_ref[rows, :] = source[chip * 256 : (chip + 1) * 256, :].astype(jnp.float32)
 
+    nothing = jnp.zeros((32, LANES), jnp.bfloat16)
+
     def outgoing_channels(block, carry):
-        for e in range(8):
-            c = block * 8 + e
+        for e in range(32):
+            c = block * 32 + e
             left = left_ref[pl.ds(c, 16, stride=128), :].astype(jnp.bfloat16)
             right = right_ref[pl.ds(c, 32, stride=128), :]
-            moved = pltpu.roll(right, half, 1)
+            moved = pltpu.roll(right, half, 1).astype(jnp.bfloat16)
+            right = right.astype(jnp.bfloat16)
             spread = jnp.concatenate(
                 [
-                    jnp.where(low_short, right, 0.0),
-                    jnp.where(low_short, moved, 0.0),
-                    jnp.where(low_short, 0.0, moved),
-                    jnp.where(low_short, 0.0, right),
+                    jnp.where(low_short, right, nothing),
+                    jnp.where(low_short, moved, nothing),
+                    jnp.where(low_short, nothing, moved),
+                    jnp.where(low_short, nothing, right),
                 ],
                 axis=0,
-            ).astype(jnp.bfloat16)
+            )
             product_ref[pl.ds(c, 16, stride=128), :] = contract_last(left, spread)
         return carry
 
-    lax.fori_loop(0, 16, outgoing_channels, 0)
+    lax.fori_loop(0, 4, outgoing_channels, 0)
 
     column = lax.broadcasted_iota(jnp.int32, (1, 256), 1)
     which = column // 16
@@ -285,14 +288,14 @@
         own_left_ref[m * 128 : (m + 1) * 128, :] = part
 
     def incoming_channels(block, carry):
-        for e in range(8):
-            c = block * 8 + e
+        for e in range(32):
+            c = block * 32 + e
             left = own_left_ref[pl.ds(c, 16, stride=128), :][:, 0:16].astype(jnp.bfloat16)
             right = right_ref[pl.ds(c, 16, stride=128), :].astype(jnp.bfloat16)
             own_product_ref[pl.ds(c, 16, stride=128), :] = mix(left, right)
         return carry
 
-    lax.fori_loop(0, 16, incoming_channels, 0)
+    lax.fori_loop(0, 4, incoming_channels, 0)
 
     def block_of(b, e, residue):
         m = 8 * b + 4 * e + residue
@@ -339,7 +342,20 @@
     )
 
 
-def rows_kernel(rows_ref, pair_ref, blocks_ref, own_pair_ref, wide_ref):
+def rows_kernel(
+    rows_source, pair_source, blocks_ref, own_pair_ref, rows_ref, pair_ref, wide_ref, arrived
+):
+    rows_copy = pltpu.make_async_copy(rows_source, rows_ref, arrived.at[0])
+    pair_copy = pltpu.make_async_copy(pair_source, pair_ref, arrived.at[1])
+    pair_copy.start()
+    rows_copy.start()
+    pair_copy.wait()
+    order = lane_order_matrix()
+    for t in range(2):
+        own_pair_ref[t] = contract_first(
+            pair_ref[2 * t : 2 * t + 2].reshape(LANES, LANES), order
+        ).astype(jnp.bfloat16)
+    rows_copy.wait()
     residues = rows_ref.shape[1]
     count = 8 * residues
     rows = rows_ref[...].astype(jnp.float32).reshape(count, 2 * LANES)
@@ -353,11 +369,6 @@
             blocks_ref[p, :, e * LANES : (e + 1) * LANES] = jnp.concatenate(block, axis=0).astype(
                 jnp.bfloat16
             )
-    order = lane_order_matrix()
-    for t in range(2):
-        own_pair_ref[t] = contract_first(
-            pair_ref[2 * t : 2 * t + 2].reshape(LANES, LANES), order
-        ).astype(jnp.bfloat16)
 
 
 TURNED = {
@@ -376,8 +387,9 @@
     table_ref,
     *rest,
 ):
-    sources, (embedding_out, turned_out, wide_out) = rest[:9], rest[9:12]
-    landed, (table_wide_ref, mean_wide_ref, arrived) = rest[12:21], rest[21:]
+    sources, (embedding_out, turned_out, wide_out, ready_out) = rest[:9], rest[9:13]
+    landed, (table_wide_ref, mean_wide_ref, arrived) = rest[13:22], rest[22:]
+    ready_out[...] = jnp.zeros_like(ready_out)
     copies = [
         pltpu.make_async_copy(sources[k], landed[k], arrived.at[k]) for k in range(len(sources))
     ]
@@ -441,9 +453,11 @@
     up_ref,
     down_ref,
     outer_ref,
+    ready_ref,
     result_ref,
     parts_ref,
     wide_ref,
+    attended_ref,
     final_ref,
 ):
     for p in range(16):
@@ -455,32 +469,38 @@
     width = HM * HEAD_SIZE
     head_of = lax.broadcasted_iota(jnp.int32, (128, width), 1) // HEAD_SIZE
     zero = jnp.zeros((128, width), jnp.bfloat16)
+    one = jnp.ones((128, width), jnp.bfloat16)
+
+    def by_head(values):
+        return jnp.concatenate([jnp.where(head_of == h, values, zero) for h in range(HM)], axis=0)
+
+    heads = by_head(one)
+    normed = normalize_rows(wide_ref[...])
+    query = (mix(normed, query_ref[...]) * HEAD_SIZE ** (-0.5)).astype(jnp.bfloat16)
+    key = mix(normed, key_ref[...]).astype(jnp.bfloat16)
+    value_gate = mix(normed, value_gate_ref[...])
+    value = value_gate[:, :width].astype(jnp.bfloat16)
     for i in range(4):
         rows = slice(i * 128, (i + 1) * 128)
-        current = wide_ref[rows, :]
-        normed = normalize_rows(current)
-        query = (mix(normed, query_ref[...]) * HEAD_SIZE ** (-0.5)).astype(jnp.bfloat16)
-        key = mix(normed, key_ref[...]).astype(jnp.bfloat16)
-        value_gate = mix(normed, value_gate_ref[...])
-        value = value_gate[:, :width].astype(jnp.bfloat16)
-        keys = jnp.concatenate([jnp.where(head_of == h, key, zero) for h in range(HM)], axis=0)
-        values = jnp.concatenate([jnp.where(head_of == h, value, zero) for h in range(HM)], axis=0)
-        scores = contract_last(query, keys)
-        heads = []
+        scores = contract_last(query[rows], by_head(key[rows]))
+        raised = []
         for h in range(HM):
             score = jnp.where(alive, scores[:, h * 128 : (h + 1) * 128], -1000000000.0)
-            raised = jnp.exp(score - jnp.max(score, axis=1, keepdims=True))
-            heads.append((raised / jnp.sum(raised, axis=1, keepdims=True)).astype(jnp.bfloat16))
-        attended = mix(jnp.concatenate(heads, axis=1), values)
-        gated = (gate_curve(value_gate[:, width:]) * attended).astype(jnp.bfloat16)
-        current = current + mix(gated, output_ref[...])
-        hidden = jnp.maximum(mix(normalize_rows(current), up_ref[...]), 0.0).astype(jnp.bfloat16)
-        final = (current + mix(hidden, down_ref[...])).astype(jnp.bfloat16).astype(jnp.float32)
-        final_ref[pl.ds(i, 128, stride=4), :] = final[:, :128]
-        final_ref[pl.ds(512 + i, 128, stride=4), :] = final[:, 128:]
-        outer = (contract_last(outer_ref[...], normalize_rows(final)) * live).astype(jnp.bfloat16)
-        parts_ref[i * CO : (i + 1) * CO, :] = outer[:CO, :]
-        parts_ref[128 + i * CO : 128 + (i + 1) * CO, :] = outer[CO:, :]
+            raised.append(jnp.exp(score - jnp.max(score, axis=1, keepdims=True)).astype(jnp.bfloat16))
+        raised = jnp.concatenate(raised, axis=1)
+        attended_ref[rows, :] = mix(raised, by_head(value[rows])) / mix(raised, heads)
+    gated = (gate_curve(value_gate[:, width:]) * attended_ref[...]).astype(jnp.bfloat16)
+    current = wide_ref[...] + mix(gated, output_ref[...])
+    hidden = jnp.maximum(mix(normalize_rows(current), up_ref[...]), 0.0).astype(jnp.bfloat16)
+    final = (current + mix(hidden, down_ref[...])).astype(jnp.bfloat16).astype(jnp.float32)
+    outer = contract_last(outer_ref[...], normalize_rows(final))
+    for i in range(4):
+        rows = slice(i * 128, (i + 1) * 128)
+        part = (outer[:, rows] * live).astype(jnp.bfloat16)
+        parts_ref[i * CO : (i + 1) * CO, :] = part[:CO, :]
+        parts_ref[128 + i * CO : 128 + (i + 1) * CO, :] = part[CO:, :]
+        final_ref[pl.ds(i, 128, stride=4), :] = final[rows, :128]
+        final_ref[pl.ds(512 + i, 128, stride=4), :] = final[rows, 128:]
     result_ref[:, :128] = final_ref[:512, :].astype(jnp.bfloat16)
     result_ref[:, 128:] = final_ref[512:, :].astype(jnp.bfloat16)
 
@@ -524,9 +544,14 @@
     blocks, own_pair = pl.pallas_call(
         rows_kernel,
         out_shape=[array(16, 32, channels), array(2, width, LANES)],
-        in_specs=[vmem, vmem],
+        in_specs=[hbm, hbm],
         out_specs=[vmem, vmem],
-        scratch_shapes=[pltpu.VMEM((1024, LANES), jnp.float32)],
+        scratch_shapes=[
+            pltpu.VMEM(alignment_input.shape, jnp.bfloat16),
+            pltpu.VMEM(pair_state_input.shape, jnp.bfloat16),
+            pltpu.VMEM((1024, LANES), jnp.float32),
+            pltpu.SemaphoreType.DMA((2,)),
+        ],
         compiler_params=limit(16),
         name="rows_by_device",
     )(alignment_input, pair_state_input)
@@ -536,11 +561,11 @@
     pair_near = exchange(jnp.stack([own_pair, pair_far]), 4)
     pair_line = jnp.concatenate([jnp.stack([own_pair, pair_far]), pair_near])
 
-    embedding, turned_weights, wide_weights = pl.pallas_call(
+    embedding, turned_weights, wide_weights, ready = pl.pallas_call(
         weights_kernel,
-        out_shape=[array(32, width, LANES), array(2048, LANES), array(384, 512)],
+        out_shape=[array(32, width, LANES), array(2048, LANES), array(384, 512), wide(8, LANES)],
         in_specs=[vmem] * 2 + [hbm] * 9,
-        out_specs=[vmem] * 3,
+        out_specs=[vmem] * 4,
         scratch_shapes=[pltpu.VMEM(w.shape, jnp.bfloat16) for w in pair_weights]
         + [
             pltpu.VMEM((LANES, LANES), jnp.float32),
@@ -563,9 +588,10 @@
     result, parts = pl.pallas_call(
         msa_kernel,
         out_shape=(array(512, channels), array(256, LANES)),
-        in_specs=[vmem] * 9,
+        in_specs=[vmem] * 10,
         out_specs=(vmem, vmem),
         scratch_shapes=[
+            pltpu.VMEM((512, channels), jnp.float32),
             pltpu.VMEM((512, channels), jnp.float32),
             pltpu.VMEM((1024, LANES), jnp.float32),
         ],
@@ -584,6 +610,7 @@
         alignment_transition_up,
         alignment_transition_down,
         outer_input_weight.T,
+        ready,
     )
     parts, pair_across = lax.optimization_barrier((parts, pair_across))
     far = exchange(parts, 8)
@@ -598,7 +625,7 @@
     pair_mid, left, gating, right = pl.pallas_call(
         start_kernel,
         out_shape=[wide(*slabs), wide(*tall), wide(*slabs), array(*tall)],
-        in_specs=[smem, smem] + [vmem] * 9,
+        in_specs=[smem] + [vmem] * 10,
         out_specs=[vmem] * 4,
         scratch_shapes=[
             pltpu.VMEM((2048, LANES), jnp.float32),
@@ -610,7 +637,7 @@
         name="pair_start",
     )(
         place,
-        jnp.sum(live_row_float).reshape(1),
+        live_row_float.reshape(1, LANES),
         line,
         across,
         core_line,

time: 73.9 us -> 75.7 us (1.024)
  local copies, waits for them, and re-layouts: 3.72 us -> 11.5 us
  Pallas kernels: 29.4 us -> 22.4 us
    unnamed x44 -> x46, local copies, waits for them, and re-layouts: 2.47 us -> 9.61 us
    pallas_call x1, Pallas kernels: 10.9 us -> 7.48 us  [whole_block(): pl.pallas_call(triangle_kernel, out_shape=[wide(2, 128, LANES)] * 3, in_s...]
    pallas_call x1, Pallas kernels: 7.22 us -> 4.09 us  [whole_block(): pl.pallas_call(msa_kernel, out_shape=(array(512, channels), array(256, LA...]
  transfers between devices with their start and end apart: 12 -> 12, of which waited for: 8 -> 9; matrix products, arithmetic and copies ran while one was open for 3% -> 4% of each run, Pallas kernels for 14% -> 9%
where the time goes in v6:
time: 75.7 us; the launch traced here: 75 us
  waiting for transfers between devices  23 us (30%)
  Pallas kernels  22.4 us (30%)
  starting transfers between devices  15.8 us (21%)
  local copies, waits for them, and re-layouts  11.5 us (15%)
  other arithmetic  1.47 us (2%)
  between operations  0.86 us (1%)
    ppermute x11, waiting for transfers between devices, exchange(): return lax.ppermute(values, 'dap', [(q, q ^ offset) for q in range(pieces)])  22.6 us
    ppermute x11, starting transfers between devices, exchange(): return lax.ppermute(values, 'dap', [(q, q ^ offset) for q in range(pieces)])  11.7 us
    unnamed x46, local copies, waits for them, and re-layouts  9.61 us
    pallas_call x1, Pallas kernels, whole_block(): pl.pallas_call(triangle_kernel, out_shape=[wide(2, 128, LANES)] * 3, in_s...  7.48 us
    pallas_call x1, Pallas kernels, whole_block(): pl.pallas_call(start_kernel, out_shape=[wide(*slabs), wide(*tall), wide(*...  4.92 us
    pallas_call x1, Pallas kernels, whole_block(): pl.pallas_call(msa_kernel, out_shape=(array(512, channels), array(256, LA...  4.09 us
    all_to_all x1, starting transfers between devices, whole_block(): lax.all_to_all(blocks, 'dap', split_axis=0, concat_axis=0, tiled=True)  4.04 us
    pallas_call x1, Pallas kernels, whole_block(): pl.pallas_call(weights_kernel, out_shape=[array(32, width, LANES), array(...  3.03 us
  transfers between devices with their start and end apart: 12, of which 9 were waited for; matrix products, arithmetic and copies ran while one was open for 4% of the time, Pallas kernels for 9%

profile of v6, /device:TPU:0, one launch (start us, length us, event | category | flops | bytes accessed | tf_op | source)
XLA Modules:
  0.0 75.0 jit_solution(15835604410336782973)
XLA Ops:
  0.6 0.9 %copy-done = bf16[8,64,256]{2,1,0:T(8,128)(2,1)S(1)} copy-done((bf16[8,64,256]{2,1,0:T(8,128)(2,1)S(1)}, bf16[8,64,256]{2,1,0:T(8,128)(2,1)}, u32[]{:S(2)}) %copy-start) | copy-done | bytes 262168
  1.6 0.8 %copy-done.6 = bf16[4,64,128]{2,1,0:T(8,128)(2,1)S(1)} copy-done((bf16[4,64,128]{2,1,0:T(8,128)(2,1)S(1)}, bf16[4,64,128]{2,1,0:T(8,128)(2,1)}, u32[]{:S(2)}) %copy-start.6) | copy-done | bytes 65560
  2.4 1.3 %rows_by_device.1 = (bf16[16,32,256]{2,1,0:T(8,128)(2,1)}, bf16[2,128,128]{2,1,0:T(8,128)(2,1)S(1)}) custom-call(bf16[8,64,256]{2,1,0:T(8,128)(2,1)S(1)} %copy-done, bf16[4,64,128]{2,1,0:T(8,128)(2,1)S(1)} %copy-done.6), custom_call_target="tpu_custom_call" | custom-call | tf_op jit(solution)/shard_map/rows_by_device/pallas_call | solution.py:544
  3.8 4.1 %collective-permute-start = (bf16[2,128,128]{2,1,0:T(8,128)(2,1)S(1)}, bf16[2,128,128]{2,1,0:T(8,128)(2,1)S(1)}, u32[]{:S(2)}, u32[]{:S(2)}) collective-permute-start(bf16[2,128,128]{2,1,0:T(8,128)(2,1)S(1)} %get-tuple-element.22), channel_id=1, source_target_pairs={{0,8},{1,9},{2,10},{3,11},{4,12},{5,13},{6,14},{7,15},{8,0},{9,1},... | collective-permute-start | bytes 196616 | tf_op jit(solution)/shard_map/ppermute | solution.py:510
  7.9 4.0 %all-to-all-start = ((bf16[16,32,256]{2,1,0:T(8,128)(2,1)}), bf16[16,32,256]{2,1,0:T(8,128)(2,1)S(1)}, u32[]{:S(2)}, u32[]{:S(2)}) async-start(bf16[16,32,256]{2,1,0:T(8,128)(2,1)} %get-tuple-element.21), calls=%async_computation | async-start | bytes 524288 | tf_op jit(solution)/shard_map/all_to_all | solution.py:558
  12.9 2.0 %collective-permute-start.1 = (bf16[2,2,128,128]{3,2,1,0:T(8,128)(2,1)S(1)}, bf16[2,2,128,128]{3,2,1,0:T(8,128)(2,1)S(1)}, u32[]{:S(2)}, u32[]{:S(2)}) collective-permute-start(bf16[2,2,128,128]{3,2,1,0:T(8,128)(2,1)S(1)} %pad_maximum_fusion.2), channel_id=1, source_target_pairs={{0,4},{1,5},{2,6},{3,7},{4,0},{5,1},{6,2},{7,3},{8,12},{9,13},{10,... | collective-permute-start | bytes 393224 | tf_op jit(solution)/shard_map/ppermute | solution.py:510
  15.1 6.9 %collective-permute-done.1 = bf16[2,2,128,128]{3,2,1,0:T(8,128)(2,1)S(1)} collective-permute-done((bf16[2,2,128,128]{3,2,1,0:T(8,128)(2,1)S(1)}, bf16[2,2,128,128]{3,2,1,0:T(8,128)(2,1)S(1)}, u32[]{:S(2)}, u32[]{:S(2)}) %collective-permute-start.1) | collective-permute-done | bytes 131104 | tf_op jit(solution)/shard_map/ppermute | solution.py:510
  22.4 1.2 %collective-permute-start.2 = (bf16[4,2,128,128]{3,2,1,0:T(8,128)(2,1)S(1)}, bf16[4,2,128,128]{3,2,1,0:T(8,128)(2,1)S(1)}, u32[]{:S(2)}, u32[]{:S(2)}) collective-permute-start(bf16[4,2,128,128]{3,2,1,0:T(8,128)(2,1)S(1)} %pad_maximum_fusion.pair_line_ref), channel_id=1, source_target_pairs={{0,2},{1,3},{2,0},{3,1},{4,6},{5,7},{6,4},{7,5},{8,10},{9,11},{10,... | collective-permute-start | bytes 786440 | tf_op jit(solution)/shard_map/ppermute | solution.py:510
  24.3 0.7 copy-done.7
  25.1 0.8 %copy-done.8 = bf16[128,128]{1,0:T(8,128)(2,1)S(1)} copy-done((bf16[128,128]{1,0:T(8,128)(2,1)S(1)}, bf16[128,128]{1,0:T(8,128)(2,1)}, u32[]{:S(2)}) %copy-start.8) | copy-done | bytes 32792
  25.8 0.8 %copy-done.9 = bf16[128,128]{1,0:T(8,128)(2,1)S(1)} copy-done((bf16[128,128]{1,0:T(8,128)(2,1)S(1)}, bf16[128,128]{1,0:T(8,128)(2,1)}, u32[]{:S(2)}) %copy-start.9) | copy-done | bytes 32792
  26.6 0.8 %copy-done.10 = bf16[128,128]{1,0:T(8,128)(2,1)S(1)} copy-done((bf16[128,128]{1,0:T(8,128)(2,1)S(1)}, bf16[128,128]{1,0:T(8,128)(2,1)}, u32[]{:S(2)}) %copy-start.10) | copy-done | bytes 32792
  27.3 0.7 copy-done.11
  28.1 3.0 %turn_weights.1 = (bf16[32,128,128]{2,1,0:T(8,128)(2,1)S(1)}, bf16[2048,128]{1,0:T(8,128)(2,1)S(1)}, bf16[384,512]{1,0:T(8,128)(2,1)S(1)}, f32[8,128]{1,0:T(8,128)S(1)}) custom-call(s32[32,128]{1,0:T(8,128)S(1)} %select_n.11.bins_ref, bf16[66,128]{1,0:T(8,128)(2,1)S(1)} %copy-done.11, bf16[1024,128]{1,0:T(8,128)(2,1)S(1)} %copy-done.1, ...), custom_call_target="tpu_custom_call" | custom-call | flops 200000000 | bytes 8000000 | tf_op jit(solution)/shard_map/turn_weights/pallas_call | solution.py:564
  31.2 0.6 copy-done.12
  31.8 1.0 %copy-done.14 = bf16[1024,256]{1,0:T(8,128)(2,1)S(1)} copy-done((bf16[1024,256]{1,0:T(8,128)(2,1)S(1)}, bf16[1024,256]{1,0:T(8,128)(2,1)}, u32[]{:S(2)}) %copy-start.14) | copy-done | bytes 524312
  32.8 0.9 %copy-done.17 = bf16[256,256]{1,0:T(8,128)(2,1)S(1)} copy-done((bf16[256,256]{1,0:T(8,128)(2,1)S(1)}, bf16[256,256]{1,0:T(8,128)(2,1)}, u32[]{:S(2)}) %copy-start.17) | copy-done | bytes 131096
  33.7 0.9 %copy-done.18 = bf16[256,256]{1,0:T(8,128)(2,1)S(1)} copy-done((bf16[256,256]{1,0:T(8,128)(2,1)S(1)}, bf16[256,256]{1,0:T(8,128)(2,1)}, u32[]{:S(2)}) %copy-start.18) | copy-done | bytes 131096
  34.6 4.1 %msa_whole.1 = (bf16[512,256]{1,0:T(8,128)(2,1)S(1)}, bf16[256,128]{1,0:T(8,128)(2,1)S(1)}) custom-call(f32[1,128]{1,0:T(1,128)S(1)} %copy-done.12, bf16[16,32,256]{2,1,0:T(8,128)(2,1)S(1)} %all-to-all-done.blocks_ref, bf16[256,256]{1,0:T(8,128)(2,1)S(1)} %copy-done.16, bf16[256,256]{1,0:T(8,128)(2,1)S(1)} %copy-done.17, bf16[256,512]{1,0:T(8,128)(2,1)S(1)} %copy-done.15, ...), custom_call_target="tpu_custom_call" | custom-call | flops 2000000000 | bytes 10000000 | tf_op jit(solution)/shard_map/msa_whole/pallas_call | solution.py:588
  38.7 2.4 %collective-permute-start.3 = (bf16[256,128]{1,0:T(8,128)(2,1)S(1)}, bf16[256,128]{1,0:T(8,128)(2,1)S(1)}, u32[]{:S(2)}, u32[]{:S(2)}) collective-permute-start(bf16[256,128]{1,0:T(8,128)(2,1)S(1)} %get-tuple-element.28), channel_id=1, source_target_pairs={{0,8},{1,9},{2,10},{3,11},{4,12},{5,13},{6,14},{7,15},{8,0},{9,1},... | collective-permute-start | bytes 196616 | tf_op jit(solution)/shard_map/ppermute | solution.py:510
  41.7 2.9 %collective-permute-done.3 = bf16[256,128]{1,0:T(8,128)(2,1)S(1)} collective-permute-done((bf16[256,128]{1,0:T(8,128)(2,1)S(1)}, bf16[256,128]{1,0:T(8,128)(2,1)S(1)}, u32[]{:S(2)}, u32[]{:S(2)}) %collective-permute-start.3) | collective-permute-done | bytes 65568 | tf_op jit(solution)/shard_map/ppermute | solution.py:510
  45.4 3.5 %collective-permute-done.5 = bf16[256,128]{1,0:T(8,128)(2,1)S(1)} collective-permute-done((bf16[256,128]{1,0:T(8,128)(2,1)S(1)}, bf16[256,128]{1,0:T(8,128)(2,1)S(1)}, u32[]{:S(2)}, u32[]{:S(2)}) %collective-permute-start.5) | collective-permute-done | bytes 65568 | tf_op jit(solution)/shard_map/ppermute | solution.py:510
  49.0 0.7 collective-permute-start.6
  49.7 0.7 pad_maximum_fusion.3
  50.3 5.1 %collective-permute-done.6.across_ref = bf16[4,256,128]{2,1,0:T(8,128)(2,1)S(1)} collective-permute-done((bf16[4,256,128]{2,1,0:T(8,128)(2,1)S(1)}, bf16[4,256,128]{2,1,0:T(8,128)(2,1)S(1)}, u32[]{:S(2)}, u32[]{:S(2)}) %collective-permute-start.6) | collective-permute-done | bytes 262176 | tf_op jit(solution)/shard_map/ppermute | solution.py:510
  55.4 0.7 slice.23
  56.1 1.6 %collective-permute-done.8.core_across_ref = bf16[4,128,128]{2,1,0:T(8,128)(2,1)S(1)} collective-permute-done((bf16[4,128,128]{2,1,0:T(8,128)(2,1)}, bf16[4,128,128]{2,1,0:T(8,128)(2,1)S(1)}, u32[]{:S(2)}, u32[]{:S(2)}) %collective-permute-start.8) | collective-permute-done | bytes 131104 | tf_op jit(solution)/shard_map/ppermute | solution.py:510
  57.6 4.9 %pair_start.1 = (f32[16,128,128]{2,1,0:T(8,128)S(1)}, f32[2048,128]{1,0:T(8,128)S(1)}, f32[16,128,128]{2,1,0:T(8,128)S(1)}, bf16[2048,128]{1,0:T(8,128)(2,1)S(1)}) custom-call(s32[1]{0:T(128)} %bitcast.6.place_ref, f32[1,128]{1,0:T(1,128)S(1)} %copy-done.12, bf16[4,256,128]{2,1,0:T(8,128)(2,1)S(1)} %pad_maximum_fusion.1.line_ref, ...), custom_call_target="tpu_custom_call" | custom-call | tf_op jit(solution)/shard_map/pair_start/pallas_call | solution.py:625
  62.8 1.8 %collective-permute-done.9.right_other_ref = bf16[2048,128]{1,0:T(8,128)(2,1)S(1)} collective-permute-done((bf16[2048,128]{1,0:T(8,128)(2,1)S(1)}, bf16[2048,128]{1,0:T(8,128)(2,1)S(1)}, u32[]{:S(2)}, u32[]{:S(2)}) %collective-permute-start.9) | collective-permute-done | bytes 524320 | tf_op jit(solution)/shard_map/ppermute | solution.py:510
  64.5 7.5 %pair_triangles.1 = (f32[2,128,128]{2,1,0:T(8,128)S(1)}, f32[2,128,128]{2,1,0:T(8,128)S(1)}, f32[2,128,128]{2,1,0:T(8,128)S(1)}) custom-call(s32[1]{0:T(128)} %bitcast.6.place_ref, f32[16,128,128]{2,1,0:T(8,128)S(1)} %get-tuple-element.33.pair_mid_ref, f32[2048,128]{1,0:T(8,128)S(1)} %get-tuple-element.34.left_ref, ...), custom_call_target="tpu_custom_call" | custom-call | tf_op jit(solution)/shard_map/pair_triangles/pallas_call | solution.py:651
  72.2 0.8 %reshape.59 = bf16[128,4,256]{2,1,0:T(4,128)(2,1)} reshape(bf16[512,256]{1,0:T(8,128)(2,1)S(1)} %get-tuple-element.25) | data formatting | bytes 524288 | tf_op jit(solution)/shard_map/reshape | solution.py:675
  73.4 1.5 %pair_finish.1 = bf16[256,128]{1,0:T(8,128)(2,1)} custom-call(f32[2,128,128]{2,1,0:T(8,128)S(1)} %get-tuple-element.37.own_pair_ref, f32[2,128,128]{2,1,0:T(8,128)S(1)} %get-tuple-element.38.own_part_ref, f32[2,128,128]{2,1,0:T(8,128)S(1)} %collective-permute-done.10.other_part_ref, bf16[2048,128]{1,0:T(8,128)(2,1)S(1)} %get-tuple-element.31.turned_ref, ...), custom_call_target="tpu_custom_call" | custom-call | tf_op jit(solution)/shard_map/pair_finish/pallas_call | solution.py:667
  (61 shorter events, 4.4 us)
Async XLA Ops:
  0.6 1.0 %copy-start = (bf16[8,64,256]{2,1,0:T(8,128)(2,1)S(1)}, bf16[8,64,256]{2,1,0:T(8,128)(2,1)}, u32[]{:S(2)}) copy-start(bf16[8,64,256]{2,1,0:T(8,128)(2,1)} %rows_source.1) | copy-start | bytes 786436
  1.6 0.8 %copy-start.6 = (bf16[4,64,128]{2,1,0:T(8,128)(2,1)S(1)}, bf16[4,64,128]{2,1,0:T(8,128)(2,1)}, u32[]{:S(2)}) copy-start(bf16[4,64,128]{2,1,0:T(8,128)(2,1)} %pair_source.1) | copy-start | bytes 196612
  3.8 9.1 %collective-permute-start = (bf16[2,128,128]{2,1,0:T(8,128)(2,1)S(1)}, bf16[2,128,128]{2,1,0:T(8,128)(2,1)S(1)}, u32[]{:S(2)}, u32[]{:S(2)}) collective-permute-start(bf16[2,128,128]{2,1,0:T(8,128)(2,1)S(1)} %get-tuple-element.22), channel_id=1, source_target_pairs={{0,8},{1,9},{2,10},{3,11},{4,12},{5,13},{6,14},{7,15},{8,0},{9,1},... | collective-permute-start | bytes 196616 | tf_op jit(solution)/shard_map/ppermute | solution.py:510
  7.9 4.1 %copy-start.20 = (s32[64]{0:T(128)S(1)}, s32[64]{0:T(128)}, u32[]{:S(2)}) copy-start(s32[64]{0:T(128)} %param.24) | copy-start | bytes 772
  7.9 14.6 %all-to-all-start = ((bf16[16,32,256]{2,1,0:T(8,128)(2,1)}), bf16[16,32,256]{2,1,0:T(8,128)(2,1)S(1)}, u32[]{:S(2)}, u32[]{:S(2)}) async-start(bf16[16,32,256]{2,1,0:T(8,128)(2,1)} %get-tuple-element.21), calls=%async_computation | async-start | bytes 524288 | tf_op jit(solution)/shard_map/all_to_all | solution.py:558
  12.9 11.4 %copy-start.5 = (bf16[512,128]{1,0:T(8,128)(2,1)S(1)}, bf16[512,128]{1,0:T(8,128)(2,1)}, u32[]{:S(2)}) copy-start(bf16[512,128]{1,0:T(8,128)(2,1)} %rest_8_.1) | copy-start | bytes 393220
  12.9 9.2 %collective-permute-start.1 = (bf16[2,2,128,128]{3,2,1,0:T(8,128)(2,1)S(1)}, bf16[2,2,128,128]{3,2,1,0:T(8,128)(2,1)S(1)}, u32[]{:S(2)}, u32[]{:S(2)}) collective-permute-start(bf16[2,2,128,128]{3,2,1,0:T(8,128)(2,1)S(1)} %pad_maximum_fusion.2), channel_id=1, source_target_pairs={{0,4},{1,5},{2,6},{3,7},{4,0},{5,1},{6,2},{7,3},{8,12},{9,13},{10,... | collective-permute-start | bytes 393224 | tf_op jit(solution)/shard_map/ppermute | solution.py:510
  14.9 9.4 %copy-start.4 = (bf16[128,512]{1,0:T(8,128)(2,1)S(1)}, bf16[128,512]{1,0:T(8,128)(2,1)}, u32[]{:S(2)}) copy-start(bf16[128,512]{1,0:T(8,128)(2,1)} %rest_7_.1) | copy-start | bytes 393220
  15.1 8.5 %copy-start.22 = (s32[128]{0:T(128)S(1)}, s32[128]{0:T(128)}, u32[]{:S(2)}) copy-start(s32[128]{0:T(128)} %param.26) | copy-start | bytes 1540
  15.1 9.2 %copy-start.1 = (bf16[1024,128]{1,0:T(8,128)(2,1)S(1)}, bf16[1024,128]{1,0:T(8,128)(2,1)}, u32[]{:S(2)}) copy-start(bf16[1024,128]{1,0:T(8,128)(2,1)} %rest_0_.1) | copy-start | bytes 786436
  22.1 2.2 %copy-start.2 = (bf16[128,512]{1,0:T(8,128)(2,1)S(1)}, bf16[128,512]{1,0:T(8,128)(2,1)}, u32[]{:S(2)}) copy-start(bf16[128,512]{1,0:T(8,128)(2,1)} %rest_1_.1) | copy-start | bytes 393220
  22.1 2.2 %copy-start.3 = (bf16[128,512]{1,0:T(8,128)(2,1)S(1)}, bf16[128,512]{1,0:T(8,128)(2,1)}, u32[]{:S(2)}) copy-start(bf16[128,512]{1,0:T(8,128)(2,1)} %rest_4_.1) | copy-start | bytes 393220
  22.4 16.3 %collective-permute-start.2 = (bf16[4,2,128,128]{3,2,1,0:T(8,128)(2,1)S(1)}, bf16[4,2,128,128]{3,2,1,0:T(8,128)(2,1)S(1)}, u32[]{:S(2)}, u32[]{:S(2)}) collective-permute-start(bf16[4,2,128,128]{3,2,1,0:T(8,128)(2,1)S(1)} %pad_maximum_fusion.pair_line_ref), channel_id=1, source_target_pairs={{0,2},{1,3},{2,0},{3,1},{4,6},{5,7},{6,4},{7,5},{8,10},{9,11},{10,... | collective-permute-start | bytes 786440 | tf_op jit(solution)/shard_map/ppermute | solution.py:510
  24.3 0.8 %copy-start.7 = (bf16[128,128]{1,0:T(8,128)(2,1)S(1)}, bf16[128,128]{1,0:T(8,128)(2,1)}, u32[]{:S(2)}) copy-start(bf16[128,128]{1,0:T(8,128)(2,1)} %rest_2_.1) | copy-start | bytes 98308
  25.1 0.8 %copy-start.8 = (bf16[128,128]{1,0:T(8,128)(2,1)S(1)}, bf16[128,128]{1,0:T(8,128)(2,1)}, u32[]{:S(2)}) copy-start(bf16[128,128]{1,0:T(8,128)(2,1)} %rest_3_.1) | copy-start | bytes 98308
  25.8 0.8 %copy-start.9 = (bf16[128,128]{1,0:T(8,128)(2,1)S(1)}, bf16[128,128]{1,0:T(8,128)(2,1)}, u32[]{:S(2)}) copy-start(bf16[128,128]{1,0:T(8,128)(2,1)} %rest_5_.1) | copy-start | bytes 98308
  26.6 0.8 %copy-start.10 = (bf16[128,128]{1,0:T(8,128)(2,1)S(1)}, bf16[128,128]{1,0:T(8,128)(2,1)}, u32[]{:S(2)}) copy-start(bf16[128,128]{1,0:T(8,128)(2,1)} %rest_6_.1) | copy-start | bytes 98308
  28.1 3.1 %copy-start.13 = (bf16[256,1024]{1,0:T(8,128)(2,1)S(1)}, bf16[256,1024]{1,0:T(8,128)(2,1)}, u32[]{:S(2)}) copy-start(bf16[256,1024]{1,0:T(8,128)(2,1)} %up_ref.1) | copy-start | bytes 1572868
  28.1 3.1 %copy-start.15 = (bf16[256,512]{1,0:T(8,128)(2,1)S(1)}, bf16[256,512]{1,0:T(8,128)(2,1)}, u32[]{:S(2)}) copy-start(bf16[256,512]{1,0:T(8,128)(2,1)} %value_gate_ref.1) | copy-start | bytes 786436
  28.1 3.1 %copy-start.16 = (bf16[256,256]{1,0:T(8,128)(2,1)S(1)}, bf16[256,256]{1,0:T(8,128)(2,1)}, u32[]{:S(2)}) copy-start(bf16[256,256]{1,0:T(8,128)(2,1)} %query_ref.1) | copy-start | bytes 393220
  28.1 3.1 %copy-start.19 = (bf16[256,64]{0,1:T(8,128)(2,1)S(1)}, bf16[256,64]{0,1:T(8,128)(2,1)}, u32[]{:S(2)}) copy-start(bf16[256,64]{0,1:T(8,128)(2,1)} %param.34) | copy-start | bytes 98308
  31.8 1.0 %copy-start.14 = (bf16[1024,256]{1,0:T(8,128)(2,1)S(1)}, bf16[1024,256]{1,0:T(8,128)(2,1)}, u32[]{:S(2)}) copy-start(bf16[1024,256]{1,0:T(8,128)(2,1)} %down_ref.1) | copy-start | bytes 1572868
  32.8 0.9 %copy-start.17 = (bf16[256,256]{1,0:T(8,128)(2,1)S(1)}, bf16[256,256]{1,0:T(8,128)(2,1)}, u32[]{:S(2)}) copy-start(bf16[256,256]{1,0:T(8,128)(2,1)} %key_ref.1) | copy-start | bytes 393220
  33.7 0.9 %copy-start.18 = (bf16[256,256]{1,0:T(8,128)(2,1)S(1)}, bf16[256,256]{1,0:T(8,128)(2,1)}, u32[]{:S(2)}) copy-start(bf16[256,256]{1,0:T(8,128)(2,1)} %output_ref.1) | copy-start | bytes 393220
  38.7 5.9 %collective-permute-start.3 = (bf16[256,128]{1,0:T(8,128)(2,1)S(1)}, bf16[256,128]{1,0:T(8,128)(2,1)S(1)}, u32[]{:S(2)}, u32[]{:S(2)}) collective-permute-start(bf16[256,128]{1,0:T(8,128)(2,1)S(1)} %get-tuple-element.28), channel_id=1, source_target_pairs={{0,8},{1,9},{2,10},{3,11},{4,12},{5,13},{6,14},{7,15},{8,0},{9,1},... | collective-permute-start | bytes 196616 | tf_op jit(solution)/shard_map/ppermute | solution.py:510
  41.2 4.3 %collective-permute-start.4 = (bf16[256,128]{1,0:T(8,128)(2,1)S(1)}, bf16[256,128]{1,0:T(8,128)(2,1)S(1)}, u32[]{:S(2)}, u32[]{:S(2)}) collective-permute-start(bf16[256,128]{1,0:T(8,128)(2,1)S(1)} %get-tuple-element.28), channel_id=1, source_target_pairs={{0,4},{1,5},{2,6},{3,7},{4,0},{5,1},{6,2},{7,3},{8,12},{9,13},{10,... | collective-permute-start | bytes 196616 | tf_op jit(solution)/shard_map/ppermute | solution.py:510
  44.7 4.3 %collective-permute-start.5 = (bf16[256,128]{1,0:T(8,128)(2,1)S(1)}, bf16[256,128]{1,0:T(8,128)(2,1)S(1)}, u32[]{:S(2)}, u32[]{:S(2)}) collective-permute-start(bf16[256,128]{1,0:T(8,128)(2,1)S(1)} %collective-permute-done.3), channel_id=1, source_target_pairs={{0,4},{1,5},{2,6},{3,7},{4,0},{5,1},{6,2},{7,3},{8,12},{9,13},{10,... | collective-permute-start | bytes 196616 | tf_op jit(solution)/shard_map/ppermute | solution.py:510
  49.0 6.4 %collective-permute-start.6 = (bf16[4,256,128]{2,1,0:T(8,128)(2,1)S(1)}, bf16[4,256,128]{2,1,0:T(8,128)(2,1)S(1)}, u32[]{:S(2)}, u32[]{:S(2)}) collective-permute-start(bf16[4,256,128]{2,1,0:T(8,128)(2,1)S(1)} %pad_maximum_fusion.1.line_ref), channel_id=1, source_target_pairs={{0,2},{1,3},{2,0},{3,1},{4,6},{5,7},{6,4},{7,5},{8,10},{9,11},{10,... | collective-permute-start | bytes 786440 | tf_op jit(solution)/shard_map/ppermute | solution.py:510
  50.3 5.7 %collective-permute-start.7 = (bf16[4,128,128]{2,1,0:T(8,128)(2,1)}, bf16[4,128,128]{2,1,0:T(8,128)(2,1)S(1)}, u32[]{:S(2)}, u32[]{:S(2)}) collective-permute-start(bf16[4,128,128]{2,1,0:T(8,128)(2,1)} %pad_maximum_fusion.3), channel_id=1, source_target_pairs={{0,1},{1,0},{2,3},{3,2},{4,5},{5,4},{6,7},{7,6},{8,9},{9,8},{10,11... | collective-permute-start | bytes 393224 | tf_op jit(solution)/shard_map/ppermute | solution.py:510
  56.1 1.6 %collective-permute-start.8 = (bf16[4,128,128]{2,1,0:T(8,128)(2,1)}, bf16[4,128,128]{2,1,0:T(8,128)(2,1)S(1)}, u32[]{:S(2)}, u32[]{:S(2)}) collective-permute-start(bf16[4,128,128]{2,1,0:T(8,128)(2,1)} %slice.23), channel_id=1, source_target_pairs={{0,1},{1,0},{2,3},{3,2},{4,5},{5,4},{6,7},{7,6},{8,9},{9,8},{10,11... | collective-permute-start | bytes 393224 | tf_op jit(solution)/shard_map/ppermute | solution.py:510
  62.6 2.0 %collective-permute-start.9 = (bf16[2048,128]{1,0:T(8,128)(2,1)S(1)}, bf16[2048,128]{1,0:T(8,128)(2,1)S(1)}, u32[]{:S(2)}, u32[]{:S(2)}) collective-permute-start(bf16[2048,128]{1,0:T(8,128)(2,1)S(1)} %get-tuple-element.36.right_own_ref), channel_id=1, source_target_pairs={{0,1},{1,0},{2,3},{3,2},{4,5},{5,4},{6,7},{7,6},{8,9},{9,8},{10,11... | collective-permute-start | bytes 1572872 | tf_op jit(solution)/shard_map/ppermute | solution.py:510
  72.0 1.4 %collective-permute-start.10 = (f32[2,128,128]{2,1,0:T(8,128)S(1)}, f32[2,128,128]{2,1,0:T(8,128)S(1)}, u32[]{:S(2)}, u32[]{:S(2)}) collective-permute-start(f32[2,128,128]{2,1,0:T(8,128)S(1)} %get-tuple-element.39), channel_id=1, source_target_pairs={{0,1},{1,0},{2,3},{3,2},{4,5},{5,4},{6,7},{7,6},{8,9},{9,8},{10,11... | collective-permute-start | bytes 393224 | tf_op jit(solution)/shard_map/ppermute | solution.py:510
  (3 other events, 2.0 us)

commit v7 on v6

--- a/solution.py
+++ b/solution.py
@@ -133,8 +133,8 @@
         for part, device in (
             (line_ref[m, 128:256, :], place ^ OFFSETS[m]),
             (across_ref[m, 128:256, :], place ^ OFFSETS[m] ^ 2),
-            (core_line_ref[m], place ^ OFFSETS[m] ^ 1),
-            (core_across_ref[m], place ^ OFFSETS[m] ^ 3),
+            (core_line_ref[m, 128:256, :], place ^ OFFSETS[m] ^ 1),
+            (core_across_ref[m, 128:256, :], place ^ OFFSETS[m] ^ 3),
         ):
             wide_ref[pl.ds(pl.multiple_of(device * 128, 128), 128), :] = part.astype(jnp.float32)
     for d in range(0, CO, 2):
@@ -385,11 +385,14 @@
 def weights_kernel(
     bins_ref,
     table_ref,
+    own_pair_ref,
+    far_pair_ref,
     *rest,
 ):
-    sources, (embedding_out, turned_out, wide_out, ready_out) = rest[:9], rest[9:13]
+    sources, (embedding_out, turned_out, wide_out, both_out) = rest[:9], rest[9:13]
     landed, (table_wide_ref, mean_wide_ref, arrived) = rest[13:22], rest[22:]
-    ready_out[...] = jnp.zeros_like(ready_out)
+    both_out[0] = own_pair_ref[...]
+    both_out[1] = far_pair_ref[...]
     copies = [
         pltpu.make_async_copy(sources[k], landed[k], arrived.at[k]) for k in range(len(sources))
     ]
@@ -453,13 +456,21 @@
     up_ref,
     down_ref,
     outer_ref,
-    ready_ref,
     result_ref,
     parts_ref,
     wide_ref,
     attended_ref,
     final_ref,
+    *landed,
 ):
+    arrived = landed[-1]
+    sources = (query_ref, key_ref, value_gate_ref, output_ref, up_ref, down_ref)
+    copies = [
+        pltpu.make_async_copy(source, landed[k], arrived.at[k]) for k, source in enumerate(sources)
+    ]
+    for copy in copies:
+        copy.start()
+    query_ref, key_ref, value_gate_ref, output_ref, up_ref, down_ref = landed[:6]
     for p in range(16):
         block = blocks_ref[p].astype(jnp.float32)
         for i in range(4):
@@ -476,6 +487,8 @@
 
     heads = by_head(one)
     normed = normalize_rows(wide_ref[...])
+    for copy in copies[:3]:
+        copy.wait()
     query = (mix(normed, query_ref[...]) * HEAD_SIZE ** (-0.5)).astype(jnp.bfloat16)
     key = mix(normed, key_ref[...]).astype(jnp.bfloat16)
     value_gate = mix(normed, value_gate_ref[...])
@@ -490,6 +503,8 @@
         raised = jnp.concatenate(raised, axis=1)
         attended_ref[rows, :] = mix(raised, by_head(value[rows])) / mix(raised, heads)
     gated = (gate_curve(value_gate[:, width:]) * attended_ref[...]).astype(jnp.bfloat16)
+    for copy in copies[3:]:
+        copy.wait()
     current = wide_ref[...] + mix(gated, output_ref[...])
     hidden = jnp.maximum(mix(normalize_rows(current), up_ref[...]), 0.0).astype(jnp.bfloat16)
     final = (current + mix(hidden, down_ref[...])).astype(jnp.bfloat16).astype(jnp.float32)
@@ -552,19 +567,16 @@
             pltpu.VMEM((1024, LANES), jnp.float32),
             pltpu.SemaphoreType.DMA((2,)),
         ],
-        compiler_params=limit(16),
+        compiler_params=limit(56),
         name="rows_by_device",
     )(alignment_input, pair_state_input)
     blocks = lax.all_to_all(blocks, "dap", split_axis=0, concat_axis=0, tiled=True)
 
     pair_far = exchange(own_pair, 8)
-    pair_near = exchange(jnp.stack([own_pair, pair_far]), 4)
-    pair_line = jnp.concatenate([jnp.stack([own_pair, pair_far]), pair_near])
-
-    embedding, turned_weights, wide_weights, ready = pl.pallas_call(
+    embedding, turned_weights, wide_weights, pair_both = pl.pallas_call(
         weights_kernel,
-        out_shape=[array(32, width, LANES), array(2048, LANES), array(384, 512), wide(8, LANES)],
-        in_specs=[vmem] * 2 + [hbm] * 9,
+        out_shape=[array(32, width, LANES), array(2048, LANES), array(384, 512), array(2, 2, width, LANES)],
+        in_specs=[vmem] * 4 + [hbm] * 9,
         out_specs=[vmem] * 4,
         scratch_shapes=[pltpu.VMEM(w.shape, jnp.bfloat16) for w in pair_weights]
         + [
@@ -572,7 +584,7 @@
             pltpu.VMEM((1024, LANES), jnp.float32),
             pltpu.SemaphoreType.DMA((9,)),
         ],
-        compiler_params=limit(24),
+        compiler_params=limit(56),
         cost_estimate=pl.CostEstimate(
             flops=200_000_000, bytes_accessed=8_000_000, transcendentals=0
         ),
@@ -580,22 +592,37 @@
     )(
         lanes_order(bin_all).reshape(32, LANES),
         relative_position_table,
+        own_pair,
+        pair_far,
         *pair_weights,
     )
+    pair_line = jnp.concatenate([pair_both, exchange(pair_both, 4)])
     blocks, pair_line = lax.optimization_barrier((blocks, pair_line))
     pair_across = exchange(pair_line, 2)
 
     result, parts = pl.pallas_call(
         msa_kernel,
         out_shape=(array(512, channels), array(256, LANES)),
-        in_specs=[vmem] * 10,
+        in_specs=[vmem] * 2 + [hbm] * 6 + [vmem],
         out_specs=(vmem, vmem),
         scratch_shapes=[
             pltpu.VMEM((512, channels), jnp.float32),
             pltpu.VMEM((512, channels), jnp.float32),
             pltpu.VMEM((1024, LANES), jnp.float32),
-        ],
-        compiler_params=limit(32),
+        ]
+        + [
+            pltpu.VMEM(w.shape, jnp.bfloat16)
+            for w in (
+                column_query_weight,
+                column_key_weight,
+                column_value_gate_weight,
+                column_output_weight,
+                alignment_transition_up,
+                alignment_transition_down,
+            )
+        ]
+        + [pltpu.SemaphoreType.DMA((6,))],
+        compiler_params=limit(56),
         cost_estimate=pl.CostEstimate(
             flops=2_000_000_000, bytes_accessed=10_000_000, transcendentals=1_000_000
         ),
@@ -610,15 +637,13 @@
         alignment_transition_up,
         alignment_transition_down,
         outer_input_weight.T,
-        ready,
-    )
-    parts, pair_across = lax.optimization_barrier((parts, pair_across))
+    )
     far = exchange(parts, 8)
     near = [exchange(parts, 4), exchange(far, 4)]
     line = jnp.stack([parts, far] + near)
     across = exchange(line, 2)
-    core_line = exchange(jnp.stack([part[128:256] for part in (parts, far, *near)]), 1)
-    core_across = exchange(across[:, 128:256, :], 1)
+    core_line = exchange(line, 1)
+    core_across = exchange(across, 1)
 
     slabs = (16, 128, LANES)
     tall = (16 * 128, LANES)

time: 75.7 us -> 81.2 us (1.073)
  waiting for transfers between devices: 23 us -> 30.5 us
  local copies, waits for them, and re-layouts: 11.5 us -> 4.97 us
  Pallas kernels: 22.4 us -> 26.8 us
  other arithmetic: 1.47 us -> 2.61 us
    ppermute x11, waiting for transfers between devices: 22.6 us -> 30.5 us  [exchange(): return lax.ppermute(values, 'dap', [(q, q ^ offset) for q in range(pieces)])]
    unnamed x46 -> x22, local copies, waits for them, and re-layouts: 9.61 us -> 3.15 us
    ppermute x11, starting transfers between devices: 11.7 us -> 7.53 us  [exchange(): return lax.ppermute(values, 'dap', [(q, q ^ offset) for q in range(pieces)])]
    all_to_all x1, starting transfers between devices: 4.04 us -> 7.53 us  [whole_block(): lax.all_to_all(blocks, 'dap', split_axis=0, concat_axis=0, tiled=True)]
    pallas_call x1, Pallas kernels: 4.09 us -> 6.86 us  [whole_block(): pl.pallas_call(msa_kernel, out_shape=(array(512, channels), array(256, LA...]
    pallas_call x1, Pallas kernels: 3.03 us -> 3.98 us  [whole_block(): pl.pallas_call(weights_kernel, out_shape=[array(32, width, LANES), array(...]
    concatenate x1, other arithmetic: 0.03 us -> 0.93 us  [whole_block(): pair_line = jnp.concatenate([pair_both, exchange(pair_both, 4)])]
    another operation x1, other arithmetic: 0.04 us -> 0.87 us  [whole_block(): line = jnp.stack([parts, far] + near)]
  transfers between devices with their start and end apart: 12 -> 12, of which waited for: 9 -> 8; matrix products, arithmetic and copies ran while one was open for 4% -> 4% of each run, Pallas kernels for 9% -> 5%
where the time goes in v7:
time: 81.2 us; the launch traced here: 80.8 us
  waiting for transfers between devices  30.5 us (38%)
  Pallas kernels  26.8 us (33%)
  starting transfers between devices  15.1 us (19%)
  local copies, waits for them, and re-layouts  4.97 us (6%)
  other arithmetic  2.61 us (3%)
  between operations  0.83 us (1%)
    ppermute x11, waiting for transfers between devices, exchange(): return lax.ppermute(values, 'dap', [(q, q ^ offset) for q in range(pieces)])  30.5 us
    all_to_all x1, starting transfers between devices, whole_block(): lax.all_to_all(blocks, 'dap', split_axis=0, concat_axis=0, tiled=True)  7.53 us
    ppermute x11, starting transfers between devices, exchange(): return lax.ppermute(values, 'dap', [(q, q ^ offset) for q in range(pieces)])  7.53 us
    pallas_call x1, Pallas kernels, whole_block(): pl.pallas_call(triangle_kernel, out_shape=[wide(2, 128, LANES)] * 3, in_s...  7.44 us
    pallas_call x1, Pallas kernels, whole_block(): pl.pallas_call(msa_kernel, out_shape=(array(512, channels), array(256, LA...  6.86 us
    pallas_call x1, Pallas kernels, whole_block(): pl.pallas_call(start_kernel, out_shape=[wide(*slabs), wide(*tall), wide(*...  4.91 us
    pallas_call x1, Pallas kernels, whole_block(): pl.pallas_call(weights_kernel, out_shape=[array(32, width, LANES), array(...  3.98 us
    unnamed x22, local copies, waits for them, and re-layouts  3.15 us
  transfers between devices with their start and end apart: 12, of which 8 were waited for; matrix products, arithmetic and copies ran while one was open for 4% of the time, Pallas kernels for 5%

profile of v7, /device:TPU:0, one launch (start us, length us, event | category | flops | bytes accessed | tf_op | source)
XLA Modules:
  0.0 80.8 jit_solution(4355692914202264092)
XLA Ops:
  0.6 2.1 %rows_by_device.1 = (bf16[16,32,256]{2,1,0:T(8,128)(2,1)}, bf16[2,128,128]{2,1,0:T(8,128)(2,1)}) custom-call(bf16[8,64,256]{2,1,0:T(8,128)(2,1)} %rows_source.1, bf16[4,64,128]{2,1,0:T(8,128)(2,1)} %pair_source.1), custom_call_target="tpu_custom_call" | custom-call | tf_op jit(solution)/shard_map/rows_by_device/pallas_call | solution.py:559
  2.7 7.5 %all-to-all-start = ((bf16[16,32,256]{2,1,0:T(8,128)(2,1)}), bf16[16,32,256]{2,1,0:T(8,128)(2,1)S(1)}, u32[]{:S(2)}, u32[]{:S(2)}) async-start(bf16[16,32,256]{2,1,0:T(8,128)(2,1)} %get-tuple-element.19), calls=%async_computation | async-start | bytes 524288 | tf_op jit(solution)/shard_map/all_to_all | solution.py:573
  10.3 2.9 %collective-permute-start = (bf16[2,128,128]{2,1,0:T(8,128)(2,1)S(1)}, bf16[2,128,128]{2,1,0:T(8,128)(2,1)S(1)}, u32[]{:S(2)}, u32[]{:S(2)}) collective-permute-start(bf16[2,128,128]{2,1,0:T(8,128)(2,1)S(1)} %copy-done.6), channel_id=1, source_target_pairs={{0,8},{1,9},{2,10},{3,11},{4,12},{5,13},{6,14},{7,15},{8,0},{9,1},... | collective-permute-start | bytes 196616 | tf_op jit(solution)/shard_map/ppermute | solution.py:525
  13.4 0.6 copy-done.9
  14.1 0.2 compare_select_fusion
  14.4 0.7 select_n.11.bins_ref
  15.1 7.7 %collective-permute-done.far_pair_ref = bf16[2,128,128]{2,1,0:T(8,128)(2,1)S(1)} collective-permute-done((bf16[2,128,128]{2,1,0:T(8,128)(2,1)S(1)}, bf16[2,128,128]{2,1,0:T(8,128)(2,1)S(1)}, u32[]{:S(2)}, u32[]{:S(2)}) %collective-permute-start) | collective-permute-done | bytes 65568 | tf_op jit(solution)/shard_map/ppermute | solution.py:525
  22.7 0.6 copy-done.7
  23.4 4.0 %turn_weights.1 = (bf16[32,128,128]{2,1,0:T(8,128)(2,1)}, bf16[2048,128]{1,0:T(8,128)(2,1)}, bf16[384,512]{1,0:T(8,128)(2,1)}, bf16[2,2,128,128]{3,2,1,0:T(8,128)(2,1)}) custom-call(s32[32,128]{1,0:T(8,128)} %select_n.11.bins_ref, bf16[66,128]{1,0:T(8,128)(2,1)} %table_ref.1, bf16[2,128,128]{2,1,0:T(8,128)(2,1)} %get-tuple-element.20.own_pair_ref, ...), custom_call_target="tpu_custom_call" | custom-call | flops 200000000 | bytes 8000000 | tf_op jit(solution)/shard_map/turn_weights/pallas_call | solution.py:576
  27.4 0.6 copy-done.10
  28.0 0.6 fusion.live_ref
  28.6 4.1 %collective-permute-done.1 = bf16[2,2,128,128]{3,2,1,0:T(8,128)(2,1)S(1)} collective-permute-done((bf16[2,2,128,128]{3,2,1,0:T(8,128)(2,1)}, bf16[2,2,128,128]{3,2,1,0:T(8,128)(2,1)S(1)}, u32[]{:S(2)}, u32[]{:S(2)}) %collective-permute-start.1) | collective-permute-done | bytes 131104 | tf_op jit(solution)/shard_map/ppermute | solution.py:525
  32.7 0.9 %pad_maximum_fusion.pair_line_ref = bf16[4,2,128,128]{3,2,1,0:T(8,128)(2,1)S(1)} fusion(bf16[2,2,128,128]{3,2,1,0:T(8,128)(2,1)S(1)} %collective-permute-done.1, bf16[2,2,128,128]{3,2,1,0:T(8,128)(2,1)} %get-tuple-element.21), kind=kLoop, calls=%fused_computation | loop fusion | flops 131072 | bytes 524288 | tf_op jit(solution)/shard_map/concatenate | solution.py:599
  33.6 0.7 copy-done.5
  34.3 6.9 %msa_whole.1 = (bf16[512,256]{1,0:T(8,128)(2,1)}, bf16[256,128]{1,0:T(8,128)(2,1)}) custom-call(f32[1,128]{1,0:T(1,128)} %fusion.live_ref, bf16[16,32,256]{2,1,0:T(8,128)(2,1)} %copy-done.5, bf16[256,256]{1,0:T(8,128)(2,1)} %query_ref.1, bf16[256,256]{1,0:T(8,128)(2,1)} %key_ref.1, bf16[256,512]{1,0:T(8,128)(2,1)} %value_gate_ref.1, ...), custom_call_target="tpu_custom_call" | custom-call | flops 2000000000 | bytes 10000000 | tf_op jit(solution)/shard_map/msa_whole/pallas_call | solution.py:603
  41.2 0.5 collective-permute-start.2
  41.7 1.7 %collective-permute-start.3 = (bf16[256,128]{1,0:T(8,128)(2,1)}, bf16[256,128]{1,0:T(8,128)(2,1)S(1)}, u32[]{:S(2)}, u32[]{:S(2)}) collective-permute-start(bf16[256,128]{1,0:T(8,128)(2,1)} %get-tuple-element.24), channel_id=1, source_target_pairs={{0,4},{1,5},{2,6},{3,7},{4,0},{5,1},{6,2},{7,3},{8,12},{9,13},{10,... | collective-permute-start | bytes 196616 | tf_op jit(solution)/shard_map/ppermute | solution.py:525
  43.4 3.7 %collective-permute-done.2 = bf16[256,128]{1,0:T(8,128)(2,1)S(1)} collective-permute-done((bf16[256,128]{1,0:T(8,128)(2,1)}, bf16[256,128]{1,0:T(8,128)(2,1)S(1)}, u32[]{:S(2)}, u32[]{:S(2)}) %collective-permute-start.2) | collective-permute-done | bytes 65568 | tf_op jit(solution)/shard_map/ppermute | solution.py:525
  47.1 4.3 %collective-permute-done.4 = bf16[256,128]{1,0:T(8,128)(2,1)S(1)} collective-permute-done((bf16[256,128]{1,0:T(8,128)(2,1)S(1)}, bf16[256,128]{1,0:T(8,128)(2,1)S(1)}, u32[]{:S(2)}, u32[]{:S(2)}) %collective-permute-start.4) | collective-permute-done | bytes 65568 | tf_op jit(solution)/shard_map/ppermute | solution.py:525
  51.3 0.9 %pad_maximum_fusion.1.line_ref = bf16[4,256,128]{2,1,0:T(8,128)(2,1)S(1)} fusion(bf16[1,256,128]{2,1,0:T(8,128)(2,1)S(1)} %bitcast.16, bf16[1,256,128]{2,1,0:T(8,128)(2,1)S(1)} %bitcast.15, bf16[1,256,128]{2,1,0:T(8,128)(2,1)S(1)} %bitcast.14, bf16[1,256,128]{2,1,0:T(8,128)(2,1)} %bitcast.13), kind=kLoop, calls=%fused_computation.1 | loop fusion | flops 393216 | bytes 524288 | tf_op jit(solution)/shard_map/stack | solution.py:643
  52.2 1.5 %collective-permute-start.5 = (bf16[4,256,128]{2,1,0:T(8,128)(2,1)S(1)}, bf16[4,256,128]{2,1,0:T(8,128)(2,1)S(1)}, u32[]{:S(2)}, u32[]{:S(2)}) collective-permute-start(bf16[4,256,128]{2,1,0:T(8,128)(2,1)S(1)} %pad_maximum_fusion.1.line_ref), channel_id=1, source_target_pairs={{0,2},{1,3},{2,0},{3,1},{4,6},{5,7},{6,4},{7,5},{8,10},{9,11},{10,... | collective-permute-start | bytes 786440 | tf_op jit(solution)/shard_map/ppermute | solution.py:525
  53.8 0.6 collective-permute-start.8
  54.3 5.7 %collective-permute-done.5.across_ref = bf16[4,256,128]{2,1,0:T(8,128)(2,1)S(1)} collective-permute-done((bf16[4,256,128]{2,1,0:T(8,128)(2,1)S(1)}, bf16[4,256,128]{2,1,0:T(8,128)(2,1)S(1)}, u32[]{:S(2)}, u32[]{:S(2)}) %collective-permute-start.5) | collective-permute-done | bytes 262176 | tf_op jit(solution)/shard_map/ppermute | solution.py:525
  60.0 2.8 %collective-permute-done.8.pair_across_ref = bf16[4,2,128,128]{3,2,1,0:T(8,128)(2,1)S(1)} collective-permute-done((bf16[4,2,128,128]{3,2,1,0:T(8,128)(2,1)S(1)}, bf16[4,2,128,128]{3,2,1,0:T(8,128)(2,1)S(1)}, u32[]{:S(2)}, u32[]{:S(2)}) %collective-permute-start.8) | collective-permute-done | bytes 262176 | tf_op jit(solution)/shard_map/ppermute | solution.py:525
  62.9 0.6 copy-done.3
  63.5 4.9 %pair_start.1 = (f32[16,128,128]{2,1,0:T(8,128)S(1)}, f32[2048,128]{1,0:T(8,128)S(1)}, f32[16,128,128]{2,1,0:T(8,128)S(1)}, bf16[2048,128]{1,0:T(8,128)(2,1)S(1)}) custom-call(s32[1]{0:T(128)} %bitcast.4.place_ref, f32[1,128]{1,0:T(1,128)S(1)} %copy-done.3, bf16[4,256,128]{2,1,0:T(8,128)(2,1)S(1)} %pad_maximum_fusion.1.line_ref, ...), custom_call_target="tpu_custom_call" | custom-call | tf_op jit(solution)/shard_map/pair_start/pallas_call | solution.py:650
  68.5 1.9 %collective-permute-done.9.right_other_ref = bf16[2048,128]{1,0:T(8,128)(2,1)S(1)} collective-permute-done((bf16[2048,128]{1,0:T(8,128)(2,1)S(1)}, bf16[2048,128]{1,0:T(8,128)(2,1)S(1)}, u32[]{:S(2)}, u32[]{:S(2)}) %collective-permute-start.9) | collective-permute-done | bytes 524320 | tf_op jit(solution)/shard_map/ppermute | solution.py:525
  70.4 7.4 %pair_triangles.1 = (f32[2,128,128]{2,1,0:T(8,128)S(1)}, f32[2,128,128]{2,1,0:T(8,128)S(1)}, f32[2,128,128]{2,1,0:T(8,128)S(1)}) custom-call(s32[1]{0:T(128)} %bitcast.4.place_ref, f32[16,128,128]{2,1,0:T(8,128)S(1)} %get-tuple-element.29.pair_mid_ref, f32[2048,128]{1,0:T(8,128)S(1)} %get-tuple-element.30.left_ref, ...), custom_call_target="tpu_custom_call" | custom-call | tf_op jit(solution)/shard_map/pair_triangles/pallas_call | solution.py:676
  77.9 0.2 collective-permute-start.10
  78.1 0.8 reshape.59
  78.8 0.4 collective-permute-done.10.other_part_ref
  79.3 1.5 %pair_finish.1 = bf16[256,128]{1,0:T(8,128)(2,1)} custom-call(f32[2,128,128]{2,1,0:T(8,128)S(1)} %get-tuple-element.33.own_pair_ref, f32[2,128,128]{2,1,0:T(8,128)S(1)} %get-tuple-element.34.own_part_ref, f32[2,128,128]{2,1,0:T(8,128)S(1)} %collective-permute-done.10.other_part_ref, bf16[2048,128]{1,0:T(8,128)(2,1)S(1)} %copy-done, ...), custom_call_target="tpu_custom_call" | custom-call | tf_op jit(solution)/shard_map/pair_finish/pallas_call | solution.py:692
  (30 shorter events, 0.5 us)
Async XLA Ops:
  2.7 7.6 %copy-start.6 = (bf16[2,128,128]{2,1,0:T(8,128)(2,1)S(1)}, bf16[2,128,128]{2,1,0:T(8,128)(2,1)}, u32[]{:S(2)}) copy-start(bf16[2,128,128]{2,1,0:T(8,128)(2,1)} %get-tuple-element.20.own_pair_ref) | copy-start | bytes 196612
  2.7 30.9 %all-to-all-start = ((bf16[16,32,256]{2,1,0:T(8,128)(2,1)}), bf16[16,32,256]{2,1,0:T(8,128)(2,1)S(1)}, u32[]{:S(2)}, u32[]{:S(2)}) async-start(bf16[16,32,256]{2,1,0:T(8,128)(2,1)} %get-tuple-element.19), calls=%async_computation | async-start | bytes 524288 | tf_op jit(solution)/shard_map/all_to_all | solution.py:573
  10.3 2.9 %copy-start.8 = (s32[64]{0:T(128)S(1)}, s32[64]{0:T(128)}, u32[]{:S(2)}) copy-start(s32[64]{0:T(128)} %param.24) | copy-start | bytes 772
  10.3 12.4 %collective-permute-start = (bf16[2,128,128]{2,1,0:T(8,128)(2,1)S(1)}, bf16[2,128,128]{2,1,0:T(8,128)(2,1)S(1)}, u32[]{:S(2)}, u32[]{:S(2)}) collective-permute-start(bf16[2,128,128]{2,1,0:T(8,128)(2,1)S(1)} %copy-done.6), channel_id=1, source_target_pairs={{0,8},{1,9},{2,10},{3,11},{4,12},{5,13},{6,14},{7,15},{8,0},{9,1},... | collective-permute-start | bytes 196616 | tf_op jit(solution)/shard_map/ppermute | solution.py:525
  13.3 0.7 copy-start.9
  22.7 0.6 copy-start.7
  27.4 0.7 copy-start.10
  27.4 5.3 %collective-permute-start.1 = (bf16[2,2,128,128]{3,2,1,0:T(8,128)(2,1)}, bf16[2,2,128,128]{3,2,1,0:T(8,128)(2,1)S(1)}, u32[]{:S(2)}, u32[]{:S(2)}) collective-permute-start(bf16[2,2,128,128]{3,2,1,0:T(8,128)(2,1)} %get-tuple-element.21), channel_id=1, source_target_pairs={{0,4},{1,5},{2,6},{3,7},{4,0},{5,1},{6,2},{7,3},{8,12},{9,13},{10,... | collective-permute-start | bytes 393224 | tf_op jit(solution)/shard_map/ppermute | solution.py:525
  33.6 0.7 copy-start.5
  34.3 28.5 %copy-start.1 = (bf16[384,512]{1,0:T(8,128)(2,1)S(1)}, bf16[384,512]{1,0:T(8,128)(2,1)}, u32[]{:S(2)}) copy-start(bf16[384,512]{1,0:T(8,128)(2,1)} %get-tuple-element.28.wide_weight_ref) | copy-start | bytes 1179652
  34.3 28.5 %copy-start.2 = (bf16[32,128,128]{2,1,0:T(8,128)(2,1)S(1)}, bf16[32,128,128]{2,1,0:T(8,128)(2,1)}, u32[]{:S(2)}) copy-start(bf16[32,128,128]{2,1,0:T(8,128)(2,1)} %get-tuple-element.26.embedding_ref) | copy-start | bytes 3145732
  41.2 21.7 %copy-start = (bf16[2048,128]{1,0:T(8,128)(2,1)S(1)}, bf16[2048,128]{1,0:T(8,128)(2,1)}, u32[]{:S(2)}) copy-start(bf16[2048,128]{1,0:T(8,128)(2,1)} %get-tuple-element.27.turned_ref) | copy-start | bytes 1572868
  41.2 5.9 %collective-permute-start.2 = (bf16[256,128]{1,0:T(8,128)(2,1)}, bf16[256,128]{1,0:T(8,128)(2,1)S(1)}, u32[]{:S(2)}, u32[]{:S(2)}) collective-permute-start(bf16[256,128]{1,0:T(8,128)(2,1)} %get-tuple-element.24), channel_id=1, source_target_pairs={{0,8},{1,9},{2,10},{3,11},{4,12},{5,13},{6,14},{7,15},{8,0},{9,1},... | collective-permute-start | bytes 196616 | tf_op jit(solution)/shard_map/ppermute | solution.py:525
  41.7 5.4 %collective-permute-start.3 = (bf16[256,128]{1,0:T(8,128)(2,1)}, bf16[256,128]{1,0:T(8,128)(2,1)S(1)}, u32[]{:S(2)}, u32[]{:S(2)}) collective-permute-start(bf16[256,128]{1,0:T(8,128)(2,1)} %get-tuple-element.24), channel_id=1, source_target_pairs={{0,4},{1,5},{2,6},{3,7},{4,0},{5,1},{6,2},{7,3},{8,12},{9,13},{10,... | collective-permute-start | bytes 196616 | tf_op jit(solution)/shard_map/ppermute | solution.py:525
  47.1 4.3 %collective-permute-start.4 = (bf16[256,128]{1,0:T(8,128)(2,1)S(1)}, bf16[256,128]{1,0:T(8,128)(2,1)S(1)}, u32[]{:S(2)}, u32[]{:S(2)}) collective-permute-start(bf16[256,128]{1,0:T(8,128)(2,1)S(1)} %collective-permute-done.2), channel_id=1, source_target_pairs={{0,4},{1,5},{2,6},{3,7},{4,0},{5,1},{6,2},{7,3},{8,12},{9,13},{10,... | collective-permute-start | bytes 196616 | tf_op jit(solution)/shard_map/ppermute | solution.py:525
  52.2 7.8 %collective-permute-start.5 = (bf16[4,256,128]{2,1,0:T(8,128)(2,1)S(1)}, bf16[4,256,128]{2,1,0:T(8,128)(2,1)S(1)}, u32[]{:S(2)}, u32[]{:S(2)}) collective-permute-start(bf16[4,256,128]{2,1,0:T(8,128)(2,1)S(1)} %pad_maximum_fusion.1.line_ref), channel_id=1, source_target_pairs={{0,2},{1,3},{2,0},{3,1},{4,6},{5,7},{6,4},{7,5},{8,10},{9,11},{10,... | collective-permute-start | bytes 786440 | tf_op jit(solution)/shard_map/ppermute | solution.py:525
  53.8 9.1 %collective-permute-start.8 = (bf16[4,2,128,128]{3,2,1,0:T(8,128)(2,1)S(1)}, bf16[4,2,128,128]{3,2,1,0:T(8,128)(2,1)S(1)}, u32[]{:S(2)}, u32[]{:S(2)}) collective-permute-start(bf16[4,2,128,128]{3,2,1,0:T(8,128)(2,1)S(1)} %pad_maximum_fusion.pair_line_ref), channel_id=1, source_target_pairs={{0,2},{1,3},{2,0},{3,1},{4,6},{5,7},{6,4},{7,5},{8,10},{9,11},{10,... | collective-permute-start | bytes 786440 | tf_op jit(solution)/shard_map/ppermute | solution.py:525
  54.3 8.5 %collective-permute-start.6 = (bf16[4,256,128]{2,1,0:T(8,128)(2,1)S(1)}, bf16[4,256,128]{2,1,0:T(8,128)(2,1)S(1)}, u32[]{:S(2)}, u32[]{:S(2)}) collective-permute-start(bf16[4,256,128]{2,1,0:T(8,128)(2,1)S(1)} %pad_maximum_fusion.1.line_ref), channel_id=1, source_target_pairs={{0,1},{1,0},{2,3},{3,2},{4,5},{5,4},{6,7},{7,6},{8,9},{9,8},{10,11... | collective-permute-start | bytes 786440 | tf_op jit(solution)/shard_map/ppermute | solution.py:525
  60.0 2.8 %collective-permute-start.7 = (bf16[4,256,128]{2,1,0:T(8,128)(2,1)S(1)}, bf16[4,256,128]{2,1,0:T(8,128)(2,1)S(1)}, u32[]{:S(2)}, u32[]{:S(2)}) collective-permute-start(bf16[4,256,128]{2,1,0:T(8,128)(2,1)S(1)} %collective-permute-done.5.across_ref), channel_id=1, source_target_pairs={{0,1},{1,0},{2,3},{3,2},{4,5},{5,4},{6,7},{7,6},{8,9},{9,8},{10,11... | collective-permute-start | bytes 786440 | tf_op jit(solution)/shard_map/ppermute | solution.py:525
  62.8 0.7 copy-start.3
  68.4 2.0 %collective-permute-start.9 = (bf16[2048,128]{1,0:T(8,128)(2,1)S(1)}, bf16[2048,128]{1,0:T(8,128)(2,1)S(1)}, u32[]{:S(2)}, u32[]{:S(2)}) collective-permute-start(bf16[2048,128]{1,0:T(8,128)(2,1)S(1)} %get-tuple-element.32.right_own_ref), channel_id=1, source_target_pairs={{0,1},{1,0},{2,3},{3,2},{4,5},{5,4},{6,7},{7,6},{8,9},{9,8},{10,11... | collective-permute-start | bytes 1572872 | tf_op jit(solution)/shard_map/ppermute | solution.py:525
  70.4 7.6 %copy-start.4 = (bf16[512,256]{1,0:T(8,128)(2,1)S(1)}, bf16[512,256]{1,0:T(8,128)(2,1)}, u32[]{:S(2)}) copy-start(bf16[512,256]{1,0:T(8,128)(2,1)} %get-tuple-element.23) | copy-start | bytes 786436
  77.9 1.4 %collective-permute-start.10 = (f32[2,128,128]{2,1,0:T(8,128)S(1)}, f32[2,128,128]{2,1,0:T(8,128)S(1)}, u32[]{:S(2)}, u32[]{:S(2)}) collective-permute-start(f32[2,128,128]{2,1,0:T(8,128)S(1)} %get-tuple-element.35), channel_id=1, source_target_pairs={{0,1},{1,0},{2,3},{3,2},{4,5},{5,4},{6,7},{7,6},{8,9},{9,8},{10,11... | collective-permute-start | bytes 393224 | tf_op jit(solution)/shard_map/ppermute | solution.py:525

commit v8 on v6

--- a/solution.py
+++ b/solution.py
@@ -96,47 +96,57 @@
     return straight + pltpu.roll(crossed, LANES // 2, 1)
 
 
-def turned(ref, name):
-    first, last = TURNED[name]
-    return ref[first:last, :]
-
-
-OFFSETS = (0, 8, 4, 12)
-
-
-def start_kernel(
-    place_ref,
-    live_ref,
-    line_ref,
-    across_ref,
-    core_line_ref,
-    core_across_ref,
-    pair_line_ref,
-    pair_across_ref,
-    embedding_ref,
-    turned_ref,
-    wide_weight_ref,
-    pair_mid_ref,
-    left_ref,
-    gating_ref,
-    right_ref,
-    wide_ref,
-    right_cols_ref,
-    *stack_refs,
-):
+def transpose_blocks(ref):
+    rows, columns = ref.shape
+    return jnp.concatenate(
+        [
+            jnp.concatenate(
+                [
+                    ref[a : a + LANES, b : b + LANES].astype(jnp.float32).T.astype(jnp.bfloat16)
+                    for a in range(0, rows, LANES)
+                ],
+                axis=1,
+            )
+            for b in range(0, columns, LANES)
+        ],
+        axis=0,
+    )
+
+
+def start_copies(sources, landed, arrived):
+    copies = [
+        pltpu.make_async_copy(source, landed[k], arrived.at[k]) for k, source in enumerate(sources)
+    ]
+    for copy in copies:
+        copy.start()
+    return copies
+
+
+FIRSTS = (0, 4, 2, 6)
+
+
+def start_kernel(place_ref, live_ref, bins_ref, table_ref, *rest):
+    part_refs, core_refs, pair_refs, sources = rest[:4], rest[4:8], rest[8:12], rest[12:15]
+    pair_mid_ref, left_ref, gating_ref, right_ref = rest[15:19]
+    wide_ref, right_cols_ref, mean_wide_ref, mean_weight_ref, table_wide_ref = rest[19:24]
+    stack_refs, landed, arrived = rest[24:26], rest[26:29], rest[29]
+    copies = start_copies(sources, landed, arrived)
     place = place_ref[0]
     inverse_live = 1.0 / jnp.sum(live_ref[...], axis=1, keepdims=True)
     half = LANES // 2
+    channel = lax.broadcasted_iota(jnp.int32, (LANES, LANES), 0)
+    table_wide_ref[...] = jnp.zeros_like(table_wide_ref)
+    table_wide_ref[0:NBINS, :] = table_ref[...].astype(jnp.float32)
+    table = table_wide_ref[...].T.astype(jnp.bfloat16)
     low_half = lax.broadcasted_iota(jnp.int32, (LANES, LANES), 1) < half
 
-    for m in range(4):
-        for part, device in (
-            (line_ref[m, 128:256, :], place ^ OFFSETS[m]),
-            (across_ref[m, 128:256, :], place ^ OFFSETS[m] ^ 2),
-            (core_line_ref[m], place ^ OFFSETS[m] ^ 1),
-            (core_across_ref[m], place ^ OFFSETS[m] ^ 3),
-        ):
-            wide_ref[pl.ds(pl.multiple_of(device * 128, 128), 128), :] = part.astype(jnp.float32)
+    for g in range(4):
+        for m in range(2):
+            device = place ^ FIRSTS[g] ^ (8 * m)
+            for part, owner in ((part_refs[g], device), (core_refs[g], device ^ 1)):
+                wide_ref[pl.ds(pl.multiple_of(owner * 128, 128), 128), :] = part[
+                    m, 128:256, :
+                ].astype(jnp.float32)
     for d in range(0, CO, 2):
         rows = [
             wide_ref[pl.ds(par * CO + d + e, 32, stride=2 * CO), :]
@@ -147,41 +157,57 @@
             jnp.concatenate(rows, axis=0).T.astype(jnp.bfloat16)
         )
 
+    for copy in copies:
+        copy.wait()
+    mean_wide_ref[...] = landed[0][...].astype(jnp.float32)
+    for e in range(2):
+        for block in range(4):
+            rows = [
+                mean_wide_ref[pl.ds(2 * (4 * block + k) + e, CO, stride=CO), :] for k in range(4)
+            ]
+            mean_weight_ref[e * LANES : (e + 1) * LANES, block * LANES : (block + 1) * LANES] = (
+                jnp.concatenate(rows, axis=0).T.astype(jnp.bfloat16)
+            )
+    out_mix = transpose_blocks(landed[1])
+    out_gate = transpose_blocks(landed[2])
+
     for g in range(4):
-        parts_ref = (line_ref, across_ref)[g // 2]
-        pair_ref = (pair_line_ref, pair_across_ref)[g // 2]
         stack_ref = stack_refs[g % 2]
-        first = 2 * (g % 2)
-        left_rows = parts_ref[first : first + 2, 0:128, :].reshape(256, LANES)
+        left_rows = part_refs[g][:, 0:128, :].reshape(256, LANES)
         outer = mix(left_rows, right_cols_ref[...]).astype(jnp.bfloat16)
         for i in range(8):
             for d in range(16):
                 stack_ref[d * 32 : (d + 1) * 32, i * LANES : (i + 1) * LANES] = outer[
                     i * 32 : (i + 1) * 32, d * LANES : (d + 1) * LANES
                 ]
-        mixed = mix(wide_weight_ref[0:256, :], stack_ref[...])
+        mixed = mix(mean_weight_ref[...], stack_ref[...])
         slabs = []
         places = []
+        devices = [place ^ FIRSTS[g] ^ (8 * m) for m in range(2)]
+        one_hot = [
+            (channel == bins_ref[pl.ds(2 * devices[q // 2] + q % 2, 1), :]).astype(jnp.float32)
+            for q in range(4)
+        ]
+        embedding = mix(table, jnp.concatenate(one_hot, axis=1).astype(jnp.bfloat16))
         for q in range(4):
-            m = first + q // 2
-            device = place ^ OFFSETS[m] ^ (2 * (g // 2))
+            device = devices[q // 2]
             here = 2 * (device // 2) + q % 2
             even = slice(2 * q * LANES, (2 * q + 1) * LANES)
             odd = slice((2 * q + 1) * LANES, (2 * q + 2) * LANES)
             outer_mean = fold_halves(
                 mixed[0:128, even], mixed[0:128, odd], mixed[128:256, even], mixed[128:256, odd], low_half
             )
-            start = pair_ref[m, q % 2].astype(jnp.float32)
-            start = start + embedding_ref[2 * device + q % 2].astype(jnp.float32)
+            start = pair_refs[g][q // 2, q % 2].astype(jnp.float32)
+            start = start + embedding[:, q * LANES : (q + 1) * LANES]
             slab = start + outer_mean * inverse_live
             pair_mid_ref[here] = slab
             slabs.append(normalize_channels(slab))
             places.append(here)
         normed = jnp.concatenate(slabs, axis=1)
-        combined = mix(turned(turned_ref, "out_mix"), normed)
+        combined = mix(out_mix, normed)
         left = gate_curve(combined[128:256]) * combined[0:128]
         right = gate_curve(combined[384:512]) * combined[256:384]
-        gating = gate_curve(mix(turned(turned_ref, "out_gate"), normed))
+        gating = gate_curve(mix(out_gate, normed))
         for q in range(4):
             lanes = slice(q * LANES, (q + 1) * LANES)
             rows = pl.ds(pl.multiple_of(places[q] * 128, 128), 128)
@@ -197,17 +223,13 @@
     gating_ref,
     right_own_ref,
     right_other_ref,
-    turned_ref,
-    own_pair_ref,
-    own_part_ref,
-    other_part_ref,
-    right_ref,
-    product_ref,
-    pair_now_ref,
-    chosen_ref,
-    own_left_ref,
-    own_product_ref,
+    *rest,
 ):
+    sources, (own_pair_ref, own_part_ref, other_part_ref) = rest[:6], rest[6:9]
+    narrow_ref, wide_out_ref = rest[9:11]
+    right_ref, product_ref, pair_now_ref, chosen_ref, own_left_ref, own_product_ref = rest[11:17]
+    landed, arrived = rest[17:23], rest[23]
+    copies = start_copies(sources, landed, arrived)
     place = place_ref[0]
     core = place % 2
     half = LANES // 2
@@ -241,6 +263,15 @@
 
     lax.fori_loop(0, 4, outgoing_channels, 0)
 
+    for copy in copies:
+        copy.wait()
+    out_final = transpose_blocks(landed[0])
+    in_mix = transpose_blocks(landed[1])
+    narrow_ref[0:128, :] = transpose_blocks(landed[3])
+    narrow_ref[128:256, :] = transpose_blocks(landed[2])
+    narrow_ref[256:768, :] = transpose_blocks(landed[4])
+    wide_out_ref[...] = transpose_blocks(landed[5])
+
     column = lax.broadcasted_iota(jnp.int32, (1, 256), 1)
     which = column // 16
     residue = which % 4
@@ -253,7 +284,7 @@
             normalize_channels(product_ref[(4 * g + q) * 128 : (4 * g + q + 1) * 128, :])
             for q in range(4)
         ]
-        finished = mix(turned(turned_ref, "out_final"), jnp.concatenate(products, axis=1))
+        finished = mix(out_final, jnp.concatenate(products, axis=1))
         slabs = []
         picks = []
         for q in range(4):
@@ -270,7 +301,7 @@
             chosen_ref[...] += chosen
         else:
             chosen_ref[...] = chosen
-        combined = mix(turned(turned_ref, "in_mix")[256:512, :], normed)
+        combined = mix(in_mix[256:512], normed)
         right = gate_curve(combined[128:256]) * combined[0:128]
         for q in range(4):
             right_ref[(4 * g + q) * 128 : (4 * g + q + 1) * 128, :] = right[
@@ -279,7 +310,7 @@
     for t in range(2):
         own_pair_ref[t] = pair_now_ref[2 * (place // 2) + t]
 
-    combined = mix(turned(turned_ref, "in_mix")[0:256, :], chosen_ref[...].astype(jnp.bfloat16))
+    combined = mix(in_mix[0:256], chosen_ref[...].astype(jnp.bfloat16))
     own_left = gate_curve(combined[128:256]) * combined[0:128]
     for m in range(16):
         part = own_left[:, (m // 8) * LANES : (m // 8 + 1) * LANES]
@@ -312,14 +343,14 @@
             )
 
 
-def finish_kernel(own_pair_ref, own_part_ref, other_part_ref, turned_ref, wide_weight_ref, result_ref):
+def finish_kernel(own_pair_ref, own_part_ref, other_part_ref, narrow_ref, down_ref, result_ref):
     products = [normalize_channels(own_part_ref[t] + other_part_ref[t]) for t in range(2)]
-    finished = mix(turned(turned_ref, "in_final"), jnp.concatenate(products, axis=1))
+    finished = mix(narrow_ref[0:128, :], jnp.concatenate(products, axis=1))
     own_pair = jnp.concatenate([own_pair_ref[t] for t in range(2)], axis=1)
-    gating = gate_curve(mix(turned(turned_ref, "in_gate"), normalize_channels(own_pair)))
+    gating = gate_curve(mix(narrow_ref[128:256, :], normalize_channels(own_pair)))
     own_pair = own_pair + gating * finished
-    hidden = jnp.maximum(mix(turned(turned_ref, "up"), normalize_channels(own_pair)), 0.0)
-    own_pair = own_pair + mix(wide_weight_ref[256:384, :], hidden.astype(jnp.bfloat16))
+    hidden = jnp.maximum(mix(narrow_ref[256:768, :], normalize_channels(own_pair)), 0.0)
+    own_pair = own_pair + mix(down_ref[...], hidden.astype(jnp.bfloat16))
     own_pair = own_pair.astype(jnp.bfloat16)
     order = lane_order_matrix()
     for t in range(2):
@@ -371,65 +402,6 @@
             )
 
 
-TURNED = {
-    "out_mix": (0, 512),
-    "out_gate": (512, 640),
-    "out_final": (640, 768),
-    "in_mix": (768, 1280),
-    "in_gate": (1280, 1408),
-    "in_final": (1408, 1536),
-    "up": (1536, 2048),
-}
-
-
-def weights_kernel(
-    bins_ref,
-    table_ref,
-    *rest,
-):
-    sources, (embedding_out, turned_out, wide_out, ready_out) = rest[:9], rest[9:13]
-    landed, (table_wide_ref, mean_wide_ref, arrived) = rest[13:22], rest[22:]
-    ready_out[...] = jnp.zeros_like(ready_out)
-    copies = [
-        pltpu.make_async_copy(sources[k], landed[k], arrived.at[k]) for k in range(len(sources))
-    ]
-    for copy in copies:
-        copy.start()
-    table_wide_ref[...] = jnp.zeros_like(table_wide_ref)
-    table_wide_ref[0:NBINS, :] = table_ref[...].astype(jnp.float32)
-    table = table_wide_ref[...].T.astype(jnp.bfloat16)
-    channel = lax.broadcasted_iota(jnp.int32, (LANES, LANES), 0)
-
-    def embed(g, carry):
-        for q in range(4):
-            h = 4 * g + q
-            one_hot = (channel == bins_ref[pl.ds(h, 1), :]).astype(jnp.float32).astype(jnp.bfloat16)
-            embedding_out[h] = mix(table, one_hot).astype(jnp.bfloat16)
-        return carry
-
-    lax.fori_loop(0, 8, embed, 0)
-    for copy in copies:
-        copy.wait()
-    mean_wide_ref[...] = landed[0][...].astype(jnp.float32)
-    for e in range(2):
-        for block in range(4):
-            rows = [
-                mean_wide_ref[pl.ds(2 * (4 * block + k) + e, CO, stride=CO), :] for k in range(4)
-            ]
-            wide_out[e * LANES : (e + 1) * LANES, block * LANES : (block + 1) * LANES] = (
-                jnp.concatenate(rows, axis=0).T.astype(jnp.bfloat16)
-            )
-    first = 0
-    for source in landed[1:8]:
-        for b in range(source.shape[1] // LANES):
-            part = source[:, b * LANES : (b + 1) * LANES].astype(jnp.float32)
-            turned_out[first : first + LANES, :] = part.T.astype(jnp.bfloat16)
-            first += LANES
-    for a in range(4):
-        part = landed[8][a * LANES : (a + 1) * LANES, :].astype(jnp.float32)
-        wide_out[256:384, a * LANES : (a + 1) * LANES] = part.T.astype(jnp.bfloat16)
-
-
 def normalize_rows(values):
     center = jnp.mean(values, axis=1, keepdims=True)
     shifted = values - center
@@ -453,7 +425,6 @@
     up_ref,
     down_ref,
     outer_ref,
-    ready_ref,
     result_ref,
     parts_ref,
     wide_ref,
@@ -552,43 +523,20 @@
             pltpu.VMEM((1024, LANES), jnp.float32),
             pltpu.SemaphoreType.DMA((2,)),
         ],
-        compiler_params=limit(16),
+        compiler_params=limit(56),
         name="rows_by_device",
     )(alignment_input, pair_state_input)
     blocks = lax.all_to_all(blocks, "dap", split_axis=0, concat_axis=0, tiled=True)
 
-    pair_far = exchange(own_pair, 8)
-    pair_near = exchange(jnp.stack([own_pair, pair_far]), 4)
-    pair_line = jnp.concatenate([jnp.stack([own_pair, pair_far]), pair_near])
-
-    embedding, turned_weights, wide_weights, ready = pl.pallas_call(
-        weights_kernel,
-        out_shape=[array(32, width, LANES), array(2048, LANES), array(384, 512), wide(8, LANES)],
-        in_specs=[vmem] * 2 + [hbm] * 9,
-        out_specs=[vmem] * 4,
-        scratch_shapes=[pltpu.VMEM(w.shape, jnp.bfloat16) for w in pair_weights]
-        + [
-            pltpu.VMEM((LANES, LANES), jnp.float32),
-            pltpu.VMEM((1024, LANES), jnp.float32),
-            pltpu.SemaphoreType.DMA((9,)),
-        ],
-        compiler_params=limit(24),
-        cost_estimate=pl.CostEstimate(
-            flops=200_000_000, bytes_accessed=8_000_000, transcendentals=0
-        ),
-        name="turn_weights",
-    )(
-        lanes_order(bin_all).reshape(32, LANES),
-        relative_position_table,
-        *pair_weights,
-    )
-    blocks, pair_line = lax.optimization_barrier((blocks, pair_line))
-    pair_across = exchange(pair_line, 2)
+    pair_first = jnp.stack([own_pair, exchange(own_pair, 8)])
+    pair_second = exchange(pair_first, 4)
+    blocks, pair_first, pair_second = lax.optimization_barrier((blocks, pair_first, pair_second))
+    pair_pieces = [pair_first, pair_second, exchange(pair_first, 2), exchange(pair_second, 2)]
 
     result, parts = pl.pallas_call(
         msa_kernel,
         out_shape=(array(512, channels), array(256, LANES)),
-        in_specs=[vmem] * 10,
+        in_specs=[vmem] * 9,
         out_specs=(vmem, vmem),
         scratch_shapes=[
             pltpu.VMEM((512, channels), jnp.float32),
@@ -610,49 +558,47 @@
         alignment_transition_up,
         alignment_transition_down,
         outer_input_weight.T,
-        ready,
-    )
-    parts, pair_across = lax.optimization_barrier((parts, pair_across))
-    far = exchange(parts, 8)
-    near = [exchange(parts, 4), exchange(far, 4)]
-    line = jnp.stack([parts, far] + near)
-    across = exchange(line, 2)
-    core_line = exchange(jnp.stack([part[128:256] for part in (parts, far, *near)]), 1)
-    core_across = exchange(across[:, 128:256, :], 1)
+    )
+    first = jnp.stack([parts, exchange(parts, 8)])
+    second = exchange(first, 4)
+    pieces = [first, second, exchange(first, 2), exchange(second, 2)]
+    core_pieces = [exchange(piece, 1) for piece in pieces]
 
     slabs = (16, 128, LANES)
     tall = (16 * 128, LANES)
     pair_mid, left, gating, right = pl.pallas_call(
         start_kernel,
         out_shape=[wide(*slabs), wide(*tall), wide(*slabs), array(*tall)],
-        in_specs=[smem] + [vmem] * 10,
+        in_specs=[smem] + [vmem] * 15 + [hbm] * 3,
         out_specs=[vmem] * 4,
         scratch_shapes=[
             pltpu.VMEM((2048, LANES), jnp.float32),
             pltpu.VMEM((128, 2048), jnp.bfloat16),
+            pltpu.VMEM((1024, LANES), jnp.float32),
+            pltpu.VMEM((256, 512), jnp.bfloat16),
+            pltpu.VMEM((LANES, LANES), jnp.float32),
             pltpu.VMEM((512, 1024), jnp.bfloat16),
             pltpu.VMEM((512, 1024), jnp.bfloat16),
-        ],
-        compiler_params=limit(32),
+        ]
+        + [pltpu.VMEM(w.shape, jnp.bfloat16) for w in pair_weights[:3]]
+        + [pltpu.SemaphoreType.DMA((3,))],
+        compiler_params=limit(48),
         name="pair_start",
     )(
         place,
         live_row_float.reshape(1, LANES),
-        line,
-        across,
-        core_line,
-        core_across,
-        pair_line,
-        pair_across,
-        embedding,
-        turned_weights,
-        wide_weights,
-    )
-    own_pair, own_part, other_part = pl.pallas_call(
+        lanes_order(bin_all).reshape(32, LANES),
+        relative_position_table,
+        *pieces,
+        *core_pieces,
+        *pair_pieces,
+        *pair_weights[:3],
+    )
+    own_pair, own_part, other_part, narrow_weights, down_weight = pl.pallas_call(
         triangle_kernel,
-        out_shape=[wide(2, 128, LANES)] * 3,
-        in_specs=[smem] + [vmem] * 6,
-        out_specs=[vmem] * 3,
+        out_shape=[wide(2, 128, LANES)] * 3 + [array(768, LANES), array(128, 512)],
+        in_specs=[smem] + [vmem] * 5 + [hbm] * 6,
+        out_specs=[vmem] * 5,
         scratch_shapes=[
             pltpu.VMEM((32 * 128, LANES), jnp.float32),
             pltpu.VMEM(tall, jnp.float32),
@@ -660,10 +606,12 @@
             pltpu.VMEM((128, 256), jnp.float32),
             pltpu.VMEM(tall, jnp.float32),
             pltpu.VMEM(tall, jnp.float32),
-        ],
-        compiler_params=limit(32),
+        ]
+        + [pltpu.VMEM(w.shape, jnp.bfloat16) for w in pair_weights[3:]]
+        + [pltpu.SemaphoreType.DMA((6,))],
+        compiler_params=limit(48),
         name="pair_triangles",
-    )(place, pair_mid, left, gating, right, exchange(right, 1), turned_weights)
+    )(place, pair_mid, left, gating, right, exchange(right, 1), *pair_weights[3:])
     pair_output = pl.pallas_call(
         finish_kernel,
         out_shape=array(256, LANES),
@@ -671,7 +619,7 @@
         out_specs=vmem,
         compiler_params=limit(16),
         name="pair_finish",
-    )(own_pair, own_part, exchange(other_part, 1), turned_weights, wide_weights)
+    )(own_pair, own_part, exchange(other_part, 1), narrow_weights, down_weight)
     return result.reshape(128, 4, channels), pair_output.reshape(pair_state_input.shape)
 
 

time: 75.7 us -> 73.4 us (0.970)
  local copies, waits for them, and re-layouts: 11.5 us -> 4.97 us
  waiting for transfers between devices: 23 us -> 28.8 us
  Pallas kernels: 22.4 us -> 21.4 us
    ppermute x11 -> x14, waiting for transfers between devices: 22.6 us -> 28.8 us  [exchange(): return lax.ppermute(values, 'dap', [(q, q ^ offset) for q in range(pieces)])]
    unnamed x46 -> x40, local copies, waits for them, and re-layouts: 9.61 us -> 3.74 us
    all_to_all x1, starting transfers between devices: 4.04 us -> 7.4 us  [whole_block(): lax.all_to_all(blocks, 'dap', split_axis=0, concat_axis=0, tiled=True)]
    ppermute x11 -> x14, starting transfers between devices: 11.7 us -> 8.41 us  [exchange(): return lax.ppermute(values, 'dap', [(q, q ^ offset) for q in range(pieces)])]
    pallas_call x2 -> x1, Pallas kernels: 10.5 us -> 8.06 us  [whole_block(): pl.pallas_call(triangle_kernel, out_shape=[wide(2, 128, LANES)] * 3 + [ar...]
    pallas_call x1, Pallas kernels: 1.33 us -> 2.18 us  [whole_block(): pl.pallas_call(rows_kernel, out_shape=[array(16, 32, channels), array(2,...]
  transfers between devices with their start and end apart: 12 -> 15, of which waited for: 9 -> 9; matrix products, arithmetic and copies ran while one was open for 4% -> 3% of each run, Pallas kernels for 9% -> 0%
where the time goes in v8:
time: 73.4 us; the launch traced here: 73.1 us
  waiting for transfers between devices  28.8 us (39%)
  Pallas kernels  21.4 us (29%)
  starting transfers between devices  15.8 us (22%)
  local copies, waits for them, and re-layouts  4.97 us (7%)
  other arithmetic  1.08 us (1%)
  between operations  0.93 us (1%)
    ppermute x14, waiting for transfers between devices, exchange(): return lax.ppermute(values, 'dap', [(q, q ^ offset) for q in range(pieces)])  28.8 us
    ppermute x14, starting transfers between devices, exchange(): return lax.ppermute(values, 'dap', [(q, q ^ offset) for q in range(pieces)])  8.41 us
    pallas_call x1, Pallas kernels, whole_block(): pl.pallas_call(triangle_kernel, out_shape=[wide(2, 128, LANES)] * 3 + [ar...  8.06 us
    all_to_all x1, starting transfers between devices, whole_block(): lax.all_to_all(blocks, 'dap', split_axis=0, concat_axis=0, tiled=True)  7.4 us
    pallas_call x1, Pallas kernels, whole_block(): pl.pallas_call(start_kernel, out_shape=[wide(*slabs), wide(*tall), wide(*...  5.58 us
    pallas_call x1, Pallas kernels, whole_block(): pl.pallas_call(msa_kernel, out_shape=(array(512, channels), array(256, LA...  4.1 us
    unnamed x40, local copies, waits for them, and re-layouts  3.74 us
    pallas_call x1, Pallas kernels, whole_block(): pl.pallas_call(rows_kernel, out_shape=[array(16, 32, channels), array(2,...  2.18 us
  transfers between devices with their start and end apart: 15, of which 9 were waited for; matrix products, arithmetic and copies ran while one was open for 3% of the time, Pallas kernels for 0%

profile of v8, /device:TPU:0, one launch (start us, length us, event | category | flops | bytes accessed | tf_op | source)
XLA Modules:
  0.0 73.1 jit_solution(16762594010063675201)
XLA Ops:
  0.7 2.2 %rows_by_device.1 = (bf16[16,32,256]{2,1,0:T(8,128)(2,1)}, bf16[2,128,128]{2,1,0:T(8,128)(2,1)}) custom-call(bf16[8,64,256]{2,1,0:T(8,128)(2,1)} %rows_source.1, bf16[4,64,128]{2,1,0:T(8,128)(2,1)} %pair_source.1), custom_call_target="tpu_custom_call" | custom-call | tf_op jit(solution)/shard_map/rows_by_device/pallas_call | solution.py:515
  2.8 7.4 %all-to-all-start = ((bf16[16,32,256]{2,1,0:T(8,128)(2,1)}), bf16[16,32,256]{2,1,0:T(8,128)(2,1)S(1)}, u32[]{:S(2)}, u32[]{:S(2)}) async-start(bf16[16,32,256]{2,1,0:T(8,128)(2,1)} %get-tuple-element.18), calls=%async_computation | async-start | bytes 524288 | tf_op jit(solution)/shard_map/all_to_all | solution.py:529
  10.2 2.8 %collective-permute-start = (bf16[2,128,128]{2,1,0:T(8,128)(2,1)}, bf16[2,128,128]{2,1,0:T(8,128)(2,1)S(1)}, u32[]{:S(2)}, u32[]{:S(2)}) collective-permute-start(bf16[2,128,128]{2,1,0:T(8,128)(2,1)} %get-tuple-element.19), channel_id=1, source_target_pairs={{0,8},{1,9},{2,10},{3,11},{4,12},{5,13},{6,14},{7,15},{8,0},{9,1},... | collective-permute-start | bytes 196616 | tf_op jit(solution)/shard_map/ppermute | solution.py:481
  13.1 9.6 %collective-permute-done = bf16[2,128,128]{2,1,0:T(8,128)(2,1)S(1)} collective-permute-done((bf16[2,128,128]{2,1,0:T(8,128)(2,1)}, bf16[2,128,128]{2,1,0:T(8,128)(2,1)S(1)}, u32[]{:S(2)}, u32[]{:S(2)}) %collective-permute-start) | collective-permute-done | bytes 65568 | tf_op jit(solution)/shard_map/ppermute | solution.py:481
  22.7 0.9 %pad_maximum_fusion.rest_8_ = bf16[2,2,128,128]{3,2,1,0:T(8,128)(2,1)S(1)} fusion(bf16[1,2,128,128]{3,2,1,0:T(8,128)(2,1)S(1)} %bitcast.17, bf16[1,2,128,128]{3,2,1,0:T(8,128)(2,1)} %bitcast.16), kind=kLoop, calls=%fused_computation | loop fusion | flops 65536 | bytes 262144 | tf_op jit(solution)/shard_map/stack | solution.py:531
  23.7 5.0 %collective-permute-done.1.rest_9_ = bf16[2,2,128,128]{3,2,1,0:T(8,128)(2,1)S(1)} collective-permute-done((bf16[2,2,128,128]{3,2,1,0:T(8,128)(2,1)S(1)}, bf16[2,2,128,128]{3,2,1,0:T(8,128)(2,1)S(1)}, u32[]{:S(2)}, u32[]{:S(2)}) %collective-permute-start.1) | collective-permute-done | bytes 131104 | tf_op jit(solution)/shard_map/ppermute | solution.py:481
  28.7 0.9 %copy-done.12 = bf16[256,512]{1,0:T(8,128)(2,1)S(1)} copy-done((bf16[256,512]{1,0:T(8,128)(2,1)S(1)}, bf16[256,512]{1,0:T(8,128)(2,1)}, u32[]{:S(2)}) %copy-start.12) | copy-done | bytes 262168
  29.7 0.9 %copy-done.13 = bf16[256,256]{1,0:T(8,128)(2,1)S(1)} copy-done((bf16[256,256]{1,0:T(8,128)(2,1)S(1)}, bf16[256,256]{1,0:T(8,128)(2,1)}, u32[]{:S(2)}) %copy-start.13) | copy-done | bytes 131096
  30.6 0.9 %copy-done.14 = bf16[256,256]{1,0:T(8,128)(2,1)S(1)} copy-done((bf16[256,256]{1,0:T(8,128)(2,1)S(1)}, bf16[256,256]{1,0:T(8,128)(2,1)}, u32[]{:S(2)}) %copy-start.14) | copy-done | bytes 131096
  31.5 0.9 %copy-done.15 = bf16[256,256]{1,0:T(8,128)(2,1)S(1)} copy-done((bf16[256,256]{1,0:T(8,128)(2,1)S(1)}, bf16[256,256]{1,0:T(8,128)(2,1)}, u32[]{:S(2)}) %copy-start.15) | copy-done | bytes 131096
  32.4 4.1 %msa_whole.1 = (bf16[512,256]{1,0:T(8,128)(2,1)S(1)}, bf16[256,128]{1,0:T(8,128)(2,1)S(1)}) custom-call(f32[1,128]{1,0:T(1,128)S(1)} %fusion.live_ref, bf16[16,32,256]{2,1,0:T(8,128)(2,1)S(1)} %all-to-all-done.blocks_ref, bf16[256,256]{1,0:T(8,128)(2,1)S(1)} %copy-done.13, bf16[256,256]{1,0:T(8,128)(2,1)S(1)} %copy-done.14, bf16[256,512]{1,0:T(8,128)(2,1)S(1)} %copy-done.12, ...), custom_call_target="tpu_custom_call" | custom-call | flops 2000000000 | bytes 10000000 | tf_op jit(solution)/shard_map/msa_whole/pallas_call | solution.py:536
  36.5 0.5 collective-permute-start.2
  37.0 5.2 %collective-permute-done.2 = bf16[256,128]{1,0:T(8,128)(2,1)S(1)} collective-permute-done((bf16[256,128]{1,0:T(8,128)(2,1)S(1)}, bf16[256,128]{1,0:T(8,128)(2,1)S(1)}, u32[]{:S(2)}, u32[]{:S(2)}) %collective-permute-start.2) | collective-permute-done | bytes 65568 | tf_op jit(solution)/shard_map/ppermute | solution.py:481
  42.3 1.5 %collective-permute-start.10 = (bf16[2,2,128,128]{3,2,1,0:T(8,128)(2,1)S(1)}, bf16[2,2,128,128]{3,2,1,0:T(8,128)(2,1)S(1)}, u32[]{:S(2)}, u32[]{:S(2)}) collective-permute-start(bf16[2,2,128,128]{3,2,1,0:T(8,128)(2,1)S(1)} %pad_maximum_fusion.rest_8_), channel_id=1, source_target_pairs={{0,2},{1,3},{2,0},{3,1},{4,6},{5,7},{6,4},{7,5},{8,10},{9,11},{10,... | collective-permute-start | bytes 393224 | tf_op jit(solution)/shard_map/ppermute | solution.py:481
  43.8 0.6 collective-permute-start.4
  44.3 2.9 %collective-permute-done.3.rest_1_ = bf16[2,256,128]{2,1,0:T(8,128)(2,1)S(1)} collective-permute-done((bf16[2,256,128]{2,1,0:T(8,128)(2,1)S(1)}, bf16[2,256,128]{2,1,0:T(8,128)(2,1)S(1)}, u32[]{:S(2)}, u32[]{:S(2)}) %collective-permute-start.3) | collective-permute-done | bytes 131104 | tf_op jit(solution)/shard_map/ppermute | solution.py:481
  47.2 1.5 %collective-permute-start.5 = (bf16[2,256,128]{2,1,0:T(8,128)(2,1)S(1)}, bf16[2,256,128]{2,1,0:T(8,128)(2,1)S(1)}, u32[]{:S(2)}, u32[]{:S(2)}) collective-permute-start(bf16[2,256,128]{2,1,0:T(8,128)(2,1)S(1)} %collective-permute-done.3.rest_1_), channel_id=1, source_target_pairs={{0,2},{1,3},{2,0},{3,1},{4,6},{5,7},{6,4},{7,5},{8,10},{9,11},{10,... | collective-permute-start | bytes 393224 | tf_op jit(solution)/shard_map/ppermute | solution.py:481
  49.0 0.6 collective-permute-start.11
  49.6 0.5 collective-permute-start.7
  50.1 0.8 %collective-permute-done.4.rest_2_ = bf16[2,256,128]{2,1,0:T(8,128)(2,1)S(1)} collective-permute-done((bf16[2,256,128]{2,1,0:T(8,128)(2,1)S(1)}, bf16[2,256,128]{2,1,0:T(8,128)(2,1)S(1)}, u32[]{:S(2)}, u32[]{:S(2)}) %collective-permute-start.4) | collective-permute-done | bytes 131104 | tf_op jit(solution)/shard_map/ppermute | solution.py:481
  50.9 2.0 %collective-permute-done.5.rest_3_ = bf16[2,256,128]{2,1,0:T(8,128)(2,1)S(1)} collective-permute-done((bf16[2,256,128]{2,1,0:T(8,128)(2,1)S(1)}, bf16[2,256,128]{2,1,0:T(8,128)(2,1)S(1)}, u32[]{:S(2)}, u32[]{:S(2)}) %collective-permute-start.5) | collective-permute-done | bytes 131104 | tf_op jit(solution)/shard_map/ppermute | solution.py:481
  52.9 0.2 compare_select_fusion
  53.1 0.1 select_n.11.bins_ref
  53.3 1.1 %collective-permute-done.11.rest_11_ = bf16[2,2,128,128]{3,2,1,0:T(8,128)(2,1)S(1)} collective-permute-done((bf16[2,2,128,128]{3,2,1,0:T(8,128)(2,1)S(1)}, bf16[2,2,128,128]{3,2,1,0:T(8,128)(2,1)S(1)}, u32[]{:S(2)}, u32[]{:S(2)}) %collective-permute-start.11) | collective-permute-done | bytes 131104 | tf_op jit(solution)/shard_map/ppermute | solution.py:481
  54.4 5.6 %pair_start.1 = (f32[16,128,128]{2,1,0:T(8,128)S(1)}, f32[2048,128]{1,0:T(8,128)S(1)}, f32[16,128,128]{2,1,0:T(8,128)S(1)}, bf16[2048,128]{1,0:T(8,128)(2,1)S(1)}) custom-call(s32[1]{0:T(128)} %bitcast.4.place_ref, f32[1,128]{1,0:T(1,128)S(1)} %fusion.live_ref, s32[32,128]{1,0:T(8,128)S(1)} %select_n.11.bins_ref, bf16[66,128]{1,0:T(8,128)(2,1)S(1)} %copy-done.9, ...), custom_call_target="tpu_custom_call" | custom-call | tf_op jit(solution)/shard_map/pair_start/pallas_call | solution.py:569
  60.0 0.1 collective-permute-start.12
  60.2 1.8 %collective-permute-done.12.right_other_ref = bf16[2048,128]{1,0:T(8,128)(2,1)S(1)} collective-permute-done((bf16[2048,128]{1,0:T(8,128)(2,1)S(1)}, bf16[2048,128]{1,0:T(8,128)(2,1)S(1)}, u32[]{:S(2)}, u32[]{:S(2)}) %collective-permute-start.12) | collective-permute-done | bytes 524320 | tf_op jit(solution)/shard_map/ppermute | solution.py:481
  62.1 8.1 %pair_triangles.1 = (f32[2,128,128]{2,1,0:T(8,128)S(1)}, f32[2,128,128]{2,1,0:T(8,128)S(1)}, f32[2,128,128]{2,1,0:T(8,128)S(1)}, bf16[768,128]{1,0:T(8,128)(2,1)S(1)}, bf16[128,512]{1,0:T(8,128)(2,1)S(1)}) custom-call(s32[1]{0:T(128)} %bitcast.4.place_ref, f32[16,128,128]{2,1,0:T(8,128)S(1)} %get-tuple-element.25.pair_mid_ref, ...), custom_call_target="tpu_custom_call" | custom-call | tf_op jit(solution)/shard_map/pair_triangles/pallas_call | solution.py:597
  70.1 0.2 collective-permute-start.13
  70.3 0.8 %reshape.59 = bf16[128,4,256]{2,1,0:T(4,128)(2,1)} reshape(bf16[512,256]{1,0:T(8,128)(2,1)S(1)} %get-tuple-element.21) | data formatting | bytes 524288 | tf_op jit(solution)/shard_map/reshape | solution.py:623
  71.1 0.4 collective-permute-done.13.other_part_ref
  71.5 1.5 %pair_finish.1 = bf16[256,128]{1,0:T(8,128)(2,1)} custom-call(f32[2,128,128]{2,1,0:T(8,128)S(1)} %get-tuple-element.29.own_pair_ref, f32[2,128,128]{2,1,0:T(8,128)S(1)} %get-tuple-element.30.own_part_ref, f32[2,128,128]{2,1,0:T(8,128)S(1)} %collective-permute-done.13.other_part_ref, bf16[768,128]{1,0:T(8,128)(2,1)S(1)} %get-tuple-element.32.narrow_ref, ...), custom_call_target="tpu_custom_call" | custom-call | tf_op jit(solution)/shard_map/pair_finish/pallas_call | solution.py:615
  (53 shorter events, 0.6 us)
Async XLA Ops:
  0.6 28.1 %copy-start.11 = (bf16[1024,256]{1,0:T(8,128)(2,1)S(1)}, bf16[1024,256]{1,0:T(8,128)(2,1)}, u32[]{:S(2)}) copy-start(bf16[1024,256]{1,0:T(8,128)(2,1)} %down_ref.1) | copy-start | bytes 1572868
  0.6 28.0 %copy-start.10 = (bf16[256,1024]{1,0:T(8,128)(2,1)S(1)}, bf16[256,1024]{1,0:T(8,128)(2,1)}, u32[]{:S(2)}) copy-start(bf16[256,1024]{1,0:T(8,128)(2,1)} %up_ref.1) | copy-start | bytes 1572868
  2.8 25.8 %all-to-all-start = ((bf16[16,32,256]{2,1,0:T(8,128)(2,1)}), bf16[16,32,256]{2,1,0:T(8,128)(2,1)S(1)}, u32[]{:S(2)}, u32[]{:S(2)}) async-start(bf16[16,32,256]{2,1,0:T(8,128)(2,1)} %get-tuple-element.18), calls=%async_computation | async-start | bytes 524288 | tf_op jit(solution)/shard_map/all_to_all | solution.py:529
  10.2 12.5 %collective-permute-start = (bf16[2,128,128]{2,1,0:T(8,128)(2,1)}, bf16[2,128,128]{2,1,0:T(8,128)(2,1)S(1)}, u32[]{:S(2)}, u32[]{:S(2)}) collective-permute-start(bf16[2,128,128]{2,1,0:T(8,128)(2,1)} %get-tuple-element.19), channel_id=1, source_target_pairs={{0,8},{1,9},{2,10},{3,11},{4,12},{5,13},{6,14},{7,15},{8,0},{9,1},... | collective-permute-start | bytes 196616 | tf_op jit(solution)/shard_map/ppermute | solution.py:481
  22.7 1.0 %copy-start.19 = (s32[128]{0:T(128)S(1)}, s32[128]{0:T(128)}, u32[]{:S(2)}) copy-start(s32[128]{0:T(128)} %param.26) | copy-start | bytes 1540
  22.7 6.0 %copy-start.16 = (bf16[256,64]{0,1:T(8,128)(2,1)S(1)}, bf16[256,64]{0,1:T(8,128)(2,1)}, u32[]{:S(2)}) copy-start(bf16[256,64]{0,1:T(8,128)(2,1)} %param.34) | copy-start | bytes 98308
  23.6 5.1 %collective-permute-start.1 = (bf16[2,2,128,128]{3,2,1,0:T(8,128)(2,1)S(1)}, bf16[2,2,128,128]{3,2,1,0:T(8,128)(2,1)S(1)}, u32[]{:S(2)}, u32[]{:S(2)}) collective-permute-start(bf16[2,2,128,128]{3,2,1,0:T(8,128)(2,1)S(1)} %pad_maximum_fusion.rest_8_), channel_id=1, source_target_pairs={{0,4},{1,5},{2,6},{3,7},{4,0},{5,1},{6,2},{7,3},{8,12},{9,13},{10,... | collective-permute-start | bytes 393224 | tf_op jit(solution)/shard_map/ppermute | solution.py:481
  28.7 1.0 %copy-start.12 = (bf16[256,512]{1,0:T(8,128)(2,1)S(1)}, bf16[256,512]{1,0:T(8,128)(2,1)}, u32[]{:S(2)}) copy-start(bf16[256,512]{1,0:T(8,128)(2,1)} %value_gate_ref.1) | copy-start | bytes 786436
  36.5 17.9 %copy-start = (bf16[1024,128]{1,0:T(8,128)(2,1)S(1)}, bf16[1024,128]{1,0:T(8,128)(2,1)}, u32[]{:S(2)}) copy-start(bf16[1024,128]{1,0:T(8,128)(2,1)} %rest_12_.1) | copy-start | bytes 786436
  36.5 5.7 %collective-permute-start.2 = (bf16[256,128]{1,0:T(8,128)(2,1)S(1)}, bf16[256,128]{1,0:T(8,128)(2,1)S(1)}, u32[]{:S(2)}, u32[]{:S(2)}) collective-permute-start(bf16[256,128]{1,0:T(8,128)(2,1)S(1)} %get-tuple-element.22), channel_id=1, source_target_pairs={{0,8},{1,9},{2,10},{3,11},{4,12},{5,13},{6,14},{7,15},{8,0},{9,1},... | collective-permute-start | bytes 196616 | tf_op jit(solution)/shard_map/ppermute | solution.py:481
  42.1 6.5 %copy-start.17 = (s32[64]{0:T(128)S(1)}, s32[64]{0:T(128)}, u32[]{:S(2)}) copy-start(s32[64]{0:T(128)} %param.24) | copy-start | bytes 772
  42.1 6.7 %copy-start.18 = (s32[64]{0:T(128)S(1)}, s32[64]{0:T(128)}, u32[]{:S(2)}) copy-start(s32[64]{0:T(128)} %param.25) | copy-start | bytes 772
  42.2 12.2 %copy-start.1 = (bf16[128,512]{1,0:T(8,128)(2,1)S(1)}, bf16[128,512]{1,0:T(8,128)(2,1)}, u32[]{:S(2)}) copy-start(bf16[128,512]{1,0:T(8,128)(2,1)} %rest_13_.1) | copy-start | bytes 393220
  42.2 5.0 %collective-permute-start.3 = (bf16[2,256,128]{2,1,0:T(8,128)(2,1)S(1)}, bf16[2,256,128]{2,1,0:T(8,128)(2,1)S(1)}, u32[]{:S(2)}, u32[]{:S(2)}) collective-permute-start(bf16[2,256,128]{2,1,0:T(8,128)(2,1)S(1)} %pad_maximum_fusion.1.rest_0_), channel_id=1, source_target_pairs={{0,4},{1,5},{2,6},{3,7},{4,0},{5,1},{6,2},{7,3},{8,12},{9,13},{10,... | collective-permute-start | bytes 393224 | tf_op jit(solution)/shard_map/ppermute | solution.py:481
  42.3 7.4 %collective-permute-start.10 = (bf16[2,2,128,128]{3,2,1,0:T(8,128)(2,1)S(1)}, bf16[2,2,128,128]{3,2,1,0:T(8,128)(2,1)S(1)}, u32[]{:S(2)}, u32[]{:S(2)}) collective-permute-start(bf16[2,2,128,128]{3,2,1,0:T(8,128)(2,1)S(1)} %pad_maximum_fusion.rest_8_), channel_id=1, source_target_pairs={{0,2},{1,3},{2,0},{3,1},{4,6},{5,7},{6,4},{7,5},{8,10},{9,11},{10,... | collective-permute-start | bytes 393224 | tf_op jit(solution)/shard_map/ppermute | solution.py:481
  43.8 7.1 %collective-permute-start.4 = (bf16[2,256,128]{2,1,0:T(8,128)(2,1)S(1)}, bf16[2,256,128]{2,1,0:T(8,128)(2,1)S(1)}, u32[]{:S(2)}, u32[]{:S(2)}) collective-permute-start(bf16[2,256,128]{2,1,0:T(8,128)(2,1)S(1)} %pad_maximum_fusion.1.rest_0_), channel_id=1, source_target_pairs={{0,2},{1,3},{2,0},{3,1},{4,6},{5,7},{6,4},{7,5},{8,10},{9,11},{10,... | collective-permute-start | bytes 393224 | tf_op jit(solution)/shard_map/ppermute | solution.py:481
  47.2 5.7 %collective-permute-start.5 = (bf16[2,256,128]{2,1,0:T(8,128)(2,1)S(1)}, bf16[2,256,128]{2,1,0:T(8,128)(2,1)S(1)}, u32[]{:S(2)}, u32[]{:S(2)}) collective-permute-start(bf16[2,256,128]{2,1,0:T(8,128)(2,1)S(1)} %collective-permute-done.3.rest_1_), channel_id=1, source_target_pairs={{0,2},{1,3},{2,0},{3,1},{4,6},{5,7},{6,4},{7,5},{8,10},{9,11},{10,... | collective-permute-start | bytes 393224 | tf_op jit(solution)/shard_map/ppermute | solution.py:481
  49.0 5.3 %collective-permute-start.11 = (bf16[2,2,128,128]{3,2,1,0:T(8,128)(2,1)S(1)}, bf16[2,2,128,128]{3,2,1,0:T(8,128)(2,1)S(1)}, u32[]{:S(2)}, u32[]{:S(2)}) collective-permute-start(bf16[2,2,128,128]{3,2,1,0:T(8,128)(2,1)S(1)} %collective-permute-done.1.rest_9_), channel_id=1, source_target_pairs={{0,2},{1,3},{2,0},{3,1},{4,6},{5,7},{6,4},{7,5},{8,10},{9,11},{10,... | collective-permute-start | bytes 393224 | tf_op jit(solution)/shard_map/ppermute | solution.py:481
  49.6 4.7 %collective-permute-start.6 = (bf16[2,256,128]{2,1,0:T(8,128)(2,1)S(1)}, bf16[2,256,128]{2,1,0:T(8,128)(2,1)S(1)}, u32[]{:S(2)}, u32[]{:S(2)}) collective-permute-start(bf16[2,256,128]{2,1,0:T(8,128)(2,1)S(1)} %pad_maximum_fusion.1.rest_0_), channel_id=1, source_target_pairs={{0,1},{1,0},{2,3},{3,2},{4,5},{5,4},{6,7},{7,6},{8,9},{9,8},{10,11... | collective-permute-start | bytes 393224 | tf_op jit(solution)/shard_map/ppermute | solution.py:481
  49.6 4.7 %collective-permute-start.7 = (bf16[2,256,128]{2,1,0:T(8,128)(2,1)S(1)}, bf16[2,256,128]{2,1,0:T(8,128)(2,1)S(1)}, u32[]{:S(2)}, u32[]{:S(2)}) collective-permute-start(bf16[2,256,128]{2,1,0:T(8,128)(2,1)S(1)} %collective-permute-done.3.rest_1_), channel_id=1, source_target_pairs={{0,1},{1,0},{2,3},{3,2},{4,5},{5,4},{6,7},{7,6},{8,9},{9,8},{10,11... | collective-permute-start | bytes 393224 | tf_op jit(solution)/shard_map/ppermute | solution.py:481
  50.9 3.4 %collective-permute-start.8 = (bf16[2,256,128]{2,1,0:T(8,128)(2,1)S(1)}, bf16[2,256,128]{2,1,0:T(8,128)(2,1)S(1)}, u32[]{:S(2)}, u32[]{:S(2)}) collective-permute-start(bf16[2,256,128]{2,1,0:T(8,128)(2,1)S(1)} %collective-permute-done.4.rest_2_), channel_id=1, source_target_pairs={{0,1},{1,0},{2,3},{3,2},{4,5},{5,4},{6,7},{7,6},{8,9},{9,8},{10,11... | collective-permute-start | bytes 393224 | tf_op jit(solution)/shard_map/ppermute | solution.py:481
  52.9 1.4 %collective-permute-start.9 = (bf16[2,256,128]{2,1,0:T(8,128)(2,1)S(1)}, bf16[2,256,128]{2,1,0:T(8,128)(2,1)S(1)}, u32[]{:S(2)}, u32[]{:S(2)}) collective-permute-start(bf16[2,256,128]{2,1,0:T(8,128)(2,1)S(1)} %collective-permute-done.5.rest_3_), channel_id=1, source_target_pairs={{0,1},{1,0},{2,3},{3,2},{4,5},{5,4},{6,7},{7,6},{8,9},{9,8},{10,11... | collective-permute-start | bytes 393224 | tf_op jit(solution)/shard_map/ppermute | solution.py:481
  53.1 1.2 %copy-start.5 = (bf16[128,128]{1,0:T(8,128)(2,1)S(1)}, bf16[128,128]{1,0:T(8,128)(2,1)}, u32[]{:S(2)}) copy-start(bf16[128,128]{1,0:T(8,128)(2,1)} %rest_14_.1) | copy-start | bytes 98308
  53.1 1.2 %copy-start.9 = (bf16[66,128]{1,0:T(8,128)(2,1)S(1)}, bf16[66,128]{1,0:T(8,128)(2,1)}, u32[]{:S(2)}) copy-start(bf16[66,128]{1,0:T(8,128)(2,1)} %table_ref.1) | copy-start | bytes 50692
  54.4 7.6 %copy-start.2 = (bf16[128,512]{1,0:T(8,128)(2,1)S(1)}, bf16[128,512]{1,0:T(8,128)(2,1)}, u32[]{:S(2)}) copy-start(bf16[128,512]{1,0:T(8,128)(2,1)} %rest_1_.1) | copy-start | bytes 393220
  54.4 7.6 %copy-start.3 = (bf16[128,512]{1,0:T(8,128)(2,1)S(1)}, bf16[128,512]{1,0:T(8,128)(2,1)}, u32[]{:S(2)}) copy-start(bf16[128,512]{1,0:T(8,128)(2,1)} %rest_4_.1) | copy-start | bytes 393220
  54.4 7.6 %copy-start.4 = (bf16[512,128]{1,0:T(8,128)(2,1)S(1)}, bf16[512,128]{1,0:T(8,128)(2,1)}, u32[]{:S(2)}) copy-start(bf16[512,128]{1,0:T(8,128)(2,1)} %rest_5_.1) | copy-start | bytes 393220
  54.4 7.6 %copy-start.6 = (bf16[128,128]{1,0:T(8,128)(2,1)S(1)}, bf16[128,128]{1,0:T(8,128)(2,1)}, u32[]{:S(2)}) copy-start(bf16[128,128]{1,0:T(8,128)(2,1)} %rest_0_.1) | copy-start | bytes 98308
  54.4 7.6 %copy-start.7 = (bf16[128,128]{1,0:T(8,128)(2,1)S(1)}, bf16[128,128]{1,0:T(8,128)(2,1)}, u32[]{:S(2)}) copy-start(bf16[128,128]{1,0:T(8,128)(2,1)} %rest_2_.1) | copy-start | bytes 98308
  54.4 7.6 %copy-start.8 = (bf16[128,128]{1,0:T(8,128)(2,1)S(1)}, bf16[128,128]{1,0:T(8,128)(2,1)}, u32[]{:S(2)}) copy-start(bf16[128,128]{1,0:T(8,128)(2,1)} %rest_3_.1) | copy-start | bytes 98308
  60.0 2.0 %collective-permute-start.12 = (bf16[2048,128]{1,0:T(8,128)(2,1)S(1)}, bf16[2048,128]{1,0:T(8,128)(2,1)S(1)}, u32[]{:S(2)}, u32[]{:S(2)}) collective-permute-start(bf16[2048,128]{1,0:T(8,128)(2,1)S(1)} %get-tuple-element.28.right_own_ref), channel_id=1, source_target_pairs={{0,1},{1,0},{2,3},{3,2},{4,5},{5,4},{6,7},{7,6},{8,9},{9,8},{10,11... | collective-permute-start | bytes 1572872 | tf_op jit(solution)/shard_map/ppermute | solution.py:481
  70.1 1.4 %collective-permute-start.13 = (f32[2,128,128]{2,1,0:T(8,128)S(1)}, f32[2,128,128]{2,1,0:T(8,128)S(1)}, u32[]{:S(2)}, u32[]{:S(2)}) collective-permute-start(f32[2,128,128]{2,1,0:T(8,128)S(1)} %get-tuple-element.31), channel_id=1, source_target_pairs={{0,1},{1,0},{2,3},{3,2},{4,5},{5,4},{6,7},{7,6},{8,9},{9,8},{10,11... | collective-permute-start | bytes 393224 | tf_op jit(solution)/shard_map/ppermute | solution.py:481
  (3 other events, 2.7 us)

commit v9 on v8

--- a/solution.py
+++ b/solution.py
@@ -373,20 +373,12 @@
     )
 
 
-def rows_kernel(
-    rows_source, pair_source, blocks_ref, own_pair_ref, rows_ref, pair_ref, wide_ref, arrived
-):
-    rows_copy = pltpu.make_async_copy(rows_source, rows_ref, arrived.at[0])
-    pair_copy = pltpu.make_async_copy(pair_source, pair_ref, arrived.at[1])
-    pair_copy.start()
-    rows_copy.start()
-    pair_copy.wait()
+def rows_kernel(rows_ref, pair_ref, blocks_ref, own_pair_ref, wide_ref):
     order = lane_order_matrix()
     for t in range(2):
         own_pair_ref[t] = contract_first(
             pair_ref[2 * t : 2 * t + 2].reshape(LANES, LANES), order
         ).astype(jnp.bfloat16)
-    rows_copy.wait()
     residues = rows_ref.shape[1]
     count = 8 * residues
     rows = rows_ref[...].astype(jnp.float32).reshape(count, 2 * LANES)
@@ -515,15 +507,10 @@
     blocks, own_pair = pl.pallas_call(
         rows_kernel,
         out_shape=[array(16, 32, channels), array(2, width, LANES)],
-        in_specs=[hbm, hbm],
+        in_specs=[vmem, vmem],
         out_specs=[vmem, vmem],
-        scratch_shapes=[
-            pltpu.VMEM(alignment_input.shape, jnp.bfloat16),
-            pltpu.VMEM(pair_state_input.shape, jnp.bfloat16),
-            pltpu.VMEM((1024, LANES), jnp.float32),
-            pltpu.SemaphoreType.DMA((2,)),
-        ],
-        compiler_params=limit(56),
+        scratch_shapes=[pltpu.VMEM((1024, LANES), jnp.float32)],
+        compiler_params=limit(16),
         name="rows_by_device",
     )(alignment_input, pair_state_input)
     blocks = lax.all_to_all(blocks, "dap", split_axis=0, concat_axis=0, tiled=True)

time: 73.4 us -> 73.4 us (level)
  local copies, waits for them, and re-layouts: 4.97 us -> 7.31 us
  Pallas kernels: 21.4 us -> 20.4 us
  other arithmetic: 1.08 us -> 0.23 us
    unnamed x40 -> x44, local copies, waits for them, and re-layouts: 3.74 us -> 6.08 us
    pallas_call x1, Pallas kernels: 2.18 us -> 1.13 us  [whole_block(): pl.pallas_call(rows_kernel, out_shape=[array(16, 32, channels), array(2,...]
    another operation x1, other arithmetic: 0.86 us -> 0.01 us  [whole_block(): pair_first = jnp.stack([own_pair, exchange(own_pair, 8)])]
  transfers between devices with their start and end apart: 15 -> 15, of which waited for: 9 -> 9; matrix products, arithmetic and copies ran while one was open for 3% -> 2% of each run, Pallas kernels for 0% -> 0%
where the time goes in v9:
time: 73.4 us; the launch traced here: 72.9 us
  waiting for transfers between devices  28.3 us (39%)
  Pallas kernels  20.4 us (28%)
  starting transfers between devices  15.8 us (22%)
  local copies, waits for them, and re-layouts  7.31 us (10%)
  between operations  0.9 us (1%)
    ppermute x14, waiting for transfers between devices, exchange(): return lax.ppermute(values, 'dap', [(q, q ^ offset) for q in range(pieces)])  28.3 us
    ppermute x14, starting transfers between devices, exchange(): return lax.ppermute(values, 'dap', [(q, q ^ offset) for q in range(pieces)])  8.38 us
    pallas_call x1, Pallas kernels, whole_block(): pl.pallas_call(triangle_kernel, out_shape=[wide(2, 128, LANES)] * 3 + [ar...  8.08 us
    all_to_all x1, starting transfers between devices, whole_block(): lax.all_to_all(blocks, 'dap', split_axis=0, concat_axis=0, tiled=True)  7.38 us
    unnamed x44, local copies, waits for them, and re-layouts  6.08 us
    pallas_call x1, Pallas kernels, whole_block(): pl.pallas_call(start_kernel, out_shape=[wide(*slabs), wide(*tall), wide(*...  5.59 us
    pallas_call x1, Pallas kernels, whole_block(): pl.pallas_call(msa_kernel, out_shape=(array(512, channels), array(256, LA...  4.11 us
    pallas_call x1, Pallas kernels, whole_block(): pl.pallas_call(finish_kernel, out_shape=array(256, LANES), in_specs=[vmem...  1.52 us
  transfers between devices with their start and end apart: 15, of which 9 were waited for; matrix products, arithmetic and copies ran while one was open for 2% of the time, Pallas kernels for 0%

profile of v9, /device:TPU:0, one launch (start us, length us, event | category | flops | bytes accessed | tf_op | source)
XLA Modules:
  0.0 72.9 jit_solution(8125898597945312971)
XLA Ops:
  0.6 0.9 %copy-done.1 = bf16[8,64,256]{2,1,0:T(8,128)(2,1)S(1)} copy-done((bf16[8,64,256]{2,1,0:T(8,128)(2,1)S(1)}, bf16[8,64,256]{2,1,0:T(8,128)(2,1)}, u32[]{:S(2)}) %copy-start.1) | copy-done | bytes 262168
  1.6 0.8 %copy-done.6 = bf16[4,64,128]{2,1,0:T(8,128)(2,1)S(1)} copy-done((bf16[4,64,128]{2,1,0:T(8,128)(2,1)S(1)}, bf16[4,64,128]{2,1,0:T(8,128)(2,1)}, u32[]{:S(2)}) %copy-start.6) | copy-done | bytes 65560
  2.4 1.1 %rows_by_device.1 = (bf16[16,32,256]{2,1,0:T(8,128)(2,1)}, bf16[2,128,128]{2,1,0:T(8,128)(2,1)S(1)}) custom-call(bf16[8,64,256]{2,1,0:T(8,128)(2,1)S(1)} %copy-done.1, bf16[4,64,128]{2,1,0:T(8,128)(2,1)S(1)} %copy-done.6), custom_call_target="tpu_custom_call" | custom-call | tf_op jit(solution)/shard_map/rows_by_device/pallas_call | solution.py:507
  3.6 7.4 %all-to-all-start = ((bf16[16,32,256]{2,1,0:T(8,128)(2,1)}), bf16[16,32,256]{2,1,0:T(8,128)(2,1)S(1)}, u32[]{:S(2)}, u32[]{:S(2)}) async-start(bf16[16,32,256]{2,1,0:T(8,128)(2,1)} %get-tuple-element.18), calls=%async_computation | async-start | bytes 524288 | tf_op jit(solution)/shard_map/all_to_all | solution.py:516
  11.0 2.8 %collective-permute-start = (bf16[2,128,128]{2,1,0:T(8,128)(2,1)S(1)}, bf16[2,128,128]{2,1,0:T(8,128)(2,1)S(1)}, u32[]{:S(2)}, u32[]{:S(2)}) collective-permute-start(bf16[2,128,128]{2,1,0:T(8,128)(2,1)S(1)} %get-tuple-element.19), channel_id=1, source_target_pairs={{0,8},{1,9},{2,10},{3,11},{4,12},{5,13},{6,14},{7,15},{8,0},{9,1},... | collective-permute-start | bytes 196616 | tf_op jit(solution)/shard_map/ppermute | solution.py:473
  13.8 9.6 %collective-permute-done = bf16[2,128,128]{2,1,0:T(8,128)(2,1)S(1)} collective-permute-done((bf16[2,128,128]{2,1,0:T(8,128)(2,1)S(1)}, bf16[2,128,128]{2,1,0:T(8,128)(2,1)S(1)}, u32[]{:S(2)}, u32[]{:S(2)}) %collective-permute-start) | collective-permute-done | bytes 65568 | tf_op jit(solution)/shard_map/ppermute | solution.py:473
  23.5 0.6 copy-done.21
  24.1 4.5 %collective-permute-done.1.rest_9_ = bf16[2,2,128,128]{3,2,1,0:T(8,128)(2,1)S(1)} collective-permute-done((bf16[2,2,128,128]{3,2,1,0:T(8,128)(2,1)S(1)}, bf16[2,2,128,128]{3,2,1,0:T(8,128)(2,1)S(1)}, u32[]{:S(2)}, u32[]{:S(2)}) %collective-permute-start.1) | collective-permute-done | bytes 131104 | tf_op jit(solution)/shard_map/ppermute | solution.py:473
  28.6 0.9 %copy-done.14 = bf16[256,512]{1,0:T(8,128)(2,1)S(1)} copy-done((bf16[256,512]{1,0:T(8,128)(2,1)S(1)}, bf16[256,512]{1,0:T(8,128)(2,1)}, u32[]{:S(2)}) %copy-start.14) | copy-done | bytes 262168
  29.5 0.9 %copy-done.15 = bf16[256,256]{1,0:T(8,128)(2,1)S(1)} copy-done((bf16[256,256]{1,0:T(8,128)(2,1)S(1)}, bf16[256,256]{1,0:T(8,128)(2,1)}, u32[]{:S(2)}) %copy-start.15) | copy-done | bytes 131096
  30.4 0.9 %copy-done.16 = bf16[256,256]{1,0:T(8,128)(2,1)S(1)} copy-done((bf16[256,256]{1,0:T(8,128)(2,1)S(1)}, bf16[256,256]{1,0:T(8,128)(2,1)}, u32[]{:S(2)}) %copy-start.16) | copy-done | bytes 131096
  31.3 0.9 %copy-done.17 = bf16[256,256]{1,0:T(8,128)(2,1)S(1)} copy-done((bf16[256,256]{1,0:T(8,128)(2,1)S(1)}, bf16[256,256]{1,0:T(8,128)(2,1)}, u32[]{:S(2)}) %copy-start.17) | copy-done | bytes 131096
  32.2 4.1 %msa_whole.1 = (bf16[512,256]{1,0:T(8,128)(2,1)S(1)}, bf16[256,128]{1,0:T(8,128)(2,1)S(1)}) custom-call(f32[1,128]{1,0:T(1,128)S(1)} %fusion.live_ref, bf16[16,32,256]{2,1,0:T(8,128)(2,1)S(1)} %all-to-all-done.blocks_ref, bf16[256,256]{1,0:T(8,128)(2,1)S(1)} %copy-done.15, bf16[256,256]{1,0:T(8,128)(2,1)S(1)} %copy-done.16, bf16[256,512]{1,0:T(8,128)(2,1)S(1)} %copy-done.14, ...), custom_call_target="tpu_custom_call" | custom-call | flops 2000000000 | bytes 10000000 | tf_op jit(solution)/shard_map/msa_whole/pallas_call | solution.py:523
  36.3 0.5 collective-permute-start.2
  36.8 5.2 %collective-permute-done.2 = bf16[256,128]{1,0:T(8,128)(2,1)S(1)} collective-permute-done((bf16[256,128]{1,0:T(8,128)(2,1)S(1)}, bf16[256,128]{1,0:T(8,128)(2,1)S(1)}, u32[]{:S(2)}, u32[]{:S(2)}) %collective-permute-start.2) | collective-permute-done | bytes 65568 | tf_op jit(solution)/shard_map/ppermute | solution.py:473
  42.1 1.5 %collective-permute-start.10 = (bf16[2,2,128,128]{3,2,1,0:T(8,128)(2,1)S(1)}, bf16[2,2,128,128]{3,2,1,0:T(8,128)(2,1)S(1)}, u32[]{:S(2)}, u32[]{:S(2)}) collective-permute-start(bf16[2,2,128,128]{3,2,1,0:T(8,128)(2,1)S(1)} %pad_maximum_fusion.rest_8_), channel_id=1, source_target_pairs={{0,2},{1,3},{2,0},{3,1},{4,6},{5,7},{6,4},{7,5},{8,10},{9,11},{10,... | collective-permute-start | bytes 393224 | tf_op jit(solution)/shard_map/ppermute | solution.py:473
  43.6 0.6 collective-permute-start.4
  44.2 2.9 %collective-permute-done.3.rest_1_ = bf16[2,256,128]{2,1,0:T(8,128)(2,1)S(1)} collective-permute-done((bf16[2,256,128]{2,1,0:T(8,128)(2,1)S(1)}, bf16[2,256,128]{2,1,0:T(8,128)(2,1)S(1)}, u32[]{:S(2)}, u32[]{:S(2)}) %collective-permute-start.3) | collective-permute-done | bytes 131104 | tf_op jit(solution)/shard_map/ppermute | solution.py:473
  47.1 1.4 %collective-permute-start.5 = (bf16[2,256,128]{2,1,0:T(8,128)(2,1)S(1)}, bf16[2,256,128]{2,1,0:T(8,128)(2,1)S(1)}, u32[]{:S(2)}, u32[]{:S(2)}) collective-permute-start(bf16[2,256,128]{2,1,0:T(8,128)(2,1)S(1)} %collective-permute-done.3.rest_1_), channel_id=1, source_target_pairs={{0,2},{1,3},{2,0},{3,1},{4,6},{5,7},{6,4},{7,5},{8,10},{9,11},{10,... | collective-permute-start | bytes 393224 | tf_op jit(solution)/shard_map/ppermute | solution.py:473
  48.9 0.6 collective-permute-start.11
  49.5 0.5 collective-permute-start.7
  50.0 0.8 %collective-permute-done.4.rest_2_ = bf16[2,256,128]{2,1,0:T(8,128)(2,1)S(1)} collective-permute-done((bf16[2,256,128]{2,1,0:T(8,128)(2,1)S(1)}, bf16[2,256,128]{2,1,0:T(8,128)(2,1)S(1)}, u32[]{:S(2)}, u32[]{:S(2)}) %collective-permute-start.4) | collective-permute-done | bytes 131104 | tf_op jit(solution)/shard_map/ppermute | solution.py:473
  50.8 2.0 %collective-permute-done.5.rest_3_ = bf16[2,256,128]{2,1,0:T(8,128)(2,1)S(1)} collective-permute-done((bf16[2,256,128]{2,1,0:T(8,128)(2,1)S(1)}, bf16[2,256,128]{2,1,0:T(8,128)(2,1)S(1)}, u32[]{:S(2)}, u32[]{:S(2)}) %collective-permute-start.5) | collective-permute-done | bytes 131104 | tf_op jit(solution)/shard_map/ppermute | solution.py:473
  52.8 0.2 compare_select_fusion
  53.1 1.1 %collective-permute-done.11.rest_11_ = bf16[2,2,128,128]{3,2,1,0:T(8,128)(2,1)S(1)} collective-permute-done((bf16[2,2,128,128]{3,2,1,0:T(8,128)(2,1)S(1)}, bf16[2,2,128,128]{3,2,1,0:T(8,128)(2,1)S(1)}, u32[]{:S(2)}, u32[]{:S(2)}) %collective-permute-start.11) | collective-permute-done | bytes 131104 | tf_op jit(solution)/shard_map/ppermute | solution.py:473
  54.3 5.6 %pair_start.1 = (f32[16,128,128]{2,1,0:T(8,128)S(1)}, f32[2048,128]{1,0:T(8,128)S(1)}, f32[16,128,128]{2,1,0:T(8,128)S(1)}, bf16[2048,128]{1,0:T(8,128)(2,1)S(1)}) custom-call(s32[1]{0:T(128)} %bitcast.4.place_ref, f32[1,128]{1,0:T(1,128)S(1)} %fusion.live_ref, s32[32,128]{1,0:T(8,128)S(1)} %select_n.11.bins_ref, bf16[66,128]{1,0:T(8,128)(2,1)S(1)} %copy-done.11, ...), custom_call_target="tpu_custom_call" | custom-call | tf_op jit(solution)/shard_map/pair_start/pallas_call | solution.py:556
  60.0 1.9 %collective-permute-done.12.right_other_ref = bf16[2048,128]{1,0:T(8,128)(2,1)S(1)} collective-permute-done((bf16[2048,128]{1,0:T(8,128)(2,1)S(1)}, bf16[2048,128]{1,0:T(8,128)(2,1)S(1)}, u32[]{:S(2)}, u32[]{:S(2)}) %collective-permute-start.12) | collective-permute-done | bytes 524320 | tf_op jit(solution)/shard_map/ppermute | solution.py:473
  61.9 8.1 %pair_triangles.1 = (f32[2,128,128]{2,1,0:T(8,128)S(1)}, f32[2,128,128]{2,1,0:T(8,128)S(1)}, f32[2,128,128]{2,1,0:T(8,128)S(1)}, bf16[768,128]{1,0:T(8,128)(2,1)S(1)}, bf16[128,512]{1,0:T(8,128)(2,1)S(1)}) custom-call(s32[1]{0:T(128)} %bitcast.4.place_ref, f32[16,128,128]{2,1,0:T(8,128)S(1)} %get-tuple-element.25.pair_mid_ref, ...), custom_call_target="tpu_custom_call" | custom-call | tf_op jit(solution)/shard_map/pair_triangles/pallas_call | solution.py:584
  70.0 0.2 collective-permute-start.13
  70.2 0.8 %reshape.59 = bf16[128,4,256]{2,1,0:T(4,128)(2,1)} reshape(bf16[512,256]{1,0:T(8,128)(2,1)S(1)} %get-tuple-element.21) | data formatting | bytes 524288 | tf_op jit(solution)/shard_map/reshape | solution.py:610
  71.0 0.5 collective-permute-done.13.other_part_ref
  71.4 1.5 %pair_finish.1 = bf16[256,128]{1,0:T(8,128)(2,1)} custom-call(f32[2,128,128]{2,1,0:T(8,128)S(1)} %get-tuple-element.29.own_pair_ref, f32[2,128,128]{2,1,0:T(8,128)S(1)} %get-tuple-element.30.own_part_ref, f32[2,128,128]{2,1,0:T(8,128)S(1)} %collective-permute-done.13.other_part_ref, bf16[768,128]{1,0:T(8,128)(2,1)S(1)} %get-tuple-element.32.narrow_ref, ...), custom_call_target="tpu_custom_call" | custom-call | tf_op jit(solution)/shard_map/pair_finish/pallas_call | solution.py:602
  (57 shorter events, 0.9 us)
Async XLA Ops:
  0.6 1.0 %copy-start.1 = (bf16[8,64,256]{2,1,0:T(8,128)(2,1)S(1)}, bf16[8,64,256]{2,1,0:T(8,128)(2,1)}, u32[]{:S(2)}) copy-start(bf16[8,64,256]{2,1,0:T(8,128)(2,1)} %rows_ref.1) | copy-start | bytes 786436
  2.4 26.1 %copy-start.12 = (bf16[256,1024]{1,0:T(8,128)(2,1)S(1)}, bf16[256,1024]{1,0:T(8,128)(2,1)}, u32[]{:S(2)}) copy-start(bf16[256,1024]{1,0:T(8,128)(2,1)} %up_ref.1) | copy-start | bytes 1572868
  2.4 26.1 %copy-start.13 = (bf16[1024,256]{1,0:T(8,128)(2,1)S(1)}, bf16[1024,256]{1,0:T(8,128)(2,1)}, u32[]{:S(2)}) copy-start(bf16[1024,256]{1,0:T(8,128)(2,1)} %down_ref.1) | copy-start | bytes 1572868
  3.6 25.0 %all-to-all-start = ((bf16[16,32,256]{2,1,0:T(8,128)(2,1)}), bf16[16,32,256]{2,1,0:T(8,128)(2,1)S(1)}, u32[]{:S(2)}, u32[]{:S(2)}) async-start(bf16[16,32,256]{2,1,0:T(8,128)(2,1)} %get-tuple-element.18), calls=%async_computation | async-start | bytes 524288 | tf_op jit(solution)/shard_map/all_to_all | solution.py:516
  11.0 12.5 %collective-permute-start = (bf16[2,128,128]{2,1,0:T(8,128)(2,1)S(1)}, bf16[2,128,128]{2,1,0:T(8,128)(2,1)S(1)}, u32[]{:S(2)}, u32[]{:S(2)}) collective-permute-start(bf16[2,128,128]{2,1,0:T(8,128)(2,1)S(1)} %get-tuple-element.19), channel_id=1, source_target_pairs={{0,8},{1,9},{2,10},{3,11},{4,12},{5,13},{6,14},{7,15},{8,0},{9,1},... | collective-permute-start | bytes 196616 | tf_op jit(solution)/shard_map/ppermute | solution.py:473
  23.4 5.1 %copy-start.18 = (bf16[256,64]{0,1:T(8,128)(2,1)S(1)}, bf16[256,64]{0,1:T(8,128)(2,1)}, u32[]{:S(2)}) copy-start(bf16[256,64]{0,1:T(8,128)(2,1)} %param.34) | copy-start | bytes 98308
  23.4 5.1 %collective-permute-start.1 = (bf16[2,2,128,128]{3,2,1,0:T(8,128)(2,1)S(1)}, bf16[2,2,128,128]{3,2,1,0:T(8,128)(2,1)S(1)}, u32[]{:S(2)}, u32[]{:S(2)}) collective-permute-start(bf16[2,2,128,128]{3,2,1,0:T(8,128)(2,1)S(1)} %pad_maximum_fusion.rest_8_), channel_id=1, source_target_pairs={{0,4},{1,5},{2,6},{3,7},{4,0},{5,1},{6,2},{7,3},{8,12},{9,13},{10,... | collective-permute-start | bytes 393224 | tf_op jit(solution)/shard_map/ppermute | solution.py:473
  28.6 1.0 %copy-start.14 = (bf16[256,512]{1,0:T(8,128)(2,1)S(1)}, bf16[256,512]{1,0:T(8,128)(2,1)}, u32[]{:S(2)}) copy-start(bf16[256,512]{1,0:T(8,128)(2,1)} %value_gate_ref.1) | copy-start | bytes 786436
  36.3 17.9 %copy-start = (bf16[1024,128]{1,0:T(8,128)(2,1)S(1)}, bf16[1024,128]{1,0:T(8,128)(2,1)}, u32[]{:S(2)}) copy-start(bf16[1024,128]{1,0:T(8,128)(2,1)} %rest_12_.1) | copy-start | bytes 786436
  36.3 5.7 %collective-permute-start.2 = (bf16[256,128]{1,0:T(8,128)(2,1)S(1)}, bf16[256,128]{1,0:T(8,128)(2,1)S(1)}, u32[]{:S(2)}, u32[]{:S(2)}) collective-permute-start(bf16[256,128]{1,0:T(8,128)(2,1)S(1)} %get-tuple-element.22), channel_id=1, source_target_pairs={{0,8},{1,9},{2,10},{3,11},{4,12},{5,13},{6,14},{7,15},{8,0},{9,1},... | collective-permute-start | bytes 196616 | tf_op jit(solution)/shard_map/ppermute | solution.py:473
  42.0 6.5 %copy-start.19 = (s32[64]{0:T(128)S(1)}, s32[64]{0:T(128)}, u32[]{:S(2)}) copy-start(s32[64]{0:T(128)} %param.24) | copy-start | bytes 772
  42.0 6.7 %copy-start.20 = (s32[64]{0:T(128)S(1)}, s32[64]{0:T(128)}, u32[]{:S(2)}) copy-start(s32[64]{0:T(128)} %param.25) | copy-start | bytes 772
  42.0 12.2 %copy-start.2 = (bf16[128,512]{1,0:T(8,128)(2,1)S(1)}, bf16[128,512]{1,0:T(8,128)(2,1)}, u32[]{:S(2)}) copy-start(bf16[128,512]{1,0:T(8,128)(2,1)} %rest_13_.1) | copy-start | bytes 393220
  42.0 5.0 %collective-permute-start.3 = (bf16[2,256,128]{2,1,0:T(8,128)(2,1)S(1)}, bf16[2,256,128]{2,1,0:T(8,128)(2,1)S(1)}, u32[]{:S(2)}, u32[]{:S(2)}) collective-permute-start(bf16[2,256,128]{2,1,0:T(8,128)(2,1)S(1)} %pad_maximum_fusion.1.rest_0_), channel_id=1, source_target_pairs={{0,4},{1,5},{2,6},{3,7},{4,0},{5,1},{6,2},{7,3},{8,12},{9,13},{10,... | collective-permute-start | bytes 393224 | tf_op jit(solution)/shard_map/ppermute | solution.py:473
  42.1 7.4 %collective-permute-start.10 = (bf16[2,2,128,128]{3,2,1,0:T(8,128)(2,1)S(1)}, bf16[2,2,128,128]{3,2,1,0:T(8,128)(2,1)S(1)}, u32[]{:S(2)}, u32[]{:S(2)}) collective-permute-start(bf16[2,2,128,128]{3,2,1,0:T(8,128)(2,1)S(1)} %pad_maximum_fusion.rest_8_), channel_id=1, source_target_pairs={{0,2},{1,3},{2,0},{3,1},{4,6},{5,7},{6,4},{7,5},{8,10},{9,11},{10,... | collective-permute-start | bytes 393224 | tf_op jit(solution)/shard_map/ppermute | solution.py:473
  43.6 7.2 %collective-permute-start.4 = (bf16[2,256,128]{2,1,0:T(8,128)(2,1)S(1)}, bf16[2,256,128]{2,1,0:T(8,128)(2,1)S(1)}, u32[]{:S(2)}, u32[]{:S(2)}) collective-permute-start(bf16[2,256,128]{2,1,0:T(8,128)(2,1)S(1)} %pad_maximum_fusion.1.rest_0_), channel_id=1, source_target_pairs={{0,2},{1,3},{2,0},{3,1},{4,6},{5,7},{6,4},{7,5},{8,10},{9,11},{10,... | collective-permute-start | bytes 393224 | tf_op jit(solution)/shard_map/ppermute | solution.py:473
  47.1 5.7 %collective-permute-start.5 = (bf16[2,256,128]{2,1,0:T(8,128)(2,1)S(1)}, bf16[2,256,128]{2,1,0:T(8,128)(2,1)S(1)}, u32[]{:S(2)}, u32[]{:S(2)}) collective-permute-start(bf16[2,256,128]{2,1,0:T(8,128)(2,1)S(1)} %collective-permute-done.3.rest_1_), channel_id=1, source_target_pairs={{0,2},{1,3},{2,0},{3,1},{4,6},{5,7},{6,4},{7,5},{8,10},{9,11},{10,... | collective-permute-start | bytes 393224 | tf_op jit(solution)/shard_map/ppermute | solution.py:473
  48.9 5.3 %collective-permute-start.11 = (bf16[2,2,128,128]{3,2,1,0:T(8,128)(2,1)S(1)}, bf16[2,2,128,128]{3,2,1,0:T(8,128)(2,1)S(1)}, u32[]{:S(2)}, u32[]{:S(2)}) collective-permute-start(bf16[2,2,128,128]{3,2,1,0:T(8,128)(2,1)S(1)} %collective-permute-done.1.rest_9_), channel_id=1, source_target_pairs={{0,2},{1,3},{2,0},{3,1},{4,6},{5,7},{6,4},{7,5},{8,10},{9,11},{10,... | collective-permute-start | bytes 393224 | tf_op jit(solution)/shard_map/ppermute | solution.py:473
  49.5 4.7 %collective-permute-start.6 = (bf16[2,256,128]{2,1,0:T(8,128)(2,1)S(1)}, bf16[2,256,128]{2,1,0:T(8,128)(2,1)S(1)}, u32[]{:S(2)}, u32[]{:S(2)}) collective-permute-start(bf16[2,256,128]{2,1,0:T(8,128)(2,1)S(1)} %pad_maximum_fusion.1.rest_0_), channel_id=1, source_target_pairs={{0,1},{1,0},{2,3},{3,2},{4,5},{5,4},{6,7},{7,6},{8,9},{9,8},{10,11... | collective-permute-start | bytes 393224 | tf_op jit(solution)/shard_map/ppermute | solution.py:473
  49.5 4.7 %collective-permute-start.7 = (bf16[2,256,128]{2,1,0:T(8,128)(2,1)S(1)}, bf16[2,256,128]{2,1,0:T(8,128)(2,1)S(1)}, u32[]{:S(2)}, u32[]{:S(2)}) collective-permute-start(bf16[2,256,128]{2,1,0:T(8,128)(2,1)S(1)} %collective-permute-done.3.rest_1_), channel_id=1, source_target_pairs={{0,1},{1,0},{2,3},{3,2},{4,5},{5,4},{6,7},{7,6},{8,9},{9,8},{10,11... | collective-permute-start | bytes 393224 | tf_op jit(solution)/shard_map/ppermute | solution.py:473
  50.8 3.4 %collective-permute-start.8 = (bf16[2,256,128]{2,1,0:T(8,128)(2,1)S(1)}, bf16[2,256,128]{2,1,0:T(8,128)(2,1)S(1)}, u32[]{:S(2)}, u32[]{:S(2)}) collective-permute-start(bf16[2,256,128]{2,1,0:T(8,128)(2,1)S(1)} %collective-permute-done.4.rest_2_), channel_id=1, source_target_pairs={{0,1},{1,0},{2,3},{3,2},{4,5},{5,4},{6,7},{7,6},{8,9},{9,8},{10,11... | collective-permute-start | bytes 393224 | tf_op jit(solution)/shard_map/ppermute | solution.py:473
  52.8 1.4 %collective-permute-start.9 = (bf16[2,256,128]{2,1,0:T(8,128)(2,1)S(1)}, bf16[2,256,128]{2,1,0:T(8,128)(2,1)S(1)}, u32[]{:S(2)}, u32[]{:S(2)}) collective-permute-start(bf16[2,256,128]{2,1,0:T(8,128)(2,1)S(1)} %collective-permute-done.5.rest_3_), channel_id=1, source_target_pairs={{0,1},{1,0},{2,3},{3,2},{4,5},{5,4},{6,7},{7,6},{8,9},{9,8},{10,11... | collective-permute-start | bytes 393224 | tf_op jit(solution)/shard_map/ppermute | solution.py:473
  53.0 1.2 %copy-start.7 = (bf16[128,128]{1,0:T(8,128)(2,1)S(1)}, bf16[128,128]{1,0:T(8,128)(2,1)}, u32[]{:S(2)}) copy-start(bf16[128,128]{1,0:T(8,128)(2,1)} %rest_14_.1) | copy-start | bytes 98308
  53.0 1.2 %copy-start.11 = (bf16[66,128]{1,0:T(8,128)(2,1)S(1)}, bf16[66,128]{1,0:T(8,128)(2,1)}, u32[]{:S(2)}) copy-start(bf16[66,128]{1,0:T(8,128)(2,1)} %table_ref.1) | copy-start | bytes 50692
  54.2 7.6 %copy-start.3 = (bf16[128,512]{1,0:T(8,128)(2,1)S(1)}, bf16[128,512]{1,0:T(8,128)(2,1)}, u32[]{:S(2)}) copy-start(bf16[128,512]{1,0:T(8,128)(2,1)} %rest_1_.1) | copy-start | bytes 393220
  54.3 7.6 %copy-start.4 = (bf16[128,512]{1,0:T(8,128)(2,1)S(1)}, bf16[128,512]{1,0:T(8,128)(2,1)}, u32[]{:S(2)}) copy-start(bf16[128,512]{1,0:T(8,128)(2,1)} %rest_4_.1) | copy-start | bytes 393220
  54.3 7.6 %copy-start.5 = (bf16[512,128]{1,0:T(8,128)(2,1)S(1)}, bf16[512,128]{1,0:T(8,128)(2,1)}, u32[]{:S(2)}) copy-start(bf16[512,128]{1,0:T(8,128)(2,1)} %rest_5_.1) | copy-start | bytes 393220
  54.3 7.6 %copy-start.8 = (bf16[128,128]{1,0:T(8,128)(2,1)S(1)}, bf16[128,128]{1,0:T(8,128)(2,1)}, u32[]{:S(2)}) copy-start(bf16[128,128]{1,0:T(8,128)(2,1)} %rest_0_.1) | copy-start | bytes 98308
  54.3 7.6 %copy-start.9 = (bf16[128,128]{1,0:T(8,128)(2,1)S(1)}, bf16[128,128]{1,0:T(8,128)(2,1)}, u32[]{:S(2)}) copy-start(bf16[128,128]{1,0:T(8,128)(2,1)} %rest_2_.1) | copy-start | bytes 98308
  54.3 7.6 %copy-start.10 = (bf16[128,128]{1,0:T(8,128)(2,1)S(1)}, bf16[128,128]{1,0:T(8,128)(2,1)}, u32[]{:S(2)}) copy-start(bf16[128,128]{1,0:T(8,128)(2,1)} %rest_3_.1) | copy-start | bytes 98308
  59.9 2.0 %collective-permute-start.12 = (bf16[2048,128]{1,0:T(8,128)(2,1)S(1)}, bf16[2048,128]{1,0:T(8,128)(2,1)S(1)}, u32[]{:S(2)}, u32[]{:S(2)}) collective-permute-start(bf16[2048,128]{1,0:T(8,128)(2,1)S(1)} %get-tuple-element.28.right_own_ref), channel_id=1, source_target_pairs={{0,1},{1,0},{2,3},{3,2},{4,5},{5,4},{6,7},{7,6},{8,9},{9,8},{10,11... | collective-permute-start | bytes 1572872 | tf_op jit(solution)/shard_map/ppermute | solution.py:473
  70.0 1.4 %collective-permute-start.13 = (f32[2,128,128]{2,1,0:T(8,128)S(1)}, f32[2,128,128]{2,1,0:T(8,128)S(1)}, u32[]{:S(2)}, u32[]{:S(2)}) collective-permute-start(f32[2,128,128]{2,1,0:T(8,128)S(1)} %get-tuple-element.31), channel_id=1, source_target_pairs={{0,1},{1,0},{2,3},{3,2},{4,5},{5,4},{6,7},{7,6},{8,9},{9,8},{10,11... | collective-permute-start | bytes 393224 | tf_op jit(solution)/shard_map/ppermute | solution.py:473
  (5 other events, 4.2 us)

commit v10 on v9

--- a/solution.py
+++ b/solution.py
@@ -422,7 +422,10 @@
     wide_ref,
     attended_ref,
     final_ref,
+    *landed,
 ):
+    copies = start_copies((output_ref, up_ref, down_ref), landed, landed[3])
+    output_ref, up_ref, down_ref = landed[:3]
     for p in range(16):
         block = blocks_ref[p].astype(jnp.float32)
         for i in range(4):
@@ -453,6 +456,8 @@
         raised = jnp.concatenate(raised, axis=1)
         attended_ref[rows, :] = mix(raised, by_head(value[rows])) / mix(raised, heads)
     gated = (gate_curve(value_gate[:, width:]) * attended_ref[...]).astype(jnp.bfloat16)
+    for copy in copies:
+        copy.wait()
     current = wide_ref[...] + mix(gated, output_ref[...])
     hidden = jnp.maximum(mix(normalize_rows(current), up_ref[...]), 0.0).astype(jnp.bfloat16)
     final = (current + mix(hidden, down_ref[...])).astype(jnp.bfloat16).astype(jnp.float32)
@@ -523,14 +528,18 @@
     result, parts = pl.pallas_call(
         msa_kernel,
         out_shape=(array(512, channels), array(256, LANES)),
-        in_specs=[vmem] * 9,
+        in_specs=[vmem] * 5 + [hbm] * 3 + [vmem],
         out_specs=(vmem, vmem),
         scratch_shapes=[
             pltpu.VMEM((512, channels), jnp.float32),
             pltpu.VMEM((512, channels), jnp.float32),
             pltpu.VMEM((1024, LANES), jnp.float32),
+            pltpu.VMEM(column_output_weight.shape, jnp.bfloat16),
+            pltpu.VMEM(alignment_transition_up.shape, jnp.bfloat16),
+            pltpu.VMEM(alignment_transition_down.shape, jnp.bfloat16),
+            pltpu.SemaphoreType.DMA((3,)),
         ],
-        compiler_params=limit(32),
+        compiler_params=limit(54),
         cost_estimate=pl.CostEstimate(
             flops=2_000_000_000, bytes_accessed=10_000_000, transcendentals=1_000_000
         ),
@@ -546,6 +555,7 @@
         alignment_transition_down,
         outer_input_weight.T,
     )
+    parts, pair_pieces = lax.optimization_barrier((parts, pair_pieces))
     first = jnp.stack([parts, exchange(parts, 8)])
     second = exchange(first, 4)
     pieces = [first, second, exchange(first, 2), exchange(second, 2)]

time: 73.4 us -> 74.1 us (level)
  local copies, waits for them, and re-layouts: 7.31 us -> 3.66 us
  Pallas kernels: 20.4 us -> 22.6 us
  other arithmetic: 0.23 us -> 1.6 us
  starting transfers between devices: 15.8 us -> 16.8 us
    unnamed x44 -> x36, local copies, waits for them, and re-layouts: 6.08 us -> 2.42 us
    pallas_call x1, Pallas kernels: 4.11 us -> 6.1 us  [whole_block(): pl.pallas_call(msa_kernel, out_shape=(array(512, channels), array(256, LA...]
    ppermute x14, starting transfers between devices: 8.38 us -> 9.44 us  [exchange(): return lax.ppermute(values, 'dap', [(q, q ^ offset) for q in range(pieces)])]
    another operation x1, other arithmetic: 0.01 us -> 0.88 us  [whole_block(): first = jnp.stack([parts, exchange(parts, 8)])]
  transfers between devices with their start and end apart: 15 -> 15, of which waited for: 9 -> 8; matrix products, arithmetic and copies ran while one was open for 2% -> 3% of each run, Pallas kernels for 0% -> 8%
where the time goes in v10:
time: 74.1 us; the launch traced here: 73.7 us
  waiting for transfers between devices  28.2 us (38%)
  Pallas kernels  22.6 us (30%)
  starting transfers between devices  16.8 us (23%)
  local copies, waits for them, and re-layouts  3.66 us (5%)
  other arithmetic  1.6 us (2%)
  between operations  0.91 us (1%)
    ppermute x14, waiting for transfers between devices, exchange(): return lax.ppermute(values, 'dap', [(q, q ^ offset) for q in range(pieces)])  28.2 us
    ppermute x14, starting transfers between devices, exchange(): return lax.ppermute(values, 'dap', [(q, q ^ offset) for q in range(pieces)])  9.44 us
    pallas_call x1, Pallas kernels, whole_block(): pl.pallas_call(triangle_kernel, out_shape=[wide(2, 128, LANES)] * 3 + [ar...  8.25 us
    all_to_all x1, starting transfers between devices, whole_block(): lax.all_to_all(blocks, 'dap', split_axis=0, concat_axis=0, tiled=True)  7.39 us
    pallas_call x1, Pallas kernels, whole_block(): pl.pallas_call(msa_kernel, out_shape=(array(512, channels), array(256, LA...  6.1 us
    pallas_call x1, Pallas kernels, whole_block(): pl.pallas_call(start_kernel, out_shape=[wide(*slabs), wide(*tall), wide(*...  5.58 us
    unnamed x36, local copies, waits for them, and re-layouts  2.42 us
    pallas_call x1, Pallas kernels, whole_block(): pl.pallas_call(finish_kernel, out_shape=array(256, LANES), in_specs=[vmem...  1.52 us
  transfers between devices with their start and end apart: 15, of which 8 were waited for; matrix products, arithmetic and copies ran while one was open for 3% of the time, Pallas kernels for 8%

profile of v10, /device:TPU:0, one launch (start us, length us, event | category | flops | bytes accessed | tf_op | source)
XLA Modules:
  0.0 73.7 jit_solution(7529379448838423007)
XLA Ops:
  0.6 0.9 %copy-done.1 = bf16[8,64,256]{2,1,0:T(8,128)(2,1)S(1)} copy-done((bf16[8,64,256]{2,1,0:T(8,128)(2,1)S(1)}, bf16[8,64,256]{2,1,0:T(8,128)(2,1)}, u32[]{:S(2)}) %copy-start.1) | copy-done | bytes 262168
  1.6 0.8 %copy-done.6 = bf16[4,64,128]{2,1,0:T(8,128)(2,1)S(1)} copy-done((bf16[4,64,128]{2,1,0:T(8,128)(2,1)S(1)}, bf16[4,64,128]{2,1,0:T(8,128)(2,1)}, u32[]{:S(2)}) %copy-start.6) | copy-done | bytes 65560
  2.4 1.1 %rows_by_device.1 = (bf16[16,32,256]{2,1,0:T(8,128)(2,1)}, bf16[2,128,128]{2,1,0:T(8,128)(2,1)S(1)}) custom-call(bf16[8,64,256]{2,1,0:T(8,128)(2,1)S(1)} %copy-done.1, bf16[4,64,128]{2,1,0:T(8,128)(2,1)S(1)} %copy-done.6), custom_call_target="tpu_custom_call" | custom-call | tf_op jit(solution)/shard_map/rows_by_device/pallas_call | solution.py:512
  3.6 7.4 %all-to-all-start = ((bf16[16,32,256]{2,1,0:T(8,128)(2,1)}), bf16[16,32,256]{2,1,0:T(8,128)(2,1)S(1)}, u32[]{:S(2)}, u32[]{:S(2)}) async-start(bf16[16,32,256]{2,1,0:T(8,128)(2,1)} %get-tuple-element.23), calls=%async_computation | async-start | bytes 524288 | tf_op jit(solution)/shard_map/all_to_all | solution.py:521
  10.9 2.8 %collective-permute-start = (bf16[2,128,128]{2,1,0:T(8,128)(2,1)S(1)}, bf16[2,128,128]{2,1,0:T(8,128)(2,1)S(1)}, u32[]{:S(2)}, u32[]{:S(2)}) collective-permute-start(bf16[2,128,128]{2,1,0:T(8,128)(2,1)S(1)} %get-tuple-element.24), channel_id=1, source_target_pairs={{0,8},{1,9},{2,10},{3,11},{4,12},{5,13},{6,14},{7,15},{8,0},{9,1},... | collective-permute-start | bytes 196616 | tf_op jit(solution)/shard_map/ppermute | solution.py:478
  13.8 9.6 %collective-permute-done = bf16[2,128,128]{2,1,0:T(8,128)(2,1)S(1)} collective-permute-done((bf16[2,128,128]{2,1,0:T(8,128)(2,1)S(1)}, bf16[2,128,128]{2,1,0:T(8,128)(2,1)S(1)}, u32[]{:S(2)}, u32[]{:S(2)}) %collective-permute-start) | collective-permute-done | bytes 65568 | tf_op jit(solution)/shard_map/ppermute | solution.py:478
  23.5 0.6 copy-done.17
  24.1 0.5 fusion.live_ref
  24.6 4.0 %collective-permute-done.1.rest_9_ = bf16[2,2,128,128]{3,2,1,0:T(8,128)(2,1)S(1)} collective-permute-done((bf16[2,2,128,128]{3,2,1,0:T(8,128)(2,1)S(1)}, bf16[2,2,128,128]{3,2,1,0:T(8,128)(2,1)S(1)}, u32[]{:S(2)}, u32[]{:S(2)}) %collective-permute-start.1) | collective-permute-done | bytes 131104 | tf_op jit(solution)/shard_map/ppermute | solution.py:478
  28.5 1.5 %collective-permute-start.2 = (bf16[2,2,128,128]{3,2,1,0:T(8,128)(2,1)S(1)}, bf16[2,2,128,128]{3,2,1,0:T(8,128)(2,1)S(1)}, u32[]{:S(2)}, u32[]{:S(2)}) collective-permute-start(bf16[2,2,128,128]{3,2,1,0:T(8,128)(2,1)S(1)} %pad_maximum_fusion.rest_8_), channel_id=1, source_target_pairs={{0,2},{1,3},{2,0},{3,1},{4,6},{5,7},{6,4},{7,5},{8,10},{9,11},{10,... | collective-permute-start | bytes 393224 | tf_op jit(solution)/shard_map/ppermute | solution.py:478
  30.0 0.6 collective-permute-start.3
  30.6 6.1 %msa_whole.1 = (bf16[512,256]{1,0:T(8,128)(2,1)}, bf16[256,128]{1,0:T(8,128)(2,1)}) custom-call(f32[1,128]{1,0:T(1,128)} %fusion.live_ref, bf16[16,32,256]{2,1,0:T(8,128)(2,1)} %copy-done.14, bf16[256,256]{1,0:T(8,128)(2,1)} %query_ref.1, bf16[256,256]{1,0:T(8,128)(2,1)} %key_ref.1, bf16[256,512]{1,0:T(8,128)(2,1)} %value_gate_ref.1, ...), custom_call_target="tpu_custom_call" | custom-call | flops 2000000000 | bytes 10000000 | tf_op jit(solution)/shard_map/msa_whole/pallas_call | solution.py:528
  36.7 0.5 collective-permute-start.4
  37.2 5.4 %collective-permute-done.4 = bf16[256,128]{1,0:T(8,128)(2,1)S(1)} collective-permute-done((bf16[256,128]{1,0:T(8,128)(2,1)}, bf16[256,128]{1,0:T(8,128)(2,1)S(1)}, u32[]{:S(2)}, u32[]{:S(2)}) %collective-permute-start.4) | collective-permute-done | bytes 65568 | tf_op jit(solution)/shard_map/ppermute | solution.py:478
  42.6 0.9 %pad_maximum_fusion.1.rest_0_ = bf16[2,256,128]{2,1,0:T(8,128)(2,1)S(1)} fusion(bf16[1,256,128]{2,1,0:T(8,128)(2,1)S(1)} %bitcast.17, bf16[1,256,128]{2,1,0:T(8,128)(2,1)} %bitcast.15), kind=kLoop, calls=%fused_computation.1 | loop fusion | flops 65536 | bytes 262144 | tf_op jit(solution)/shard_map/stack | solution.py:559
  43.5 1.5 %collective-permute-start.6 = (bf16[2,256,128]{2,1,0:T(8,128)(2,1)S(1)}, bf16[2,256,128]{2,1,0:T(8,128)(2,1)S(1)}, u32[]{:S(2)}, u32[]{:S(2)}) collective-permute-start(bf16[2,256,128]{2,1,0:T(8,128)(2,1)S(1)} %pad_maximum_fusion.1.rest_0_), channel_id=1, source_target_pairs={{0,2},{1,3},{2,0},{3,1},{4,6},{5,7},{6,4},{7,5},{8,10},{9,11},{10,... | collective-permute-start | bytes 393224 | tf_op jit(solution)/shard_map/ppermute | solution.py:478
  45.1 3.4 %collective-permute-done.5.rest_1_ = bf16[2,256,128]{2,1,0:T(8,128)(2,1)S(1)} collective-permute-done((bf16[2,256,128]{2,1,0:T(8,128)(2,1)S(1)}, bf16[2,256,128]{2,1,0:T(8,128)(2,1)S(1)}, u32[]{:S(2)}, u32[]{:S(2)}) %collective-permute-start.5) | collective-permute-done | bytes 131104 | tf_op jit(solution)/shard_map/ppermute | solution.py:478
  48.5 1.5 %collective-permute-start.7 = (bf16[2,256,128]{2,1,0:T(8,128)(2,1)S(1)}, bf16[2,256,128]{2,1,0:T(8,128)(2,1)S(1)}, u32[]{:S(2)}, u32[]{:S(2)}) collective-permute-start(bf16[2,256,128]{2,1,0:T(8,128)(2,1)S(1)} %collective-permute-done.5.rest_1_), channel_id=1, source_target_pairs={{0,2},{1,3},{2,0},{3,1},{4,6},{5,7},{6,4},{7,5},{8,10},{9,11},{10,... | collective-permute-start | bytes 393224 | tf_op jit(solution)/shard_map/ppermute | solution.py:478
  50.1 0.1 eq.22
  50.4 0.5 collective-permute-start.9
  50.9 2.5 %collective-permute-done.7.rest_3_ = bf16[2,256,128]{2,1,0:T(8,128)(2,1)S(1)} collective-permute-done((bf16[2,256,128]{2,1,0:T(8,128)(2,1)S(1)}, bf16[2,256,128]{2,1,0:T(8,128)(2,1)S(1)}, u32[]{:S(2)}, u32[]{:S(2)}) %collective-permute-start.7) | collective-permute-done | bytes 131104 | tf_op jit(solution)/shard_map/ppermute | solution.py:478
  53.5 0.2 compare_select_fusion
  53.7 0.1 select_n.11.bins_ref
  53.8 1.0 %collective-permute-done.11.rest_7_ = bf16[2,256,128]{2,1,0:T(8,128)(2,1)S(1)} collective-permute-done((bf16[2,256,128]{2,1,0:T(8,128)(2,1)S(1)}, bf16[2,256,128]{2,1,0:T(8,128)(2,1)S(1)}, u32[]{:S(2)}, u32[]{:S(2)}) %collective-permute-start.11) | collective-permute-done | bytes 131104 | tf_op jit(solution)/shard_map/ppermute | solution.py:478
  54.9 5.6 %pair_start.1 = (f32[16,128,128]{2,1,0:T(8,128)S(1)}, f32[2048,128]{1,0:T(8,128)S(1)}, f32[16,128,128]{2,1,0:T(8,128)S(1)}, bf16[2048,128]{1,0:T(8,128)(2,1)S(1)}) custom-call(s32[1]{0:T(128)} %bitcast.4.place_ref, f32[1,128]{1,0:T(1,128)S(1)} %copy-done.12, s32[32,128]{1,0:T(8,128)S(1)} %select_n.11.bins_ref, bf16[66,128]{1,0:T(8,128)(2,1)S(1)} %copy-done.11, ...), custom_call_target="tpu_custom_call" | custom-call | tf_op jit(solution)/shard_map/pair_start/pallas_call | solution.py:566
  60.5 0.2 collective-permute-start.12
  60.7 1.8 %collective-permute-done.12.right_other_ref = bf16[2048,128]{1,0:T(8,128)(2,1)S(1)} collective-permute-done((bf16[2048,128]{1,0:T(8,128)(2,1)S(1)}, bf16[2048,128]{1,0:T(8,128)(2,1)S(1)}, u32[]{:S(2)}, u32[]{:S(2)}) %collective-permute-start.12) | collective-permute-done | bytes 524320 | tf_op jit(solution)/shard_map/ppermute | solution.py:478
  62.5 8.3 %pair_triangles.1 = (f32[2,128,128]{2,1,0:T(8,128)S(1)}, f32[2,128,128]{2,1,0:T(8,128)S(1)}, f32[2,128,128]{2,1,0:T(8,128)S(1)}, bf16[768,128]{1,0:T(8,128)(2,1)S(1)}, bf16[128,512]{1,0:T(8,128)(2,1)S(1)}) custom-call(s32[1]{0:T(128)} %bitcast.4.place_ref, f32[16,128,128]{2,1,0:T(8,128)S(1)} %get-tuple-element.35.pair_mid_ref, ...), custom_call_target="tpu_custom_call" | custom-call | tf_op jit(solution)/shard_map/pair_triangles/pallas_call | solution.py:594
  70.8 0.2 collective-permute-start.13
  71.0 0.8 %reshape.59 = bf16[128,4,256]{2,1,0:T(4,128)(2,1)} reshape(bf16[512,256]{1,0:T(8,128)(2,1)S(1)} %copy-done.13) | data formatting | bytes 524288 | tf_op jit(solution)/shard_map/reshape | solution.py:620
  71.8 0.4 collective-permute-done.13.other_part_ref
  72.2 1.5 %pair_finish.1 = bf16[256,128]{1,0:T(8,128)(2,1)} custom-call(f32[2,128,128]{2,1,0:T(8,128)S(1)} %get-tuple-element.39.own_pair_ref, f32[2,128,128]{2,1,0:T(8,128)S(1)} %get-tuple-element.40.own_part_ref, f32[2,128,128]{2,1,0:T(8,128)S(1)} %collective-permute-done.13.other_part_ref, bf16[768,128]{1,0:T(8,128)(2,1)S(1)} %get-tuple-element.42.narrow_ref, ...), custom_call_target="tpu_custom_call" | custom-call | tf_op jit(solution)/shard_map/pair_finish/pallas_call | solution.py:612
  (49 shorter events, 0.6 us)
Async XLA Ops:
  0.6 1.0 %copy-start.1 = (bf16[8,64,256]{2,1,0:T(8,128)(2,1)S(1)}, bf16[8,64,256]{2,1,0:T(8,128)(2,1)}, u32[]{:S(2)}) copy-start(bf16[8,64,256]{2,1,0:T(8,128)(2,1)} %rows_ref.1) | copy-start | bytes 786436
  1.6 0.8 %copy-start.6 = (bf16[4,64,128]{2,1,0:T(8,128)(2,1)S(1)}, bf16[4,64,128]{2,1,0:T(8,128)(2,1)}, u32[]{:S(2)}) copy-start(bf16[4,64,128]{2,1,0:T(8,128)(2,1)} %pair_ref.1) | copy-start | bytes 196612
  3.6 25.0 %all-to-all-start = ((bf16[16,32,256]{2,1,0:T(8,128)(2,1)}), bf16[16,32,256]{2,1,0:T(8,128)(2,1)S(1)}, u32[]{:S(2)}, u32[]{:S(2)}) async-start(bf16[16,32,256]{2,1,0:T(8,128)(2,1)} %get-tuple-element.23), calls=%async_computation | async-start | bytes 524288 | tf_op jit(solution)/shard_map/all_to_all | solution.py:521
  10.9 12.5 %collective-permute-start = (bf16[2,128,128]{2,1,0:T(8,128)(2,1)S(1)}, bf16[2,128,128]{2,1,0:T(8,128)(2,1)S(1)}, u32[]{:S(2)}, u32[]{:S(2)}) collective-permute-start(bf16[2,128,128]{2,1,0:T(8,128)(2,1)S(1)} %get-tuple-element.24), channel_id=1, source_target_pairs={{0,8},{1,9},{2,10},{3,11},{4,12},{5,13},{6,14},{7,15},{8,0},{9,1},... | collective-permute-start | bytes 196616 | tf_op jit(solution)/shard_map/ppermute | solution.py:478
  23.4 5.1 %collective-permute-start.1 = (bf16[2,2,128,128]{3,2,1,0:T(8,128)(2,1)S(1)}, bf16[2,2,128,128]{3,2,1,0:T(8,128)(2,1)S(1)}, u32[]{:S(2)}, u32[]{:S(2)}) collective-permute-start(bf16[2,2,128,128]{3,2,1,0:T(8,128)(2,1)S(1)} %pad_maximum_fusion.rest_8_), channel_id=1, source_target_pairs={{0,4},{1,5},{2,6},{3,7},{4,0},{5,1},{6,2},{7,3},{8,12},{9,13},{10,... | collective-permute-start | bytes 393224 | tf_op jit(solution)/shard_map/ppermute | solution.py:478
  28.5 2.0 %copy-start.14 = (bf16[16,32,256]{2,1,0:T(8,128)(2,1)}, bf16[16,32,256]{2,1,0:T(8,128)(2,1)S(1)}, u32[]{:S(2)}) copy-start(bf16[16,32,256]{2,1,0:T(8,128)(2,1)S(1)} %all-to-all-done.blocks_ref) | copy-start | bytes 786436
  28.5 8.2 %collective-permute-start.2 = (bf16[2,2,128,128]{3,2,1,0:T(8,128)(2,1)S(1)}, bf16[2,2,128,128]{3,2,1,0:T(8,128)(2,1)S(1)}, u32[]{:S(2)}, u32[]{:S(2)}) collective-permute-start(bf16[2,2,128,128]{3,2,1,0:T(8,128)(2,1)S(1)} %pad_maximum_fusion.rest_8_), channel_id=1, source_target_pairs={{0,2},{1,3},{2,0},{3,1},{4,6},{5,7},{6,4},{7,5},{8,10},{9,11},{10,... | collective-permute-start | bytes 393224 | tf_op jit(solution)/shard_map/ppermute | solution.py:478
  30.0 6.7 %collective-permute-start.3 = (bf16[2,2,128,128]{3,2,1,0:T(8,128)(2,1)S(1)}, bf16[2,2,128,128]{3,2,1,0:T(8,128)(2,1)S(1)}, u32[]{:S(2)}, u32[]{:S(2)}) collective-permute-start(bf16[2,2,128,128]{3,2,1,0:T(8,128)(2,1)S(1)} %collective-permute-done.1.rest_9_), channel_id=1, source_target_pairs={{0,2},{1,3},{2,0},{3,1},{4,6},{5,7},{6,4},{7,5},{8,10},{9,11},{10,... | collective-permute-start | bytes 393224 | tf_op jit(solution)/shard_map/ppermute | solution.py:478
  36.7 18.2 %copy-start = (bf16[1024,128]{1,0:T(8,128)(2,1)S(1)}, bf16[1024,128]{1,0:T(8,128)(2,1)}, u32[]{:S(2)}) copy-start(bf16[1024,128]{1,0:T(8,128)(2,1)} %rest_12_.1) | copy-start | bytes 786436
  36.7 5.9 %collective-permute-start.4 = (bf16[256,128]{1,0:T(8,128)(2,1)}, bf16[256,128]{1,0:T(8,128)(2,1)S(1)}, u32[]{:S(2)}, u32[]{:S(2)}) collective-permute-start(bf16[256,128]{1,0:T(8,128)(2,1)} %get-tuple-element.30), channel_id=1, source_target_pairs={{0,8},{1,9},{2,10},{3,11},{4,12},{5,13},{6,14},{7,15},{8,0},{9,1},... | collective-permute-start | bytes 196616 | tf_op jit(solution)/shard_map/ppermute | solution.py:478
  42.6 7.4 %copy-start.15 = (s32[64]{0:T(128)S(1)}, s32[64]{0:T(128)}, u32[]{:S(2)}) copy-start(s32[64]{0:T(128)} %param.24) | copy-start | bytes 772
  42.6 7.6 %copy-start.16 = (s32[64]{0:T(128)S(1)}, s32[64]{0:T(128)}, u32[]{:S(2)}) copy-start(s32[64]{0:T(128)} %param.25) | copy-start | bytes 772
  43.5 11.4 %copy-start.2 = (bf16[128,512]{1,0:T(8,128)(2,1)S(1)}, bf16[128,512]{1,0:T(8,128)(2,1)}, u32[]{:S(2)}) copy-start(bf16[128,512]{1,0:T(8,128)(2,1)} %rest_13_.1) | copy-start | bytes 393220
  43.5 5.0 %collective-permute-start.5 = (bf16[2,256,128]{2,1,0:T(8,128)(2,1)S(1)}, bf16[2,256,128]{2,1,0:T(8,128)(2,1)S(1)}, u32[]{:S(2)}, u32[]{:S(2)}) collective-permute-start(bf16[2,256,128]{2,1,0:T(8,128)(2,1)S(1)} %pad_maximum_fusion.1.rest_0_), channel_id=1, source_target_pairs={{0,4},{1,5},{2,6},{3,7},{4,0},{5,1},{6,2},{7,3},{8,12},{9,13},{10,... | collective-permute-start | bytes 393224 | tf_op jit(solution)/shard_map/ppermute | solution.py:478
  43.5 7.3 %collective-permute-start.6 = (bf16[2,256,128]{2,1,0:T(8,128)(2,1)S(1)}, bf16[2,256,128]{2,1,0:T(8,128)(2,1)S(1)}, u32[]{:S(2)}, u32[]{:S(2)}) collective-permute-start(bf16[2,256,128]{2,1,0:T(8,128)(2,1)S(1)} %pad_maximum_fusion.1.rest_0_), channel_id=1, source_target_pairs={{0,2},{1,3},{2,0},{3,1},{4,6},{5,7},{6,4},{7,5},{8,10},{9,11},{10,... | collective-permute-start | bytes 393224 | tf_op jit(solution)/shard_map/ppermute | solution.py:478
  48.5 5.0 %collective-permute-start.7 = (bf16[2,256,128]{2,1,0:T(8,128)(2,1)S(1)}, bf16[2,256,128]{2,1,0:T(8,128)(2,1)S(1)}, u32[]{:S(2)}, u32[]{:S(2)}) collective-permute-start(bf16[2,256,128]{2,1,0:T(8,128)(2,1)S(1)} %collective-permute-done.5.rest_1_), channel_id=1, source_target_pairs={{0,2},{1,3},{2,0},{3,1},{4,6},{5,7},{6,4},{7,5},{8,10},{9,11},{10,... | collective-permute-start | bytes 393224 | tf_op jit(solution)/shard_map/ppermute | solution.py:478
  50.3 3.5 %collective-permute-start.8 = (bf16[2,256,128]{2,1,0:T(8,128)(2,1)S(1)}, bf16[2,256,128]{2,1,0:T(8,128)(2,1)S(1)}, u32[]{:S(2)}, u32[]{:S(2)}) collective-permute-start(bf16[2,256,128]{2,1,0:T(8,128)(2,1)S(1)} %pad_maximum_fusion.1.rest_0_), channel_id=1, source_target_pairs={{0,1},{1,0},{2,3},{3,2},{4,5},{5,4},{6,7},{7,6},{8,9},{9,8},{10,11... | collective-permute-start | bytes 393224 | tf_op jit(solution)/shard_map/ppermute | solution.py:478
  50.4 3.5 %collective-permute-start.9 = (bf16[2,256,128]{2,1,0:T(8,128)(2,1)S(1)}, bf16[2,256,128]{2,1,0:T(8,128)(2,1)S(1)}, u32[]{:S(2)}, u32[]{:S(2)}) collective-permute-start(bf16[2,256,128]{2,1,0:T(8,128)(2,1)S(1)} %collective-permute-done.5.rest_1_), channel_id=1, source_target_pairs={{0,1},{1,0},{2,3},{3,2},{4,5},{5,4},{6,7},{7,6},{8,9},{9,8},{10,11... | collective-permute-start | bytes 393224 | tf_op jit(solution)/shard_map/ppermute | solution.py:478
  50.9 3.0 %collective-permute-start.10 = (bf16[2,256,128]{2,1,0:T(8,128)(2,1)S(1)}, bf16[2,256,128]{2,1,0:T(8,128)(2,1)S(1)}, u32[]{:S(2)}, u32[]{:S(2)}) collective-permute-start(bf16[2,256,128]{2,1,0:T(8,128)(2,1)S(1)} %collective-permute-done.6.rest_2_), channel_id=1, source_target_pairs={{0,1},{1,0},{2,3},{3,2},{4,5},{5,4},{6,7},{7,6},{8,9},{9,8},{10,11... | collective-permute-start | bytes 393224 | tf_op jit(solution)/shard_map/ppermute | solution.py:478
  53.5 1.3 %collective-permute-start.11 = (bf16[2,256,128]{2,1,0:T(8,128)(2,1)S(1)}, bf16[2,256,128]{2,1,0:T(8,128)(2,1)S(1)}, u32[]{:S(2)}, u32[]{:S(2)}) collective-permute-start(bf16[2,256,128]{2,1,0:T(8,128)(2,1)S(1)} %collective-permute-done.7.rest_3_), channel_id=1, source_target_pairs={{0,1},{1,0},{2,3},{3,2},{4,5},{5,4},{6,7},{7,6},{8,9},{9,8},{10,11... | collective-permute-start | bytes 393224 | tf_op jit(solution)/shard_map/ppermute | solution.py:478
  53.7 1.1 %copy-start.7 = (bf16[128,128]{1,0:T(8,128)(2,1)S(1)}, bf16[128,128]{1,0:T(8,128)(2,1)}, u32[]{:S(2)}) copy-start(bf16[128,128]{1,0:T(8,128)(2,1)} %rest_14_.1) | copy-start | bytes 98308
  53.7 1.1 %copy-start.11 = (bf16[66,128]{1,0:T(8,128)(2,1)S(1)}, bf16[66,128]{1,0:T(8,128)(2,1)}, u32[]{:S(2)}) copy-start(bf16[66,128]{1,0:T(8,128)(2,1)} %table_ref.1) | copy-start | bytes 50692
  53.8 1.0 %copy-start.12 = (f32[1,128]{1,0:T(1,128)S(1)}, f32[1,128]{1,0:T(1,128)}, u32[]{:S(2)}) copy-start(f32[1,128]{1,0:T(1,128)} %fusion.live_ref) | copy-start | bytes 1540
  54.9 7.6 %copy-start.3 = (bf16[128,512]{1,0:T(8,128)(2,1)S(1)}, bf16[128,512]{1,0:T(8,128)(2,1)}, u32[]{:S(2)}) copy-start(bf16[128,512]{1,0:T(8,128)(2,1)} %rest_1_.1) | copy-start | bytes 393220
  54.9 7.6 %copy-start.4 = (bf16[128,512]{1,0:T(8,128)(2,1)S(1)}, bf16[128,512]{1,0:T(8,128)(2,1)}, u32[]{:S(2)}) copy-start(bf16[128,512]{1,0:T(8,128)(2,1)} %rest_4_.1) | copy-start | bytes 393220
  54.9 7.6 %copy-start.5 = (bf16[512,128]{1,0:T(8,128)(2,1)S(1)}, bf16[512,128]{1,0:T(8,128)(2,1)}, u32[]{:S(2)}) copy-start(bf16[512,128]{1,0:T(8,128)(2,1)} %rest_5_.1) | copy-start | bytes 393220
  54.9 7.6 %copy-start.8 = (bf16[128,128]{1,0:T(8,128)(2,1)S(1)}, bf16[128,128]{1,0:T(8,128)(2,1)}, u32[]{:S(2)}) copy-start(bf16[128,128]{1,0:T(8,128)(2,1)} %rest_0_.1) | copy-start | bytes 98308
  54.9 7.6 %copy-start.9 = (bf16[128,128]{1,0:T(8,128)(2,1)S(1)}, bf16[128,128]{1,0:T(8,128)(2,1)}, u32[]{:S(2)}) copy-start(bf16[128,128]{1,0:T(8,128)(2,1)} %rest_2_.1) | copy-start | bytes 98308
  54.9 7.6 %copy-start.10 = (bf16[128,128]{1,0:T(8,128)(2,1)S(1)}, bf16[128,128]{1,0:T(8,128)(2,1)}, u32[]{:S(2)}) copy-start(bf16[128,128]{1,0:T(8,128)(2,1)} %rest_3_.1) | copy-start | bytes 98308
  60.5 2.0 %collective-permute-start.12 = (bf16[2048,128]{1,0:T(8,128)(2,1)S(1)}, bf16[2048,128]{1,0:T(8,128)(2,1)S(1)}, u32[]{:S(2)}, u32[]{:S(2)}) collective-permute-start(bf16[2048,128]{1,0:T(8,128)(2,1)S(1)} %get-tuple-element.38.right_own_ref), channel_id=1, source_target_pairs={{0,1},{1,0},{2,3},{3,2},{4,5},{5,4},{6,7},{7,6},{8,9},{9,8},{10,11... | collective-permute-start | bytes 1572872 | tf_op jit(solution)/shard_map/ppermute | solution.py:478
  62.5 8.5 %copy-start.13 = (bf16[512,256]{1,0:T(8,128)(2,1)S(1)}, bf16[512,256]{1,0:T(8,128)(2,1)}, u32[]{:S(2)}) copy-start(bf16[512,256]{1,0:T(8,128)(2,1)} %get-tuple-element.26) | copy-start | bytes 786436
  70.8 1.4 %collective-permute-start.13 = (f32[2,128,128]{2,1,0:T(8,128)S(1)}, f32[2,128,128]{2,1,0:T(8,128)S(1)}, u32[]{:S(2)}, u32[]{:S(2)}) collective-permute-start(f32[2,128,128]{2,1,0:T(8,128)S(1)} %get-tuple-element.41), channel_id=1, source_target_pairs={{0,1},{1,0},{2,3},{3,2},{4,5},{5,4},{6,7},{7,6},{8,9},{9,8},{10,11... | collective-permute-start | bytes 393224 | tf_op jit(solution)/shard_map/ppermute | solution.py:478
  (1 other events, 0.7 us)

commit v11 on v9

--- a/solution.py
+++ b/solution.py
@@ -410,10 +410,7 @@
 def msa_kernel(
     live_ref,
     blocks_ref,
-    query_ref,
-    key_ref,
-    value_gate_ref,
-    output_ref,
+    narrow_ref,
     up_ref,
     down_ref,
     outer_ref,
@@ -439,9 +436,9 @@
 
     heads = by_head(one)
     normed = normalize_rows(wide_ref[...])
-    query = (mix(normed, query_ref[...]) * HEAD_SIZE ** (-0.5)).astype(jnp.bfloat16)
-    key = mix(normed, key_ref[...]).astype(jnp.bfloat16)
-    value_gate = mix(normed, value_gate_ref[...])
+    query = (mix(normed, narrow_ref[:, :width]) * HEAD_SIZE ** (-0.5)).astype(jnp.bfloat16)
+    key = mix(normed, narrow_ref[:, width : 2 * width]).astype(jnp.bfloat16)
+    value_gate = mix(normed, narrow_ref[:, 2 * width : 4 * width])
     value = value_gate[:, :width].astype(jnp.bfloat16)
     for i in range(4):
         rows = slice(i * 128, (i + 1) * 128)
@@ -453,7 +450,7 @@
         raised = jnp.concatenate(raised, axis=1)
         attended_ref[rows, :] = mix(raised, by_head(value[rows])) / mix(raised, heads)
     gated = (gate_curve(value_gate[:, width:]) * attended_ref[...]).astype(jnp.bfloat16)
-    current = wide_ref[...] + mix(gated, output_ref[...])
+    current = wide_ref[...] + mix(gated, narrow_ref[:, 4 * width :])
     hidden = jnp.maximum(mix(normalize_rows(current), up_ref[...]), 0.0).astype(jnp.bfloat16)
     final = (current + mix(hidden, down_ref[...])).astype(jnp.bfloat16).astype(jnp.float32)
     outer = contract_last(outer_ref[...], normalize_rows(final))
@@ -516,14 +513,13 @@
     blocks = lax.all_to_all(blocks, "dap", split_axis=0, concat_axis=0, tiled=True)
 
     pair_first = jnp.stack([own_pair, exchange(own_pair, 8)])
+    blocks, pair_first = lax.optimization_barrier((blocks, pair_first))
     pair_second = exchange(pair_first, 4)
-    blocks, pair_first, pair_second = lax.optimization_barrier((blocks, pair_first, pair_second))
-    pair_pieces = [pair_first, pair_second, exchange(pair_first, 2), exchange(pair_second, 2)]
 
     result, parts = pl.pallas_call(
         msa_kernel,
         out_shape=(array(512, channels), array(256, LANES)),
-        in_specs=[vmem] * 9,
+        in_specs=[vmem] * 6,
         out_specs=(vmem, vmem),
         scratch_shapes=[
             pltpu.VMEM((512, channels), jnp.float32),
@@ -538,14 +534,21 @@
     )(
         live_row_float.reshape(1, LANES),
         blocks,
-        column_query_weight,
-        column_key_weight,
-        column_value_gate_weight,
-        column_output_weight,
+        jnp.concatenate(
+            [
+                column_query_weight,
+                column_key_weight,
+                column_value_gate_weight,
+                column_output_weight,
+            ],
+            axis=1,
+        ),
         alignment_transition_up,
         alignment_transition_down,
         outer_input_weight.T,
     )
+    parts, pair_second = lax.optimization_barrier((parts, pair_second))
+    pair_pieces = [pair_first, pair_second, exchange(pair_first, 2), exchange(pair_second, 2)]
     first = jnp.stack([parts, exchange(parts, 8)])
     second = exchange(first, 4)
     pieces = [first, second, exchange(first, 2), exchange(second, 2)]

time: 73.4 us -> 65.9 us (0.90)
  waiting for transfers between devices: 28.3 us -> 22.2 us
  local copies, waits for them, and re-layouts: 7.31 us -> 3.11 us
  starting transfers between devices: 15.8 us -> 17.6 us
  other arithmetic: 0.23 us -> 1.39 us
    ppermute x14, waiting for transfers between devices: 28.3 us -> 22.2 us  [exchange(): return lax.ppermute(values, 'dap', [(q, q ^ offset) for q in range(pieces)])]
    unnamed x44 -> x36, local copies, waits for them, and re-layouts: 6.08 us -> 1.87 us
    ppermute x14, starting transfers between devices: 8.38 us -> 10.1 us  [exchange(): return lax.ppermute(values, 'dap', [(q, q ^ offset) for q in range(pieces)])]
    concatenate x0 -> x1, other arithmetic: none -> 1.16 us  [whole_block(): jnp.concatenate([column_query_weight, column_key_weight, column_value_gat...]
  transfers between devices with their start and end apart: 15 -> 15, of which waited for: 9 -> 10; matrix products, arithmetic and copies ran while one was open for 2% -> 4% of each run, Pallas kernels for 0% -> 6%
where the time goes in v11:
time: 65.9 us; the launch traced here: 65.6 us
  waiting for transfers between devices  22.2 us (34%)
  Pallas kernels  20.4 us (31%)
  starting transfers between devices  17.6 us (27%)
  local copies, waits for them, and re-layouts  3.11 us (5%)
  other arithmetic  1.39 us (2%)
  between operations  0.94 us (1%)
    ppermute x14, waiting for transfers between devices, exchange(): return lax.ppermute(values, 'dap', [(q, q ^ offset) for q in range(pieces)])  22.2 us
    ppermute x14, starting transfers between devices, exchange(): return lax.ppermute(values, 'dap', [(q, q ^ offset) for q in range(pieces)])  10.1 us
    pallas_call x1, Pallas kernels, whole_block(): pl.pallas_call(triangle_kernel, out_shape=[wide(2, 128, LANES)] * 3 + [ar...  8.08 us
    all_to_all x1, starting transfers between devices, whole_block(): lax.all_to_all(blocks, 'dap', split_axis=0, concat_axis=0, tiled=True)  7.52 us
    pallas_call x1, Pallas kernels, whole_block(): pl.pallas_call(start_kernel, out_shape=[wide(*slabs), wide(*tall), wide(*...  5.58 us
    pallas_call x1, Pallas kernels, whole_block(): pl.pallas_call(msa_kernel, out_shape=(array(512, channels), array(256, LA...  4.13 us
    unnamed x36, local copies, waits for them, and re-layouts  1.87 us
    pallas_call x1, Pallas kernels, whole_block(): pl.pallas_call(finish_kernel, out_shape=array(256, LANES), in_specs=[vmem...  1.52 us
  transfers between devices with their start and end apart: 15, of which 10 were waited for; matrix products, arithmetic and copies ran while one was open for 4% of the time, Pallas kernels for 6%

profile of v11, /device:TPU:0, one launch (start us, length us, event | category | flops | bytes accessed | tf_op | source)
XLA Modules:
  0.0 65.6 jit_solution(1999995887225516708)
XLA Ops:
  0.6 0.9 %copy-done.1 = bf16[8,64,256]{2,1,0:T(8,128)(2,1)S(1)} copy-done((bf16[8,64,256]{2,1,0:T(8,128)(2,1)S(1)}, bf16[8,64,256]{2,1,0:T(8,128)(2,1)}, u32[]{:S(2)}) %copy-start.1) | copy-done | bytes 262168
  1.6 0.8 %copy-done.6 = bf16[4,64,128]{2,1,0:T(8,128)(2,1)S(1)} copy-done((bf16[4,64,128]{2,1,0:T(8,128)(2,1)S(1)}, bf16[4,64,128]{2,1,0:T(8,128)(2,1)}, u32[]{:S(2)}) %copy-start.6) | copy-done | bytes 65560
  2.4 1.1 %rows_by_device.1 = (bf16[16,32,256]{2,1,0:T(8,128)(2,1)}, bf16[2,128,128]{2,1,0:T(8,128)(2,1)S(1)}) custom-call(bf16[8,64,256]{2,1,0:T(8,128)(2,1)S(1)} %copy-done.1, bf16[4,64,128]{2,1,0:T(8,128)(2,1)S(1)} %copy-done.6), custom_call_target="tpu_custom_call" | custom-call | tf_op jit(solution)/shard_map/rows_by_device/pallas_call | solution.py:504
  3.6 7.5 %all-to-all-start = ((bf16[16,32,256]{2,1,0:T(8,128)(2,1)}), bf16[16,32,256]{2,1,0:T(8,128)(2,1)S(1)}, u32[]{:S(2)}, u32[]{:S(2)}) async-start(bf16[16,32,256]{2,1,0:T(8,128)(2,1)} %get-tuple-element.19), calls=%async_computation | async-start | bytes 524288 | tf_op jit(solution)/shard_map/all_to_all | solution.py:513
  11.1 2.8 %collective-permute-start = (bf16[2,128,128]{2,1,0:T(8,128)(2,1)S(1)}, bf16[2,128,128]{2,1,0:T(8,128)(2,1)S(1)}, u32[]{:S(2)}, u32[]{:S(2)}) collective-permute-start(bf16[2,128,128]{2,1,0:T(8,128)(2,1)S(1)} %get-tuple-element.20), channel_id=1, source_target_pairs={{0,8},{1,9},{2,10},{3,11},{4,12},{5,13},{6,14},{7,15},{8,0},{9,1},... | collective-permute-start | bytes 196616 | tf_op jit(solution)/shard_map/ppermute | solution.py:470
  13.9 1.2 %pad_maximum_fusion.narrow_ref = bf16[256,1280]{1,0:T(8,128)(2,1)S(1)} fusion(bf16[256,256]{1,0:T(8,128)(2,1)} %param.31, bf16[256,512]{1,0:T(8,128)(2,1)} %param.30, bf16[256,256]{1,0:T(8,128)(2,1)} %param.29, bf16[256,256]{1,0:T(8,128)(2,1)} %param.28), kind=kLoop, calls=%fused_computation | loop fusion | flops 2621440 | bytes 1310720 | tf_op jit(solution)/shard_map/concatenate | solution.py:537
  15.1 8.4 %collective-permute-done = bf16[2,128,128]{2,1,0:T(8,128)(2,1)S(1)} collective-permute-done((bf16[2,128,128]{2,1,0:T(8,128)(2,1)S(1)}, bf16[2,128,128]{2,1,0:T(8,128)(2,1)S(1)}, u32[]{:S(2)}, u32[]{:S(2)}) %collective-permute-start) | collective-permute-done | bytes 65568 | tf_op jit(solution)/shard_map/ppermute | solution.py:470
  23.8 4.1 %msa_whole.1 = (bf16[512,256]{1,0:T(8,128)(2,1)S(1)}, bf16[256,128]{1,0:T(8,128)(2,1)S(1)}) custom-call(f32[1,128]{1,0:T(1,128)S(1)} %fusion.live_ref, bf16[16,32,256]{2,1,0:T(8,128)(2,1)S(1)} %all-to-all-done.blocks_ref, bf16[256,1280]{1,0:T(8,128)(2,1)S(1)} %pad_maximum_fusion.narrow_ref, bf16[256,1024]{1,0:T(8,128)(2,1)S(1)} %copy-done.12, ...), custom_call_target="tpu_custom_call" | custom-call | flops 2000000000 | bytes 10000000 | tf_op jit(solution)/shard_map/msa_whole/pallas_call | solution.py:519
  27.9 0.8 %collective-permute-done.1.rest_9_ = bf16[2,2,128,128]{3,2,1,0:T(8,128)(2,1)S(1)} collective-permute-done((bf16[2,2,128,128]{3,2,1,0:T(8,128)(2,1)S(1)}, bf16[2,2,128,128]{3,2,1,0:T(8,128)(2,1)S(1)}, u32[]{:S(2)}, u32[]{:S(2)}) %collective-permute-start.1) | collective-permute-done | bytes 131104 | tf_op jit(solution)/shard_map/ppermute | solution.py:470
  28.7 1.3 %collective-permute-start.2 = (bf16[256,128]{1,0:T(8,128)(2,1)S(1)}, bf16[256,128]{1,0:T(8,128)(2,1)S(1)}, u32[]{:S(2)}, u32[]{:S(2)}) collective-permute-start(bf16[256,128]{1,0:T(8,128)(2,1)S(1)} %get-tuple-element.25), channel_id=1, source_target_pairs={{0,8},{1,9},{2,10},{3,11},{4,12},{5,13},{6,14},{7,15},{8,0},{9,1},... | collective-permute-start | bytes 196616 | tf_op jit(solution)/shard_map/ppermute | solution.py:470
  29.9 3.9 %collective-permute-done.2 = bf16[256,128]{1,0:T(8,128)(2,1)S(1)} collective-permute-done((bf16[256,128]{1,0:T(8,128)(2,1)S(1)}, bf16[256,128]{1,0:T(8,128)(2,1)S(1)}, u32[]{:S(2)}, u32[]{:S(2)}) %collective-permute-start.2) | collective-permute-done | bytes 65568 | tf_op jit(solution)/shard_map/ppermute | solution.py:470
  33.9 1.3 %collective-permute-start.3 = (bf16[2,256,128]{2,1,0:T(8,128)(2,1)S(1)}, bf16[2,256,128]{2,1,0:T(8,128)(2,1)S(1)}, u32[]{:S(2)}, u32[]{:S(2)}) collective-permute-start(bf16[2,256,128]{2,1,0:T(8,128)(2,1)S(1)} %pad_maximum_fusion.2.rest_0_), channel_id=1, source_target_pairs={{0,4},{1,5},{2,6},{3,7},{4,0},{5,1},{6,2},{7,3},{8,12},{9,13},{10,... | collective-permute-start | bytes 393224 | tf_op jit(solution)/shard_map/ppermute | solution.py:470
  35.2 1.5 %collective-permute-start.10 = (bf16[2,2,128,128]{3,2,1,0:T(8,128)(2,1)S(1)}, bf16[2,2,128,128]{3,2,1,0:T(8,128)(2,1)S(1)}, u32[]{:S(2)}, u32[]{:S(2)}) collective-permute-start(bf16[2,2,128,128]{3,2,1,0:T(8,128)(2,1)S(1)} %pad_maximum_fusion.1.rest_8_), channel_id=1, source_target_pairs={{0,2},{1,3},{2,0},{3,1},{4,6},{5,7},{6,4},{7,5},{8,10},{9,11},{10,... | collective-permute-start | bytes 393224 | tf_op jit(solution)/shard_map/ppermute | solution.py:470
  36.7 0.6 collective-permute-start.4
  37.2 1.7 %collective-permute-done.3.rest_1_ = bf16[2,256,128]{2,1,0:T(8,128)(2,1)S(1)} collective-permute-done((bf16[2,256,128]{2,1,0:T(8,128)(2,1)S(1)}, bf16[2,256,128]{2,1,0:T(8,128)(2,1)S(1)}, u32[]{:S(2)}, u32[]{:S(2)}) %collective-permute-start.3) | collective-permute-done | bytes 131104 | tf_op jit(solution)/shard_map/ppermute | solution.py:470
  38.9 1.5 %collective-permute-start.5 = (bf16[2,256,128]{2,1,0:T(8,128)(2,1)S(1)}, bf16[2,256,128]{2,1,0:T(8,128)(2,1)S(1)}, u32[]{:S(2)}, u32[]{:S(2)}) collective-permute-start(bf16[2,256,128]{2,1,0:T(8,128)(2,1)S(1)} %collective-permute-done.3.rest_1_), channel_id=1, source_target_pairs={{0,2},{1,3},{2,0},{3,1},{4,6},{5,7},{6,4},{7,5},{8,10},{9,11},{10,... | collective-permute-start | bytes 393224 | tf_op jit(solution)/shard_map/ppermute | solution.py:470
  40.7 0.6 collective-permute-start.11
  41.3 0.3 collective-permute-done.10.rest_10_
  41.6 0.2 collective-permute-start.7
  41.8 2.3 %collective-permute-done.4.rest_2_ = bf16[2,256,128]{2,1,0:T(8,128)(2,1)S(1)} collective-permute-done((bf16[2,256,128]{2,1,0:T(8,128)(2,1)S(1)}, bf16[2,256,128]{2,1,0:T(8,128)(2,1)S(1)}, u32[]{:S(2)}, u32[]{:S(2)}) %collective-permute-start.4) | collective-permute-done | bytes 131104 | tf_op jit(solution)/shard_map/ppermute | solution.py:470
  44.1 1.4 %collective-permute-done.5.rest_3_ = bf16[2,256,128]{2,1,0:T(8,128)(2,1)S(1)} collective-permute-done((bf16[2,256,128]{2,1,0:T(8,128)(2,1)S(1)}, bf16[2,256,128]{2,1,0:T(8,128)(2,1)S(1)}, u32[]{:S(2)}, u32[]{:S(2)}) %collective-permute-start.5) | collective-permute-done | bytes 131104 | tf_op jit(solution)/shard_map/ppermute | solution.py:470
  45.5 0.2 compare_select_fusion
  45.8 0.1 select_n.11.bins_ref
  45.9 1.0 %collective-permute-done.11.rest_11_ = bf16[2,2,128,128]{3,2,1,0:T(8,128)(2,1)S(1)} collective-permute-done((bf16[2,2,128,128]{3,2,1,0:T(8,128)(2,1)S(1)}, bf16[2,2,128,128]{3,2,1,0:T(8,128)(2,1)S(1)}, u32[]{:S(2)}, u32[]{:S(2)}) %collective-permute-start.11) | collective-permute-done | bytes 131104 | tf_op jit(solution)/shard_map/ppermute | solution.py:470
  47.0 5.6 %pair_start.1 = (f32[16,128,128]{2,1,0:T(8,128)S(1)}, f32[2048,128]{1,0:T(8,128)S(1)}, f32[16,128,128]{2,1,0:T(8,128)S(1)}, bf16[2048,128]{1,0:T(8,128)(2,1)S(1)}) custom-call(s32[1]{0:T(128)} %bitcast.4.place_ref, f32[1,128]{1,0:T(1,128)S(1)} %fusion.live_ref, s32[32,128]{1,0:T(8,128)S(1)} %select_n.11.bins_ref, bf16[66,128]{1,0:T(8,128)(2,1)S(1)} %copy-done.11, ...), custom_call_target="tpu_custom_call" | custom-call | tf_op jit(solution)/shard_map/pair_start/pallas_call | solution.py:559
  52.6 0.1 collective-permute-start.12
  52.7 1.9 %collective-permute-done.12.right_other_ref = bf16[2048,128]{1,0:T(8,128)(2,1)S(1)} collective-permute-done((bf16[2048,128]{1,0:T(8,128)(2,1)S(1)}, bf16[2048,128]{1,0:T(8,128)(2,1)S(1)}, u32[]{:S(2)}, u32[]{:S(2)}) %collective-permute-start.12) | collective-permute-done | bytes 524320 | tf_op jit(solution)/shard_map/ppermute | solution.py:470
  54.6 8.1 %pair_triangles.1 = (f32[2,128,128]{2,1,0:T(8,128)S(1)}, f32[2,128,128]{2,1,0:T(8,128)S(1)}, f32[2,128,128]{2,1,0:T(8,128)S(1)}, bf16[768,128]{1,0:T(8,128)(2,1)S(1)}, bf16[128,512]{1,0:T(8,128)(2,1)S(1)}) custom-call(s32[1]{0:T(128)} %bitcast.4.place_ref, f32[16,128,128]{2,1,0:T(8,128)S(1)} %get-tuple-element.27.pair_mid_ref, ...), custom_call_target="tpu_custom_call" | custom-call | tf_op jit(solution)/shard_map/pair_triangles/pallas_call | solution.py:587
  62.7 0.2 collective-permute-start.13
  62.9 0.8 %reshape.59 = bf16[128,4,256]{2,1,0:T(4,128)(2,1)} reshape(bf16[512,256]{1,0:T(8,128)(2,1)S(1)} %get-tuple-element.22) | data formatting | bytes 524288 | tf_op jit(solution)/shard_map/reshape | solution.py:613
  63.7 0.5 collective-permute-done.13.other_part_ref
  64.1 1.5 %pair_finish.1 = bf16[256,128]{1,0:T(8,128)(2,1)} custom-call(f32[2,128,128]{2,1,0:T(8,128)S(1)} %get-tuple-element.31.own_pair_ref, f32[2,128,128]{2,1,0:T(8,128)S(1)} %get-tuple-element.32.own_part_ref, f32[2,128,128]{2,1,0:T(8,128)S(1)} %collective-permute-done.13.other_part_ref, bf16[768,128]{1,0:T(8,128)(2,1)S(1)} %get-tuple-element.34.narrow_ref, ...), custom_call_target="tpu_custom_call" | custom-call | tf_op jit(solution)/shard_map/pair_finish/pallas_call | solution.py:605
  (50 shorter events, 0.6 us)
Async XLA Ops:
  0.6 1.0 %copy-start.1 = (bf16[8,64,256]{2,1,0:T(8,128)(2,1)S(1)}, bf16[8,64,256]{2,1,0:T(8,128)(2,1)}, u32[]{:S(2)}) copy-start(bf16[8,64,256]{2,1,0:T(8,128)(2,1)} %rows_ref.1) | copy-start | bytes 786436
  2.4 12.7 %copy-start.17 = (s32[128]{0:T(128)S(1)}, s32[128]{0:T(128)}, u32[]{:S(2)}) copy-start(s32[128]{0:T(128)} %param.26) | copy-start | bytes 1540
  3.6 20.1 %copy-start.12 = (bf16[256,1024]{1,0:T(8,128)(2,1)S(1)}, bf16[256,1024]{1,0:T(8,128)(2,1)}, u32[]{:S(2)}) copy-start(bf16[256,1024]{1,0:T(8,128)(2,1)} %up_ref.1) | copy-start | bytes 1572868
  3.6 20.1 %copy-start.13 = (bf16[1024,256]{1,0:T(8,128)(2,1)S(1)}, bf16[1024,256]{1,0:T(8,128)(2,1)}, u32[]{:S(2)}) copy-start(bf16[1024,256]{1,0:T(8,128)(2,1)} %down_ref.1) | copy-start | bytes 1572868
  3.6 20.1 %copy-start.14 = (bf16[256,64]{0,1:T(8,128)(2,1)S(1)}, bf16[256,64]{0,1:T(8,128)(2,1)}, u32[]{:S(2)}) copy-start(bf16[256,64]{0,1:T(8,128)(2,1)} %param.34) | copy-start | bytes 98308
  3.6 20.0 %all-to-all-start = ((bf16[16,32,256]{2,1,0:T(8,128)(2,1)}), bf16[16,32,256]{2,1,0:T(8,128)(2,1)S(1)}, u32[]{:S(2)}, u32[]{:S(2)}) async-start(bf16[16,32,256]{2,1,0:T(8,128)(2,1)} %get-tuple-element.19), calls=%async_computation | async-start | bytes 524288 | tf_op jit(solution)/shard_map/all_to_all | solution.py:513
  11.1 12.5 %collective-permute-start = (bf16[2,128,128]{2,1,0:T(8,128)(2,1)S(1)}, bf16[2,128,128]{2,1,0:T(8,128)(2,1)S(1)}, u32[]{:S(2)}, u32[]{:S(2)}) collective-permute-start(bf16[2,128,128]{2,1,0:T(8,128)(2,1)S(1)} %get-tuple-element.20), channel_id=1, source_target_pairs={{0,8},{1,9},{2,10},{3,11},{4,12},{5,13},{6,14},{7,15},{8,0},{9,1},... | collective-permute-start | bytes 196616 | tf_op jit(solution)/shard_map/ppermute | solution.py:470
  23.6 5.1 %collective-permute-start.1 = (bf16[2,2,128,128]{3,2,1,0:T(8,128)(2,1)S(1)}, bf16[2,2,128,128]{3,2,1,0:T(8,128)(2,1)S(1)}, u32[]{:S(2)}, u32[]{:S(2)}) collective-permute-start(bf16[2,2,128,128]{3,2,1,0:T(8,128)(2,1)S(1)} %pad_maximum_fusion.1.rest_8_), channel_id=1, source_target_pairs={{0,4},{1,5},{2,6},{3,7},{4,0},{5,1},{6,2},{7,3},{8,12},{9,13},{10,... | collective-permute-start | bytes 393224 | tf_op jit(solution)/shard_map/ppermute | solution.py:470
  23.7 16.7 %copy-start.15 = (s32[64]{0:T(128)S(1)}, s32[64]{0:T(128)}, u32[]{:S(2)}) copy-start(s32[64]{0:T(128)} %param.24) | copy-start | bytes 772
  23.7 16.8 %copy-start.16 = (s32[64]{0:T(128)S(1)}, s32[64]{0:T(128)}, u32[]{:S(2)}) copy-start(s32[64]{0:T(128)} %param.25) | copy-start | bytes 772
  23.7 23.3 %copy-start = (bf16[1024,128]{1,0:T(8,128)(2,1)S(1)}, bf16[1024,128]{1,0:T(8,128)(2,1)}, u32[]{:S(2)}) copy-start(bf16[1024,128]{1,0:T(8,128)(2,1)} %rest_12_.1) | copy-start | bytes 786436
  23.7 23.3 %copy-start.2 = (bf16[128,512]{1,0:T(8,128)(2,1)S(1)}, bf16[128,512]{1,0:T(8,128)(2,1)}, u32[]{:S(2)}) copy-start(bf16[128,512]{1,0:T(8,128)(2,1)} %rest_13_.1) | copy-start | bytes 393220
  23.7 23.3 %copy-start.7 = (bf16[128,128]{1,0:T(8,128)(2,1)S(1)}, bf16[128,128]{1,0:T(8,128)(2,1)}, u32[]{:S(2)}) copy-start(bf16[128,128]{1,0:T(8,128)(2,1)} %rest_14_.1) | copy-start | bytes 98308
  23.7 23.3 %copy-start.11 = (bf16[66,128]{1,0:T(8,128)(2,1)S(1)}, bf16[66,128]{1,0:T(8,128)(2,1)}, u32[]{:S(2)}) copy-start(bf16[66,128]{1,0:T(8,128)(2,1)} %table_ref.1) | copy-start | bytes 50692
  28.7 5.2 %collective-permute-start.2 = (bf16[256,128]{1,0:T(8,128)(2,1)S(1)}, bf16[256,128]{1,0:T(8,128)(2,1)S(1)}, u32[]{:S(2)}, u32[]{:S(2)}) collective-permute-start(bf16[256,128]{1,0:T(8,128)(2,1)S(1)} %get-tuple-element.25), channel_id=1, source_target_pairs={{0,8},{1,9},{2,10},{3,11},{4,12},{5,13},{6,14},{7,15},{8,0},{9,1},... | collective-permute-start | bytes 196616 | tf_op jit(solution)/shard_map/ppermute | solution.py:470
  33.9 5.0 %collective-permute-start.3 = (bf16[2,256,128]{2,1,0:T(8,128)(2,1)S(1)}, bf16[2,256,128]{2,1,0:T(8,128)(2,1)S(1)}, u32[]{:S(2)}, u32[]{:S(2)}) collective-permute-start(bf16[2,256,128]{2,1,0:T(8,128)(2,1)S(1)} %pad_maximum_fusion.2.rest_0_), channel_id=1, source_target_pairs={{0,4},{1,5},{2,6},{3,7},{4,0},{5,1},{6,2},{7,3},{8,12},{9,13},{10,... | collective-permute-start | bytes 393224 | tf_op jit(solution)/shard_map/ppermute | solution.py:470
  35.2 6.4 %collective-permute-start.10 = (bf16[2,2,128,128]{3,2,1,0:T(8,128)(2,1)S(1)}, bf16[2,2,128,128]{3,2,1,0:T(8,128)(2,1)S(1)}, u32[]{:S(2)}, u32[]{:S(2)}) collective-permute-start(bf16[2,2,128,128]{3,2,1,0:T(8,128)(2,1)S(1)} %pad_maximum_fusion.1.rest_8_), channel_id=1, source_target_pairs={{0,2},{1,3},{2,0},{3,1},{4,6},{5,7},{6,4},{7,5},{8,10},{9,11},{10,... | collective-permute-start | bytes 393224 | tf_op jit(solution)/shard_map/ppermute | solution.py:470
  36.7 7.5 %collective-permute-start.4 = (bf16[2,256,128]{2,1,0:T(8,128)(2,1)S(1)}, bf16[2,256,128]{2,1,0:T(8,128)(2,1)S(1)}, u32[]{:S(2)}, u32[]{:S(2)}) collective-permute-start(bf16[2,256,128]{2,1,0:T(8,128)(2,1)S(1)} %pad_maximum_fusion.2.rest_0_), channel_id=1, source_target_pairs={{0,2},{1,3},{2,0},{3,1},{4,6},{5,7},{6,4},{7,5},{8,10},{9,11},{10,... | collective-permute-start | bytes 393224 | tf_op jit(solution)/shard_map/ppermute | solution.py:470
  38.9 6.6 %collective-permute-start.5 = (bf16[2,256,128]{2,1,0:T(8,128)(2,1)S(1)}, bf16[2,256,128]{2,1,0:T(8,128)(2,1)S(1)}, u32[]{:S(2)}, u32[]{:S(2)}) collective-permute-start(bf16[2,256,128]{2,1,0:T(8,128)(2,1)S(1)} %collective-permute-done.3.rest_1_), channel_id=1, source_target_pairs={{0,2},{1,3},{2,0},{3,1},{4,6},{5,7},{6,4},{7,5},{8,10},{9,11},{10,... | collective-permute-start | bytes 393224 | tf_op jit(solution)/shard_map/ppermute | solution.py:470
  40.7 6.2 %collective-permute-start.11 = (bf16[2,2,128,128]{3,2,1,0:T(8,128)(2,1)S(1)}, bf16[2,2,128,128]{3,2,1,0:T(8,128)(2,1)S(1)}, u32[]{:S(2)}, u32[]{:S(2)}) collective-permute-start(bf16[2,2,128,128]{3,2,1,0:T(8,128)(2,1)S(1)} %collective-permute-done.1.rest_9_), channel_id=1, source_target_pairs={{0,2},{1,3},{2,0},{3,1},{4,6},{5,7},{6,4},{7,5},{8,10},{9,11},{10,... | collective-permute-start | bytes 393224 | tf_op jit(solution)/shard_map/ppermute | solution.py:470
  41.3 5.6 %collective-permute-start.6 = (bf16[2,256,128]{2,1,0:T(8,128)(2,1)S(1)}, bf16[2,256,128]{2,1,0:T(8,128)(2,1)S(1)}, u32[]{:S(2)}, u32[]{:S(2)}) collective-permute-start(bf16[2,256,128]{2,1,0:T(8,128)(2,1)S(1)} %pad_maximum_fusion.2.rest_0_), channel_id=1, source_target_pairs={{0,1},{1,0},{2,3},{3,2},{4,5},{5,4},{6,7},{7,6},{8,9},{9,8},{10,11... | collective-permute-start | bytes 393224 | tf_op jit(solution)/shard_map/ppermute | solution.py:470
  41.6 5.3 %collective-permute-start.7 = (bf16[2,256,128]{2,1,0:T(8,128)(2,1)S(1)}, bf16[2,256,128]{2,1,0:T(8,128)(2,1)S(1)}, u32[]{:S(2)}, u32[]{:S(2)}) collective-permute-start(bf16[2,256,128]{2,1,0:T(8,128)(2,1)S(1)} %collective-permute-done.3.rest_1_), channel_id=1, source_target_pairs={{0,1},{1,0},{2,3},{3,2},{4,5},{5,4},{6,7},{7,6},{8,9},{9,8},{10,11... | collective-permute-start | bytes 393224 | tf_op jit(solution)/shard_map/ppermute | solution.py:470
  44.1 2.8 %collective-permute-start.8 = (bf16[2,256,128]{2,1,0:T(8,128)(2,1)S(1)}, bf16[2,256,128]{2,1,0:T(8,128)(2,1)S(1)}, u32[]{:S(2)}, u32[]{:S(2)}) collective-permute-start(bf16[2,256,128]{2,1,0:T(8,128)(2,1)S(1)} %collective-permute-done.4.rest_2_), channel_id=1, source_target_pairs={{0,1},{1,0},{2,3},{3,2},{4,5},{5,4},{6,7},{7,6},{8,9},{9,8},{10,11... | collective-permute-start | bytes 393224 | tf_op jit(solution)/shard_map/ppermute | solution.py:470
  45.5 1.4 %collective-permute-start.9 = (bf16[2,256,128]{2,1,0:T(8,128)(2,1)S(1)}, bf16[2,256,128]{2,1,0:T(8,128)(2,1)S(1)}, u32[]{:S(2)}, u32[]{:S(2)}) collective-permute-start(bf16[2,256,128]{2,1,0:T(8,128)(2,1)S(1)} %collective-permute-done.5.rest_3_), channel_id=1, source_target_pairs={{0,1},{1,0},{2,3},{3,2},{4,5},{5,4},{6,7},{7,6},{8,9},{9,8},{10,11... | collective-permute-start | bytes 393224 | tf_op jit(solution)/shard_map/ppermute | solution.py:470
  45.7 8.8 %copy-start.3 = (bf16[128,512]{1,0:T(8,128)(2,1)S(1)}, bf16[128,512]{1,0:T(8,128)(2,1)}, u32[]{:S(2)}) copy-start(bf16[128,512]{1,0:T(8,128)(2,1)} %rest_1_.1) | copy-start | bytes 393220
  45.8 8.8 %copy-start.4 = (bf16[128,512]{1,0:T(8,128)(2,1)S(1)}, bf16[128,512]{1,0:T(8,128)(2,1)}, u32[]{:S(2)}) copy-start(bf16[128,512]{1,0:T(8,128)(2,1)} %rest_4_.1) | copy-start | bytes 393220
  45.8 8.8 %copy-start.5 = (bf16[512,128]{1,0:T(8,128)(2,1)S(1)}, bf16[512,128]{1,0:T(8,128)(2,1)}, u32[]{:S(2)}) copy-start(bf16[512,128]{1,0:T(8,128)(2,1)} %rest_5_.1) | copy-start | bytes 393220
  45.8 8.8 %copy-start.8 = (bf16[128,128]{1,0:T(8,128)(2,1)S(1)}, bf16[128,128]{1,0:T(8,128)(2,1)}, u32[]{:S(2)}) copy-start(bf16[128,128]{1,0:T(8,128)(2,1)} %rest_0_.1) | copy-start | bytes 98308
  45.8 8.8 %copy-start.9 = (bf16[128,128]{1,0:T(8,128)(2,1)S(1)}, bf16[128,128]{1,0:T(8,128)(2,1)}, u32[]{:S(2)}) copy-start(bf16[128,128]{1,0:T(8,128)(2,1)} %rest_2_.1) | copy-start | bytes 98308
  45.8 8.8 %copy-start.10 = (bf16[128,128]{1,0:T(8,128)(2,1)S(1)}, bf16[128,128]{1,0:T(8,128)(2,1)}, u32[]{:S(2)}) copy-start(bf16[128,128]{1,0:T(8,128)(2,1)} %rest_3_.1) | copy-start | bytes 98308
  52.6 2.0 %collective-permute-start.12 = (bf16[2048,128]{1,0:T(8,128)(2,1)S(1)}, bf16[2048,128]{1,0:T(8,128)(2,1)S(1)}, u32[]{:S(2)}, u32[]{:S(2)}) collective-permute-start(bf16[2048,128]{1,0:T(8,128)(2,1)S(1)} %get-tuple-element.30.right_own_ref), channel_id=1, source_target_pairs={{0,1},{1,0},{2,3},{3,2},{4,5},{5,4},{6,7},{7,6},{8,9},{9,8},{10,11... | collective-permute-start | bytes 1572872 | tf_op jit(solution)/shard_map/ppermute | solution.py:470
  62.7 1.4 %collective-permute-start.13 = (f32[2,128,128]{2,1,0:T(8,128)S(1)}, f32[2,128,128]{2,1,0:T(8,128)S(1)}, u32[]{:S(2)}, u32[]{:S(2)}) collective-permute-start(f32[2,128,128]{2,1,0:T(8,128)S(1)} %get-tuple-element.33), channel_id=1, source_target_pairs={{0,1},{1,0},{2,3},{3,2},{4,5},{5,4},{6,7},{7,6},{8,9},{9,8},{10,11... | collective-permute-start | bytes 393224 | tf_op jit(solution)/shard_map/ppermute | solution.py:470
  (1 other events, 0.8 us)

commit v12 on v11

--- a/solution.py
+++ b/solution.py
@@ -515,6 +515,7 @@
     pair_first = jnp.stack([own_pair, exchange(own_pair, 8)])
     blocks, pair_first = lax.optimization_barrier((blocks, pair_first))
     pair_second = exchange(pair_first, 4)
+    pair_across = exchange(pair_first, 2)
 
     result, parts = pl.pallas_call(
         msa_kernel,
@@ -547,9 +548,10 @@
         alignment_transition_down,
         outer_input_weight.T,
     )
-    parts, pair_second = lax.optimization_barrier((parts, pair_second))
-    pair_pieces = [pair_first, pair_second, exchange(pair_first, 2), exchange(pair_second, 2)]
-    first = jnp.stack([parts, exchange(parts, 8)])
+    parts, pair_second, pair_across = lax.optimization_barrier((parts, pair_second, pair_across))
+    far, pair_last = lax.optimization_barrier((exchange(parts, 8), exchange(pair_second, 2)))
+    pair_pieces = [pair_first, pair_second, pair_across, pair_last]
+    first = jnp.stack([parts, far])
     second = exchange(first, 4)
     pieces = [first, second, exchange(first, 2), exchange(second, 2)]
     core_pieces = [exchange(piece, 1) for piece in pieces]

time: 65.9 us -> 66.1 us (level)
  starting transfers between devices: 17.6 us -> 19.1 us
  waiting for transfers between devices: 22.2 us -> 20.9 us
    ppermute x14, starting transfers between devices: 10.1 us -> 11.6 us  [exchange(): return lax.ppermute(values, 'dap', [(q, q ^ offset) for q in range(pieces)])]
    ppermute x14, waiting for transfers between devices: 22.2 us -> 20.9 us  [exchange(): return lax.ppermute(values, 'dap', [(q, q ^ offset) for q in range(pieces)])]
  transfers between devices with their start and end apart: 15 -> 15, of which waited for: 10 -> 8; matrix products, arithmetic and copies ran while one was open for 4% -> 4% of each run, Pallas kernels for 6% -> 6%
where the time goes in v12:
time: 66.1 us; the launch traced here: 65.8 us
  waiting for transfers between devices  20.9 us (32%)
  Pallas kernels  20.4 us (31%)
  starting transfers between devices  19.1 us (29%)
  local copies, waits for them, and re-layouts  3.11 us (5%)
  other arithmetic  1.39 us (2%)
  between operations  0.91 us (1%)
    ppermute x14, waiting for transfers between devices, exchange(): return lax.ppermute(values, 'dap', [(q, q ^ offset) for q in range(pieces)])  20.9 us
    ppermute x14, starting transfers between devices, exchange(): return lax.ppermute(values, 'dap', [(q, q ^ offset) for q in range(pieces)])  11.6 us
    pallas_call x1, Pallas kernels, whole_block(): pl.pallas_call(triangle_kernel, out_shape=[wide(2, 128, LANES)] * 3 + [ar...  8.08 us
    all_to_all x1, starting transfers between devices, whole_block(): lax.all_to_all(blocks, 'dap', split_axis=0, concat_axis=0, tiled=True)  7.52 us
    pallas_call x1, Pallas kernels, whole_block(): pl.pallas_call(start_kernel, out_shape=[wide(*slabs), wide(*tall), wide(*...  5.58 us
    pallas_call x1, Pallas kernels, whole_block(): pl.pallas_call(msa_kernel, out_shape=(array(512, channels), array(256, LA...  4.11 us
    unnamed x36, local copies, waits for them, and re-layouts  1.87 us
    pallas_call x1, Pallas kernels, whole_block(): pl.pallas_call(finish_kernel, out_shape=array(256, LANES), in_specs=[vmem...  1.52 us
  transfers between devices with their start and end apart: 15, of which 8 were waited for; matrix products, arithmetic and copies ran while one was open for 4% of the time, Pallas kernels for 6%

profile of v12, /device:TPU:0, one launch (start us, length us, event | category | flops | bytes accessed | tf_op | source)
XLA Modules:
  0.0 65.8 jit_solution(13421356390780473063)
XLA Ops:
  0.6 0.9 %copy-done.1 = bf16[8,64,256]{2,1,0:T(8,128)(2,1)S(1)} copy-done((bf16[8,64,256]{2,1,0:T(8,128)(2,1)S(1)}, bf16[8,64,256]{2,1,0:T(8,128)(2,1)}, u32[]{:S(2)}) %copy-start.1) | copy-done | bytes 262168
  1.6 0.8 %copy-done.6 = bf16[4,64,128]{2,1,0:T(8,128)(2,1)S(1)} copy-done((bf16[4,64,128]{2,1,0:T(8,128)(2,1)S(1)}, bf16[4,64,128]{2,1,0:T(8,128)(2,1)}, u32[]{:S(2)}) %copy-start.6) | copy-done | bytes 65560
  2.4 1.1 %rows_by_device.1 = (bf16[16,32,256]{2,1,0:T(8,128)(2,1)}, bf16[2,128,128]{2,1,0:T(8,128)(2,1)S(1)}) custom-call(bf16[8,64,256]{2,1,0:T(8,128)(2,1)S(1)} %copy-done.1, bf16[4,64,128]{2,1,0:T(8,128)(2,1)S(1)} %copy-done.6), custom_call_target="tpu_custom_call" | custom-call | tf_op jit(solution)/shard_map/rows_by_device/pallas_call | solution.py:504
  3.6 7.5 %all-to-all-start = ((bf16[16,32,256]{2,1,0:T(8,128)(2,1)}), bf16[16,32,256]{2,1,0:T(8,128)(2,1)S(1)}, u32[]{:S(2)}, u32[]{:S(2)}) async-start(bf16[16,32,256]{2,1,0:T(8,128)(2,1)} %get-tuple-element.22), calls=%async_computation | async-start | bytes 524288 | tf_op jit(solution)/shard_map/all_to_all | solution.py:513
  11.1 2.8 %collective-permute-start = (bf16[2,128,128]{2,1,0:T(8,128)(2,1)S(1)}, bf16[2,128,128]{2,1,0:T(8,128)(2,1)S(1)}, u32[]{:S(2)}, u32[]{:S(2)}) collective-permute-start(bf16[2,128,128]{2,1,0:T(8,128)(2,1)S(1)} %get-tuple-element.23), channel_id=1, source_target_pairs={{0,8},{1,9},{2,10},{3,11},{4,12},{5,13},{6,14},{7,15},{8,0},{9,1},... | collective-permute-start | bytes 196616 | tf_op jit(solution)/shard_map/ppermute | solution.py:470
  13.9 1.2 %pad_maximum_fusion.narrow_ref = bf16[256,1280]{1,0:T(8,128)(2,1)S(1)} fusion(bf16[256,256]{1,0:T(8,128)(2,1)} %param.31, bf16[256,512]{1,0:T(8,128)(2,1)} %param.30, bf16[256,256]{1,0:T(8,128)(2,1)} %param.29, bf16[256,256]{1,0:T(8,128)(2,1)} %param.28), kind=kLoop, calls=%fused_computation | loop fusion | flops 2621440 | bytes 1310720 | tf_op jit(solution)/shard_map/concatenate | solution.py:538
  15.1 8.4 %collective-permute-done = bf16[2,128,128]{2,1,0:T(8,128)(2,1)S(1)} collective-permute-done((bf16[2,128,128]{2,1,0:T(8,128)(2,1)S(1)}, bf16[2,128,128]{2,1,0:T(8,128)(2,1)S(1)}, u32[]{:S(2)}, u32[]{:S(2)}) %collective-permute-start) | collective-permute-done | bytes 65568 | tf_op jit(solution)/shard_map/ppermute | solution.py:470
  23.6 1.5 %collective-permute-start.2 = (bf16[2,2,128,128]{3,2,1,0:T(8,128)(2,1)S(1)}, bf16[2,2,128,128]{3,2,1,0:T(8,128)(2,1)S(1)}, u32[]{:S(2)}, u32[]{:S(2)}) collective-permute-start(bf16[2,2,128,128]{3,2,1,0:T(8,128)(2,1)S(1)} %pad_maximum_fusion.1.rest_8_), channel_id=1, source_target_pairs={{0,2},{1,3},{2,0},{3,1},{4,6},{5,7},{6,4},{7,5},{8,10},{9,11},{10,... | collective-permute-start | bytes 393224 | tf_op jit(solution)/shard_map/ppermute | solution.py:470
  25.2 4.1 %msa_whole.1 = (bf16[512,256]{1,0:T(8,128)(2,1)S(1)}, bf16[256,128]{1,0:T(8,128)(2,1)S(1)}) custom-call(f32[1,128]{1,0:T(1,128)S(1)} %fusion.live_ref, bf16[16,32,256]{2,1,0:T(8,128)(2,1)S(1)} %all-to-all-done.blocks_ref, bf16[256,1280]{1,0:T(8,128)(2,1)S(1)} %pad_maximum_fusion.narrow_ref, bf16[256,1024]{1,0:T(8,128)(2,1)S(1)} %copy-done.12, ...), custom_call_target="tpu_custom_call" | custom-call | flops 2000000000 | bytes 10000000 | tf_op jit(solution)/shard_map/msa_whole/pallas_call | solution.py:520
  29.3 0.8 %collective-permute-done.1.rest_9_ = bf16[2,2,128,128]{3,2,1,0:T(8,128)(2,1)S(1)} collective-permute-done((bf16[2,2,128,128]{3,2,1,0:T(8,128)(2,1)S(1)}, bf16[2,2,128,128]{3,2,1,0:T(8,128)(2,1)S(1)}, u32[]{:S(2)}, u32[]{:S(2)}) %collective-permute-start.1) | collective-permute-done | bytes 131104 | tf_op jit(solution)/shard_map/ppermute | solution.py:470
  30.1 0.6 collective-permute-start.4
  30.6 1.3 %collective-permute-start.3 = (bf16[256,128]{1,0:T(8,128)(2,1)S(1)}, bf16[256,128]{1,0:T(8,128)(2,1)S(1)}, u32[]{:S(2)}, u32[]{:S(2)}) collective-permute-start(bf16[256,128]{1,0:T(8,128)(2,1)S(1)} %get-tuple-element.28), channel_id=1, source_target_pairs={{0,8},{1,9},{2,10},{3,11},{4,12},{5,13},{6,14},{7,15},{8,0},{9,1},... | collective-permute-start | bytes 196616 | tf_op jit(solution)/shard_map/ppermute | solution.py:470
  32.0 3.8 %collective-permute-done.3 = bf16[256,128]{1,0:T(8,128)(2,1)S(1)} collective-permute-done((bf16[256,128]{1,0:T(8,128)(2,1)S(1)}, bf16[256,128]{1,0:T(8,128)(2,1)S(1)}, u32[]{:S(2)}, u32[]{:S(2)}) %collective-permute-start.3) | collective-permute-done | bytes 65568 | tf_op jit(solution)/shard_map/ppermute | solution.py:470
  35.8 1.4 %collective-permute-start.5 = (bf16[2,256,128]{2,1,0:T(8,128)(2,1)S(1)}, bf16[2,256,128]{2,1,0:T(8,128)(2,1)S(1)}, u32[]{:S(2)}, u32[]{:S(2)}) collective-permute-start(bf16[2,256,128]{2,1,0:T(8,128)(2,1)S(1)} %pad_maximum_fusion.2.rest_0_), channel_id=1, source_target_pairs={{0,4},{1,5},{2,6},{3,7},{4,0},{5,1},{6,2},{7,3},{8,12},{9,13},{10,... | collective-permute-start | bytes 393224 | tf_op jit(solution)/shard_map/ppermute | solution.py:470
  37.2 1.5 %collective-permute-start.6 = (bf16[2,256,128]{2,1,0:T(8,128)(2,1)S(1)}, bf16[2,256,128]{2,1,0:T(8,128)(2,1)S(1)}, u32[]{:S(2)}, u32[]{:S(2)}) collective-permute-start(bf16[2,256,128]{2,1,0:T(8,128)(2,1)S(1)} %pad_maximum_fusion.2.rest_0_), channel_id=1, source_target_pairs={{0,2},{1,3},{2,0},{3,1},{4,6},{5,7},{6,4},{7,5},{8,10},{9,11},{10,... | collective-permute-start | bytes 393224 | tf_op jit(solution)/shard_map/ppermute | solution.py:470
  38.7 2.2 %collective-permute-done.5.rest_1_ = bf16[2,256,128]{2,1,0:T(8,128)(2,1)S(1)} collective-permute-done((bf16[2,256,128]{2,1,0:T(8,128)(2,1)S(1)}, bf16[2,256,128]{2,1,0:T(8,128)(2,1)S(1)}, u32[]{:S(2)}, u32[]{:S(2)}) %collective-permute-start.5) | collective-permute-done | bytes 131104 | tf_op jit(solution)/shard_map/ppermute | solution.py:470
  40.9 1.5 %collective-permute-start.7 = (bf16[2,256,128]{2,1,0:T(8,128)(2,1)S(1)}, bf16[2,256,128]{2,1,0:T(8,128)(2,1)S(1)}, u32[]{:S(2)}, u32[]{:S(2)}) collective-permute-start(bf16[2,256,128]{2,1,0:T(8,128)(2,1)S(1)} %collective-permute-done.5.rest_1_), channel_id=1, source_target_pairs={{0,2},{1,3},{2,0},{3,1},{4,6},{5,7},{6,4},{7,5},{8,10},{9,11},{10,... | collective-permute-start | bytes 393224 | tf_op jit(solution)/shard_map/ppermute | solution.py:470
  42.3 0.1 sub.22
  42.5 0.1 eq.22
  42.7 0.5 collective-permute-start.9
  43.3 2.5 %collective-permute-done.7.rest_3_ = bf16[2,256,128]{2,1,0:T(8,128)(2,1)S(1)} collective-permute-done((bf16[2,256,128]{2,1,0:T(8,128)(2,1)S(1)}, bf16[2,256,128]{2,1,0:T(8,128)(2,1)S(1)}, u32[]{:S(2)}, u32[]{:S(2)}) %collective-permute-start.7) | collective-permute-done | bytes 131104 | tf_op jit(solution)/shard_map/ppermute | solution.py:470
  45.8 0.2 compare_select_fusion
  46.1 0.1 select_n.11.bins_ref
  46.2 0.9 %collective-permute-done.11.rest_7_ = bf16[2,256,128]{2,1,0:T(8,128)(2,1)S(1)} collective-permute-done((bf16[2,256,128]{2,1,0:T(8,128)(2,1)S(1)}, bf16[2,256,128]{2,1,0:T(8,128)(2,1)S(1)}, u32[]{:S(2)}, u32[]{:S(2)}) %collective-permute-start.11) | collective-permute-done | bytes 131104 | tf_op jit(solution)/shard_map/ppermute | solution.py:470
  47.2 5.6 %pair_start.1 = (f32[16,128,128]{2,1,0:T(8,128)S(1)}, f32[2048,128]{1,0:T(8,128)S(1)}, f32[16,128,128]{2,1,0:T(8,128)S(1)}, bf16[2048,128]{1,0:T(8,128)(2,1)S(1)}) custom-call(s32[1]{0:T(128)} %bitcast.4.place_ref, f32[1,128]{1,0:T(1,128)S(1)} %fusion.live_ref, s32[32,128]{1,0:T(8,128)S(1)} %select_n.11.bins_ref, bf16[66,128]{1,0:T(8,128)(2,1)S(1)} %copy-done.11, ...), custom_call_target="tpu_custom_call" | custom-call | tf_op jit(solution)/shard_map/pair_start/pallas_call | solution.py:561
  52.8 0.2 collective-permute-start.12
  53.0 1.8 %collective-permute-done.12.right_other_ref = bf16[2048,128]{1,0:T(8,128)(2,1)S(1)} collective-permute-done((bf16[2048,128]{1,0:T(8,128)(2,1)S(1)}, bf16[2048,128]{1,0:T(8,128)(2,1)S(1)}, u32[]{:S(2)}, u32[]{:S(2)}) %collective-permute-start.12) | collective-permute-done | bytes 524320 | tf_op jit(solution)/shard_map/ppermute | solution.py:470
  54.8 8.1 %pair_triangles.1 = (f32[2,128,128]{2,1,0:T(8,128)S(1)}, f32[2,128,128]{2,1,0:T(8,128)S(1)}, f32[2,128,128]{2,1,0:T(8,128)S(1)}, bf16[768,128]{1,0:T(8,128)(2,1)S(1)}, bf16[128,512]{1,0:T(8,128)(2,1)S(1)}) custom-call(s32[1]{0:T(128)} %bitcast.4.place_ref, f32[16,128,128]{2,1,0:T(8,128)S(1)} %get-tuple-element.33.pair_mid_ref, ...), custom_call_target="tpu_custom_call" | custom-call | tf_op jit(solution)/shard_map/pair_triangles/pallas_call | solution.py:589
  62.9 0.2 collective-permute-start.13
  63.1 0.8 %reshape.59 = bf16[128,4,256]{2,1,0:T(4,128)(2,1)} reshape(bf16[512,256]{1,0:T(8,128)(2,1)S(1)} %get-tuple-element.25) | data formatting | bytes 524288 | tf_op jit(solution)/shard_map/reshape | solution.py:615
  63.8 0.4 collective-permute-done.13.other_part_ref
  64.3 1.5 %pair_finish.1 = bf16[256,128]{1,0:T(8,128)(2,1)} custom-call(f32[2,128,128]{2,1,0:T(8,128)S(1)} %get-tuple-element.37.own_pair_ref, f32[2,128,128]{2,1,0:T(8,128)S(1)} %get-tuple-element.38.own_part_ref, f32[2,128,128]{2,1,0:T(8,128)S(1)} %collective-permute-done.13.other_part_ref, bf16[768,128]{1,0:T(8,128)(2,1)S(1)} %get-tuple-element.40.narrow_ref, ...), custom_call_target="tpu_custom_call" | custom-call | tf_op jit(solution)/shard_map/pair_finish/pallas_call | solution.py:607
  (50 shorter events, 0.4 us)
Async XLA Ops:
  0.6 1.0 %copy-start.1 = (bf16[8,64,256]{2,1,0:T(8,128)(2,1)S(1)}, bf16[8,64,256]{2,1,0:T(8,128)(2,1)}, u32[]{:S(2)}) copy-start(bf16[8,64,256]{2,1,0:T(8,128)(2,1)} %rows_ref.1) | copy-start | bytes 786436
  2.4 12.7 %copy-start.17 = (s32[128]{0:T(128)S(1)}, s32[128]{0:T(128)}, u32[]{:S(2)}) copy-start(s32[128]{0:T(128)} %param.26) | copy-start | bytes 1540
  3.6 21.5 %copy-start.12 = (bf16[256,1024]{1,0:T(8,128)(2,1)S(1)}, bf16[256,1024]{1,0:T(8,128)(2,1)}, u32[]{:S(2)}) copy-start(bf16[256,1024]{1,0:T(8,128)(2,1)} %up_ref.1) | copy-start | bytes 1572868
  3.6 21.6 %copy-start.13 = (bf16[1024,256]{1,0:T(8,128)(2,1)S(1)}, bf16[1024,256]{1,0:T(8,128)(2,1)}, u32[]{:S(2)}) copy-start(bf16[1024,256]{1,0:T(8,128)(2,1)} %down_ref.1) | copy-start | bytes 1572868
  3.6 21.6 %copy-start.14 = (bf16[256,64]{0,1:T(8,128)(2,1)S(1)}, bf16[256,64]{0,1:T(8,128)(2,1)}, u32[]{:S(2)}) copy-start(bf16[256,64]{0,1:T(8,128)(2,1)} %param.34) | copy-start | bytes 98308
  3.6 20.0 %all-to-all-start = ((bf16[16,32,256]{2,1,0:T(8,128)(2,1)}), bf16[16,32,256]{2,1,0:T(8,128)(2,1)S(1)}, u32[]{:S(2)}, u32[]{:S(2)}) async-start(bf16[16,32,256]{2,1,0:T(8,128)(2,1)} %get-tuple-element.22), calls=%async_computation | async-start | bytes 524288 | tf_op jit(solution)/shard_map/all_to_all | solution.py:513
  11.1 12.5 %collective-permute-start = (bf16[2,128,128]{2,1,0:T(8,128)(2,1)S(1)}, bf16[2,128,128]{2,1,0:T(8,128)(2,1)S(1)}, u32[]{:S(2)}, u32[]{:S(2)}) collective-permute-start(bf16[2,128,128]{2,1,0:T(8,128)(2,1)S(1)} %get-tuple-element.23), channel_id=1, source_target_pairs={{0,8},{1,9},{2,10},{3,11},{4,12},{5,13},{6,14},{7,15},{8,0},{9,1},... | collective-permute-start | bytes 196616 | tf_op jit(solution)/shard_map/ppermute | solution.py:470
  23.6 5.7 %collective-permute-start.2 = (bf16[2,2,128,128]{3,2,1,0:T(8,128)(2,1)S(1)}, bf16[2,2,128,128]{3,2,1,0:T(8,128)(2,1)S(1)}, u32[]{:S(2)}, u32[]{:S(2)}) collective-permute-start(bf16[2,2,128,128]{3,2,1,0:T(8,128)(2,1)S(1)} %pad_maximum_fusion.1.rest_8_), channel_id=1, source_target_pairs={{0,2},{1,3},{2,0},{3,1},{4,6},{5,7},{6,4},{7,5},{8,10},{9,11},{10,... | collective-permute-start | bytes 393224 | tf_op jit(solution)/shard_map/ppermute | solution.py:470
  25.1 5.0 %collective-permute-start.1 = (bf16[2,2,128,128]{3,2,1,0:T(8,128)(2,1)S(1)}, bf16[2,2,128,128]{3,2,1,0:T(8,128)(2,1)S(1)}, u32[]{:S(2)}, u32[]{:S(2)}) collective-permute-start(bf16[2,2,128,128]{3,2,1,0:T(8,128)(2,1)S(1)} %pad_maximum_fusion.1.rest_8_), channel_id=1, source_target_pairs={{0,4},{1,5},{2,6},{3,7},{4,0},{5,1},{6,2},{7,3},{8,12},{9,13},{10,... | collective-permute-start | bytes 393224 | tf_op jit(solution)/shard_map/ppermute | solution.py:470
  25.1 17.2 %copy-start.15 = (s32[64]{0:T(128)S(1)}, s32[64]{0:T(128)}, u32[]{:S(2)}) copy-start(s32[64]{0:T(128)} %param.24) | copy-start | bytes 772
  25.1 17.4 %copy-start.16 = (s32[64]{0:T(128)S(1)}, s32[64]{0:T(128)}, u32[]{:S(2)}) copy-start(s32[64]{0:T(128)} %param.25) | copy-start | bytes 772
  25.1 22.0 %copy-start = (bf16[1024,128]{1,0:T(8,128)(2,1)S(1)}, bf16[1024,128]{1,0:T(8,128)(2,1)}, u32[]{:S(2)}) copy-start(bf16[1024,128]{1,0:T(8,128)(2,1)} %rest_12_.1) | copy-start | bytes 786436
  25.2 22.0 %copy-start.2 = (bf16[128,512]{1,0:T(8,128)(2,1)S(1)}, bf16[128,512]{1,0:T(8,128)(2,1)}, u32[]{:S(2)}) copy-start(bf16[128,512]{1,0:T(8,128)(2,1)} %rest_13_.1) | copy-start | bytes 393220
  25.2 22.0 %copy-start.7 = (bf16[128,128]{1,0:T(8,128)(2,1)S(1)}, bf16[128,128]{1,0:T(8,128)(2,1)}, u32[]{:S(2)}) copy-start(bf16[128,128]{1,0:T(8,128)(2,1)} %rest_14_.1) | copy-start | bytes 98308
  25.2 22.0 %copy-start.11 = (bf16[66,128]{1,0:T(8,128)(2,1)S(1)}, bf16[66,128]{1,0:T(8,128)(2,1)}, u32[]{:S(2)}) copy-start(bf16[66,128]{1,0:T(8,128)(2,1)} %table_ref.1) | copy-start | bytes 50692
  30.1 5.7 %collective-permute-start.4 = (bf16[2,2,128,128]{3,2,1,0:T(8,128)(2,1)S(1)}, bf16[2,2,128,128]{3,2,1,0:T(8,128)(2,1)S(1)}, u32[]{:S(2)}, u32[]{:S(2)}) collective-permute-start(bf16[2,2,128,128]{3,2,1,0:T(8,128)(2,1)S(1)} %collective-permute-done.1.rest_9_), channel_id=1, source_target_pairs={{0,2},{1,3},{2,0},{3,1},{4,6},{5,7},{6,4},{7,5},{8,10},{9,11},{10,... | collective-permute-start | bytes 393224 | tf_op jit(solution)/shard_map/ppermute | solution.py:470
  30.6 5.2 %collective-permute-start.3 = (bf16[256,128]{1,0:T(8,128)(2,1)S(1)}, bf16[256,128]{1,0:T(8,128)(2,1)S(1)}, u32[]{:S(2)}, u32[]{:S(2)}) collective-permute-start(bf16[256,128]{1,0:T(8,128)(2,1)S(1)} %get-tuple-element.28), channel_id=1, source_target_pairs={{0,8},{1,9},{2,10},{3,11},{4,12},{5,13},{6,14},{7,15},{8,0},{9,1},... | collective-permute-start | bytes 196616 | tf_op jit(solution)/shard_map/ppermute | solution.py:470
  35.8 5.0 %collective-permute-start.5 = (bf16[2,256,128]{2,1,0:T(8,128)(2,1)S(1)}, bf16[2,256,128]{2,1,0:T(8,128)(2,1)S(1)}, u32[]{:S(2)}, u32[]{:S(2)}) collective-permute-start(bf16[2,256,128]{2,1,0:T(8,128)(2,1)S(1)} %pad_maximum_fusion.2.rest_0_), channel_id=1, source_target_pairs={{0,4},{1,5},{2,6},{3,7},{4,0},{5,1},{6,2},{7,3},{8,12},{9,13},{10,... | collective-permute-start | bytes 393224 | tf_op jit(solution)/shard_map/ppermute | solution.py:470
  37.2 6.0 %collective-permute-start.6 = (bf16[2,256,128]{2,1,0:T(8,128)(2,1)S(1)}, bf16[2,256,128]{2,1,0:T(8,128)(2,1)S(1)}, u32[]{:S(2)}, u32[]{:S(2)}) collective-permute-start(bf16[2,256,128]{2,1,0:T(8,128)(2,1)S(1)} %pad_maximum_fusion.2.rest_0_), channel_id=1, source_target_pairs={{0,2},{1,3},{2,0},{3,1},{4,6},{5,7},{6,4},{7,5},{8,10},{9,11},{10,... | collective-permute-start | bytes 393224 | tf_op jit(solution)/shard_map/ppermute | solution.py:470
  40.9 5.0 %collective-permute-start.7 = (bf16[2,256,128]{2,1,0:T(8,128)(2,1)S(1)}, bf16[2,256,128]{2,1,0:T(8,128)(2,1)S(1)}, u32[]{:S(2)}, u32[]{:S(2)}) collective-permute-start(bf16[2,256,128]{2,1,0:T(8,128)(2,1)S(1)} %collective-permute-done.5.rest_1_), channel_id=1, source_target_pairs={{0,2},{1,3},{2,0},{3,1},{4,6},{5,7},{6,4},{7,5},{8,10},{9,11},{10,... | collective-permute-start | bytes 393224 | tf_op jit(solution)/shard_map/ppermute | solution.py:470
  42.7 3.5 %collective-permute-start.8 = (bf16[2,256,128]{2,1,0:T(8,128)(2,1)S(1)}, bf16[2,256,128]{2,1,0:T(8,128)(2,1)S(1)}, u32[]{:S(2)}, u32[]{:S(2)}) collective-permute-start(bf16[2,256,128]{2,1,0:T(8,128)(2,1)S(1)} %pad_maximum_fusion.2.rest_0_), channel_id=1, source_target_pairs={{0,1},{1,0},{2,3},{3,2},{4,5},{5,4},{6,7},{7,6},{8,9},{9,8},{10,11... | collective-permute-start | bytes 393224 | tf_op jit(solution)/shard_map/ppermute | solution.py:470
  42.7 3.5 %collective-permute-start.9 = (bf16[2,256,128]{2,1,0:T(8,128)(2,1)S(1)}, bf16[2,256,128]{2,1,0:T(8,128)(2,1)S(1)}, u32[]{:S(2)}, u32[]{:S(2)}) collective-permute-start(bf16[2,256,128]{2,1,0:T(8,128)(2,1)S(1)} %collective-permute-done.5.rest_1_), channel_id=1, source_target_pairs={{0,1},{1,0},{2,3},{3,2},{4,5},{5,4},{6,7},{7,6},{8,9},{9,8},{10,11... | collective-permute-start | bytes 393224 | tf_op jit(solution)/shard_map/ppermute | solution.py:470
  43.2 3.0 %collective-permute-start.10 = (bf16[2,256,128]{2,1,0:T(8,128)(2,1)S(1)}, bf16[2,256,128]{2,1,0:T(8,128)(2,1)S(1)}, u32[]{:S(2)}, u32[]{:S(2)}) collective-permute-start(bf16[2,256,128]{2,1,0:T(8,128)(2,1)S(1)} %collective-permute-done.6.rest_2_), channel_id=1, source_target_pairs={{0,1},{1,0},{2,3},{3,2},{4,5},{5,4},{6,7},{7,6},{8,9},{9,8},{10,11... | collective-permute-start | bytes 393224 | tf_op jit(solution)/shard_map/ppermute | solution.py:470
  45.8 1.3 %collective-permute-start.11 = (bf16[2,256,128]{2,1,0:T(8,128)(2,1)S(1)}, bf16[2,256,128]{2,1,0:T(8,128)(2,1)S(1)}, u32[]{:S(2)}, u32[]{:S(2)}) collective-permute-start(bf16[2,256,128]{2,1,0:T(8,128)(2,1)S(1)} %collective-permute-done.7.rest_3_), channel_id=1, source_target_pairs={{0,1},{1,0},{2,3},{3,2},{4,5},{5,4},{6,7},{7,6},{8,9},{9,8},{10,11... | collective-permute-start | bytes 393224 | tf_op jit(solution)/shard_map/ppermute | solution.py:470
  46.0 8.7 %copy-start.3 = (bf16[128,512]{1,0:T(8,128)(2,1)S(1)}, bf16[128,512]{1,0:T(8,128)(2,1)}, u32[]{:S(2)}) copy-start(bf16[128,512]{1,0:T(8,128)(2,1)} %rest_1_.1) | copy-start | bytes 393220
  46.0 8.7 %copy-start.4 = (bf16[128,512]{1,0:T(8,128)(2,1)S(1)}, bf16[128,512]{1,0:T(8,128)(2,1)}, u32[]{:S(2)}) copy-start(bf16[128,512]{1,0:T(8,128)(2,1)} %rest_4_.1) | copy-start | bytes 393220
  46.1 8.7 %copy-start.5 = (bf16[512,128]{1,0:T(8,128)(2,1)S(1)}, bf16[512,128]{1,0:T(8,128)(2,1)}, u32[]{:S(2)}) copy-start(bf16[512,128]{1,0:T(8,128)(2,1)} %rest_5_.1) | copy-start | bytes 393220
  46.1 8.7 %copy-start.8 = (bf16[128,128]{1,0:T(8,128)(2,1)S(1)}, bf16[128,128]{1,0:T(8,128)(2,1)}, u32[]{:S(2)}) copy-start(bf16[128,128]{1,0:T(8,128)(2,1)} %rest_0_.1) | copy-start | bytes 98308
  46.1 8.7 %copy-start.9 = (bf16[128,128]{1,0:T(8,128)(2,1)S(1)}, bf16[128,128]{1,0:T(8,128)(2,1)}, u32[]{:S(2)}) copy-start(bf16[128,128]{1,0:T(8,128)(2,1)} %rest_2_.1) | copy-start | bytes 98308
  46.1 8.7 %copy-start.10 = (bf16[128,128]{1,0:T(8,128)(2,1)S(1)}, bf16[128,128]{1,0:T(8,128)(2,1)}, u32[]{:S(2)}) copy-start(bf16[128,128]{1,0:T(8,128)(2,1)} %rest_3_.1) | copy-start | bytes 98308
  52.8 2.0 %collective-permute-start.12 = (bf16[2048,128]{1,0:T(8,128)(2,1)S(1)}, bf16[2048,128]{1,0:T(8,128)(2,1)S(1)}, u32[]{:S(2)}, u32[]{:S(2)}) collective-permute-start(bf16[2048,128]{1,0:T(8,128)(2,1)S(1)} %get-tuple-element.36.right_own_ref), channel_id=1, source_target_pairs={{0,1},{1,0},{2,3},{3,2},{4,5},{5,4},{6,7},{7,6},{8,9},{9,8},{10,11... | collective-permute-start | bytes 1572872 | tf_op jit(solution)/shard_map/ppermute | solution.py:470
  62.9 1.4 %collective-permute-start.13 = (f32[2,128,128]{2,1,0:T(8,128)S(1)}, f32[2,128,128]{2,1,0:T(8,128)S(1)}, u32[]{:S(2)}, u32[]{:S(2)}) collective-permute-start(f32[2,128,128]{2,1,0:T(8,128)S(1)} %get-tuple-element.39), channel_id=1, source_target_pairs={{0,1},{1,0},{2,3},{3,2},{4,5},{5,4},{6,7},{7,6},{8,9},{9,8},{10,11... | collective-permute-start | bytes 393224 | tf_op jit(solution)/shard_map/ppermute | solution.py:470
  (1 other events, 0.8 us)

commit v13 on v11

--- a/solution.py
+++ b/solution.py
@@ -127,7 +127,7 @@
 
 def start_kernel(place_ref, live_ref, bins_ref, table_ref, *rest):
     part_refs, core_refs, pair_refs, sources = rest[:4], rest[4:8], rest[8:12], rest[12:15]
-    pair_mid_ref, left_ref, gating_ref, right_ref = rest[15:19]
+    pair_mid_ref, normed_ref, mix_ref, right_ref = rest[15:19]
     wide_ref, right_cols_ref, mean_wide_ref, mean_weight_ref, table_wide_ref = rest[19:24]
     stack_refs, landed, arrived = rest[24:26], rest[26:29], rest[29]
     copies = start_copies(sources, landed, arrived)
@@ -204,16 +204,28 @@
             slabs.append(normalize_channels(slab))
             places.append(here)
         normed = jnp.concatenate(slabs, axis=1)
-        combined = mix(out_mix, normed)
-        left = gate_curve(combined[128:256]) * combined[0:128]
-        right = gate_curve(combined[384:512]) * combined[256:384]
-        gating = gate_curve(mix(out_gate, normed))
+        combined = mix(out_mix[256:512], normed)
+        right = gate_curve(combined[128:256]) * combined[0:128]
         for q in range(4):
             lanes = slice(q * LANES, (q + 1) * LANES)
             rows = pl.ds(pl.multiple_of(places[q] * 128, 128), 128)
-            left_ref[rows, :] = left[:, lanes]
             right_ref[rows, :] = right[:, lanes].astype(jnp.bfloat16)
-            gating_ref[places[q]] = gating[:, lanes]
+            normed_ref[places[q]] = normed[:, lanes]
+    mix_ref[0:256, :] = out_mix[0:256]
+    mix_ref[256:384, :] = out_gate
+
+
+def gates_kernel(normed_ref, mix_ref, left_ref, gating_ref):
+    for g in range(4):
+        normed = jnp.concatenate([normed_ref[4 * g + q] for q in range(4)], axis=1)
+        combined = mix(mix_ref[...], normed)
+        left = gate_curve(combined[128:256]) * combined[0:128]
+        gating = gate_curve(combined[256:384])
+        for q in range(4):
+            h = 4 * g + q
+            lanes = slice(q * LANES, (q + 1) * LANES)
+            left_ref[h * 128 : (h + 1) * 128, :] = left[:, lanes]
+            gating_ref[h] = gating[:, lanes]
 
 
 def triangle_kernel(
@@ -556,9 +568,9 @@
 
     slabs = (16, 128, LANES)
     tall = (16 * 128, LANES)
-    pair_mid, left, gating, right = pl.pallas_call(
+    pair_mid, normed, mix_weights, right = pl.pallas_call(
         start_kernel,
-        out_shape=[wide(*slabs), wide(*tall), wide(*slabs), array(*tall)],
+        out_shape=[wide(*slabs), array(*slabs), array(384, LANES), array(*tall)],
         in_specs=[smem] + [vmem] * 15 + [hbm] * 3,
         out_specs=[vmem] * 4,
         scratch_shapes=[
@@ -584,6 +596,18 @@
         *pair_pieces,
         *pair_weights[:3],
     )
+    other_right = exchange(right, 1)
+    left, gating = pl.pallas_call(
+        gates_kernel,
+        out_shape=[wide(*tall), wide(*slabs)],
+        in_specs=[vmem] * 2,
+        out_specs=[vmem] * 2,
+        compiler_params=limit(16),
+        cost_estimate=pl.CostEstimate(
+            flops=1_000_000_000, bytes_accessed=6_000_000, transcendentals=500_000
+        ),
+        name="pair_gates",
+    )(normed, mix_weights)
     own_pair, own_part, other_part, narrow_weights, down_weight = pl.pallas_call(
         triangle_kernel,
         out_shape=[wide(2, 128, LANES)] * 3 + [array(768, LANES), array(128, 512)],
@@ -601,7 +625,7 @@
         + [pltpu.SemaphoreType.DMA((6,))],
         compiler_params=limit(48),
         name="pair_triangles",
-    )(place, pair_mid, left, gating, right, exchange(right, 1), *pair_weights[3:])
+    )(place, pair_mid, left, gating, right, other_right, *pair_weights[3:])
     pair_output = pl.pallas_call(
         finish_kernel,
         out_shape=array(256, LANES),

time: 65.9 us -> 66 us (level)
  Pallas kernels: 20.4 us -> 21.1 us
    pallas_call x1 -> x2, Pallas kernels: 5.58 us -> 5.73 us  [the longest x1 5.16 us: whole_block(): pl.pallas_call(start_kernel, out_shape=[wide(*slabs), array(*slabs), arra...]
  transfers between devices with their start and end apart: 15 -> 15, of which waited for: 10 -> 10; matrix products, arithmetic and copies ran while one was open for 4% -> 4% of each run, Pallas kernels for 6% -> 7%
where the time goes in v13:
time: 66 us; the launch traced here: 65.7 us
  waiting for transfers between devices  21.7 us (33%)
  Pallas kernels  21.1 us (32%)
  starting transfers between devices  17.6 us (27%)
  local copies, waits for them, and re-layouts  3.1 us (5%)
  other arithmetic  1.39 us (2%)
  between operations  0.92 us (1%)
    ppermute x14, waiting for transfers between devices, exchange(): return lax.ppermute(values, 'dap', [(q, q ^ offset) for q in range(pieces)])  21.7 us
    ppermute x14, starting transfers between devices, exchange(): return lax.ppermute(values, 'dap', [(q, q ^ offset) for q in range(pieces)])  10.1 us
    pallas_call x1, Pallas kernels, whole_block(): pl.pallas_call(triangle_kernel, out_shape=[wide(2, 128, LANES)] * 3 + [ar...  8.56 us
    all_to_all x1, starting transfers between devices, whole_block(): lax.all_to_all(blocks, 'dap', split_axis=0, concat_axis=0, tiled=True)  7.52 us
    pallas_call x1, Pallas kernels, whole_block(): pl.pallas_call(start_kernel, out_shape=[wide(*slabs), array(*slabs), arra...  5.16 us
    pallas_call x1, Pallas kernels, whole_block(): pl.pallas_call(msa_kernel, out_shape=(array(512, channels), array(256, LA...  4.11 us
    unnamed x36, local copies, waits for them, and re-layouts  1.86 us
    pallas_call x1, Pallas kernels, whole_block(): pl.pallas_call(finish_kernel, out_shape=array(256, LANES), in_specs=[vmem...  1.52 us
  transfers between devices with their start and end apart: 15, of which 10 were waited for; matrix products, arithmetic and copies ran while one was open for 4% of the time, Pallas kernels for 7%

profile of v13, /device:TPU:0, one launch (start us, length us, event | category | flops | bytes accessed | tf_op | source)
XLA Modules:
  0.0 65.7 jit_solution(4923970009185405084)
XLA Ops:
  0.6 0.9 %copy-done.1 = bf16[8,64,256]{2,1,0:T(8,128)(2,1)S(1)} copy-done((bf16[8,64,256]{2,1,0:T(8,128)(2,1)S(1)}, bf16[8,64,256]{2,1,0:T(8,128)(2,1)}, u32[]{:S(2)}) %copy-start.1) | copy-done | bytes 262168
  1.6 0.8 %copy-done.6 = bf16[4,64,128]{2,1,0:T(8,128)(2,1)S(1)} copy-done((bf16[4,64,128]{2,1,0:T(8,128)(2,1)S(1)}, bf16[4,64,128]{2,1,0:T(8,128)(2,1)}, u32[]{:S(2)}) %copy-start.6) | copy-done | bytes 65560
  2.4 1.1 %rows_by_device.1 = (bf16[16,32,256]{2,1,0:T(8,128)(2,1)}, bf16[2,128,128]{2,1,0:T(8,128)(2,1)S(1)}) custom-call(bf16[8,64,256]{2,1,0:T(8,128)(2,1)S(1)} %copy-done.1, bf16[4,64,128]{2,1,0:T(8,128)(2,1)S(1)} %copy-done.6), custom_call_target="tpu_custom_call" | custom-call | tf_op jit(solution)/shard_map/rows_by_device/pallas_call | solution.py:516
  3.6 7.5 %all-to-all-start = ((bf16[16,32,256]{2,1,0:T(8,128)(2,1)}), bf16[16,32,256]{2,1,0:T(8,128)(2,1)S(1)}, u32[]{:S(2)}, u32[]{:S(2)}) async-start(bf16[16,32,256]{2,1,0:T(8,128)(2,1)} %get-tuple-element.21), calls=%async_computation | async-start | bytes 524288 | tf_op jit(solution)/shard_map/all_to_all | solution.py:525
  11.1 2.8 %collective-permute-start = (bf16[2,128,128]{2,1,0:T(8,128)(2,1)S(1)}, bf16[2,128,128]{2,1,0:T(8,128)(2,1)S(1)}, u32[]{:S(2)}, u32[]{:S(2)}) collective-permute-start(bf16[2,128,128]{2,1,0:T(8,128)(2,1)S(1)} %get-tuple-element.22), channel_id=1, source_target_pairs={{0,8},{1,9},{2,10},{3,11},{4,12},{5,13},{6,14},{7,15},{8,0},{9,1},... | collective-permute-start | bytes 196616 | tf_op jit(solution)/shard_map/ppermute | solution.py:482
  13.9 1.2 %pad_maximum_fusion.narrow_ref = bf16[256,1280]{1,0:T(8,128)(2,1)S(1)} fusion(bf16[256,256]{1,0:T(8,128)(2,1)} %param.31, bf16[256,512]{1,0:T(8,128)(2,1)} %param.30, bf16[256,256]{1,0:T(8,128)(2,1)} %param.29, bf16[256,256]{1,0:T(8,128)(2,1)} %param.28), kind=kLoop, calls=%fused_computation | loop fusion | flops 2621440 | bytes 1310720 | tf_op jit(solution)/shard_map/concatenate | solution.py:549
  15.1 8.4 %collective-permute-done = bf16[2,128,128]{2,1,0:T(8,128)(2,1)S(1)} collective-permute-done((bf16[2,128,128]{2,1,0:T(8,128)(2,1)S(1)}, bf16[2,128,128]{2,1,0:T(8,128)(2,1)S(1)}, u32[]{:S(2)}, u32[]{:S(2)}) %collective-permute-start) | collective-permute-done | bytes 65568 | tf_op jit(solution)/shard_map/ppermute | solution.py:482
  23.8 4.1 %msa_whole.1 = (bf16[512,256]{1,0:T(8,128)(2,1)S(1)}, bf16[256,128]{1,0:T(8,128)(2,1)S(1)}) custom-call(f32[1,128]{1,0:T(1,128)S(1)} %fusion.live_ref, bf16[16,32,256]{2,1,0:T(8,128)(2,1)S(1)} %all-to-all-done.blocks_ref, bf16[256,1280]{1,0:T(8,128)(2,1)S(1)} %pad_maximum_fusion.narrow_ref, bf16[256,1024]{1,0:T(8,128)(2,1)S(1)} %copy-done.12, ...), custom_call_target="tpu_custom_call" | custom-call | flops 2000000000 | bytes 10000000 | tf_op jit(solution)/shard_map/msa_whole/pallas_call | solution.py:531
  27.9 0.8 %collective-permute-done.1.rest_9_ = bf16[2,2,128,128]{3,2,1,0:T(8,128)(2,1)S(1)} collective-permute-done((bf16[2,2,128,128]{3,2,1,0:T(8,128)(2,1)S(1)}, bf16[2,2,128,128]{3,2,1,0:T(8,128)(2,1)S(1)}, u32[]{:S(2)}, u32[]{:S(2)}) %collective-permute-start.1) | collective-permute-done | bytes 131104 | tf_op jit(solution)/shard_map/ppermute | solution.py:482
  28.7 1.3 %collective-permute-start.2 = (bf16[256,128]{1,0:T(8,128)(2,1)S(1)}, bf16[256,128]{1,0:T(8,128)(2,1)S(1)}, u32[]{:S(2)}, u32[]{:S(2)}) collective-permute-start(bf16[256,128]{1,0:T(8,128)(2,1)S(1)} %get-tuple-element.27), channel_id=1, source_target_pairs={{0,8},{1,9},{2,10},{3,11},{4,12},{5,13},{6,14},{7,15},{8,0},{9,1},... | collective-permute-start | bytes 196616 | tf_op jit(solution)/shard_map/ppermute | solution.py:482
  29.9 3.9 %collective-permute-done.2 = bf16[256,128]{1,0:T(8,128)(2,1)S(1)} collective-permute-done((bf16[256,128]{1,0:T(8,128)(2,1)S(1)}, bf16[256,128]{1,0:T(8,128)(2,1)S(1)}, u32[]{:S(2)}, u32[]{:S(2)}) %collective-permute-start.2) | collective-permute-done | bytes 65568 | tf_op jit(solution)/shard_map/ppermute | solution.py:482
  33.9 1.3 %collective-permute-start.3 = (bf16[2,256,128]{2,1,0:T(8,128)(2,1)S(1)}, bf16[2,256,128]{2,1,0:T(8,128)(2,1)S(1)}, u32[]{:S(2)}, u32[]{:S(2)}) collective-permute-start(bf16[2,256,128]{2,1,0:T(8,128)(2,1)S(1)} %pad_maximum_fusion.2.rest_0_), channel_id=1, source_target_pairs={{0,4},{1,5},{2,6},{3,7},{4,0},{5,1},{6,2},{7,3},{8,12},{9,13},{10,... | collective-permute-start | bytes 393224 | tf_op jit(solution)/shard_map/ppermute | solution.py:482
  35.2 1.5 %collective-permute-start.10 = (bf16[2,2,128,128]{3,2,1,0:T(8,128)(2,1)S(1)}, bf16[2,2,128,128]{3,2,1,0:T(8,128)(2,1)S(1)}, u32[]{:S(2)}, u32[]{:S(2)}) collective-permute-start(bf16[2,2,128,128]{3,2,1,0:T(8,128)(2,1)S(1)} %pad_maximum_fusion.1.rest_8_), channel_id=1, source_target_pairs={{0,2},{1,3},{2,0},{3,1},{4,6},{5,7},{6,4},{7,5},{8,10},{9,11},{10,... | collective-permute-start | bytes 393224 | tf_op jit(solution)/shard_map/ppermute | solution.py:482
  36.7 0.6 collective-permute-start.4
  37.2 1.7 %collective-permute-done.3.rest_1_ = bf16[2,256,128]{2,1,0:T(8,128)(2,1)S(1)} collective-permute-done((bf16[2,256,128]{2,1,0:T(8,128)(2,1)S(1)}, bf16[2,256,128]{2,1,0:T(8,128)(2,1)S(1)}, u32[]{:S(2)}, u32[]{:S(2)}) %collective-permute-start.3) | collective-permute-done | bytes 131104 | tf_op jit(solution)/shard_map/ppermute | solution.py:482
  38.9 1.5 %collective-permute-start.5 = (bf16[2,256,128]{2,1,0:T(8,128)(2,1)S(1)}, bf16[2,256,128]{2,1,0:T(8,128)(2,1)S(1)}, u32[]{:S(2)}, u32[]{:S(2)}) collective-permute-start(bf16[2,256,128]{2,1,0:T(8,128)(2,1)S(1)} %collective-permute-done.3.rest_1_), channel_id=1, source_target_pairs={{0,2},{1,3},{2,0},{3,1},{4,6},{5,7},{6,4},{7,5},{8,10},{9,11},{10,... | collective-permute-start | bytes 393224 | tf_op jit(solution)/shard_map/ppermute | solution.py:482
  40.7 0.6 collective-permute-start.11
  41.3 0.3 collective-permute-done.10.rest_10_
  41.6 0.2 collective-permute-start.7
  41.8 2.3 %collective-permute-done.4.rest_2_ = bf16[2,256,128]{2,1,0:T(8,128)(2,1)S(1)} collective-permute-done((bf16[2,256,128]{2,1,0:T(8,128)(2,1)S(1)}, bf16[2,256,128]{2,1,0:T(8,128)(2,1)S(1)}, u32[]{:S(2)}, u32[]{:S(2)}) %collective-permute-start.4) | collective-permute-done | bytes 131104 | tf_op jit(solution)/shard_map/ppermute | solution.py:482
  44.1 1.4 %collective-permute-done.5.rest_3_ = bf16[2,256,128]{2,1,0:T(8,128)(2,1)S(1)} collective-permute-done((bf16[2,256,128]{2,1,0:T(8,128)(2,1)S(1)}, bf16[2,256,128]{2,1,0:T(8,128)(2,1)S(1)}, u32[]{:S(2)}, u32[]{:S(2)}) %collective-permute-start.5) | collective-permute-done | bytes 131104 | tf_op jit(solution)/shard_map/ppermute | solution.py:482
  45.5 0.2 compare_select_fusion
  45.8 0.1 select_n.11.bins_ref
  45.9 1.1 %collective-permute-done.11.rest_11_ = bf16[2,2,128,128]{3,2,1,0:T(8,128)(2,1)S(1)} collective-permute-done((bf16[2,2,128,128]{3,2,1,0:T(8,128)(2,1)S(1)}, bf16[2,2,128,128]{3,2,1,0:T(8,128)(2,1)S(1)}, u32[]{:S(2)}, u32[]{:S(2)}) %collective-permute-start.11) | collective-permute-done | bytes 131104 | tf_op jit(solution)/shard_map/ppermute | solution.py:482
  47.0 5.2 %pair_start.1 = (f32[16,128,128]{2,1,0:T(8,128)S(1)}, bf16[16,128,128]{2,1,0:T(8,128)(2,1)S(1)}, bf16[384,128]{1,0:T(8,128)(2,1)S(1)}, bf16[2048,128]{1,0:T(8,128)(2,1)S(1)}) custom-call(s32[1]{0:T(128)} %bitcast.4.place_ref, f32[1,128]{1,0:T(1,128)S(1)} %fusion.live_ref, s32[32,128]{1,0:T(8,128)S(1)} %select_n.11.bins_ref, bf16[66,128]{1,0:T(8,128)(2,1)S(1)} %copy-done.11, ...), custom_call_target="tpu_custom_call" | custom-call | tf_op jit(solution)/shard_map/pair_start/pallas_call | solution.py:571
  52.3 0.6 pair_gates.1
  52.9 1.2 %collective-permute-done.12.right_other_ref = bf16[2048,128]{1,0:T(8,128)(2,1)S(1)} collective-permute-done((bf16[2048,128]{1,0:T(8,128)(2,1)S(1)}, bf16[2048,128]{1,0:T(8,128)(2,1)S(1)}, u32[]{:S(2)}, u32[]{:S(2)}) %collective-permute-start.12) | collective-permute-done | bytes 524320 | tf_op jit(solution)/shard_map/ppermute | solution.py:482
  54.2 8.6 %pair_triangles.1 = (f32[2,128,128]{2,1,0:T(8,128)S(1)}, f32[2,128,128]{2,1,0:T(8,128)S(1)}, f32[2,128,128]{2,1,0:T(8,128)S(1)}, bf16[768,128]{1,0:T(8,128)(2,1)S(1)}, bf16[128,512]{1,0:T(8,128)(2,1)S(1)}) custom-call(s32[1]{0:T(128)} %bitcast.4.place_ref, f32[16,128,128]{2,1,0:T(8,128)S(1)} %get-tuple-element.29.pair_mid_ref, ...), custom_call_target="tpu_custom_call" | custom-call | tf_op jit(solution)/shard_map/pair_triangles/pallas_call | solution.py:611
  62.8 0.2 collective-permute-start.13
  63.0 0.8 %reshape.59 = bf16[128,4,256]{2,1,0:T(4,128)(2,1)} reshape(bf16[512,256]{1,0:T(8,128)(2,1)S(1)} %get-tuple-element.24) | data formatting | bytes 524288 | tf_op jit(solution)/shard_map/reshape | solution.py:637
  63.7 0.5 collective-permute-done.13.other_part_ref
  64.2 1.5 %pair_finish.1 = bf16[256,128]{1,0:T(8,128)(2,1)} custom-call(f32[2,128,128]{2,1,0:T(8,128)S(1)} %get-tuple-element.35.own_pair_ref, f32[2,128,128]{2,1,0:T(8,128)S(1)} %get-tuple-element.36.own_part_ref, f32[2,128,128]{2,1,0:T(8,128)S(1)} %collective-permute-done.13.other_part_ref, bf16[768,128]{1,0:T(8,128)(2,1)S(1)} %get-tuple-element.38.narrow_ref, ...), custom_call_target="tpu_custom_call" | custom-call | tf_op jit(solution)/shard_map/pair_finish/pallas_call | solution.py:629
  (51 shorter events, 0.7 us)
Async XLA Ops:
  0.6 1.0 %copy-start.1 = (bf16[8,64,256]{2,1,0:T(8,128)(2,1)S(1)}, bf16[8,64,256]{2,1,0:T(8,128)(2,1)}, u32[]{:S(2)}) copy-start(bf16[8,64,256]{2,1,0:T(8,128)(2,1)} %rows_ref.1) | copy-start | bytes 786436
  2.4 12.7 %copy-start.17 = (s32[128]{0:T(128)S(1)}, s32[128]{0:T(128)}, u32[]{:S(2)}) copy-start(s32[128]{0:T(128)} %param.26) | copy-start | bytes 1540
  3.6 20.1 %copy-start.12 = (bf16[256,1024]{1,0:T(8,128)(2,1)S(1)}, bf16[256,1024]{1,0:T(8,128)(2,1)}, u32[]{:S(2)}) copy-start(bf16[256,1024]{1,0:T(8,128)(2,1)} %up_ref.1) | copy-start | bytes 1572868
  3.6 20.1 %copy-start.13 = (bf16[1024,256]{1,0:T(8,128)(2,1)S(1)}, bf16[1024,256]{1,0:T(8,128)(2,1)}, u32[]{:S(2)}) copy-start(bf16[1024,256]{1,0:T(8,128)(2,1)} %down_ref.1) | copy-start | bytes 1572868
  3.6 20.1 %copy-start.14 = (bf16[256,64]{0,1:T(8,128)(2,1)S(1)}, bf16[256,64]{0,1:T(8,128)(2,1)}, u32[]{:S(2)}) copy-start(bf16[256,64]{0,1:T(8,128)(2,1)} %param.34) | copy-start | bytes 98308
  3.6 20.0 %all-to-all-start = ((bf16[16,32,256]{2,1,0:T(8,128)(2,1)}), bf16[16,32,256]{2,1,0:T(8,128)(2,1)S(1)}, u32[]{:S(2)}, u32[]{:S(2)}) async-start(bf16[16,32,256]{2,1,0:T(8,128)(2,1)} %get-tuple-element.21), calls=%async_computation | async-start | bytes 524288 | tf_op jit(solution)/shard_map/all_to_all | solution.py:525
  11.1 12.5 %collective-permute-start = (bf16[2,128,128]{2,1,0:T(8,128)(2,1)S(1)}, bf16[2,128,128]{2,1,0:T(8,128)(2,1)S(1)}, u32[]{:S(2)}, u32[]{:S(2)}) collective-permute-start(bf16[2,128,128]{2,1,0:T(8,128)(2,1)S(1)} %get-tuple-element.22), channel_id=1, source_target_pairs={{0,8},{1,9},{2,10},{3,11},{4,12},{5,13},{6,14},{7,15},{8,0},{9,1},... | collective-permute-start | bytes 196616 | tf_op jit(solution)/shard_map/ppermute | solution.py:482
  23.6 5.1 %collective-permute-start.1 = (bf16[2,2,128,128]{3,2,1,0:T(8,128)(2,1)S(1)}, bf16[2,2,128,128]{3,2,1,0:T(8,128)(2,1)S(1)}, u32[]{:S(2)}, u32[]{:S(2)}) collective-permute-start(bf16[2,2,128,128]{3,2,1,0:T(8,128)(2,1)S(1)} %pad_maximum_fusion.1.rest_8_), channel_id=1, source_target_pairs={{0,4},{1,5},{2,6},{3,7},{4,0},{5,1},{6,2},{7,3},{8,12},{9,13},{10,... | collective-permute-start | bytes 393224 | tf_op jit(solution)/shard_map/ppermute | solution.py:482
  23.7 16.7 %copy-start.15 = (s32[64]{0:T(128)S(1)}, s32[64]{0:T(128)}, u32[]{:S(2)}) copy-start(s32[64]{0:T(128)} %param.24) | copy-start | bytes 772
  23.7 16.9 %copy-start.16 = (s32[64]{0:T(128)S(1)}, s32[64]{0:T(128)}, u32[]{:S(2)}) copy-start(s32[64]{0:T(128)} %param.25) | copy-start | bytes 772
  23.7 23.3 %copy-start = (bf16[1024,128]{1,0:T(8,128)(2,1)S(1)}, bf16[1024,128]{1,0:T(8,128)(2,1)}, u32[]{:S(2)}) copy-start(bf16[1024,128]{1,0:T(8,128)(2,1)} %rest_12_.1) | copy-start | bytes 786436
  23.7 23.3 %copy-start.2 = (bf16[128,512]{1,0:T(8,128)(2,1)S(1)}, bf16[128,512]{1,0:T(8,128)(2,1)}, u32[]{:S(2)}) copy-start(bf16[128,512]{1,0:T(8,128)(2,1)} %rest_13_.1) | copy-start | bytes 393220
  23.7 23.3 %copy-start.7 = (bf16[128,128]{1,0:T(8,128)(2,1)S(1)}, bf16[128,128]{1,0:T(8,128)(2,1)}, u32[]{:S(2)}) copy-start(bf16[128,128]{1,0:T(8,128)(2,1)} %rest_14_.1) | copy-start | bytes 98308
  23.7 23.3 %copy-start.11 = (bf16[66,128]{1,0:T(8,128)(2,1)S(1)}, bf16[66,128]{1,0:T(8,128)(2,1)}, u32[]{:S(2)}) copy-start(bf16[66,128]{1,0:T(8,128)(2,1)} %table_ref.1) | copy-start | bytes 50692
  28.7 5.2 %collective-permute-start.2 = (bf16[256,128]{1,0:T(8,128)(2,1)S(1)}, bf16[256,128]{1,0:T(8,128)(2,1)S(1)}, u32[]{:S(2)}, u32[]{:S(2)}) collective-permute-start(bf16[256,128]{1,0:T(8,128)(2,1)S(1)} %get-tuple-element.27), channel_id=1, source_target_pairs={{0,8},{1,9},{2,10},{3,11},{4,12},{5,13},{6,14},{7,15},{8,0},{9,1},... | collective-permute-start | bytes 196616 | tf_op jit(solution)/shard_map/ppermute | solution.py:482
  33.9 5.0 %collective-permute-start.3 = (bf16[2,256,128]{2,1,0:T(8,128)(2,1)S(1)}, bf16[2,256,128]{2,1,0:T(8,128)(2,1)S(1)}, u32[]{:S(2)}, u32[]{:S(2)}) collective-permute-start(bf16[2,256,128]{2,1,0:T(8,128)(2,1)S(1)} %pad_maximum_fusion.2.rest_0_), channel_id=1, source_target_pairs={{0,4},{1,5},{2,6},{3,7},{4,0},{5,1},{6,2},{7,3},{8,12},{9,13},{10,... | collective-permute-start | bytes 393224 | tf_op jit(solution)/shard_map/ppermute | solution.py:482
  35.2 6.4 %collective-permute-start.10 = (bf16[2,2,128,128]{3,2,1,0:T(8,128)(2,1)S(1)}, bf16[2,2,128,128]{3,2,1,0:T(8,128)(2,1)S(1)}, u32[]{:S(2)}, u32[]{:S(2)}) collective-permute-start(bf16[2,2,128,128]{3,2,1,0:T(8,128)(2,1)S(1)} %pad_maximum_fusion.1.rest_8_), channel_id=1, source_target_pairs={{0,2},{1,3},{2,0},{3,1},{4,6},{5,7},{6,4},{7,5},{8,10},{9,11},{10,... | collective-permute-start | bytes 393224 | tf_op jit(solution)/shard_map/ppermute | solution.py:482
  36.7 7.5 %collective-permute-start.4 = (bf16[2,256,128]{2,1,0:T(8,128)(2,1)S(1)}, bf16[2,256,128]{2,1,0:T(8,128)(2,1)S(1)}, u32[]{:S(2)}, u32[]{:S(2)}) collective-permute-start(bf16[2,256,128]{2,1,0:T(8,128)(2,1)S(1)} %pad_maximum_fusion.2.rest_0_), channel_id=1, source_target_pairs={{0,2},{1,3},{2,0},{3,1},{4,6},{5,7},{6,4},{7,5},{8,10},{9,11},{10,... | collective-permute-start | bytes 393224 | tf_op jit(solution)/shard_map/ppermute | solution.py:482
  38.9 6.6 %collective-permute-start.5 = (bf16[2,256,128]{2,1,0:T(8,128)(2,1)S(1)}, bf16[2,256,128]{2,1,0:T(8,128)(2,1)S(1)}, u32[]{:S(2)}, u32[]{:S(2)}) collective-permute-start(bf16[2,256,128]{2,1,0:T(8,128)(2,1)S(1)} %collective-permute-done.3.rest_1_), channel_id=1, source_target_pairs={{0,2},{1,3},{2,0},{3,1},{4,6},{5,7},{6,4},{7,5},{8,10},{9,11},{10,... | collective-permute-start | bytes 393224 | tf_op jit(solution)/shard_map/ppermute | solution.py:482
  40.7 6.2 %collective-permute-start.11 = (bf16[2,2,128,128]{3,2,1,0:T(8,128)(2,1)S(1)}, bf16[2,2,128,128]{3,2,1,0:T(8,128)(2,1)S(1)}, u32[]{:S(2)}, u32[]{:S(2)}) collective-permute-start(bf16[2,2,128,128]{3,2,1,0:T(8,128)(2,1)S(1)} %collective-permute-done.1.rest_9_), channel_id=1, source_target_pairs={{0,2},{1,3},{2,0},{3,1},{4,6},{5,7},{6,4},{7,5},{8,10},{9,11},{10,... | collective-permute-start | bytes 393224 | tf_op jit(solution)/shard_map/ppermute | solution.py:482
  41.3 5.6 %collective-permute-start.6 = (bf16[2,256,128]{2,1,0:T(8,128)(2,1)S(1)}, bf16[2,256,128]{2,1,0:T(8,128)(2,1)S(1)}, u32[]{:S(2)}, u32[]{:S(2)}) collective-permute-start(bf16[2,256,128]{2,1,0:T(8,128)(2,1)S(1)} %pad_maximum_fusion.2.rest_0_), channel_id=1, source_target_pairs={{0,1},{1,0},{2,3},{3,2},{4,5},{5,4},{6,7},{7,6},{8,9},{9,8},{10,11... | collective-permute-start | bytes 393224 | tf_op jit(solution)/shard_map/ppermute | solution.py:482
  41.6 5.3 %collective-permute-start.7 = (bf16[2,256,128]{2,1,0:T(8,128)(2,1)S(1)}, bf16[2,256,128]{2,1,0:T(8,128)(2,1)S(1)}, u32[]{:S(2)}, u32[]{:S(2)}) collective-permute-start(bf16[2,256,128]{2,1,0:T(8,128)(2,1)S(1)} %collective-permute-done.3.rest_1_), channel_id=1, source_target_pairs={{0,1},{1,0},{2,3},{3,2},{4,5},{5,4},{6,7},{7,6},{8,9},{9,8},{10,11... | collective-permute-start | bytes 393224 | tf_op jit(solution)/shard_map/ppermute | solution.py:482
  44.1 2.8 %collective-permute-start.8 = (bf16[2,256,128]{2,1,0:T(8,128)(2,1)S(1)}, bf16[2,256,128]{2,1,0:T(8,128)(2,1)S(1)}, u32[]{:S(2)}, u32[]{:S(2)}) collective-permute-start(bf16[2,256,128]{2,1,0:T(8,128)(2,1)S(1)} %collective-permute-done.4.rest_2_), channel_id=1, source_target_pairs={{0,1},{1,0},{2,3},{3,2},{4,5},{5,4},{6,7},{7,6},{8,9},{9,8},{10,11... | collective-permute-start | bytes 393224 | tf_op jit(solution)/shard_map/ppermute | solution.py:482
  45.5 1.4 %collective-permute-start.9 = (bf16[2,256,128]{2,1,0:T(8,128)(2,1)S(1)}, bf16[2,256,128]{2,1,0:T(8,128)(2,1)S(1)}, u32[]{:S(2)}, u32[]{:S(2)}) collective-permute-start(bf16[2,256,128]{2,1,0:T(8,128)(2,1)S(1)} %collective-permute-done.5.rest_3_), channel_id=1, source_target_pairs={{0,1},{1,0},{2,3},{3,2},{4,5},{5,4},{6,7},{7,6},{8,9},{9,8},{10,11... | collective-permute-start | bytes 393224 | tf_op jit(solution)/shard_map/ppermute | solution.py:482
  52.2 2.0 %collective-permute-start.12 = (bf16[2048,128]{1,0:T(8,128)(2,1)S(1)}, bf16[2048,128]{1,0:T(8,128)(2,1)S(1)}, u32[]{:S(2)}, u32[]{:S(2)}) collective-permute-start(bf16[2048,128]{1,0:T(8,128)(2,1)S(1)} %get-tuple-element.34.right_own_ref), channel_id=1, source_target_pairs={{0,1},{1,0},{2,3},{3,2},{4,5},{5,4},{6,7},{7,6},{8,9},{9,8},{10,11... | collective-permute-start | bytes 1572872 | tf_op jit(solution)/shard_map/ppermute | solution.py:482
  52.3 1.9 %copy-start.3 = (bf16[128,512]{1,0:T(8,128)(2,1)S(1)}, bf16[128,512]{1,0:T(8,128)(2,1)}, u32[]{:S(2)}) copy-start(bf16[128,512]{1,0:T(8,128)(2,1)} %rest_1_.1) | copy-start | bytes 393220
  52.3 1.9 %copy-start.4 = (bf16[128,512]{1,0:T(8,128)(2,1)S(1)}, bf16[128,512]{1,0:T(8,128)(2,1)}, u32[]{:S(2)}) copy-start(bf16[128,512]{1,0:T(8,128)(2,1)} %rest_4_.1) | copy-start | bytes 393220
  52.3 1.9 %copy-start.5 = (bf16[512,128]{1,0:T(8,128)(2,1)S(1)}, bf16[512,128]{1,0:T(8,128)(2,1)}, u32[]{:S(2)}) copy-start(bf16[512,128]{1,0:T(8,128)(2,1)} %rest_5_.1) | copy-start | bytes 393220
  52.3 1.9 %copy-start.8 = (bf16[128,128]{1,0:T(8,128)(2,1)S(1)}, bf16[128,128]{1,0:T(8,128)(2,1)}, u32[]{:S(2)}) copy-start(bf16[128,128]{1,0:T(8,128)(2,1)} %rest_0_.1) | copy-start | bytes 98308
  52.3 1.9 %copy-start.9 = (bf16[128,128]{1,0:T(8,128)(2,1)S(1)}, bf16[128,128]{1,0:T(8,128)(2,1)}, u32[]{:S(2)}) copy-start(bf16[128,128]{1,0:T(8,128)(2,1)} %rest_2_.1) | copy-start | bytes 98308
  52.3 1.9 %copy-start.10 = (bf16[128,128]{1,0:T(8,128)(2,1)S(1)}, bf16[128,128]{1,0:T(8,128)(2,1)}, u32[]{:S(2)}) copy-start(bf16[128,128]{1,0:T(8,128)(2,1)} %rest_3_.1) | copy-start | bytes 98308
  62.8 1.4 %collective-permute-start.13 = (f32[2,128,128]{2,1,0:T(8,128)S(1)}, f32[2,128,128]{2,1,0:T(8,128)S(1)}, u32[]{:S(2)}, u32[]{:S(2)}) collective-permute-start(f32[2,128,128]{2,1,0:T(8,128)S(1)} %get-tuple-element.37), channel_id=1, source_target_pairs={{0,1},{1,0},{2,3},{3,2},{4,5},{5,4},{6,7},{7,6},{8,9},{9,8},{10,11... | collective-permute-start | bytes 393224 | tf_op jit(solution)/shard_map/ppermute | solution.py:482
  (1 other events, 0.8 us)
